TPU v7x, 32 devices: a whole 2x2x4 slice. The times are simulated.
32 devices in a mesh: depth: 8 (over y, x, core), rows: 4 (over z).
Axes of the slice: x: 2, y: 2, z: 4, core: 2. Of those that a mesh axis runs over, the one named last changes fastest.
Arguments:
- volume: int32 [2, 64, 128, 1024], P(None, 'depth', 'rows'), may hold values from 0 to 255
- color_map: int32 [3, 256], replicated, may hold values from 0 to 255
- alpha_map: int32 [256], replicated, may hold values from 0 to 255
Outputs:
- image: float32 [4, 128, 1024], P(None, ('rows', 'depth'))
All inputs are finite; a program needn't handle non-finite values.
Results may differ from a plain program's by a relative error of at most 0.003.
Values may be sent and summed in bfloat16 or wider, within the bound.
No kernel may reach another device: no remote copies, remote signals or barrier semaphores. Data moves between devices by JAX's collectives and lax.ppermute only.
A program may use at most 64 MiB of HBM per device.

v0:
```python
import functools

import jax
import jax.numpy as jnp
from jax import lax
from jax.experimental import pallas as pl
from jax.experimental.pallas import tpu as pltpu
from jax.sharding import PartitionSpec as P

AMBIENT = 0.3
DIFFUSE = 0.7
LIGHT_DEPTH = 0.48 * DIFFUSE
LIGHT_ROWS = 0.6 * DIFFUSE
LIGHT_COLS = 0.64 * DIFFUSE
OPACITY = 4.0
LANES = 128
SUBLANES = 8
WHOLE = pl.BlockSpec(memory_space=pltpu.VMEM)


def parity(axis):
    return lax.axis_index(axis) % 2


def ends(axis):
    position = lax.axis_index(axis)
    return position == 0, position == lax.axis_size(axis) - 1


def edges_kernel(volume_ref, rows_far_out, rows_near_out, far_out, near_out, strip_ref, plane_ref, sems):
    _, slices, height, _ = volume_ref.shape
    odd, odd_row = parity("depth"), parity("rows")
    last_tile = height // SUBLANES - 1

    def tile(i):
        return pl.ds(pl.multiple_of(i * SUBLANES, SUBLANES), SUBLANES)

    copies = [
        pltpu.make_async_copy(volume_ref.at[0, :, tile((1 - odd_row) * last_tile)], strip_ref.at[0], sems.at[0]),
        pltpu.make_async_copy(volume_ref.at[0, :, tile(odd_row * last_tile)], strip_ref.at[1], sems.at[1]),
        pltpu.make_async_copy(volume_ref.at[0, odd * (slices - 1)], plane_ref.at[0], sems.at[2]),
        pltpu.make_async_copy(volume_ref.at[0, (1 - odd) * (slices - 1)], plane_ref.at[1], sems.at[3]),
    ]
    for copy in copies:
        copy.start()

    def narrow(values):
        return values.astype(jnp.float32).astype(jnp.bfloat16)

    copies[0].wait()
    rows_near_out[...] = narrow(jnp.where(odd_row == 1, strip_ref[0, :, 0, :], strip_ref[0, :, SUBLANES - 1, :]))
    copies[1].wait()
    rows_far_out[...] = narrow(jnp.where(odd_row == 1, strip_ref[1, :, SUBLANES - 1, :], strip_ref[1, :, 0, :]))
    copies[2].wait()
    far_out[...] = narrow(plane_ref[0])
    copies[3].wait()
    near_out[...] = narrow(plane_ref[1])


def cut_edges(volume):
    _, slices, height, columns = volume.shape
    plane = jax.ShapeDtypeStruct((height, columns), jnp.bfloat16)
    strip = jax.ShapeDtypeStruct((slices, columns), jnp.bfloat16)
    return pl.pallas_call(
        edges_kernel,
        in_specs=[pl.BlockSpec(memory_space=pl.ANY)],
        out_specs=[WHOLE] * 4,
        out_shape=[strip, strip, plane, plane],
        scratch_shapes=[
            pltpu.VMEM((2, slices, SUBLANES, columns), jnp.int32),
            pltpu.VMEM((2, height, columns), jnp.int32),
            pltpu.SemaphoreType.DMA((4,)),
        ],
        compiler_params=pltpu.CompilerParams(vmem_limit_bytes=52 * 1024 * 1024),
    )(volume)


def pick(entries, places):
    dims = lax.GatherDimensionNumbers(
        offset_dims=(),
        collapsed_slice_dims=(1,),
        start_index_map=(1,),
        operand_batching_dims=(0,),
        start_indices_batching_dims=(0,),
    )
    return lax.gather(entries, places[..., None], dims, (1, 1), mode=lax.GatherScatterMode.PROMISE_IN_BOUNDS)


def shade(grad_depth, facing, squares):
    facing = facing + LIGHT_DEPTH * grad_depth
    squares = squares + grad_depth * grad_depth
    return AMBIENT + jnp.abs(facing) * lax.rsqrt(jnp.maximum(squares, 4.0))


def interior_kernel(
    opacity_scale,
    volume_ref,
    color_ref,
    alpha_ref,
    base_ref,
    face_ref,
    square_ref,
    lit_ref,
    grad_ref,
    strip_ref,
    pair_ref,
    held_ref,
):
    _, slices, height, columns = volume_ref.shape
    tiles = height // SUBLANES
    chunks = columns // LANES
    tile = (SUBLANES, LANES)
    strip = (slices, LANES)

    packed = color_ref[0:1, :] + color_ref[1:2, :] * 256 + color_ref[2:3, :] * 65536
    color_low, color_high = packed[:, :LANES], packed[:, LANES:]
    alpha_both = alpha_ref[0:1, :LANES] + alpha_ref[0:1, LANES:] * 256

    def colors(value, tables):
        low, high = tables
        place = value & (LANES - 1)
        color = jnp.where(value < LANES, pick(low, place), pick(high, place))
        parts = (color & 255, lax.shift_right_logical(color, 8) & 255, lax.shift_right_logical(color, 16))
        return [part.astype(jnp.float32) for part in parts]

    def opacity(level, table):
        entry = pick(table, level & (LANES - 1))
        entry = lax.shift_right_logical(entry, lax.shift_right_logical(level & LANES, 4)) & 255
        return entry.astype(jnp.float32) * opacity_scale

    tile_colors = [jnp.broadcast_to(t, tile) for t in (color_low, color_high)]
    tile_alpha = jnp.broadcast_to(alpha_both, tile)
    strip_colors = [jnp.broadcast_to(t, strip) for t in (color_low, color_high)]

    def masks(shape):
        lane = lax.broadcasted_iota(jnp.int32, shape, 1)
        row = lax.broadcasted_iota(jnp.int32, shape, 0)
        return lane == 0, lane == LANES - 1, row == 0, row == shape[0] - 1

    first_lane, last_lane, first_row, last_row = masks(tile)
    strip_first_lane, strip_last_lane, front, back = masks(strip)

    pairs = slices // 2
    top = SUBLANES

    def clear(j, carry):
        pair_ref[j] = jnp.zeros(pair_ref.shape[1:], jnp.int32)
        return carry

    clear(0, 0)
    clear(chunks + 1, 0)
    margin = jnp.zeros((pairs, SUBLANES, LANES), jnp.int32)

    def pack(j, carry):
        here = pl.ds(pl.multiple_of(j * LANES, LANES), LANES)
        pair_ref[j + 1, :, :top] = margin
        pair_ref[j + 1, :, top + height :] = margin
        for p in range(pairs):
            pair_ref[j + 1, p, top : top + height] = volume_ref[0, p, :, here] + lax.shift_left(
                volume_ref[0, p + pairs, :, here], 16
            )
        return carry

    lax.fori_loop(0, chunks, pack, 0)

    def split(difference):
        low = lax.shift_right_arithmetic(lax.shift_left(difference, 16), 16)
        high = lax.shift_right_arithmetic(difference + 32768, 16)
        return low.astype(jnp.float32), high.astype(jnp.float32)

    def across(left_value, value, right_value, first, last):
        west = pltpu.roll(jnp.where(last, left_value, value), 1, 1)
        east = pltpu.roll(jnp.where(first, right_value, value), LANES - 1, 1)
        return split(east - west)

    def chunk(j, carry):
        here = pl.ds(pl.multiple_of(j * LANES, LANES), LANES)

        for r in range(tiles):
            rows = slice(r * SUBLANES, (r + 1) * SUBLANES)
            values = [volume_ref[0, s, rows, here] for s in range(slices)]

            def words(c, p, offset=0):
                return pair_ref[c, p, top + r * SUBLANES + offset : top + (r + 1) * SUBLANES + offset, :]

            down, right = [], []
            for p in range(pairs):
                down.append(split(words(j + 1, p, 1) - words(j + 1, p, -1)))
                right.append(across(words(j, p), words(j + 1, p), words(j + 2, p), first_lane, last_lane))
            remaining = jnp.ones(tile, jnp.float32)
            sums = [jnp.zeros(tile, jnp.float32) for _ in range(3)]
            for s in range(slices):
                value = values[s]
                grad_rows = down[s % pairs][s // pairs]
                grad_cols = right[s % pairs][s // pairs]
                squares = grad_rows * grad_rows + grad_cols * grad_cols
                facing = LIGHT_ROWS * grad_rows + LIGHT_COLS * grad_cols
                weight = remaining * opacity(volume_ref[1, s, rows, here], tile_alpha)
                remaining = remaining - weight
                if r == 0:
                    held_ref[0, s : s + 1, :] = weight[:1]
                    weight = jnp.where(first_row, 0.0, weight)
                if r == tiles - 1:
                    held_ref[1, s : s + 1, :] = weight[SUBLANES - 1 :]
                    weight = jnp.where(last_row, 0.0, weight)
                emitted = colors(value, tile_colors)
                if 0 < s < slices - 1:
                    grad_depth = (values[s + 1] - values[s - 1]).astype(jnp.float32)
                    weight = weight * shade(grad_depth, facing, squares)
                    for c in range(3):
                        sums[c] = sums[c] + emitted[c] * weight
                else:
                    end = int(s > 0)
                    face_ref[end, rows, here] = facing
                    square_ref[end, rows, here] = squares
                    weight = weight * (1.0 / 255.0)
                    for c in range(3):
                        lit_ref[end, c, rows, here] = emitted[c] * weight
            for c in range(3):
                base_ref[c, rows, here] = sums[c] * (1.0 / 255.0)
            base_ref[3, rows, here] = 1.0 - remaining

        for q, (edge, inner) in enumerate(((0, 1), (height - 1, height - 2))):
            value = volume_ref[0, :, edge, here]
            behind = pltpu.roll(jnp.where(back, 0, value), 1, 0)
            ahead = pltpu.roll(jnp.where(front, 0, value), slices - 1, 0)
            grad_ref[q, 0, :, here] = (ahead - behind).astype(jnp.float32)
            grad_ref[q, 1, :, here] = volume_ref[0, :, inner, here].astype(jnp.float32)
            word = pair_ref[j + 1, :, top + edge, :]
            low, high = across(
                pair_ref[j, :, top + edge, :],
                word,
                pair_ref[j + 2, :, top + edge, :],
                strip_first_lane[:pairs],
                strip_last_lane[:pairs],
            )
            grad_ref[q, 2, :pairs, here] = low
            grad_ref[q, 2, pairs:, here] = high
            weight = held_ref[q] * (1.0 / 255.0)
            emitted = colors(value, strip_colors)
            for c in range(3):
                strip_ref[q, c, :, here] = emitted[c] * weight
        return carry

    lax.fori_loop(0, chunks, chunk, 0)


def march_interior(volume, color_map, alpha_map, depth_count):
    _, slices, height, columns = volume.shape
    opacity_scale = OPACITY / (255.0 * slices * depth_count)
    shapes = [
        (4, height, columns),
        (2, height, columns),
        (2, height, columns),
        (2, 3, height, columns),
        (2, 3, slices, columns),
        (2, 3, slices, columns),
    ]
    voxels = slices * height * columns
    return pl.pallas_call(
        functools.partial(interior_kernel, opacity_scale),
        in_specs=[WHOLE] * 3,
        out_specs=[WHOLE] * len(shapes),
        out_shape=[jax.ShapeDtypeStruct(shape, jnp.float32) for shape in shapes],
        scratch_shapes=[
            pltpu.VMEM((columns // LANES + 2, slices // 2, height + 2 * SUBLANES, LANES), jnp.int32),
            pltpu.VMEM((2, slices, LANES), jnp.float32),
        ],
        compiler_params=pltpu.CompilerParams(vmem_limit_bytes=24 * 1024 * 1024),
        cost_estimate=pl.CostEstimate(flops=voxels * 80, bytes_accessed=voxels * 20, transcendentals=voxels),
    )(volume, color_map, alpha_map.reshape(1, -1))


def edge_kernel(
    share, volume_ref, base_ref, face_ref, square_ref, lit_ref, grad_ref, strip_ref, rows_near_ref, rows_far_ref, far_ref, near_ref, out_ref
):
    _, slices, height, columns = volume_ref.shape
    tiles = height // SUBLANES
    tile = (SUBLANES, LANES)
    row = lax.broadcasted_iota(jnp.int32, tile, 0)
    first_row, last_row = row == 0, row == SUBLANES - 1
    level = lax.broadcasted_iota(jnp.int32, (slices, LANES), 0)
    front, back = level == 0, level == slices - 1
    odd, odd_row = parity("depth") == 1, parity("rows") == 1
    front_end, back_end = ends("depth")
    top_end, bottom_end = ends("rows")

    def chunk(j, carry):
        here = pl.ds(pl.multiple_of(j * LANES, LANES), LANES)
        rows_near = rows_near_ref[:, here].astype(jnp.float32)
        rows_far = rows_far_ref[:, here].astype(jnp.float32)
        above = jnp.where(top_end, 0.0, jnp.where(odd_row, rows_near, rows_far))
        below = jnp.where(bottom_end, 0.0, jnp.where(odd_row, rows_far, rows_near))
        far = far_ref[:, here].astype(jnp.float32)
        near = near_ref[:, here].astype(jnp.float32)
        before = jnp.where(front_end, 0.0, jnp.where(odd, near, far))
        after = jnp.where(back_end, 0.0, jnp.where(odd, far, near))
        extra = []
        for q, edge in enumerate((0, height - 1)):
            inner = grad_ref[q, 1, :, here]
            grad_rows = below - inner if q else inner - above
            grad_cols = grad_ref[q, 2, :, here]
            grad_depth = grad_ref[q, 0, :, here] + jnp.where(
                back, after[edge : edge + 1], jnp.where(front, -before[edge : edge + 1], 0.0)
            )
            shading = shade(
                grad_depth,
                LIGHT_ROWS * grad_rows + LIGHT_COLS * grad_cols,
                grad_rows * grad_rows + grad_cols * grad_cols,
            )
            extra.append([jnp.sum(strip_ref[q, c, :, here] * shading, axis=0, keepdims=True) for c in range(3)])
        for r in range(tiles):
            rows = slice(r * SUBLANES, (r + 1) * SUBLANES)
            planes = [base_ref[c, rows, here] for c in range(4)]
            for end in range(2):
                if end:
                    grad_depth = after[rows] - volume_ref[0, slices - 2, rows, here].astype(jnp.float32)
                else:
                    grad_depth = volume_ref[0, 1, rows, here].astype(jnp.float32) - before[rows]
                shading = shade(grad_depth, face_ref[end, rows, here], square_ref[end, rows, here])
                for c in range(3):
                    planes[c] = planes[c] + lit_ref[end, c, rows, here] * shading
            for c in range(3):
                if r == 0:
                    planes[c] = planes[c] + jnp.where(first_row, extra[0][c], 0.0)
                if r == tiles - 1:
                    planes[c] = planes[c] + jnp.where(last_row, extra[1][c], 0.0)
            for first in range(0, SUBLANES, share):
                block = jnp.concatenate([plane[first : first + share] for plane in planes], axis=0)
                out_ref[(r * SUBLANES + first) // share, :, here] = block.astype(jnp.bfloat16)
        return carry

    lax.fori_loop(0, columns // LANES, chunk, 0)


def add_edges(volume, interior, halos, depth_count):
    _, slices, height, columns = volume.shape
    share = height // depth_count
    return pl.pallas_call(
        functools.partial(edge_kernel, share),
        in_specs=[WHOLE] * 11,
        out_specs=WHOLE,
        out_shape=jax.ShapeDtypeStruct((depth_count, 4 * share, columns), jnp.bfloat16),
        compiler_params=pltpu.CompilerParams(vmem_limit_bytes=24 * 1024 * 1024),
    )(volume, *interior, *halos)


def finish_kernel(parts_ref, out_ref):
    count = parts_ref.shape[0]
    _, share, columns = out_ref.shape
    remaining = jnp.ones((share, columns), jnp.float32)
    sums = [jnp.zeros((share, columns), jnp.float32) for _ in range(3)]
    for k in range(count):
        part = parts_ref[k].astype(jnp.float32)
        for c in range(3):
            sums[c] = sums[c] + remaining * part[c * share : (c + 1) * share]
        remaining = remaining - remaining * part[3 * share :]
    for c in range(3):
        out_ref[c] = sums[c]
    out_ref[3] = 1.0 - remaining


def finish(parts, share):
    columns = parts.shape[2]
    return pl.pallas_call(
        finish_kernel,
        in_specs=[WHOLE],
        out_specs=WHOLE,
        out_shape=jax.ShapeDtypeStruct((4, share, columns), jnp.float32),
        compiler_params=pltpu.CompilerParams(vmem_limit_bytes=4 * 1024 * 1024),
    )(parts)


def swapped(values, axis, start):
    depth_count, row_count = lax.axis_size("depth"), lax.axis_size("rows")
    size = lax.axis_size(axis)
    perm = []
    for d in range(depth_count):
        for r in range(row_count):
            i = d if axis == "depth" else r
            j = i + 1 if i % 2 == start else i - 1
            if 0 <= j < size:
                e, q = (j, r) if axis == "depth" else (d, j)
            elif axis == "depth":
                e, q = (size - 1 - d, r)
            else:
                e, q = (d ^ 1, r)
            perm.append((d * row_count + r, e * row_count + q))
    return lax.ppermute(values, ("depth", "rows"), perm)


def body(volume, color_map, alpha_map):
    depth_count = lax.axis_size("depth")
    share = volume.shape[2] // depth_count
    rows_far, rows_near, far, near = cut_edges(volume)
    rows_far = swapped(rows_far, "rows", 1)
    rows_near = swapped(rows_near, "rows", 0)
    far = swapped(far, "depth", 1)
    near = swapped(near, "depth", 0)
    interior = march_interior(volume, color_map, alpha_map, depth_count)
    parts = add_edges(volume, interior, (rows_near, rows_far, far, near), depth_count)
    parts = lax.all_to_all(parts, "depth", 0, 0, tiled=True)
    return finish(parts, share)


def solution(mesh):
    in_specs = (P(None, "depth", "rows", None), P(), P())
    out_specs = P(None, ("rows", "depth"), None)
    return jax.shard_map(body, mesh=mesh, in_specs=in_specs, out_specs=out_specs, check_vma=False)
```

profile of v0, /device:TPU:0, one launch (start us, length us, event | category | flops | bytes accessed | tf_op | source)
XLA Modules:
  0.0 20.2 jit_solution(825795526451236500)
XLA Ops:
  0.0 0.0 copy-start
  0.0 0.0 copy-start.2
  0.0 0.0 copy-start.1
  0.0 1.3 %shard_map.38 = (bf16[8,1024]{1,0:T(8,128)(2,1)S(1)}, bf16[8,1024]{1,0:T(8,128)(2,1)S(1)}, bf16[32,1024]{1,0:T(8,128)(2,1)S(1)}, bf16[32,1024]{1,0:T(8,128)(2,1)S(1)}) custom-call(s32[2,8,32,1024]{3,2,1,0:T(8,128)} %volume_ref.5), custom_call_target="tpu_custom_call" | custom-call | tf_op jit(solution)/shard_map/pallas_call | solution.py:64
  1.3 3.4 %collective-permute-start.2 = (bf16[32,1024]{1,0:T(8,128)(2,1)S(1)}, bf16[32,1024]{1,0:T(8,128)(2,1)S(1)}, u32[]{:S(2)}, u32[]{:S(2)}) collective-permute-start(bf16[32,1024]{1,0:T(8,128)(2,1)S(1)} %get-tuple-element.23), channel_id=1, source_target_pairs={{0,28},{1,29},{2,30},{3,31},{4,8},{5,9},{6,10},{7,11},{8,4},{9,5},... | collective-permute-start | bytes 196616 | tf_op jit(solution)/shard_map/ppermute | solution.py:389
  4.7 0.0 collective-permute-start.3
  4.7 1.6 %collective-permute-start = (bf16[8,1024]{1,0:T(8,128)(2,1)S(1)}, bf16[8,1024]{1,0:T(8,128)(2,1)S(1)}, u32[]{:S(2)}, u32[]{:S(2)}) collective-permute-start(bf16[8,1024]{1,0:T(8,128)(2,1)S(1)} %get-tuple-element.21), channel_id=1, source_target_pairs={{0,1},{1,0},{2,3},{3,2},{4,5},{5,4},{6,7},{7,6},{8,9},{9,8},{10,11... | collective-permute-start | bytes 49160 | tf_op jit(solution)/shard_map/ppermute | solution.py:389
  6.3 0.2 %collective-permute-start.1 = (bf16[8,1024]{1,0:T(8,128)(2,1)S(1)}, bf16[8,1024]{1,0:T(8,128)(2,1)S(1)}, u32[]{:S(2)}, u32[]{:S(2)}) collective-permute-start(bf16[8,1024]{1,0:T(8,128)(2,1)S(1)} %get-tuple-element.22), channel_id=1, source_target_pairs={{0,4},{1,2},{2,1},{3,7},{4,0},{5,6},{6,5},{7,3},{8,12},{9,10},{10,... | collective-permute-start | bytes 49160 | tf_op jit(solution)/shard_map/ppermute | solution.py:389
  6.5 0.0 copy-done
  6.5 0.0 copy-done.2
  6.5 0.0 copy-done.1
  6.5 3.0 %shard_map.37 = (f32[4,32,1024]{2,1,0:T(8,128)S(1)}, f32[2,32,1024]{2,1,0:T(8,128)S(1)}, f32[2,32,1024]{2,1,0:T(8,128)S(1)}, f32[2,3,32,1024]{3,2,1,0:T(8,128)S(...) custom-call(s32[2,8,32,1024]{3,2,1,0:T(8,128)S(1)} %copy-done, s32[3,256]{1,0:T(4,128)S(1)} %copy-done.1, ...), custom_call_target="tpu_custom_call" | custom-call | flops 20971520 | bytes 5242880 | tf_op jit(solution)/shard_map/pallas_call | solution.py:260
  9.5 0.0 collective-permute-done.rows_near_ref
  9.5 0.0 collective-permute-done.1.rows_far_ref
  9.5 0.0 collective-permute-done.2.far_ref
  9.5 0.0 collective-permute-done.3.near_ref
  9.5 0.5 %shard_map.39 = bf16[8,16,1024]{2,1,0:T(8,128)(2,1)S(1)} custom-call(s32[2,8,32,1024]{3,2,1,0:T(8,128)S(1)} %copy-done, f32[4,32,1024]{2,1,0:T(8,128)S(1)} %get-tuple-element.15.base_ref, f32[2,32,1024]{2,1,0:T(8,128)S(1)} %get-tuple-element.16.face_ref, f32[2,32,1024]{2,1,0:T(8,128)S(1)} %get-tuple-element.17.square_ref, ...), custom_call_target="tpu_custom_call" | custom-call | tf_op jit(solution)/shard_map/pallas_call | solution.py:339
  10.1 9.3 %all_to_all.5.parts_ref = bf16[8,16,1024]{2,1,0:T(8,128)(2,1)S(1)} all-to-all(bf16[8,16,1024]{2,1,0:T(8,128)(2,1)S(1)} %shard_map.39), channel_id=1, replica_groups=mesh['depth'=8,'rows'=4] {'depth'}, dimensions={0} | all-to-all | bytes 524288 | tf_op jit(solution)/shard_map/all_to_all | solution.py:402
  19.4 0.8 %shard_map.40 = f32[4,4,1024]{2,1,0:T(4,128)} custom-call(bf16[8,16,1024]{2,1,0:T(8,128)(2,1)S(1)} %all_to_all.5.parts_ref), custom_call_target="tpu_custom_call" | custom-call | tf_op jit(solution)/shard_map/pallas_call | solution.py:365
Async XLA Ops:
  0.0 6.5 %copy-start = (s32[2,8,32,1024]{3,2,1,0:T(8,128)S(1)}, s32[2,8,32,1024]{3,2,1,0:T(8,128)}, u32[]{:S(2)}) copy-start(s32[2,8,32,1024]{3,2,1,0:T(8,128)} %volume_ref.5) | copy-start | bytes 6291460
  0.0 6.5 %copy-start.2 = (s32[256]{0:T(256)S(1)}, s32[256]{0:T(256)}, u32[]{:S(2)}) copy-start(s32[256]{0:T(256)} %param.5) | copy-start | bytes 3076
  0.0 6.5 %copy-start.1 = (s32[3,256]{1,0:T(4,128)S(1)}, s32[3,256]{1,0:T(4,128)}, u32[]{:S(2)}) copy-start(s32[3,256]{1,0:T(4,128)} %color_ref.1) | copy-start | bytes 9220
  1.3 8.2 %collective-permute-start.2 = (bf16[32,1024]{1,0:T(8,128)(2,1)S(1)}, bf16[32,1024]{1,0:T(8,128)(2,1)S(1)}, u32[]{:S(2)}, u32[]{:S(2)}) collective-permute-start(bf16[32,1024]{1,0:T(8,128)(2,1)S(1)} %get-tuple-element.23), channel_id=1, source_target_pairs={{0,28},{1,29},{2,30},{3,31},{4,8},{5,9},{6,10},{7,11},{8,4},{9,5},... | collective-permute-start | bytes 196616 | tf_op jit(solution)/shard_map/ppermute | solution.py:389
  4.7 4.8 %collective-permute-start.3 = (bf16[32,1024]{1,0:T(8,128)(2,1)S(1)}, bf16[32,1024]{1,0:T(8,128)(2,1)S(1)}, u32[]{:S(2)}, u32[]{:S(2)}) collective-permute-start(bf16[32,1024]{1,0:T(8,128)(2,1)S(1)} %get-tuple-element.24), channel_id=1, source_target_pairs={{0,4},{1,5},{2,6},{3,7},{4,0},{5,1},{6,2},{7,3},{8,12},{9,13},{10,... | collective-permute-start | bytes 196616 | tf_op jit(solution)/shard_map/ppermute | solution.py:389
  4.7 4.8 %collective-permute-start = (bf16[8,1024]{1,0:T(8,128)(2,1)S(1)}, bf16[8,1024]{1,0:T(8,128)(2,1)S(1)}, u32[]{:S(2)}, u32[]{:S(2)}) collective-permute-start(bf16[8,1024]{1,0:T(8,128)(2,1)S(1)} %get-tuple-element.21), channel_id=1, source_target_pairs={{0,1},{1,0},{2,3},{3,2},{4,5},{5,4},{6,7},{7,6},{8,9},{9,8},{10,11... | collective-permute-start | bytes 49160 | tf_op jit(solution)/shard_map/ppermute | solution.py:389
  6.3 3.2 %collective-permute-start.1 = (bf16[8,1024]{1,0:T(8,128)(2,1)S(1)}, bf16[8,1024]{1,0:T(8,128)(2,1)S(1)}, u32[]{:S(2)}, u32[]{:S(2)}) collective-permute-start(bf16[8,1024]{1,0:T(8,128)(2,1)S(1)} %get-tuple-element.22), channel_id=1, source_target_pairs={{0,4},{1,2},{2,1},{3,7},{4,0},{5,6},{6,5},{7,3},{8,12},{9,10},{10,... | collective-permute-start | bytes 49160 | tf_op jit(solution)/shard_map/ppermute | solution.py:389
where the time goes:
time: 20.3 us; the launch traced here: 20.2 us
  blocking collectives  9.35 us (46%)
  Pallas kernels  5.52 us (27%)
  starting transfers between devices  5.22 us (26%)
    all_to_all x1, blocking collectives, body(): parts = lax.all_to_all(parts, 'depth', 0, 0, tiled=True)  9.35 us
    ppermute x4, starting transfers between devices, swapped(): return lax.ppermute(values, ('depth', 'rows'), perm)  5.22 us
    pallas_call x1, Pallas kernels, march_interior(): pl.pallas_call(functools.partial(interior_kernel, opacity_scale), in_spec...  2.95 us
    pallas_call x1, Pallas kernels, cut_edges(): pl.pallas_call(edges_kernel, in_specs=[pl.BlockSpec(memory_space=pl.ANY)]...  1.29 us
    pallas_call x1, Pallas kernels, finish(): pl.pallas_call(finish_kernel, in_specs=[WHOLE], out_specs=WHOLE, out_shap...  0.76 us
    pallas_call x1, Pallas kernels, add_edges(): pl.pallas_call(functools.partial(edge_kernel, share), in_specs=[WHOLE] *...  0.51 us
  transfers between devices with their start and end apart: 4, of which 0 were waited for; matrix products, arithmetic and copies ran while one was open for 0% of the time, Pallas kernels for 15%

commit v1 on v0

--- a/solution.py
+++ b/solution.py
@@ -272,7 +272,7 @@
 
 
 def edge_kernel(
-    share, volume_ref, base_ref, face_ref, square_ref, lit_ref, grad_ref, strip_ref, rows_near_ref, rows_far_ref, far_ref, near_ref, out_ref
+    share, volume_ref, base_ref, face_ref, square_ref, lit_ref, grad_ref, strip_ref, rows_near_ref, rows_far_ref, far_ref, near_ref, *out_refs
 ):
     _, slices, height, columns = volume_ref.shape
     tiles = height // SUBLANES
@@ -325,24 +325,94 @@
                     planes[c] = planes[c] + jnp.where(first_row, extra[0][c], 0.0)
                 if r == tiles - 1:
                     planes[c] = planes[c] + jnp.where(last_row, extra[1][c], 0.0)
-            for first in range(0, SUBLANES, share):
-                block = jnp.concatenate([plane[first : first + share] for plane in planes], axis=0)
-                out_ref[(r * SUBLANES + first) // share, :, here] = block.astype(jnp.bfloat16)
+            blocks = [
+                jnp.concatenate([plane[first : first + share] for plane in planes], axis=0)
+                for first in range(0, SUBLANES, share)
+            ]
+            if len(out_refs) == 1:
+                for i, block in enumerate(blocks):
+                    out_refs[0][r * len(blocks) + i, :, here] = block.astype(jnp.bfloat16)
+            else:
+                keep_ref, give_ref = out_refs
+                keep_ref[r, :, here] = jnp.where(odd, blocks[1], blocks[0])
+                give_ref[r, :, here] = jnp.where(odd, blocks[0], blocks[1]).astype(jnp.bfloat16)
         return carry
 
     lax.fori_loop(0, columns // LANES, chunk, 0)
 
 
-def add_edges(volume, interior, halos, depth_count):
+def add_edges(volume, interior, halos, depth_count, paired):
     _, slices, height, columns = volume.shape
     share = height // depth_count
+    if paired:
+        half = (depth_count // 2, 4 * share, columns)
+        shapes = [jax.ShapeDtypeStruct(half, jnp.float32), jax.ShapeDtypeStruct(half, jnp.bfloat16)]
+    else:
+        shapes = [jax.ShapeDtypeStruct((depth_count, 4 * share, columns), jnp.bfloat16)]
     return pl.pallas_call(
         functools.partial(edge_kernel, share),
         in_specs=[WHOLE] * 11,
-        out_specs=WHOLE,
-        out_shape=jax.ShapeDtypeStruct((depth_count, 4 * share, columns), jnp.bfloat16),
+        out_specs=[WHOLE] * len(shapes),
+        out_shape=shapes,
         compiler_params=pltpu.CompilerParams(vmem_limit_bytes=24 * 1024 * 1024),
     )(volume, *interior, *halos)
+
+
+def over(nearer, farther):
+    share = nearer.shape[0] // 4
+    clear = 1.0 - nearer[3 * share :]
+    return nearer + jnp.concatenate([clear] * 4, axis=0) * farther
+
+
+def merge_kernel(keep_ref, other_ref, own_ref, *send_refs):
+    position = lax.axis_index("depth")
+    odd, chip = position % 2 == 1, position // 2
+    for k, out_ref in enumerate((own_ref, *send_refs)):
+        keep = keep_ref[chip ^ k]
+        other = other_ref[chip ^ k].astype(jnp.float32)
+        out_ref[...] = over(jnp.where(odd, other, keep), jnp.where(odd, keep, other)).astype(out_ref.dtype)
+
+
+def merge(keep, other):
+    chips, rows, columns = keep.shape
+    shapes = [jax.ShapeDtypeStruct((rows, columns), jnp.float32)]
+    shapes += [jax.ShapeDtypeStruct((rows, columns), jnp.bfloat16)] * (chips - 1)
+    return pl.pallas_call(
+        merge_kernel,
+        in_specs=[WHOLE] * 2,
+        out_specs=[WHOLE] * chips,
+        out_shape=shapes,
+        compiler_params=pltpu.CompilerParams(vmem_limit_bytes=8 * 1024 * 1024),
+    )(keep, other)
+
+
+def gather_kernel(*refs):
+    *part_refs, out_ref = refs
+    count = len(part_refs)
+    share = out_ref.shape[1]
+    chip = lax.axis_index("depth") // 2
+    parts = [part_ref[...].astype(jnp.float32) for part_ref in part_refs]
+    step = 1
+    while step < count:
+        swap = (chip & step) != 0
+        parts = [
+            over(jnp.where(swap, parts[i + 1], parts[i]), jnp.where(swap, parts[i], parts[i + 1]))
+            for i in range(0, len(parts), 2)
+        ]
+        step *= 2
+    for c in range(4):
+        out_ref[c] = parts[0][c * share : (c + 1) * share]
+
+
+def gather(parts, share):
+    columns = parts[0].shape[1]
+    return pl.pallas_call(
+        gather_kernel,
+        in_specs=[WHOLE] * len(parts),
+        out_specs=WHOLE,
+        out_shape=jax.ShapeDtypeStruct((4, share, columns), jnp.float32),
+        compiler_params=pltpu.CompilerParams(vmem_limit_bytes=4 * 1024 * 1024),
+    )(*parts)
 
 
 def finish_kernel(parts_ref, out_ref):
@@ -389,6 +459,10 @@
     return lax.ppermute(values, ("depth", "rows"), perm)
 
 
+def exchanged(values, mask):
+    return lax.ppermute(values, "depth", [(d, d ^ mask) for d in range(lax.axis_size("depth"))])
+
+
 def body(volume, color_map, alpha_map):
     depth_count = lax.axis_size("depth")
     share = volume.shape[2] // depth_count
@@ -398,9 +472,15 @@
     far = swapped(far, "depth", 1)
     near = swapped(near, "depth", 0)
     interior = march_interior(volume, color_map, alpha_map, depth_count)
-    parts = add_edges(volume, interior, (rows_near, rows_far, far, near), depth_count)
-    parts = lax.all_to_all(parts, "depth", 0, 0, tiled=True)
-    return finish(parts, share)
+    halos = (rows_near, rows_far, far, near)
+    paired = depth_count == 8 and 2 * share == SUBLANES
+    outs = add_edges(volume, interior, halos, depth_count, paired)
+    if not paired:
+        return finish(lax.all_to_all(outs[0], "depth", 0, 0, tiled=True), share)
+    keep, give = outs
+    own, *sends = merge(keep, exchanged(give, 1))
+    received = [exchanged(send, 2 * k) for k, send in reversed(list(enumerate(sends, 1)))]
+    return gather((own, *reversed(received)), share)
 
 
 def solution(mesh):

time: 20.3 us -> 18.9 us (0.931)
  blocking collectives: 9.35 us -> 0 us
  waiting for transfers between devices: 0.01 us -> 4.05 us
  starting transfers between devices: 5.22 us -> 9.12 us
    all_to_all x1 -> x0, blocking collectives: 9.35 us -> none  [body(): parts = lax.all_to_all(parts, 'depth', 0, 0, tiled=True)]
    ppermute x0 -> x4, waiting for transfers between devices: none -> 4.04 us  [exchanged(): lax.ppermute(values, 'depth', [(d, d ^ mask) for d in range(lax.axis_size...]
    ppermute x0 -> x4, starting transfers between devices: none -> 3.9 us  [exchanged(): lax.ppermute(values, 'depth', [(d, d ^ mask) for d in range(lax.axis_size...]
    pallas_call x1 -> x2, Pallas kernels: 0.76 us -> 0.75 us  [the longest x1 0.68 us: gather(): pl.pallas_call(gather_kernel, in_specs=[WHOLE] * len(parts), out_specs=WH...]
  transfers between devices with their start and end apart: 4 -> 8, of which waited for: 0 -> 4; matrix products, arithmetic and copies ran while one was open for 0% -> 0% of each run, Pallas kernels for 15% -> 16%
where the time goes in v1:
time: 18.9 us; the launch traced here: 18.8 us
  starting transfers between devices  9.12 us (48%)
  Pallas kernels  5.51 us (29%)
  waiting for transfers between devices  4.05 us (21%)
    ppermute x4, starting transfers between devices, swapped(): return lax.ppermute(values, ('depth', 'rows'), perm)  5.22 us
    ppermute x4, waiting for transfers between devices, exchanged(): lax.ppermute(values, 'depth', [(d, d ^ mask) for d in range(lax.axis_size...  4.04 us
    ppermute x4, starting transfers between devices, exchanged(): lax.ppermute(values, 'depth', [(d, d ^ mask) for d in range(lax.axis_size...  3.9 us
    pallas_call x1, Pallas kernels, march_interior(): pl.pallas_call(functools.partial(interior_kernel, opacity_scale), in_spec...  2.95 us
    pallas_call x1, Pallas kernels, cut_edges(): pl.pallas_call(edges_kernel, in_specs=[pl.BlockSpec(memory_space=pl.ANY)]...  1.29 us
    pallas_call x1, Pallas kernels, gather(): pl.pallas_call(gather_kernel, in_specs=[WHOLE] * len(parts), out_specs=WH...  0.68 us
    pallas_call x1, Pallas kernels, add_edges(): pl.pallas_call(functools.partial(edge_kernel, share), in_specs=[WHOLE] *...  0.51 us
  transfers between devices with their start and end apart: 8, of which 4 were waited for; matrix products, arithmetic and copies ran while one was open for 0% of the time, Pallas kernels for 16%

profile of v1, /device:TPU:0, one launch (start us, length us, event | category | flops | bytes accessed | tf_op | source)
XLA Modules:
  0.0 18.8 jit_solution(17323022722040057704)
XLA Ops:
  0.0 0.0 copy-start
  0.0 0.0 copy-start.2
  0.0 0.0 copy-start.1
  0.0 1.3 %shard_map.38 = (bf16[8,1024]{1,0:T(8,128)(2,1)S(1)}, bf16[8,1024]{1,0:T(8,128)(2,1)S(1)}, bf16[32,1024]{1,0:T(8,128)(2,1)S(1)}, bf16[32,1024]{1,0:T(8,128)(2,1)S(1)}) custom-call(s32[2,8,32,1024]{3,2,1,0:T(8,128)} %volume_ref.5), custom_call_target="tpu_custom_call" | custom-call | tf_op jit(solution)/shard_map/pallas_call | solution.py:64
  1.3 3.4 %collective-permute-start.2 = (bf16[32,1024]{1,0:T(8,128)(2,1)S(1)}, bf16[32,1024]{1,0:T(8,128)(2,1)S(1)}, u32[]{:S(2)}, u32[]{:S(2)}) collective-permute-start(bf16[32,1024]{1,0:T(8,128)(2,1)S(1)} %get-tuple-element.29), channel_id=1, source_target_pairs={{0,28},{1,29},{2,30},{3,31},{4,8},{5,9},{6,10},{7,11},{8,4},{9,5},... | collective-permute-start | bytes 196616 | tf_op jit(solution)/shard_map/ppermute | solution.py:459
  4.7 0.0 collective-permute-start.3
  4.7 1.6 %collective-permute-start = (bf16[8,1024]{1,0:T(8,128)(2,1)S(1)}, bf16[8,1024]{1,0:T(8,128)(2,1)S(1)}, u32[]{:S(2)}, u32[]{:S(2)}) collective-permute-start(bf16[8,1024]{1,0:T(8,128)(2,1)S(1)} %get-tuple-element.27), channel_id=1, source_target_pairs={{0,1},{1,0},{2,3},{3,2},{4,5},{5,4},{6,7},{7,6},{8,9},{9,8},{10,11... | collective-permute-start | bytes 49160 | tf_op jit(solution)/shard_map/ppermute | solution.py:459
  6.3 0.2 %collective-permute-start.1 = (bf16[8,1024]{1,0:T(8,128)(2,1)S(1)}, bf16[8,1024]{1,0:T(8,128)(2,1)S(1)}, u32[]{:S(2)}, u32[]{:S(2)}) collective-permute-start(bf16[8,1024]{1,0:T(8,128)(2,1)S(1)} %get-tuple-element.28), channel_id=1, source_target_pairs={{0,4},{1,2},{2,1},{3,7},{4,0},{5,6},{6,5},{7,3},{8,12},{9,10},{10,... | collective-permute-start | bytes 49160 | tf_op jit(solution)/shard_map/ppermute | solution.py:459
  6.5 0.0 copy-done
  6.5 0.0 copy-done.2
  6.5 0.0 copy-done.1
  6.5 3.0 %shard_map.37 = (f32[4,32,1024]{2,1,0:T(8,128)S(1)}, f32[2,32,1024]{2,1,0:T(8,128)S(1)}, f32[2,32,1024]{2,1,0:T(8,128)S(1)}, f32[2,3,32,1024]{3,2,1,0:T(8,128)S(...) custom-call(s32[2,8,32,1024]{3,2,1,0:T(8,128)S(1)} %copy-done, s32[3,256]{1,0:T(4,128)S(1)} %copy-done.1, ...), custom_call_target="tpu_custom_call" | custom-call | flops 20971520 | bytes 5242880 | tf_op jit(solution)/shard_map/pallas_call | solution.py:260
  9.5 0.0 collective-permute-done.rows_near_ref
  9.5 0.0 collective-permute-done.1.rows_far_ref
  9.5 0.0 collective-permute-done.2.far_ref
  9.5 0.0 collective-permute-done.3.near_ref
  9.5 0.5 %shard_map.39 = (f32[4,16,1024]{2,1,0:T(8,128)S(1)}, bf16[4,16,1024]{2,1,0:T(8,128)(2,1)S(1)}) custom-call(s32[2,8,32,1024]{3,2,1,0:T(8,128)S(1)} %copy-done, f32[4,32,1024]{2,1,0:T(8,128)S(1)} %get-tuple-element.21.base_ref, f32[2,32,1024]{2,1,0:T(8,128)S(1)} %get-tuple-element.22.face_ref, f32[2,32,1024]{2,1,0:T(8,128)S(1)} %get-tuple-element.23.square_ref, ...), custom_call_target="tpu_custom_call" | custom-call | tf_op jit(solution)/shard_map/pallas_call | solution.py:352
  10.1 0.3 %collective-permute-start.4 = (bf16[4,16,1024]{2,1,0:T(8,128)(2,1)S(1)}, bf16[4,16,1024]{2,1,0:T(8,128)(2,1)S(1)}, u32[]{:S(2)}, u32[]{:S(2)}) collective-permute-start(bf16[4,16,1024]{2,1,0:T(8,128)(2,1)S(1)} %get-tuple-element.32), channel_id=1, source_target_pairs={{0,4},{4,0},{8,12},{12,8},{16,20},{20,16},{24,28},{28,24},{1,5},{5... | collective-permute-start | bytes 393224 | tf_op jit(solution)/shard_map/ppermute | solution.py:463
  10.4 1.1 %collective-permute-done.4.other_ref = bf16[4,16,1024]{2,1,0:T(8,128)(2,1)S(1)} collective-permute-done((bf16[4,16,1024]{2,1,0:T(8,128)(2,1)S(1)}, bf16[4,16,1024]{2,1,0:T(8,128)(2,1)S(1)}, u32[]{:S(2)}, u32[]{:S(2)}) %collective-permute-start.4) | collective-permute-done | bytes 131104 | tf_op jit(solution)/shard_map/ppermute | solution.py:463
  11.5 0.1 shard_map.40
  11.5 1.2 %collective-permute-start.5 = (bf16[16,1024]{1,0:T(8,128)(2,1)S(1)}, bf16[16,1024]{1,0:T(8,128)(2,1)S(1)}, u32[]{:S(2)}, u32[]{:S(2)}) collective-permute-start(bf16[16,1024]{1,0:T(8,128)(2,1)S(1)} %get-tuple-element.34), channel_id=1, source_target_pairs={{0,8},{4,12},{8,0},{12,4},{16,24},{20,28},{24,16},{28,20},{1,9},{5... | collective-permute-start | bytes 98312 | tf_op jit(solution)/shard_map/ppermute | solution.py:463
  12.7 0.5 %collective-permute-start.6 = (bf16[16,1024]{1,0:T(8,128)(2,1)S(1)}, bf16[16,1024]{1,0:T(8,128)(2,1)S(1)}, u32[]{:S(2)}, u32[]{:S(2)}) collective-permute-start(bf16[16,1024]{1,0:T(8,128)(2,1)S(1)} %get-tuple-element.35), channel_id=1, source_target_pairs={{0,16},{4,20},{8,24},{12,28},{16,0},{20,4},{24,8},{28,12},{1,17},{... | collective-permute-start | bytes 98312 | tf_op jit(solution)/shard_map/ppermute | solution.py:463
  13.3 1.8 %collective-permute-start.7 = (bf16[16,1024]{1,0:T(8,128)(2,1)S(1)}, bf16[16,1024]{1,0:T(8,128)(2,1)S(1)}, u32[]{:S(2)}, u32[]{:S(2)}) collective-permute-start(bf16[16,1024]{1,0:T(8,128)(2,1)S(1)} %get-tuple-element.36), channel_id=1, source_target_pairs={{0,24},{4,28},{8,16},{12,20},{16,8},{20,12},{24,0},{28,4},{1,25},{... | collective-permute-start | bytes 98312 | tf_op jit(solution)/shard_map/ppermute | solution.py:463
  15.1 0.4 %collective-permute-done.5.refs_1_ = bf16[16,1024]{1,0:T(8,128)(2,1)S(1)} collective-permute-done((bf16[16,1024]{1,0:T(8,128)(2,1)S(1)}, bf16[16,1024]{1,0:T(8,128)(2,1)S(1)}, u32[]{:S(2)}, u32[]{:S(2)}) %collective-permute-start.5) | collective-permute-done | bytes 32800 | tf_op jit(solution)/shard_map/ppermute | solution.py:463
  15.5 1.5 %collective-permute-done.6.refs_2_ = bf16[16,1024]{1,0:T(8,128)(2,1)S(1)} collective-permute-done((bf16[16,1024]{1,0:T(8,128)(2,1)S(1)}, bf16[16,1024]{1,0:T(8,128)(2,1)S(1)}, u32[]{:S(2)}, u32[]{:S(2)}) %collective-permute-start.6) | collective-permute-done | bytes 32800 | tf_op jit(solution)/shard_map/ppermute | solution.py:463
  17.0 1.1 %collective-permute-done.7.refs_3_ = bf16[16,1024]{1,0:T(8,128)(2,1)S(1)} collective-permute-done((bf16[16,1024]{1,0:T(8,128)(2,1)S(1)}, bf16[16,1024]{1,0:T(8,128)(2,1)S(1)}, u32[]{:S(2)}, u32[]{:S(2)}) %collective-permute-start.7) | collective-permute-done | bytes 32800 | tf_op jit(solution)/shard_map/ppermute | solution.py:463
  18.1 0.7 %shard_map.41 = f32[4,4,1024]{2,1,0:T(4,128)} custom-call(f32[16,1024]{1,0:T(8,128)S(1)} %get-tuple-element.33.refs_0_, bf16[16,1024]{1,0:T(8,128)(2,1)S(1)} %collective-permute-done.5.refs_1_, bf16[16,1024]{1,0:T(8,128)(2,1)S(1)} %collective-permute-done.6.refs_2_, bf16[16,1024]{1,0:T(8,128)(2,1)S(1)} %collective-permute-done.7.refs_3_), custom_call_target="tpu_custom_call" | custom-call | tf_op jit(solution)/shard_map/pallas_call | solution.py:409
Async XLA Ops:
  0.0 6.5 %copy-start = (s32[2,8,32,1024]{3,2,1,0:T(8,128)S(1)}, s32[2,8,32,1024]{3,2,1,0:T(8,128)}, u32[]{:S(2)}) copy-start(s32[2,8,32,1024]{3,2,1,0:T(8,128)} %volume_ref.5) | copy-start | bytes 6291460
  0.0 6.5 %copy-start.2 = (s32[256]{0:T(256)S(1)}, s32[256]{0:T(256)}, u32[]{:S(2)}) copy-start(s32[256]{0:T(256)} %param.5) | copy-start | bytes 3076
  0.0 6.5 %copy-start.1 = (s32[3,256]{1,0:T(4,128)S(1)}, s32[3,256]{1,0:T(4,128)}, u32[]{:S(2)}) copy-start(s32[3,256]{1,0:T(4,128)} %color_ref.1) | copy-start | bytes 9220
  1.3 8.2 %collective-permute-start.2 = (bf16[32,1024]{1,0:T(8,128)(2,1)S(1)}, bf16[32,1024]{1,0:T(8,128)(2,1)S(1)}, u32[]{:S(2)}, u32[]{:S(2)}) collective-permute-start(bf16[32,1024]{1,0:T(8,128)(2,1)S(1)} %get-tuple-element.29), channel_id=1, source_target_pairs={{0,28},{1,29},{2,30},{3,31},{4,8},{5,9},{6,10},{7,11},{8,4},{9,5},... | collective-permute-start | bytes 196616 | tf_op jit(solution)/shard_map/ppermute | solution.py:459
  4.7 4.8 %collective-permute-start.3 = (bf16[32,1024]{1,0:T(8,128)(2,1)S(1)}, bf16[32,1024]{1,0:T(8,128)(2,1)S(1)}, u32[]{:S(2)}, u32[]{:S(2)}) collective-permute-start(bf16[32,1024]{1,0:T(8,128)(2,1)S(1)} %get-tuple-element.30), channel_id=1, source_target_pairs={{0,4},{1,5},{2,6},{3,7},{4,0},{5,1},{6,2},{7,3},{8,12},{9,13},{10,... | collective-permute-start | bytes 196616 | tf_op jit(solution)/shard_map/ppermute | solution.py:459
  4.7 4.8 %collective-permute-start = (bf16[8,1024]{1,0:T(8,128)(2,1)S(1)}, bf16[8,1024]{1,0:T(8,128)(2,1)S(1)}, u32[]{:S(2)}, u32[]{:S(2)}) collective-permute-start(bf16[8,1024]{1,0:T(8,128)(2,1)S(1)} %get-tuple-element.27), channel_id=1, source_target_pairs={{0,1},{1,0},{2,3},{3,2},{4,5},{5,4},{6,7},{7,6},{8,9},{9,8},{10,11... | collective-permute-start | bytes 49160 | tf_op jit(solution)/shard_map/ppermute | solution.py:459
  6.3 3.2 %collective-permute-start.1 = (bf16[8,1024]{1,0:T(8,128)(2,1)S(1)}, bf16[8,1024]{1,0:T(8,128)(2,1)S(1)}, u32[]{:S(2)}, u32[]{:S(2)}) collective-permute-start(bf16[8,1024]{1,0:T(8,128)(2,1)S(1)} %get-tuple-element.28), channel_id=1, source_target_pairs={{0,4},{1,2},{2,1},{3,7},{4,0},{5,6},{6,5},{7,3},{8,12},{9,10},{10,... | collective-permute-start | bytes 49160 | tf_op jit(solution)/shard_map/ppermute | solution.py:459
  10.1 1.4 %collective-permute-start.4 = (bf16[4,16,1024]{2,1,0:T(8,128)(2,1)S(1)}, bf16[4,16,1024]{2,1,0:T(8,128)(2,1)S(1)}, u32[]{:S(2)}, u32[]{:S(2)}) collective-permute-start(bf16[4,16,1024]{2,1,0:T(8,128)(2,1)S(1)} %get-tuple-element.32), channel_id=1, source_target_pairs={{0,4},{4,0},{8,12},{12,8},{16,20},{20,16},{24,28},{28,24},{1,5},{5... | collective-permute-start | bytes 393224 | tf_op jit(solution)/shard_map/ppermute | solution.py:463
  11.5 4.0 %collective-permute-start.5 = (bf16[16,1024]{1,0:T(8,128)(2,1)S(1)}, bf16[16,1024]{1,0:T(8,128)(2,1)S(1)}, u32[]{:S(2)}, u32[]{:S(2)}) collective-permute-start(bf16[16,1024]{1,0:T(8,128)(2,1)S(1)} %get-tuple-element.34), channel_id=1, source_target_pairs={{0,8},{4,12},{8,0},{12,4},{16,24},{20,28},{24,16},{28,20},{1,9},{5... | collective-permute-start | bytes 98312 | tf_op jit(solution)/shard_map/ppermute | solution.py:463
  12.7 4.3 %collective-permute-start.6 = (bf16[16,1024]{1,0:T(8,128)(2,1)S(1)}, bf16[16,1024]{1,0:T(8,128)(2,1)S(1)}, u32[]{:S(2)}, u32[]{:S(2)}) collective-permute-start(bf16[16,1024]{1,0:T(8,128)(2,1)S(1)} %get-tuple-element.35), channel_id=1, source_target_pairs={{0,16},{4,20},{8,24},{12,28},{16,0},{20,4},{24,8},{28,12},{1,17},{... | collective-permute-start | bytes 98312 | tf_op jit(solution)/shard_map/ppermute | solution.py:463
  13.3 4.8 %collective-permute-start.7 = (bf16[16,1024]{1,0:T(8,128)(2,1)S(1)}, bf16[16,1024]{1,0:T(8,128)(2,1)S(1)}, u32[]{:S(2)}, u32[]{:S(2)}) collective-permute-start(bf16[16,1024]{1,0:T(8,128)(2,1)S(1)} %get-tuple-element.36), channel_id=1, source_target_pairs={{0,24},{4,28},{8,16},{12,20},{16,8},{20,12},{24,0},{28,4},{1,25},{... | collective-permute-start | bytes 98312 | tf_op jit(solution)/shard_map/ppermute | solution.py:463

commit v2 on v1

--- a/solution.py
+++ b/solution.py
@@ -334,8 +334,8 @@
                     out_refs[0][r * len(blocks) + i, :, here] = block.astype(jnp.bfloat16)
             else:
                 keep_ref, give_ref = out_refs
-                keep_ref[r, :, here] = jnp.where(odd, blocks[1], blocks[0])
-                give_ref[r, :, here] = jnp.where(odd, blocks[0], blocks[1]).astype(jnp.bfloat16)
+                keep_ref[r, :, here] = jnp.where(odd, blocks[0], blocks[1])
+                give_ref[r, :, here] = jnp.where(odd, blocks[1], blocks[0]).astype(jnp.bfloat16)
         return carry
 
     lax.fori_loop(0, columns // LANES, chunk, 0)
@@ -364,10 +364,10 @@
     return nearer + jnp.concatenate([clear] * 4, axis=0) * farther
 
 
-def merge_kernel(keep_ref, other_ref, own_ref, *send_refs):
+def merge_kernel(keep_ref, other_ref, *send_refs):
     position = lax.axis_index("depth")
     odd, chip = position % 2 == 1, position // 2
-    for k, out_ref in enumerate((own_ref, *send_refs)):
+    for k, out_ref in enumerate(send_refs):
         keep = keep_ref[chip ^ k]
         other = other_ref[chip ^ k].astype(jnp.float32)
         out_ref[...] = over(jnp.where(odd, other, keep), jnp.where(odd, keep, other)).astype(out_ref.dtype)
@@ -375,19 +375,18 @@
 
 def merge(keep, other):
     chips, rows, columns = keep.shape
-    shapes = [jax.ShapeDtypeStruct((rows, columns), jnp.float32)]
-    shapes += [jax.ShapeDtypeStruct((rows, columns), jnp.bfloat16)] * (chips - 1)
     return pl.pallas_call(
         merge_kernel,
         in_specs=[WHOLE] * 2,
         out_specs=[WHOLE] * chips,
-        out_shape=shapes,
+        out_shape=[jax.ShapeDtypeStruct((rows, columns), jnp.bfloat16)] * chips,
         compiler_params=pltpu.CompilerParams(vmem_limit_bytes=8 * 1024 * 1024),
     )(keep, other)
 
 
 def gather_kernel(*refs):
     *part_refs, out_ref = refs
+    part_refs.reverse()
     count = len(part_refs)
     share = out_ref.shape[1]
     chip = lax.axis_index("depth") // 2
@@ -478,9 +477,8 @@
     if not paired:
         return finish(lax.all_to_all(outs[0], "depth", 0, 0, tiled=True), share)
     keep, give = outs
-    own, *sends = merge(keep, exchanged(give, 1))
-    received = [exchanged(send, 2 * k) for k, send in reversed(list(enumerate(sends, 1)))]
-    return gather((own, *reversed(received)), share)
+    sends = merge(keep, exchanged(give, 1))
+    return gather([exchanged(send, 2 * k + 1) for k, send in reversed(list(enumerate(sends)))], share)
 
 
 def solution(mesh):

time: 18.9 us -> 18.4 us (0.974)
  the two profiles are of different devices: /device:TPU:0 before, /device:TPU:9 now
where the time goes in v2:
time: 18.4 us; the launch traced here: 18.3 us
  starting transfers between devices  9.25 us (50%)
  Pallas kernels  5.53 us (30%)
  waiting for transfers between devices  3.41 us (19%)
    ppermute x4, starting transfers between devices, swapped(): return lax.ppermute(values, ('depth', 'rows'), perm)  5.22 us
    ppermute x5, starting transfers between devices, exchanged(): lax.ppermute(values, 'depth', [(d, d ^ mask) for d in range(lax.axis_size...  4.03 us
    ppermute x5, waiting for transfers between devices, exchanged(): lax.ppermute(values, 'depth', [(d, d ^ mask) for d in range(lax.axis_size...  3.4 us
    pallas_call x1, Pallas kernels, march_interior(): pl.pallas_call(functools.partial(interior_kernel, opacity_scale), in_spec...  2.95 us
    pallas_call x1, Pallas kernels, cut_edges(): pl.pallas_call(edges_kernel, in_specs=[pl.BlockSpec(memory_space=pl.ANY)]...  1.31 us
    pallas_call x1, Pallas kernels, gather(): pl.pallas_call(gather_kernel, in_specs=[WHOLE] * len(parts), out_specs=WH...  0.69 us
    pallas_call x1, Pallas kernels, add_edges(): pl.pallas_call(functools.partial(edge_kernel, share), in_specs=[WHOLE] *...  0.51 us
  transfers between devices with their start and end apart: 9, of which 4 were waited for; matrix products, arithmetic and copies ran while one was open for 0% of the time, Pallas kernels for 16%

profile of v2, /device:TPU:9, one launch (start us, length us, event | category | flops | bytes accessed | tf_op | source)
XLA Modules:
  0.0 18.3 jit_solution(14909615370714670412)
XLA Ops:
  0.0 0.0 copy-start
  0.0 0.0 copy-start.2
  0.0 0.0 copy-start.1
  0.0 1.3 %shard_map.38 = (bf16[8,1024]{1,0:T(8,128)(2,1)S(1)}, bf16[8,1024]{1,0:T(8,128)(2,1)S(1)}, bf16[32,1024]{1,0:T(8,128)(2,1)S(1)}, bf16[32,1024]{1,0:T(8,128)(2,1)S(1)}) custom-call(s32[2,8,32,1024]{3,2,1,0:T(8,128)} %volume_ref.5), custom_call_target="tpu_custom_call" | custom-call | tf_op jit(solution)/shard_map/pallas_call | solution.py:64
  1.3 1.8 %collective-permute-start.2 = (bf16[32,1024]{1,0:T(8,128)(2,1)S(1)}, bf16[32,1024]{1,0:T(8,128)(2,1)S(1)}, u32[]{:S(2)}, u32[]{:S(2)}) collective-permute-start(bf16[32,1024]{1,0:T(8,128)(2,1)S(1)} %get-tuple-element.29), channel_id=1, source_target_pairs={{0,28},{1,29},{2,30},{3,31},{4,8},{5,9},{6,10},{7,11},{8,4},{9,5},... | collective-permute-start | bytes 196616 | tf_op jit(solution)/shard_map/ppermute | solution.py:458
  3.2 0.8 %collective-permute-start.3 = (bf16[32,1024]{1,0:T(8,128)(2,1)S(1)}, bf16[32,1024]{1,0:T(8,128)(2,1)S(1)}, u32[]{:S(2)}, u32[]{:S(2)}) collective-permute-start(bf16[32,1024]{1,0:T(8,128)(2,1)S(1)} %get-tuple-element.30), channel_id=1, source_target_pairs={{0,4},{1,5},{2,6},{3,7},{4,0},{5,1},{6,2},{7,3},{8,12},{9,13},{10,... | collective-permute-start | bytes 196616 | tf_op jit(solution)/shard_map/ppermute | solution.py:458
  4.0 0.2 collective-permute-start
  4.1 2.4 %collective-permute-start.1 = (bf16[8,1024]{1,0:T(8,128)(2,1)S(1)}, bf16[8,1024]{1,0:T(8,128)(2,1)S(1)}, u32[]{:S(2)}, u32[]{:S(2)}) collective-permute-start(bf16[8,1024]{1,0:T(8,128)(2,1)S(1)} %get-tuple-element.28), channel_id=1, source_target_pairs={{0,4},{1,2},{2,1},{3,7},{4,0},{5,6},{6,5},{7,3},{8,12},{9,10},{10,... | collective-permute-start | bytes 49160 | tf_op jit(solution)/shard_map/ppermute | solution.py:458
  6.5 0.0 copy-done
  6.5 0.0 copy-done.2
  6.5 0.0 copy-done.1
  6.6 3.0 %shard_map.37 = (f32[4,32,1024]{2,1,0:T(8,128)S(1)}, f32[2,32,1024]{2,1,0:T(8,128)S(1)}, f32[2,32,1024]{2,1,0:T(8,128)S(1)}, f32[2,3,32,1024]{3,2,1,0:T(8,128)S(...) custom-call(s32[2,8,32,1024]{3,2,1,0:T(8,128)S(1)} %copy-done, s32[3,256]{1,0:T(4,128)S(1)} %copy-done.1, ...), custom_call_target="tpu_custom_call" | custom-call | flops 20971520 | bytes 5242880 | tf_op jit(solution)/shard_map/pallas_call | solution.py:260
  9.5 0.0 collective-permute-done.rows_near_ref
  9.5 0.0 collective-permute-done.1.rows_far_ref
  9.5 0.0 collective-permute-done.2.far_ref
  9.5 0.0 collective-permute-done.3.near_ref
  9.6 0.5 %shard_map.39 = (f32[4,16,1024]{2,1,0:T(8,128)S(1)}, bf16[4,16,1024]{2,1,0:T(8,128)(2,1)S(1)}) custom-call(s32[2,8,32,1024]{3,2,1,0:T(8,128)S(1)} %copy-done, f32[4,32,1024]{2,1,0:T(8,128)S(1)} %get-tuple-element.21.base_ref, f32[2,32,1024]{2,1,0:T(8,128)S(1)} %get-tuple-element.22.face_ref, f32[2,32,1024]{2,1,0:T(8,128)S(1)} %get-tuple-element.23.square_ref, ...), custom_call_target="tpu_custom_call" | custom-call | tf_op jit(solution)/shard_map/pallas_call | solution.py:352
  10.1 0.6 %collective-permute-start.4 = (bf16[4,16,1024]{2,1,0:T(8,128)(2,1)S(1)}, bf16[4,16,1024]{2,1,0:T(8,128)(2,1)S(1)}, u32[]{:S(2)}, u32[]{:S(2)}) collective-permute-start(bf16[4,16,1024]{2,1,0:T(8,128)(2,1)S(1)} %get-tuple-element.32), channel_id=1, source_target_pairs={{0,4},{4,0},{8,12},{12,8},{16,20},{20,16},{24,28},{28,24},{1,5},{5... | collective-permute-start | bytes 393224 | tf_op jit(solution)/shard_map/ppermute | solution.py:462
  10.7 1.0 %collective-permute-done.4.other_ref = bf16[4,16,1024]{2,1,0:T(8,128)(2,1)S(1)} collective-permute-done((bf16[4,16,1024]{2,1,0:T(8,128)(2,1)S(1)}, bf16[4,16,1024]{2,1,0:T(8,128)(2,1)S(1)}, u32[]{:S(2)}, u32[]{:S(2)}) %collective-permute-start.4) | collective-permute-done | bytes 131104 | tf_op jit(solution)/shard_map/ppermute | solution.py:462
  11.7 0.1 shard_map.40
  11.8 1.2 %collective-permute-start.5 = (bf16[16,1024]{1,0:T(8,128)(2,1)S(1)}, bf16[16,1024]{1,0:T(8,128)(2,1)S(1)}, u32[]{:S(2)}, u32[]{:S(2)}) collective-permute-start(bf16[16,1024]{1,0:T(8,128)(2,1)S(1)} %get-tuple-element.33), channel_id=1, source_target_pairs={{0,28},{4,24},{8,20},{12,16},{16,12},{20,8},{24,4},{28,0},{1,29},{... | collective-permute-start | bytes 98312 | tf_op jit(solution)/shard_map/ppermute | solution.py:462
  12.9 1.3 %collective-permute-start.6 = (bf16[16,1024]{1,0:T(8,128)(2,1)S(1)}, bf16[16,1024]{1,0:T(8,128)(2,1)S(1)}, u32[]{:S(2)}, u32[]{:S(2)}) collective-permute-start(bf16[16,1024]{1,0:T(8,128)(2,1)S(1)} %get-tuple-element.34), channel_id=1, source_target_pairs={{0,20},{4,16},{8,28},{12,24},{16,4},{20,0},{24,12},{28,8},{1,21},{... | collective-permute-start | bytes 98312 | tf_op jit(solution)/shard_map/ppermute | solution.py:462
  14.2 0.8 %collective-permute-start.7 = (bf16[16,1024]{1,0:T(8,128)(2,1)S(1)}, bf16[16,1024]{1,0:T(8,128)(2,1)S(1)}, u32[]{:S(2)}, u32[]{:S(2)}) collective-permute-start(bf16[16,1024]{1,0:T(8,128)(2,1)S(1)} %get-tuple-element.35), channel_id=1, source_target_pairs={{0,12},{4,8},{8,4},{12,0},{16,28},{20,24},{24,20},{28,16},{1,13},{... | collective-permute-start | bytes 98312 | tf_op jit(solution)/shard_map/ppermute | solution.py:462
  15.0 0.2 collective-permute-start.8
  15.2 1.0 %collective-permute-done.5.refs_0_ = bf16[16,1024]{1,0:T(8,128)(2,1)S(1)} collective-permute-done((bf16[16,1024]{1,0:T(8,128)(2,1)S(1)}, bf16[16,1024]{1,0:T(8,128)(2,1)S(1)}, u32[]{:S(2)}, u32[]{:S(2)}) %collective-permute-start.5) | collective-permute-done | bytes 32800 | tf_op jit(solution)/shard_map/ppermute | solution.py:462
  16.2 0.9 %collective-permute-done.6.refs_1_ = bf16[16,1024]{1,0:T(8,128)(2,1)S(1)} collective-permute-done((bf16[16,1024]{1,0:T(8,128)(2,1)S(1)}, bf16[16,1024]{1,0:T(8,128)(2,1)S(1)}, u32[]{:S(2)}, u32[]{:S(2)}) %collective-permute-start.6) | collective-permute-done | bytes 32800 | tf_op jit(solution)/shard_map/ppermute | solution.py:462
  17.0 0.5 %collective-permute-done.7.refs_2_ = bf16[16,1024]{1,0:T(8,128)(2,1)S(1)} collective-permute-done((bf16[16,1024]{1,0:T(8,128)(2,1)S(1)}, bf16[16,1024]{1,0:T(8,128)(2,1)S(1)}, u32[]{:S(2)}, u32[]{:S(2)}) %collective-permute-start.7) | collective-permute-done | bytes 32800 | tf_op jit(solution)/shard_map/ppermute | solution.py:462
  17.6 0.0 collective-permute-done.8.refs_3_
  17.6 0.7 %shard_map.41 = f32[4,4,1024]{2,1,0:T(4,128)} custom-call(bf16[16,1024]{1,0:T(8,128)(2,1)S(1)} %collective-permute-done.5.refs_0_, bf16[16,1024]{1,0:T(8,128)(2,1)S(1)} %collective-permute-done.6.refs_1_, bf16[16,1024]{1,0:T(8,128)(2,1)S(1)} %collective-permute-done.7.refs_2_, bf16[16,1024]{1,0:T(8,128)(2,1)S(1)} %collective-permute-done.8.refs_3_), custom_call_target="tpu_custom_call" | custom-call | tf_op jit(solution)/shard_map/pallas_call | solution.py:408
Async XLA Ops:
  0.0 6.5 %copy-start = (s32[2,8,32,1024]{3,2,1,0:T(8,128)S(1)}, s32[2,8,32,1024]{3,2,1,0:T(8,128)}, u32[]{:S(2)}) copy-start(s32[2,8,32,1024]{3,2,1,0:T(8,128)} %volume_ref.5) | copy-start | bytes 6291460
  0.0 6.5 %copy-start.2 = (s32[256]{0:T(256)S(1)}, s32[256]{0:T(256)}, u32[]{:S(2)}) copy-start(s32[256]{0:T(256)} %param.5) | copy-start | bytes 3076
  0.0 6.5 %copy-start.1 = (s32[3,256]{1,0:T(4,128)S(1)}, s32[3,256]{1,0:T(4,128)}, u32[]{:S(2)}) copy-start(s32[3,256]{1,0:T(4,128)} %color_ref.1) | copy-start | bytes 9220
  1.3 8.2 %collective-permute-start.2 = (bf16[32,1024]{1,0:T(8,128)(2,1)S(1)}, bf16[32,1024]{1,0:T(8,128)(2,1)S(1)}, u32[]{:S(2)}, u32[]{:S(2)}) collective-permute-start(bf16[32,1024]{1,0:T(8,128)(2,1)S(1)} %get-tuple-element.29), channel_id=1, source_target_pairs={{0,28},{1,29},{2,30},{3,31},{4,8},{5,9},{6,10},{7,11},{8,4},{9,5},... | collective-permute-start | bytes 196616 | tf_op jit(solution)/shard_map/ppermute | solution.py:458
  3.2 6.4 %collective-permute-start.3 = (bf16[32,1024]{1,0:T(8,128)(2,1)S(1)}, bf16[32,1024]{1,0:T(8,128)(2,1)S(1)}, u32[]{:S(2)}, u32[]{:S(2)}) collective-permute-start(bf16[32,1024]{1,0:T(8,128)(2,1)S(1)} %get-tuple-element.30), channel_id=1, source_target_pairs={{0,4},{1,5},{2,6},{3,7},{4,0},{5,1},{6,2},{7,3},{8,12},{9,13},{10,... | collective-permute-start | bytes 196616 | tf_op jit(solution)/shard_map/ppermute | solution.py:458
  4.0 5.6 %collective-permute-start = (bf16[8,1024]{1,0:T(8,128)(2,1)S(1)}, bf16[8,1024]{1,0:T(8,128)(2,1)S(1)}, u32[]{:S(2)}, u32[]{:S(2)}) collective-permute-start(bf16[8,1024]{1,0:T(8,128)(2,1)S(1)} %get-tuple-element.27), channel_id=1, source_target_pairs={{0,1},{1,0},{2,3},{3,2},{4,5},{5,4},{6,7},{7,6},{8,9},{9,8},{10,11... | collective-permute-start | bytes 49160 | tf_op jit(solution)/shard_map/ppermute | solution.py:458
  4.1 5.4 %collective-permute-start.1 = (bf16[8,1024]{1,0:T(8,128)(2,1)S(1)}, bf16[8,1024]{1,0:T(8,128)(2,1)S(1)}, u32[]{:S(2)}, u32[]{:S(2)}) collective-permute-start(bf16[8,1024]{1,0:T(8,128)(2,1)S(1)} %get-tuple-element.28), channel_id=1, source_target_pairs={{0,4},{1,2},{2,1},{3,7},{4,0},{5,6},{6,5},{7,3},{8,12},{9,10},{10,... | collective-permute-start | bytes 49160 | tf_op jit(solution)/shard_map/ppermute | solution.py:458
  10.1 1.6 %collective-permute-start.4 = (bf16[4,16,1024]{2,1,0:T(8,128)(2,1)S(1)}, bf16[4,16,1024]{2,1,0:T(8,128)(2,1)S(1)}, u32[]{:S(2)}, u32[]{:S(2)}) collective-permute-start(bf16[4,16,1024]{2,1,0:T(8,128)(2,1)S(1)} %get-tuple-element.32), channel_id=1, source_target_pairs={{0,4},{4,0},{8,12},{12,8},{16,20},{20,16},{24,28},{28,24},{1,5},{5... | collective-permute-start | bytes 393224 | tf_op jit(solution)/shard_map/ppermute | solution.py:462
  11.8 4.4 %collective-permute-start.5 = (bf16[16,1024]{1,0:T(8,128)(2,1)S(1)}, bf16[16,1024]{1,0:T(8,128)(2,1)S(1)}, u32[]{:S(2)}, u32[]{:S(2)}) collective-permute-start(bf16[16,1024]{1,0:T(8,128)(2,1)S(1)} %get-tuple-element.33), channel_id=1, source_target_pairs={{0,28},{4,24},{8,20},{12,16},{16,12},{20,8},{24,4},{28,0},{1,29},{... | collective-permute-start | bytes 98312 | tf_op jit(solution)/shard_map/ppermute | solution.py:462
  12.9 4.1 %collective-permute-start.6 = (bf16[16,1024]{1,0:T(8,128)(2,1)S(1)}, bf16[16,1024]{1,0:T(8,128)(2,1)S(1)}, u32[]{:S(2)}, u32[]{:S(2)}) collective-permute-start(bf16[16,1024]{1,0:T(8,128)(2,1)S(1)} %get-tuple-element.34), channel_id=1, source_target_pairs={{0,20},{4,16},{8,28},{12,24},{16,4},{20,0},{24,12},{28,8},{1,21},{... | collective-permute-start | bytes 98312 | tf_op jit(solution)/shard_map/ppermute | solution.py:462
  14.2 3.3 %collective-permute-start.7 = (bf16[16,1024]{1,0:T(8,128)(2,1)S(1)}, bf16[16,1024]{1,0:T(8,128)(2,1)S(1)}, u32[]{:S(2)}, u32[]{:S(2)}) collective-permute-start(bf16[16,1024]{1,0:T(8,128)(2,1)S(1)} %get-tuple-element.35), channel_id=1, source_target_pairs={{0,12},{4,8},{8,4},{12,0},{16,28},{20,24},{24,20},{28,16},{1,13},{... | collective-permute-start | bytes 98312 | tf_op jit(solution)/shard_map/ppermute | solution.py:462
  15.0 2.6 %collective-permute-start.8 = (bf16[16,1024]{1,0:T(8,128)(2,1)S(1)}, bf16[16,1024]{1,0:T(8,128)(2,1)S(1)}, u32[]{:S(2)}, u32[]{:S(2)}) collective-permute-start(bf16[16,1024]{1,0:T(8,128)(2,1)S(1)} %get-tuple-element.36), channel_id=1, source_target_pairs={{0,4},{4,0},{8,12},{12,8},{16,20},{20,16},{24,28},{28,24},{1,5},{5... | collective-permute-start | bytes 98312 | tf_op jit(solution)/shard_map/ppermute | solution.py:462

commit v3 on v2

--- a/solution.py
+++ b/solution.py
@@ -281,6 +281,8 @@
     first_row, last_row = row == 0, row == SUBLANES - 1
     level = lax.broadcasted_iota(jnp.int32, (slices, LANES), 0)
     front, back = level == 0, level == slices - 1
+    if len(out_refs) > 1:
+        keep_ref, give_ref, same_ref, cross_ref, theirs_ref, mine_ref = out_refs
     odd, odd_row = parity("depth") == 1, parity("rows") == 1
     front_end, back_end = ends("depth")
     top_end, bottom_end = ends("rows")
@@ -333,20 +335,35 @@
                 for i, block in enumerate(blocks):
                     out_refs[0][r * len(blocks) + i, :, here] = block.astype(jnp.bfloat16)
             else:
-                keep_ref, give_ref = out_refs
-                keep_ref[r, :, here] = jnp.where(odd, blocks[0], blocks[1])
-                give_ref[r, :, here] = jnp.where(odd, blocks[1], blocks[0]).astype(jnp.bfloat16)
+                theirs_ref[r, :, here] = jnp.where(odd, blocks[0], blocks[1])
+                mine_ref[r, :, here] = jnp.where(odd, blocks[1], blocks[0]).astype(jnp.bfloat16)
         return carry
 
     lax.fori_loop(0, columns // LANES, chunk, 0)
+    if len(out_refs) > 1:
+        chip = lax.axis_index("depth") // 2
+        last = theirs_ref.shape[0] - 1
+        for k in range(last):
+            keep_ref[k] = theirs_ref[chip ^ k]
+            give_ref[k] = mine_ref[chip ^ k]
+        same_ref[...] = mine_ref[chip ^ last]
+        cross_ref[...] = theirs_ref[chip ^ last].astype(jnp.bfloat16)
 
 
 def add_edges(volume, interior, halos, depth_count, paired):
     _, slices, height, columns = volume.shape
     share = height // depth_count
+    scratch = []
     if paired:
-        half = (depth_count // 2, 4 * share, columns)
-        shapes = [jax.ShapeDtypeStruct(half, jnp.float32), jax.ShapeDtypeStruct(half, jnp.bfloat16)]
+        chips = depth_count // 2
+        block = (4 * share, columns)
+        shapes = [
+            jax.ShapeDtypeStruct((chips - 1, *block), jnp.float32),
+            jax.ShapeDtypeStruct((chips - 1, *block), jnp.bfloat16),
+            jax.ShapeDtypeStruct(block, jnp.bfloat16),
+            jax.ShapeDtypeStruct(block, jnp.bfloat16),
+        ]
+        scratch = [pltpu.VMEM((chips, *block), jnp.float32), pltpu.VMEM((chips, *block), jnp.bfloat16)]
     else:
         shapes = [jax.ShapeDtypeStruct((depth_count, 4 * share, columns), jnp.bfloat16)]
     return pl.pallas_call(
@@ -354,6 +371,7 @@
         in_specs=[WHOLE] * 11,
         out_specs=[WHOLE] * len(shapes),
         out_shape=shapes,
+        scratch_shapes=scratch,
         compiler_params=pltpu.CompilerParams(vmem_limit_bytes=24 * 1024 * 1024),
     )(volume, *interior, *halos)
 
@@ -365,34 +383,34 @@
 
 
 def merge_kernel(keep_ref, other_ref, *send_refs):
-    position = lax.axis_index("depth")
-    odd, chip = position % 2 == 1, position // 2
+    odd = parity("depth") == 1
     for k, out_ref in enumerate(send_refs):
-        keep = keep_ref[chip ^ k]
-        other = other_ref[chip ^ k].astype(jnp.float32)
+        keep = keep_ref[k]
+        other = other_ref[k].astype(jnp.float32)
         out_ref[...] = over(jnp.where(odd, other, keep), jnp.where(odd, keep, other)).astype(out_ref.dtype)
 
 
 def merge(keep, other):
-    chips, rows, columns = keep.shape
+    count, rows, columns = keep.shape
     return pl.pallas_call(
         merge_kernel,
         in_specs=[WHOLE] * 2,
-        out_specs=[WHOLE] * chips,
-        out_shape=[jax.ShapeDtypeStruct((rows, columns), jnp.bfloat16)] * chips,
-        compiler_params=pltpu.CompilerParams(vmem_limit_bytes=8 * 1024 * 1024),
+        out_specs=[WHOLE] * count,
+        out_shape=[jax.ShapeDtypeStruct((rows, columns), jnp.bfloat16)] * count,
+        compiler_params=pltpu.CompilerParams(vmem_limit_bytes=4 * 1024 * 1024),
     )(keep, other)
 
 
-def gather_kernel(*refs):
+def gather_kernel(same_ref, cross_ref, *refs):
     *part_refs, out_ref = refs
-    part_refs.reverse()
-    count = len(part_refs)
     share = out_ref.shape[1]
-    chip = lax.axis_index("depth") // 2
-    parts = [part_ref[...].astype(jnp.float32) for part_ref in part_refs]
+    position = lax.axis_index("depth")
+    odd, chip = position % 2 == 1, position // 2
+    parts = [part_ref[...].astype(jnp.float32) for part_ref in reversed(part_refs)]
+    same, cross = same_ref[...].astype(jnp.float32), cross_ref[...].astype(jnp.float32)
+    parts.append(over(jnp.where(odd, cross, same), jnp.where(odd, same, cross)))
     step = 1
-    while step < count:
+    while len(parts) > 1:
         swap = (chip & step) != 0
         parts = [
             over(jnp.where(swap, parts[i + 1], parts[i]), jnp.where(swap, parts[i], parts[i + 1]))
@@ -476,9 +494,12 @@
     outs = add_edges(volume, interior, halos, depth_count, paired)
     if not paired:
         return finish(lax.all_to_all(outs[0], "depth", 0, 0, tiled=True), share)
-    keep, give = outs
-    sends = merge(keep, exchanged(give, 1))
-    return gather([exchanged(send, 2 * k + 1) for k, send in reversed(list(enumerate(sends)))], share)
+    keep, give, same, cross = outs
+    other = exchanged(give, 1)
+    same, cross = exchanged(same, depth_count - 2), exchanged(cross, depth_count - 1)
+    sends = merge(keep, other)
+    received = [exchanged(send, 2 * k + 1) for k, send in reversed(list(enumerate(sends)))]
+    return gather((same, cross, *received), share)
 
 
 def solution(mesh):

time: 18.4 us -> 19 us (1.033)
  the two profiles are of different devices: /device:TPU:9 before, /device:TPU:0 now
where the time goes in v3:
time: 19 us; the launch traced here: 18.8 us
  starting transfers between devices  10.1 us (53%)
  Pallas kernels  5.56 us (29%)
  waiting for transfers between devices  3.09 us (16%)
    ppermute x4, starting transfers between devices, swapped(): return lax.ppermute(values, ('depth', 'rows'), perm)  5.22 us
    ppermute x6, starting transfers between devices, exchanged(): lax.ppermute(values, 'depth', [(d, d ^ mask) for d in range(lax.axis_size...  4.89 us
    ppermute x6, waiting for transfers between devices, exchanged(): lax.ppermute(values, 'depth', [(d, d ^ mask) for d in range(lax.axis_size...  3.08 us
    pallas_call x1, Pallas kernels, march_interior(): pl.pallas_call(functools.partial(interior_kernel, opacity_scale), in_spec...  2.95 us
    pallas_call x1, Pallas kernels, cut_edges(): pl.pallas_call(edges_kernel, in_specs=[pl.BlockSpec(memory_space=pl.ANY)]...  1.29 us
    pallas_call x1, Pallas kernels, gather(): pl.pallas_call(gather_kernel, in_specs=[WHOLE] * len(parts), out_specs=WH...  0.71 us
    pallas_call x1, Pallas kernels, add_edges(): pl.pallas_call(functools.partial(edge_kernel, share), in_specs=[WHOLE] *...  0.54 us
  transfers between devices with their start and end apart: 10, of which 4 were waited for; matrix products, arithmetic and copies ran while one was open for 0% of the time, Pallas kernels for 16%

profile of v3, /device:TPU:0, one launch (start us, length us, event | category | flops | bytes accessed | tf_op | source)
XLA Modules:
  0.0 18.8 jit_solution(9252193088518064736)
XLA Ops:
  0.0 0.0 copy-start
  0.0 0.0 copy-start.2
  0.0 0.0 copy-start.1
  0.0 1.3 %shard_map.38 = (bf16[8,1024]{1,0:T(8,128)(2,1)S(1)}, bf16[8,1024]{1,0:T(8,128)(2,1)S(1)}, bf16[32,1024]{1,0:T(8,128)(2,1)S(1)}, bf16[32,1024]{1,0:T(8,128)(2,1)S(1)}) custom-call(s32[2,8,32,1024]{3,2,1,0:T(8,128)} %volume_ref.5), custom_call_target="tpu_custom_call" | custom-call | tf_op jit(solution)/shard_map/pallas_call | solution.py:64
  1.3 3.4 %collective-permute-start.2 = (bf16[32,1024]{1,0:T(8,128)(2,1)S(1)}, bf16[32,1024]{1,0:T(8,128)(2,1)S(1)}, u32[]{:S(2)}, u32[]{:S(2)}) collective-permute-start(bf16[32,1024]{1,0:T(8,128)(2,1)S(1)} %get-tuple-element.30), channel_id=1, source_target_pairs={{0,28},{1,29},{2,30},{3,31},{4,8},{5,9},{6,10},{7,11},{8,4},{9,5},... | collective-permute-start | bytes 196616 | tf_op jit(solution)/shard_map/ppermute | solution.py:476
  4.7 0.0 collective-permute-start.3
  4.7 1.6 %collective-permute-start = (bf16[8,1024]{1,0:T(8,128)(2,1)S(1)}, bf16[8,1024]{1,0:T(8,128)(2,1)S(1)}, u32[]{:S(2)}, u32[]{:S(2)}) collective-permute-start(bf16[8,1024]{1,0:T(8,128)(2,1)S(1)} %get-tuple-element.28), channel_id=1, source_target_pairs={{0,1},{1,0},{2,3},{3,2},{4,5},{5,4},{6,7},{7,6},{8,9},{9,8},{10,11... | collective-permute-start | bytes 49160 | tf_op jit(solution)/shard_map/ppermute | solution.py:476
  6.3 0.2 %collective-permute-start.1 = (bf16[8,1024]{1,0:T(8,128)(2,1)S(1)}, bf16[8,1024]{1,0:T(8,128)(2,1)S(1)}, u32[]{:S(2)}, u32[]{:S(2)}) collective-permute-start(bf16[8,1024]{1,0:T(8,128)(2,1)S(1)} %get-tuple-element.29), channel_id=1, source_target_pairs={{0,4},{1,2},{2,1},{3,7},{4,0},{5,6},{6,5},{7,3},{8,12},{9,10},{10,... | collective-permute-start | bytes 49160 | tf_op jit(solution)/shard_map/ppermute | solution.py:476
  6.5 0.0 copy-done
  6.5 0.0 copy-done.2
  6.5 0.0 copy-done.1
  6.5 3.0 %shard_map.37 = (f32[4,32,1024]{2,1,0:T(8,128)S(1)}, f32[2,32,1024]{2,1,0:T(8,128)S(1)}, f32[2,32,1024]{2,1,0:T(8,128)S(1)}, f32[2,3,32,1024]{3,2,1,0:T(8,128)S(...) custom-call(s32[2,8,32,1024]{3,2,1,0:T(8,128)S(1)} %copy-done, s32[3,256]{1,0:T(4,128)S(1)} %copy-done.1, ...), custom_call_target="tpu_custom_call" | custom-call | flops 20971520 | bytes 5242880 | tf_op jit(solution)/shard_map/pallas_call | solution.py:260
  9.5 0.0 collective-permute-done.rows_near_ref
  9.5 0.0 collective-permute-done.1.rows_far_ref
  9.5 0.0 collective-permute-done.2.far_ref
  9.5 0.0 collective-permute-done.3.near_ref
  9.5 0.5 %shard_map.39 = (f32[3,16,1024]{2,1,0:T(8,128)S(1)}, bf16[3,16,1024]{2,1,0:T(8,128)(2,1)S(1)}, bf16[16,1024]{1,0:T(8,128)(2,1)S(1)}, bf16[16,1024]{1,0:T(8,128)(2,1)S(1)}) custom-call(s32[2,8,32,1024]{3,2,1,0:T(8,128)S(1)} %copy-done, f32[4,32,1024]{2,1,0:T(8,128)S(1)} %get-tuple-element.22.base_ref, f32[2,32,1024]{2,1,0:T(8,128)S(1)} %get-tuple-element.23.face_ref, ...), custom_call_target="tpu_custom_call" | custom-call | tf_op jit(solution)/shard_map/pallas_call | solution.py:369
  10.1 0.3 %collective-permute-start.6 = (bf16[3,16,1024]{2,1,0:T(8,128)(2,1)S(1)}, bf16[3,16,1024]{2,1,0:T(8,128)(2,1)S(1)}, u32[]{:S(2)}, u32[]{:S(2)}) collective-permute-start(bf16[3,16,1024]{2,1,0:T(8,128)(2,1)S(1)} %get-tuple-element.35), channel_id=1, source_target_pairs={{0,4},{4,0},{8,12},{12,8},{16,20},{20,16},{24,28},{28,24},{1,5},{5... | collective-permute-start | bytes 294920 | tf_op jit(solution)/shard_map/ppermute | solution.py:480
  10.4 1.2 %collective-permute-start.4 = (bf16[16,1024]{1,0:T(8,128)(2,1)S(1)}, bf16[16,1024]{1,0:T(8,128)(2,1)S(1)}, u32[]{:S(2)}, u32[]{:S(2)}) collective-permute-start(bf16[16,1024]{1,0:T(8,128)(2,1)S(1)} %get-tuple-element.32), channel_id=1, source_target_pairs={{0,24},{4,28},{8,16},{12,20},{16,8},{20,12},{24,0},{28,4},{1,25},{... | collective-permute-start | bytes 98312 | tf_op jit(solution)/shard_map/ppermute | solution.py:480
  11.6 1.3 %collective-permute-start.5 = (bf16[16,1024]{1,0:T(8,128)(2,1)S(1)}, bf16[16,1024]{1,0:T(8,128)(2,1)S(1)}, u32[]{:S(2)}, u32[]{:S(2)}) collective-permute-start(bf16[16,1024]{1,0:T(8,128)(2,1)S(1)} %get-tuple-element.33), channel_id=1, source_target_pairs={{0,28},{4,24},{8,20},{12,16},{16,12},{20,8},{24,4},{28,0},{1,29},{... | collective-permute-start | bytes 98312 | tf_op jit(solution)/shard_map/ppermute | solution.py:480
  12.9 0.0 collective-permute-done.6.other_ref
  12.9 0.1 shard_map.40
  13.0 1.5 %collective-permute-start.7 = (bf16[16,1024]{1,0:T(8,128)(2,1)S(1)}, bf16[16,1024]{1,0:T(8,128)(2,1)S(1)}, u32[]{:S(2)}, u32[]{:S(2)}) collective-permute-start(bf16[16,1024]{1,0:T(8,128)(2,1)S(1)} %get-tuple-element.36), channel_id=1, source_target_pairs={{0,20},{4,16},{8,28},{12,24},{16,4},{20,0},{24,12},{28,8},{1,21},{... | collective-permute-start | bytes 98312 | tf_op jit(solution)/shard_map/ppermute | solution.py:480
  14.5 0.1 collective-permute-start.8
  14.5 0.5 %collective-permute-start.9 = (bf16[16,1024]{1,0:T(8,128)(2,1)S(1)}, bf16[16,1024]{1,0:T(8,128)(2,1)S(1)}, u32[]{:S(2)}, u32[]{:S(2)}) collective-permute-start(bf16[16,1024]{1,0:T(8,128)(2,1)S(1)} %get-tuple-element.38), channel_id=1, source_target_pairs={{0,4},{4,0},{8,12},{12,8},{16,20},{20,16},{24,28},{28,24},{1,5},{5... | collective-permute-start | bytes 98312 | tf_op jit(solution)/shard_map/ppermute | solution.py:480
  15.1 0.2 %collective-permute-done.4.same_ref = bf16[16,1024]{1,0:T(8,128)(2,1)S(1)} collective-permute-done((bf16[16,1024]{1,0:T(8,128)(2,1)S(1)}, bf16[16,1024]{1,0:T(8,128)(2,1)S(1)}, u32[]{:S(2)}, u32[]{:S(2)}) %collective-permute-start.4) | collective-permute-done | bytes 32800 | tf_op jit(solution)/shard_map/ppermute | solution.py:480
  15.2 0.9 %collective-permute-done.5.cross_ref = bf16[16,1024]{1,0:T(8,128)(2,1)S(1)} collective-permute-done((bf16[16,1024]{1,0:T(8,128)(2,1)S(1)}, bf16[16,1024]{1,0:T(8,128)(2,1)S(1)}, u32[]{:S(2)}, u32[]{:S(2)}) %collective-permute-start.5) | collective-permute-done | bytes 32800 | tf_op jit(solution)/shard_map/ppermute | solution.py:480
  16.2 0.3 %collective-permute-done.7.refs_0_ = bf16[16,1024]{1,0:T(8,128)(2,1)S(1)} collective-permute-done((bf16[16,1024]{1,0:T(8,128)(2,1)S(1)}, bf16[16,1024]{1,0:T(8,128)(2,1)S(1)}, u32[]{:S(2)}, u32[]{:S(2)}) %collective-permute-start.7) | collective-permute-done | bytes 32800 | tf_op jit(solution)/shard_map/ppermute | solution.py:480
  16.5 1.6 %collective-permute-done.8.refs_1_ = bf16[16,1024]{1,0:T(8,128)(2,1)S(1)} collective-permute-done((bf16[16,1024]{1,0:T(8,128)(2,1)S(1)}, bf16[16,1024]{1,0:T(8,128)(2,1)S(1)}, u32[]{:S(2)}, u32[]{:S(2)}) %collective-permute-start.8) | collective-permute-done | bytes 32800 | tf_op jit(solution)/shard_map/ppermute | solution.py:480
  18.1 0.0 collective-permute-done.9.refs_2_
  18.1 0.7 %shard_map.41 = f32[4,4,1024]{2,1,0:T(4,128)} custom-call(bf16[16,1024]{1,0:T(8,128)(2,1)S(1)} %collective-permute-done.4.same_ref, bf16[16,1024]{1,0:T(8,128)(2,1)S(1)} %collective-permute-done.5.cross_ref, bf16[16,1024]{1,0:T(8,128)(2,1)S(1)} %collective-permute-done.7.refs_0_, bf16[16,1024]{1,0:T(8,128)(2,1)S(1)} %collective-permute-done.8.refs_1_, ...), custom_call_target="tpu_custom_call" | custom-call | tf_op jit(solution)/shard_map/pallas_call | solution.py:426
Async XLA Ops:
  0.0 6.5 %copy-start = (s32[2,8,32,1024]{3,2,1,0:T(8,128)S(1)}, s32[2,8,32,1024]{3,2,1,0:T(8,128)}, u32[]{:S(2)}) copy-start(s32[2,8,32,1024]{3,2,1,0:T(8,128)} %volume_ref.5) | copy-start | bytes 6291460
  0.0 6.5 %copy-start.2 = (s32[256]{0:T(256)S(1)}, s32[256]{0:T(256)}, u32[]{:S(2)}) copy-start(s32[256]{0:T(256)} %param.5) | copy-start | bytes 3076
  0.0 6.5 %copy-start.1 = (s32[3,256]{1,0:T(4,128)S(1)}, s32[3,256]{1,0:T(4,128)}, u32[]{:S(2)}) copy-start(s32[3,256]{1,0:T(4,128)} %color_ref.1) | copy-start | bytes 9220
  1.3 8.2 %collective-permute-start.2 = (bf16[32,1024]{1,0:T(8,128)(2,1)S(1)}, bf16[32,1024]{1,0:T(8,128)(2,1)S(1)}, u32[]{:S(2)}, u32[]{:S(2)}) collective-permute-start(bf16[32,1024]{1,0:T(8,128)(2,1)S(1)} %get-tuple-element.30), channel_id=1, source_target_pairs={{0,28},{1,29},{2,30},{3,31},{4,8},{5,9},{6,10},{7,11},{8,4},{9,5},... | collective-permute-start | bytes 196616 | tf_op jit(solution)/shard_map/ppermute | solution.py:476
  4.7 4.8 %collective-permute-start.3 = (bf16[32,1024]{1,0:T(8,128)(2,1)S(1)}, bf16[32,1024]{1,0:T(8,128)(2,1)S(1)}, u32[]{:S(2)}, u32[]{:S(2)}) collective-permute-start(bf16[32,1024]{1,0:T(8,128)(2,1)S(1)} %get-tuple-element.31), channel_id=1, source_target_pairs={{0,4},{1,5},{2,6},{3,7},{4,0},{5,1},{6,2},{7,3},{8,12},{9,13},{10,... | collective-permute-start | bytes 196616 | tf_op jit(solution)/shard_map/ppermute | solution.py:476
  4.7 4.8 %collective-permute-start = (bf16[8,1024]{1,0:T(8,128)(2,1)S(1)}, bf16[8,1024]{1,0:T(8,128)(2,1)S(1)}, u32[]{:S(2)}, u32[]{:S(2)}) collective-permute-start(bf16[8,1024]{1,0:T(8,128)(2,1)S(1)} %get-tuple-element.28), channel_id=1, source_target_pairs={{0,1},{1,0},{2,3},{3,2},{4,5},{5,4},{6,7},{7,6},{8,9},{9,8},{10,11... | collective-permute-start | bytes 49160 | tf_op jit(solution)/shard_map/ppermute | solution.py:476
  6.3 3.2 %collective-permute-start.1 = (bf16[8,1024]{1,0:T(8,128)(2,1)S(1)}, bf16[8,1024]{1,0:T(8,128)(2,1)S(1)}, u32[]{:S(2)}, u32[]{:S(2)}) collective-permute-start(bf16[8,1024]{1,0:T(8,128)(2,1)S(1)} %get-tuple-element.29), channel_id=1, source_target_pairs={{0,4},{1,2},{2,1},{3,7},{4,0},{5,6},{6,5},{7,3},{8,12},{9,10},{10,... | collective-permute-start | bytes 49160 | tf_op jit(solution)/shard_map/ppermute | solution.py:476
  10.1 2.8 %collective-permute-start.6 = (bf16[3,16,1024]{2,1,0:T(8,128)(2,1)S(1)}, bf16[3,16,1024]{2,1,0:T(8,128)(2,1)S(1)}, u32[]{:S(2)}, u32[]{:S(2)}) collective-permute-start(bf16[3,16,1024]{2,1,0:T(8,128)(2,1)S(1)} %get-tuple-element.35), channel_id=1, source_target_pairs={{0,4},{4,0},{8,12},{12,8},{16,20},{20,16},{24,28},{28,24},{1,5},{5... | collective-permute-start | bytes 294920 | tf_op jit(solution)/shard_map/ppermute | solution.py:480
  10.4 4.8 %collective-permute-start.4 = (bf16[16,1024]{1,0:T(8,128)(2,1)S(1)}, bf16[16,1024]{1,0:T(8,128)(2,1)S(1)}, u32[]{:S(2)}, u32[]{:S(2)}) collective-permute-start(bf16[16,1024]{1,0:T(8,128)(2,1)S(1)} %get-tuple-element.32), channel_id=1, source_target_pairs={{0,24},{4,28},{8,16},{12,20},{16,8},{20,12},{24,0},{28,4},{1,25},{... | collective-permute-start | bytes 98312 | tf_op jit(solution)/shard_map/ppermute | solution.py:480
  11.6 4.6 %collective-permute-start.5 = (bf16[16,1024]{1,0:T(8,128)(2,1)S(1)}, bf16[16,1024]{1,0:T(8,128)(2,1)S(1)}, u32[]{:S(2)}, u32[]{:S(2)}) collective-permute-start(bf16[16,1024]{1,0:T(8,128)(2,1)S(1)} %get-tuple-element.33), channel_id=1, source_target_pairs={{0,28},{4,24},{8,20},{12,16},{16,12},{20,8},{24,4},{28,0},{1,29},{... | collective-permute-start | bytes 98312 | tf_op jit(solution)/shard_map/ppermute | solution.py:480
  13.0 3.5 %collective-permute-start.7 = (bf16[16,1024]{1,0:T(8,128)(2,1)S(1)}, bf16[16,1024]{1,0:T(8,128)(2,1)S(1)}, u32[]{:S(2)}, u32[]{:S(2)}) collective-permute-start(bf16[16,1024]{1,0:T(8,128)(2,1)S(1)} %get-tuple-element.36), channel_id=1, source_target_pairs={{0,20},{4,16},{8,28},{12,24},{16,4},{20,0},{24,12},{28,8},{1,21},{... | collective-permute-start | bytes 98312 | tf_op jit(solution)/shard_map/ppermute | solution.py:480
  14.5 3.7 %collective-permute-start.8 = (bf16[16,1024]{1,0:T(8,128)(2,1)S(1)}, bf16[16,1024]{1,0:T(8,128)(2,1)S(1)}, u32[]{:S(2)}, u32[]{:S(2)}) collective-permute-start(bf16[16,1024]{1,0:T(8,128)(2,1)S(1)} %get-tuple-element.37), channel_id=1, source_target_pairs={{0,12},{4,8},{8,4},{12,0},{16,28},{20,24},{24,20},{28,16},{1,13},{... | collective-permute-start | bytes 98312 | tf_op jit(solution)/shard_map/ppermute | solution.py:480
  14.5 3.6 %collective-permute-start.9 = (bf16[16,1024]{1,0:T(8,128)(2,1)S(1)}, bf16[16,1024]{1,0:T(8,128)(2,1)S(1)}, u32[]{:S(2)}, u32[]{:S(2)}) collective-permute-start(bf16[16,1024]{1,0:T(8,128)(2,1)S(1)} %get-tuple-element.38), channel_id=1, source_target_pairs={{0,4},{4,0},{8,12},{12,8},{16,20},{20,16},{24,28},{28,24},{1,5},{5... | collective-permute-start | bytes 98312 | tf_op jit(solution)/shard_map/ppermute | solution.py:480

commit v4 on v2

--- a/solution.py
+++ b/solution.py
@@ -30,14 +30,10 @@
 def edges_kernel(volume_ref, rows_far_out, rows_near_out, far_out, near_out, strip_ref, plane_ref, sems):
     _, slices, height, _ = volume_ref.shape
     odd, odd_row = parity("depth"), parity("rows")
-    last_tile = height // SUBLANES - 1
-
-    def tile(i):
-        return pl.ds(pl.multiple_of(i * SUBLANES, SUBLANES), SUBLANES)
 
     copies = [
-        pltpu.make_async_copy(volume_ref.at[0, :, tile((1 - odd_row) * last_tile)], strip_ref.at[0], sems.at[0]),
-        pltpu.make_async_copy(volume_ref.at[0, :, tile(odd_row * last_tile)], strip_ref.at[1], sems.at[1]),
+        pltpu.make_async_copy(volume_ref.at[0, :, (1 - odd_row) * (height - 1)], strip_ref.at[0], sems.at[0]),
+        pltpu.make_async_copy(volume_ref.at[0, :, odd_row * (height - 1)], strip_ref.at[1], sems.at[1]),
         pltpu.make_async_copy(volume_ref.at[0, odd * (slices - 1)], plane_ref.at[0], sems.at[2]),
         pltpu.make_async_copy(volume_ref.at[0, (1 - odd) * (slices - 1)], plane_ref.at[1], sems.at[3]),
     ]
@@ -48,9 +44,9 @@
         return values.astype(jnp.float32).astype(jnp.bfloat16)
 
     copies[0].wait()
-    rows_near_out[...] = narrow(jnp.where(odd_row == 1, strip_ref[0, :, 0, :], strip_ref[0, :, SUBLANES - 1, :]))
+    rows_near_out[...] = narrow(strip_ref[0])
     copies[1].wait()
-    rows_far_out[...] = narrow(jnp.where(odd_row == 1, strip_ref[1, :, SUBLANES - 1, :], strip_ref[1, :, 0, :]))
+    rows_far_out[...] = narrow(strip_ref[1])
     copies[2].wait()
     far_out[...] = narrow(plane_ref[0])
     copies[3].wait()
@@ -67,7 +63,7 @@
         out_specs=[WHOLE] * 4,
         out_shape=[strip, strip, plane, plane],
         scratch_shapes=[
-            pltpu.VMEM((2, slices, SUBLANES, columns), jnp.int32),
+            pltpu.VMEM((2, slices, columns), jnp.int32),
             pltpu.VMEM((2, height, columns), jnp.int32),
             pltpu.SemaphoreType.DMA((4,)),
         ],
@@ -271,6 +267,17 @@
     )(volume, color_map, alpha_map.reshape(1, -1))
 
 
+def row_sums(first, second):
+    count = first.shape[0]
+    if count != SUBLANES:
+        return jnp.sum(first, axis=0, keepdims=True), jnp.sum(second, axis=0, keepdims=True)
+    upper = lax.broadcasted_iota(jnp.int32, first.shape, 0) < 4
+    both = jnp.where(upper, first, second) + pltpu.roll(jnp.where(upper, second, first), 4, 0)
+    both = both + pltpu.roll(both, 6, 0)
+    both = both + pltpu.roll(both, 7, 0)
+    return both, pltpu.roll(both, 3, 0)
+
+
 def edge_kernel(
     share, volume_ref, base_ref, face_ref, square_ref, lit_ref, grad_ref, strip_ref, rows_near_ref, rows_far_ref, far_ref, near_ref, *out_refs
 ):
@@ -278,7 +285,7 @@
     tiles = height // SUBLANES
     tile = (SUBLANES, LANES)
     row = lax.broadcasted_iota(jnp.int32, tile, 0)
-    first_row, last_row = row == 0, row == SUBLANES - 1
+    first_row, last_row, upper = row == 0, row == SUBLANES - 1, row < SUBLANES // 2
     level = lax.broadcasted_iota(jnp.int32, (slices, LANES), 0)
     front, back = level == 0, level == slices - 1
     odd, odd_row = parity("depth") == 1, parity("rows") == 1
@@ -308,7 +315,8 @@
                 LIGHT_ROWS * grad_rows + LIGHT_COLS * grad_cols,
                 grad_rows * grad_rows + grad_cols * grad_cols,
             )
-            extra.append([jnp.sum(strip_ref[q, c, :, here] * shading, axis=0, keepdims=True) for c in range(3)])
+            extra.append([strip_ref[q, c, :, here] * shading for c in range(3)])
+        extra = [row_sums(extra[0][c], extra[1][c]) for c in range(3)]
         for r in range(tiles):
             rows = slice(r * SUBLANES, (r + 1) * SUBLANES)
             planes = [base_ref[c, rows, here] for c in range(4)]
@@ -322,20 +330,20 @@
                     planes[c] = planes[c] + lit_ref[end, c, rows, here] * shading
             for c in range(3):
                 if r == 0:
-                    planes[c] = planes[c] + jnp.where(first_row, extra[0][c], 0.0)
+                    planes[c] = planes[c] + jnp.where(first_row, extra[c][0], 0.0)
                 if r == tiles - 1:
-                    planes[c] = planes[c] + jnp.where(last_row, extra[1][c], 0.0)
-            blocks = [
-                jnp.concatenate([plane[first : first + share] for plane in planes], axis=0)
-                for first in range(0, SUBLANES, share)
-            ]
+                    planes[c] = planes[c] + jnp.where(last_row, extra[c][1], 0.0)
             if len(out_refs) == 1:
-                for i, block in enumerate(blocks):
-                    out_refs[0][r * len(blocks) + i, :, here] = block.astype(jnp.bfloat16)
+                for i, first in enumerate(range(0, SUBLANES, share)):
+                    block = jnp.concatenate([plane[first : first + share] for plane in planes], axis=0)
+                    out_refs[0][r * (SUBLANES // share) + i, :, here] = block.astype(jnp.bfloat16)
             else:
                 keep_ref, give_ref = out_refs
-                keep_ref[r, :, here] = jnp.where(odd, blocks[0], blocks[1])
-                give_ref[r, :, here] = jnp.where(odd, blocks[1], blocks[0]).astype(jnp.bfloat16)
+                halves = [(planes[c], pltpu.roll(planes[c + 1], SUBLANES // 2, 0)) for c in (0, 2)]
+                even = jnp.concatenate([jnp.where(upper, own, turned) for own, turned in halves], axis=0)
+                uneven = jnp.concatenate([jnp.where(upper, turned, own) for own, turned in halves], axis=0)
+                keep_ref[r, :, here] = jnp.where(odd, even, uneven)
+                give_ref[r, :, here] = jnp.where(odd, uneven, even).astype(jnp.bfloat16)
         return carry
 
     lax.fori_loop(0, columns // LANES, chunk, 0)
@@ -358,9 +366,9 @@
     )(volume, *interior, *halos)
 
 
-def over(nearer, farther):
+def over(nearer, farther, uneven):
     share = nearer.shape[0] // 4
-    clear = 1.0 - nearer[3 * share :]
+    clear = 1.0 - jnp.where(uneven, nearer[2 * share : 3 * share], nearer[3 * share :])
     return nearer + jnp.concatenate([clear] * 4, axis=0) * farther
 
 
@@ -370,7 +378,8 @@
     for k, out_ref in enumerate(send_refs):
         keep = keep_ref[chip ^ k]
         other = other_ref[chip ^ k].astype(jnp.float32)
-        out_ref[...] = over(jnp.where(odd, other, keep), jnp.where(odd, keep, other)).astype(out_ref.dtype)
+        block = over(jnp.where(odd, other, keep), jnp.where(odd, keep, other), jnp.logical_not(odd))
+        out_ref[...] = block.astype(out_ref.dtype)
 
 
 def merge(keep, other):
@@ -389,18 +398,20 @@
     part_refs.reverse()
     count = len(part_refs)
     share = out_ref.shape[1]
-    chip = lax.axis_index("depth") // 2
+    position = lax.axis_index("depth")
+    odd, chip = position % 2 == 1, position // 2
     parts = [part_ref[...].astype(jnp.float32) for part_ref in part_refs]
     step = 1
     while step < count:
         swap = (chip & step) != 0
         parts = [
-            over(jnp.where(swap, parts[i + 1], parts[i]), jnp.where(swap, parts[i], parts[i + 1]))
+            over(jnp.where(swap, parts[i + 1], parts[i]), jnp.where(swap, parts[i], parts[i + 1]), odd)
             for i in range(0, len(parts), 2)
         ]
         step *= 2
+    planes = [parts[0][c * share : (c + 1) * share] for c in range(4)]
     for c in range(4):
-        out_ref[c] = parts[0][c * share : (c + 1) * share]
+        out_ref[c] = jnp.where(odd, planes[c ^ 1], planes[c])
 
 
 def gather(parts, share):

time: 18.4 us -> 18.3 us (level)
  no operation moved by 1% of the time
where the time goes in v4:
time: 18.3 us; the launch traced here: 18.2 us
  starting transfers between devices  9.25 us (51%)
  Pallas kernels  5.42 us (30%)
  waiting for transfers between devices  3.41 us (19%)
    ppermute x4, starting transfers between devices, swapped(): return lax.ppermute(values, ('depth', 'rows'), perm)  5.22 us
    ppermute x5, starting transfers between devices, exchanged(): lax.ppermute(values, 'depth', [(d, d ^ mask) for d in range(lax.axis_size...  4.03 us
    ppermute x5, waiting for transfers between devices, exchanged(): lax.ppermute(values, 'depth', [(d, d ^ mask) for d in range(lax.axis_size...  3.4 us
    pallas_call x1, Pallas kernels, march_interior(): pl.pallas_call(functools.partial(interior_kernel, opacity_scale), in_spec...  2.95 us
    pallas_call x1, Pallas kernels, cut_edges(): pl.pallas_call(edges_kernel, in_specs=[pl.BlockSpec(memory_space=pl.ANY)]...  1.21 us
    pallas_call x1, Pallas kernels, gather(): pl.pallas_call(gather_kernel, in_specs=[WHOLE] * len(parts), out_specs=WH...  0.7 us
    pallas_call x1, Pallas kernels, add_edges(): pl.pallas_call(functools.partial(edge_kernel, share), in_specs=[WHOLE] *...  0.48 us
  transfers between devices with their start and end apart: 9, of which 4 were waited for; matrix products, arithmetic and copies ran while one was open for 0% of the time, Pallas kernels for 16%

profile of v4, /device:TPU:9, one launch (start us, length us, event | category | flops | bytes accessed | tf_op | source)
XLA Modules:
  0.0 18.2 jit_solution(17102653332075426182)
XLA Ops:
  0.0 0.0 copy-start
  0.0 0.0 copy-start.2
  0.0 0.0 copy-start.1
  0.0 1.2 %shard_map.38 = (bf16[8,1024]{1,0:T(8,128)(2,1)S(1)}, bf16[8,1024]{1,0:T(8,128)(2,1)S(1)}, bf16[32,1024]{1,0:T(8,128)(2,1)S(1)}, bf16[32,1024]{1,0:T(8,128)(2,1)S(1)}) custom-call(s32[2,8,32,1024]{3,2,1,0:T(8,128)} %volume_ref.5), custom_call_target="tpu_custom_call" | custom-call | tf_op jit(solution)/shard_map/pallas_call | solution.py:60
  1.2 1.8 %collective-permute-start.2 = (bf16[32,1024]{1,0:T(8,128)(2,1)S(1)}, bf16[32,1024]{1,0:T(8,128)(2,1)S(1)}, u32[]{:S(2)}, u32[]{:S(2)}) collective-permute-start(bf16[32,1024]{1,0:T(8,128)(2,1)S(1)} %get-tuple-element.29), channel_id=1, source_target_pairs={{0,28},{1,29},{2,30},{3,31},{4,8},{5,9},{6,10},{7,11},{8,4},{9,5},... | collective-permute-start | bytes 196616 | tf_op jit(solution)/shard_map/ppermute | solution.py:469
  3.1 0.8 %collective-permute-start.3 = (bf16[32,1024]{1,0:T(8,128)(2,1)S(1)}, bf16[32,1024]{1,0:T(8,128)(2,1)S(1)}, u32[]{:S(2)}, u32[]{:S(2)}) collective-permute-start(bf16[32,1024]{1,0:T(8,128)(2,1)S(1)} %get-tuple-element.30), channel_id=1, source_target_pairs={{0,4},{1,5},{2,6},{3,7},{4,0},{5,1},{6,2},{7,3},{8,12},{9,13},{10,... | collective-permute-start | bytes 196616 | tf_op jit(solution)/shard_map/ppermute | solution.py:469
  3.9 0.2 collective-permute-start
  4.0 2.4 %collective-permute-start.1 = (bf16[8,1024]{1,0:T(8,128)(2,1)S(1)}, bf16[8,1024]{1,0:T(8,128)(2,1)S(1)}, u32[]{:S(2)}, u32[]{:S(2)}) collective-permute-start(bf16[8,1024]{1,0:T(8,128)(2,1)S(1)} %get-tuple-element.28), channel_id=1, source_target_pairs={{0,4},{1,2},{2,1},{3,7},{4,0},{5,6},{6,5},{7,3},{8,12},{9,10},{10,... | collective-permute-start | bytes 49160 | tf_op jit(solution)/shard_map/ppermute | solution.py:469
  6.5 0.0 copy-done
  6.5 0.0 copy-done.2
  6.5 0.0 copy-done.1
  6.5 3.0 %shard_map.37 = (f32[4,32,1024]{2,1,0:T(8,128)S(1)}, f32[2,32,1024]{2,1,0:T(8,128)S(1)}, f32[2,32,1024]{2,1,0:T(8,128)S(1)}, f32[2,3,32,1024]{3,2,1,0:T(8,128)S(...) custom-call(s32[2,8,32,1024]{3,2,1,0:T(8,128)S(1)} %copy-done, s32[3,256]{1,0:T(4,128)S(1)} %copy-done.1, ...), custom_call_target="tpu_custom_call" | custom-call | flops 20971520 | bytes 5242880 | tf_op jit(solution)/shard_map/pallas_call | solution.py:256
  9.4 0.0 collective-permute-done.rows_near_ref
  9.4 0.0 collective-permute-done.1.rows_far_ref
  9.4 0.0 collective-permute-done.2.far_ref
  9.4 0.0 collective-permute-done.3.near_ref
  9.5 0.5 %shard_map.39 = (f32[4,16,1024]{2,1,0:T(8,128)S(1)}, bf16[4,16,1024]{2,1,0:T(8,128)(2,1)S(1)}) custom-call(s32[2,8,32,1024]{3,2,1,0:T(8,128)S(1)} %copy-done, f32[4,32,1024]{2,1,0:T(8,128)S(1)} %get-tuple-element.21.base_ref, f32[2,32,1024]{2,1,0:T(8,128)S(1)} %get-tuple-element.22.face_ref, f32[2,32,1024]{2,1,0:T(8,128)S(1)} %get-tuple-element.23.square_ref, ...), custom_call_target="tpu_custom_call" | custom-call | tf_op jit(solution)/shard_map/pallas_call | solution.py:360
  9.9 0.6 %collective-permute-start.4 = (bf16[4,16,1024]{2,1,0:T(8,128)(2,1)S(1)}, bf16[4,16,1024]{2,1,0:T(8,128)(2,1)S(1)}, u32[]{:S(2)}, u32[]{:S(2)}) collective-permute-start(bf16[4,16,1024]{2,1,0:T(8,128)(2,1)S(1)} %get-tuple-element.32), channel_id=1, source_target_pairs={{0,4},{4,0},{8,12},{12,8},{16,20},{20,16},{24,28},{28,24},{1,5},{5... | collective-permute-start | bytes 393224 | tf_op jit(solution)/shard_map/ppermute | solution.py:473
  10.6 1.0 %collective-permute-done.4.other_ref = bf16[4,16,1024]{2,1,0:T(8,128)(2,1)S(1)} collective-permute-done((bf16[4,16,1024]{2,1,0:T(8,128)(2,1)S(1)}, bf16[4,16,1024]{2,1,0:T(8,128)(2,1)S(1)}, u32[]{:S(2)}, u32[]{:S(2)}) %collective-permute-start.4) | collective-permute-done | bytes 131104 | tf_op jit(solution)/shard_map/ppermute | solution.py:473
  11.6 0.1 shard_map.40
  11.6 1.2 %collective-permute-start.5 = (bf16[16,1024]{1,0:T(8,128)(2,1)S(1)}, bf16[16,1024]{1,0:T(8,128)(2,1)S(1)}, u32[]{:S(2)}, u32[]{:S(2)}) collective-permute-start(bf16[16,1024]{1,0:T(8,128)(2,1)S(1)} %get-tuple-element.33), channel_id=1, source_target_pairs={{0,28},{4,24},{8,20},{12,16},{16,12},{20,8},{24,4},{28,0},{1,29},{... | collective-permute-start | bytes 98312 | tf_op jit(solution)/shard_map/ppermute | solution.py:473
  12.8 1.3 %collective-permute-start.6 = (bf16[16,1024]{1,0:T(8,128)(2,1)S(1)}, bf16[16,1024]{1,0:T(8,128)(2,1)S(1)}, u32[]{:S(2)}, u32[]{:S(2)}) collective-permute-start(bf16[16,1024]{1,0:T(8,128)(2,1)S(1)} %get-tuple-element.34), channel_id=1, source_target_pairs={{0,20},{4,16},{8,28},{12,24},{16,4},{20,0},{24,12},{28,8},{1,21},{... | collective-permute-start | bytes 98312 | tf_op jit(solution)/shard_map/ppermute | solution.py:473
  14.1 0.8 %collective-permute-start.7 = (bf16[16,1024]{1,0:T(8,128)(2,1)S(1)}, bf16[16,1024]{1,0:T(8,128)(2,1)S(1)}, u32[]{:S(2)}, u32[]{:S(2)}) collective-permute-start(bf16[16,1024]{1,0:T(8,128)(2,1)S(1)} %get-tuple-element.35), channel_id=1, source_target_pairs={{0,12},{4,8},{8,4},{12,0},{16,28},{20,24},{24,20},{28,16},{1,13},{... | collective-permute-start | bytes 98312 | tf_op jit(solution)/shard_map/ppermute | solution.py:473
  14.9 0.2 collective-permute-start.8
  15.0 1.0 %collective-permute-done.5.refs_0_ = bf16[16,1024]{1,0:T(8,128)(2,1)S(1)} collective-permute-done((bf16[16,1024]{1,0:T(8,128)(2,1)S(1)}, bf16[16,1024]{1,0:T(8,128)(2,1)S(1)}, u32[]{:S(2)}, u32[]{:S(2)}) %collective-permute-start.5) | collective-permute-done | bytes 32800 | tf_op jit(solution)/shard_map/ppermute | solution.py:473
  16.0 0.9 %collective-permute-done.6.refs_1_ = bf16[16,1024]{1,0:T(8,128)(2,1)S(1)} collective-permute-done((bf16[16,1024]{1,0:T(8,128)(2,1)S(1)}, bf16[16,1024]{1,0:T(8,128)(2,1)S(1)}, u32[]{:S(2)}, u32[]{:S(2)}) %collective-permute-start.6) | collective-permute-done | bytes 32800 | tf_op jit(solution)/shard_map/ppermute | solution.py:473
  16.9 0.5 %collective-permute-done.7.refs_2_ = bf16[16,1024]{1,0:T(8,128)(2,1)S(1)} collective-permute-done((bf16[16,1024]{1,0:T(8,128)(2,1)S(1)}, bf16[16,1024]{1,0:T(8,128)(2,1)S(1)}, u32[]{:S(2)}, u32[]{:S(2)}) %collective-permute-start.7) | collective-permute-done | bytes 32800 | tf_op jit(solution)/shard_map/ppermute | solution.py:473
  17.5 0.0 collective-permute-done.8.refs_3_
  17.5 0.7 %shard_map.41 = f32[4,4,1024]{2,1,0:T(4,128)} custom-call(bf16[16,1024]{1,0:T(8,128)(2,1)S(1)} %collective-permute-done.5.refs_0_, bf16[16,1024]{1,0:T(8,128)(2,1)S(1)} %collective-permute-done.6.refs_1_, bf16[16,1024]{1,0:T(8,128)(2,1)S(1)} %collective-permute-done.7.refs_2_, bf16[16,1024]{1,0:T(8,128)(2,1)S(1)} %collective-permute-done.8.refs_3_), custom_call_target="tpu_custom_call" | custom-call | tf_op jit(solution)/shard_map/pallas_call | solution.py:419
Async XLA Ops:
  0.0 6.5 %copy-start = (s32[2,8,32,1024]{3,2,1,0:T(8,128)S(1)}, s32[2,8,32,1024]{3,2,1,0:T(8,128)}, u32[]{:S(2)}) copy-start(s32[2,8,32,1024]{3,2,1,0:T(8,128)} %volume_ref.5) | copy-start | bytes 6291460
  0.0 6.5 %copy-start.2 = (s32[256]{0:T(256)S(1)}, s32[256]{0:T(256)}, u32[]{:S(2)}) copy-start(s32[256]{0:T(256)} %param.5) | copy-start | bytes 3076
  0.0 6.5 %copy-start.1 = (s32[3,256]{1,0:T(4,128)S(1)}, s32[3,256]{1,0:T(4,128)}, u32[]{:S(2)}) copy-start(s32[3,256]{1,0:T(4,128)} %color_ref.1) | copy-start | bytes 9220
  1.2 8.2 %collective-permute-start.2 = (bf16[32,1024]{1,0:T(8,128)(2,1)S(1)}, bf16[32,1024]{1,0:T(8,128)(2,1)S(1)}, u32[]{:S(2)}, u32[]{:S(2)}) collective-permute-start(bf16[32,1024]{1,0:T(8,128)(2,1)S(1)} %get-tuple-element.29), channel_id=1, source_target_pairs={{0,28},{1,29},{2,30},{3,31},{4,8},{5,9},{6,10},{7,11},{8,4},{9,5},... | collective-permute-start | bytes 196616 | tf_op jit(solution)/shard_map/ppermute | solution.py:469
  3.1 6.4 %collective-permute-start.3 = (bf16[32,1024]{1,0:T(8,128)(2,1)S(1)}, bf16[32,1024]{1,0:T(8,128)(2,1)S(1)}, u32[]{:S(2)}, u32[]{:S(2)}) collective-permute-start(bf16[32,1024]{1,0:T(8,128)(2,1)S(1)} %get-tuple-element.30), channel_id=1, source_target_pairs={{0,4},{1,5},{2,6},{3,7},{4,0},{5,1},{6,2},{7,3},{8,12},{9,13},{10,... | collective-permute-start | bytes 196616 | tf_op jit(solution)/shard_map/ppermute | solution.py:469
  3.9 5.6 %collective-permute-start = (bf16[8,1024]{1,0:T(8,128)(2,1)S(1)}, bf16[8,1024]{1,0:T(8,128)(2,1)S(1)}, u32[]{:S(2)}, u32[]{:S(2)}) collective-permute-start(bf16[8,1024]{1,0:T(8,128)(2,1)S(1)} %get-tuple-element.27), channel_id=1, source_target_pairs={{0,1},{1,0},{2,3},{3,2},{4,5},{5,4},{6,7},{7,6},{8,9},{9,8},{10,11... | collective-permute-start | bytes 49160 | tf_op jit(solution)/shard_map/ppermute | solution.py:469
  4.0 5.4 %collective-permute-start.1 = (bf16[8,1024]{1,0:T(8,128)(2,1)S(1)}, bf16[8,1024]{1,0:T(8,128)(2,1)S(1)}, u32[]{:S(2)}, u32[]{:S(2)}) collective-permute-start(bf16[8,1024]{1,0:T(8,128)(2,1)S(1)} %get-tuple-element.28), channel_id=1, source_target_pairs={{0,4},{1,2},{2,1},{3,7},{4,0},{5,6},{6,5},{7,3},{8,12},{9,10},{10,... | collective-permute-start | bytes 49160 | tf_op jit(solution)/shard_map/ppermute | solution.py:469
  9.9 1.6 %collective-permute-start.4 = (bf16[4,16,1024]{2,1,0:T(8,128)(2,1)S(1)}, bf16[4,16,1024]{2,1,0:T(8,128)(2,1)S(1)}, u32[]{:S(2)}, u32[]{:S(2)}) collective-permute-start(bf16[4,16,1024]{2,1,0:T(8,128)(2,1)S(1)} %get-tuple-element.32), channel_id=1, source_target_pairs={{0,4},{4,0},{8,12},{12,8},{16,20},{20,16},{24,28},{28,24},{1,5},{5... | collective-permute-start | bytes 393224 | tf_op jit(solution)/shard_map/ppermute | solution.py:473
  11.6 4.4 %collective-permute-start.5 = (bf16[16,1024]{1,0:T(8,128)(2,1)S(1)}, bf16[16,1024]{1,0:T(8,128)(2,1)S(1)}, u32[]{:S(2)}, u32[]{:S(2)}) collective-permute-start(bf16[16,1024]{1,0:T(8,128)(2,1)S(1)} %get-tuple-element.33), channel_id=1, source_target_pairs={{0,28},{4,24},{8,20},{12,16},{16,12},{20,8},{24,4},{28,0},{1,29},{... | collective-permute-start | bytes 98312 | tf_op jit(solution)/shard_map/ppermute | solution.py:473
  12.8 4.1 %collective-permute-start.6 = (bf16[16,1024]{1,0:T(8,128)(2,1)S(1)}, bf16[16,1024]{1,0:T(8,128)(2,1)S(1)}, u32[]{:S(2)}, u32[]{:S(2)}) collective-permute-start(bf16[16,1024]{1,0:T(8,128)(2,1)S(1)} %get-tuple-element.34), channel_id=1, source_target_pairs={{0,20},{4,16},{8,28},{12,24},{16,4},{20,0},{24,12},{28,8},{1,21},{... | collective-permute-start | bytes 98312 | tf_op jit(solution)/shard_map/ppermute | solution.py:473
  14.1 3.3 %collective-permute-start.7 = (bf16[16,1024]{1,0:T(8,128)(2,1)S(1)}, bf16[16,1024]{1,0:T(8,128)(2,1)S(1)}, u32[]{:S(2)}, u32[]{:S(2)}) collective-permute-start(bf16[16,1024]{1,0:T(8,128)(2,1)S(1)} %get-tuple-element.35), channel_id=1, source_target_pairs={{0,12},{4,8},{8,4},{12,0},{16,28},{20,24},{24,20},{28,16},{1,13},{... | collective-permute-start | bytes 98312 | tf_op jit(solution)/shard_map/ppermute | solution.py:473
  14.9 2.6 %collective-permute-start.8 = (bf16[16,1024]{1,0:T(8,128)(2,1)S(1)}, bf16[16,1024]{1,0:T(8,128)(2,1)S(1)}, u32[]{:S(2)}, u32[]{:S(2)}) collective-permute-start(bf16[16,1024]{1,0:T(8,128)(2,1)S(1)} %get-tuple-element.36), channel_id=1, source_target_pairs={{0,4},{4,0},{8,12},{12,8},{16,20},{20,16},{24,28},{28,24},{1,5},{5... | collective-permute-start | bytes 98312 | tf_op jit(solution)/shard_map/ppermute | solution.py:473

commit v5 on v4

--- a/solution.py
+++ b/solution.py
@@ -27,15 +27,16 @@
     return position == 0, position == lax.axis_size(axis) - 1
 
 
-def edges_kernel(volume_ref, rows_far_out, rows_near_out, far_out, near_out, strip_ref, plane_ref, sems):
-    _, slices, height, _ = volume_ref.shape
+def edges_kernel(volume_ref, first_out, rows_near_out, second_out, rows_far_out, strip_ref, plane_ref, sems):
+    _, slices, height, columns = volume_ref.shape
     odd, odd_row = parity("depth"), parity("rows")
-
+    far_first = 1 - odd_row
+    last_first = odd ^ far_first ^ 1
     copies = [
-        pltpu.make_async_copy(volume_ref.at[0, :, (1 - odd_row) * (height - 1)], strip_ref.at[0], sems.at[0]),
-        pltpu.make_async_copy(volume_ref.at[0, :, odd_row * (height - 1)], strip_ref.at[1], sems.at[1]),
-        pltpu.make_async_copy(volume_ref.at[0, odd * (slices - 1)], plane_ref.at[0], sems.at[2]),
-        pltpu.make_async_copy(volume_ref.at[0, (1 - odd) * (slices - 1)], plane_ref.at[1], sems.at[3]),
+        pltpu.make_async_copy(volume_ref.at[0, last_first * (slices - 1)], plane_ref.at[0], sems.at[0]),
+        pltpu.make_async_copy(volume_ref.at[0, :, (1 - odd_row) * (height - 1)], strip_ref.at[0], sems.at[1]),
+        pltpu.make_async_copy(volume_ref.at[0, (1 - last_first) * (slices - 1)], plane_ref.at[1], sems.at[2]),
+        pltpu.make_async_copy(volume_ref.at[0, :, odd_row * (height - 1)], strip_ref.at[1], sems.at[3]),
     ]
     for copy in copies:
         copy.start()
@@ -43,25 +44,27 @@
     def narrow(values):
         return values.astype(jnp.float32).astype(jnp.bfloat16)
 
+    def padded(strip):
+        return narrow(jnp.concatenate([strip, jnp.zeros((height - slices, columns), jnp.int32)], axis=0))
+
     copies[0].wait()
-    rows_near_out[...] = narrow(strip_ref[0])
+    first_out[...] = narrow(plane_ref[0])
     copies[1].wait()
-    rows_far_out[...] = narrow(strip_ref[1])
+    rows_near_out[...] = padded(strip_ref[0])
     copies[2].wait()
-    far_out[...] = narrow(plane_ref[0])
+    second_out[...] = narrow(plane_ref[1])
     copies[3].wait()
-    near_out[...] = narrow(plane_ref[1])
+    rows_far_out[...] = padded(strip_ref[1])
 
 
 def cut_edges(volume):
     _, slices, height, columns = volume.shape
     plane = jax.ShapeDtypeStruct((height, columns), jnp.bfloat16)
-    strip = jax.ShapeDtypeStruct((slices, columns), jnp.bfloat16)
     return pl.pallas_call(
         edges_kernel,
         in_specs=[pl.BlockSpec(memory_space=pl.ANY)],
         out_specs=[WHOLE] * 4,
-        out_shape=[strip, strip, plane, plane],
+        out_shape=[plane] * 4,
         scratch_shapes=[
             pltpu.VMEM((2, slices, columns), jnp.int32),
             pltpu.VMEM((2, height, columns), jnp.int32),
@@ -279,7 +282,7 @@
 
 
 def edge_kernel(
-    share, volume_ref, base_ref, face_ref, square_ref, lit_ref, grad_ref, strip_ref, rows_near_ref, rows_far_ref, far_ref, near_ref, *out_refs
+    share, volume_ref, base_ref, face_ref, square_ref, lit_ref, grad_ref, strip_ref, first_ref, rows_near_ref, second_ref, rows_far_ref, *out_refs
 ):
     _, slices, height, columns = volume_ref.shape
     tiles = height // SUBLANES
@@ -289,19 +292,20 @@
     level = lax.broadcasted_iota(jnp.int32, (slices, LANES), 0)
     front, back = level == 0, level == slices - 1
     odd, odd_row = parity("depth") == 1, parity("rows") == 1
+    front_came_first = odd == odd_row
     front_end, back_end = ends("depth")
     top_end, bottom_end = ends("rows")
 
     def chunk(j, carry):
         here = pl.ds(pl.multiple_of(j * LANES, LANES), LANES)
-        rows_near = rows_near_ref[:, here].astype(jnp.float32)
-        rows_far = rows_far_ref[:, here].astype(jnp.float32)
+        rows_near = rows_near_ref[:, here].astype(jnp.float32)[:slices]
+        rows_far = rows_far_ref[:, here].astype(jnp.float32)[:slices]
         above = jnp.where(top_end, 0.0, jnp.where(odd_row, rows_near, rows_far))
         below = jnp.where(bottom_end, 0.0, jnp.where(odd_row, rows_far, rows_near))
-        far = far_ref[:, here].astype(jnp.float32)
-        near = near_ref[:, here].astype(jnp.float32)
-        before = jnp.where(front_end, 0.0, jnp.where(odd, near, far))
-        after = jnp.where(back_end, 0.0, jnp.where(odd, far, near))
+        first = first_ref[:, here].astype(jnp.float32)
+        second = second_ref[:, here].astype(jnp.float32)
+        before = jnp.where(front_end, 0.0, jnp.where(front_came_first, first, second))
+        after = jnp.where(back_end, 0.0, jnp.where(front_came_first, second, first))
         extra = []
         for q, edge in enumerate((0, height - 1)):
             inner = grad_ref[q, 1, :, here]
@@ -451,20 +455,22 @@
     )(parts)
 
 
-def swapped(values, axis, start):
+def swapped(values, kinds):
     depth_count, row_count = lax.axis_size("depth"), lax.axis_size("rows")
-    size = lax.axis_size(axis)
     perm = []
     for d in range(depth_count):
         for r in range(row_count):
-            i = d if axis == "depth" else r
-            j = i + 1 if i % 2 == start else i - 1
-            if 0 <= j < size:
-                e, q = (j, r) if axis == "depth" else (d, j)
-            elif axis == "depth":
-                e, q = (size - 1 - d, r)
+            kind = kinds[r % 2]
+            e, q = d, r
+            if kind == "near slab":
+                e = d ^ 1
+            elif kind == "far slab":
+                e = d + 1 if d % 2 else d - 1
+                e = depth_count - 1 - d if not 0 <= e < depth_count else e
             else:
-                e, q = (d ^ 1, r)
+                q = r ^ 1 if kind == "near row" else (r + 1 if r % 2 else r - 1)
+                if not 0 <= q < row_count:
+                    e, q = d ^ 1, r
             perm.append((d * row_count + r, e * row_count + q))
     return lax.ppermute(values, ("depth", "rows"), perm)
 
@@ -476,13 +482,13 @@
 def body(volume, color_map, alpha_map):
     depth_count = lax.axis_size("depth")
     share = volume.shape[2] // depth_count
-    rows_far, rows_near, far, near = cut_edges(volume)
-    rows_far = swapped(rows_far, "rows", 1)
-    rows_near = swapped(rows_near, "rows", 0)
-    far = swapped(far, "depth", 1)
-    near = swapped(near, "depth", 0)
+    first, rows_near, second, rows_far = cut_edges(volume)
+    first = swapped(first, ("far slab", "near slab"))
+    rows_near = swapped(rows_near, ("near row", "near row"))
+    second = swapped(second, ("near slab", "far slab"))
+    rows_far = swapped(rows_far, ("far row", "far row"))
     interior = march_interior(volume, color_map, alpha_map, depth_count)
-    halos = (rows_near, rows_far, far, near)
+    halos = (first, rows_near, second, rows_far)
     paired = depth_count == 8 and 2 * share == SUBLANES
     outs = add_edges(volume, interior, halos, depth_count, paired)
     if not paired:

time: 18.3 us -> 17.3 us (0.945)
  starting transfers between devices: 9.25 us -> 8.49 us
    ppermute x4, starting transfers between devices: 5.22 us -> 3.93 us  [swapped(): return lax.ppermute(values, ('depth', 'rows'), perm)]
    ppermute x5, starting transfers between devices: 4.03 us -> 4.56 us  [exchanged(): lax.ppermute(values, 'depth', [(d, d ^ mask) for d in range(lax.axis_size...]
    ppermute x5, waiting for transfers between devices: 3.4 us -> 3.22 us  [exchanged(): lax.ppermute(values, 'depth', [(d, d ^ mask) for d in range(lax.axis_size...]
  transfers between devices with their start and end apart: 9 -> 9, of which waited for: 4 -> 4; matrix products, arithmetic and copies ran while one was open for 0% -> 0% of each run, Pallas kernels for 16% -> 17%
where the time goes in v5:
time: 17.3 us; the launch traced here: 17.2 us
  starting transfers between devices  8.49 us (49%)
  Pallas kernels  5.41 us (31%)
  waiting for transfers between devices  3.23 us (19%)
    ppermute x5, starting transfers between devices, exchanged(): lax.ppermute(values, 'depth', [(d, d ^ mask) for d in range(lax.axis_size...  4.56 us
    ppermute x4, starting transfers between devices, swapped(): return lax.ppermute(values, ('depth', 'rows'), perm)  3.93 us
    ppermute x5, waiting for transfers between devices, exchanged(): lax.ppermute(values, 'depth', [(d, d ^ mask) for d in range(lax.axis_size...  3.22 us
    pallas_call x1, Pallas kernels, march_interior(): pl.pallas_call(functools.partial(interior_kernel, opacity_scale), in_spec...  2.95 us
    pallas_call x1, Pallas kernels, cut_edges(): pl.pallas_call(edges_kernel, in_specs=[pl.BlockSpec(memory_space=pl.ANY)]...  1.2 us
    pallas_call x1, Pallas kernels, gather(): pl.pallas_call(gather_kernel, in_specs=[WHOLE] * len(parts), out_specs=WH...  0.7 us
    pallas_call x1, Pallas kernels, add_edges(): pl.pallas_call(functools.partial(edge_kernel, share), in_specs=[WHOLE] *...  0.48 us
  transfers between devices with their start and end apart: 9, of which 4 were waited for; matrix products, arithmetic and copies ran while one was open for 0% of the time, Pallas kernels for 17%

profile of v5, /device:TPU:9, one launch (start us, length us, event | category | flops | bytes accessed | tf_op | source)
XLA Modules:
  0.0 17.2 jit_solution(14795002817697972088)
XLA Ops:
  0.0 0.0 copy-start
  0.0 0.0 copy-start.2
  0.0 0.0 copy-start.1
  0.0 1.2 %shard_map.38 = (bf16[32,1024]{1,0:T(8,128)(2,1)S(1)}, bf16[32,1024]{1,0:T(8,128)(2,1)S(1)}, bf16[32,1024]{1,0:T(8,128)(2,1)S(1)}, bf16[32,1024]{1,0:T(8,128)(2,1)S(1)}) custom-call(s32[2,8,32,1024]{3,2,1,0:T(8,128)} %volume_ref.5), custom_call_target="tpu_custom_call" | custom-call | tf_op jit(solution)/shard_map/pallas_call | solution.py:63
  1.2 0.7 %collective-permute-start = (bf16[32,1024]{1,0:T(8,128)(2,1)S(1)}, bf16[32,1024]{1,0:T(8,128)(2,1)S(1)}, u32[]{:S(2)}, u32[]{:S(2)}) collective-permute-start(bf16[32,1024]{1,0:T(8,128)(2,1)S(1)} %get-tuple-element.27), channel_id=1, source_target_pairs={{0,28},{1,5},{2,30},{3,7},{4,8},{5,1},{6,10},{7,3},{8,4},{9,13},{1... | collective-permute-start | bytes 196616 | tf_op jit(solution)/shard_map/ppermute | solution.py:475
  2.0 1.3 %collective-permute-start.1 = (bf16[32,1024]{1,0:T(8,128)(2,1)S(1)}, bf16[32,1024]{1,0:T(8,128)(2,1)S(1)}, u32[]{:S(2)}, u32[]{:S(2)}) collective-permute-start(bf16[32,1024]{1,0:T(8,128)(2,1)S(1)} %get-tuple-element.28), channel_id=1, source_target_pairs={{0,1},{1,0},{2,3},{3,2},{4,5},{5,4},{6,7},{7,6},{8,9},{9,8},{10,11... | collective-permute-start | bytes 196616 | tf_op jit(solution)/shard_map/ppermute | solution.py:475
  3.2 0.4 %collective-permute-start.2 = (bf16[32,1024]{1,0:T(8,128)(2,1)S(1)}, bf16[32,1024]{1,0:T(8,128)(2,1)S(1)}, u32[]{:S(2)}, u32[]{:S(2)}) collective-permute-start(bf16[32,1024]{1,0:T(8,128)(2,1)S(1)} %get-tuple-element.29), channel_id=1, source_target_pairs={{0,4},{1,29},{2,6},{3,31},{4,0},{5,9},{6,2},{7,11},{8,12},{9,5},{1... | collective-permute-start | bytes 196616 | tf_op jit(solution)/shard_map/ppermute | solution.py:475
  3.6 1.6 %collective-permute-start.3 = (bf16[32,1024]{1,0:T(8,128)(2,1)S(1)}, bf16[32,1024]{1,0:T(8,128)(2,1)S(1)}, u32[]{:S(2)}, u32[]{:S(2)}) collective-permute-start(bf16[32,1024]{1,0:T(8,128)(2,1)S(1)} %get-tuple-element.30), channel_id=1, source_target_pairs={{0,4},{1,2},{2,1},{3,7},{4,0},{5,6},{6,5},{7,3},{8,12},{9,10},{10,... | collective-permute-start | bytes 196616 | tf_op jit(solution)/shard_map/ppermute | solution.py:475
  5.1 0.0 copy-done
  5.1 0.0 copy-done.2
  5.1 0.0 copy-done.1
  5.2 3.0 %shard_map.37 = (f32[4,32,1024]{2,1,0:T(8,128)S(1)}, f32[2,32,1024]{2,1,0:T(8,128)S(1)}, f32[2,32,1024]{2,1,0:T(8,128)S(1)}, f32[2,3,32,1024]{3,2,1,0:T(8,128)S(...) custom-call(s32[2,8,32,1024]{3,2,1,0:T(8,128)S(1)} %copy-done, s32[3,256]{1,0:T(4,128)S(1)} %copy-done.1, ...), custom_call_target="tpu_custom_call" | custom-call | flops 20971520 | bytes 5242880 | tf_op jit(solution)/shard_map/pallas_call | solution.py:259
  8.1 0.0 collective-permute-done.first_ref
  8.1 0.0 collective-permute-done.1.rows_near_ref
  8.1 0.0 collective-permute-done.2.second_ref
  8.1 0.0 collective-permute-done.3.rows_far_ref
  8.2 0.5 %shard_map.39 = (f32[4,16,1024]{2,1,0:T(8,128)S(1)}, bf16[4,16,1024]{2,1,0:T(8,128)(2,1)S(1)}) custom-call(s32[2,8,32,1024]{3,2,1,0:T(8,128)S(1)} %copy-done, f32[4,32,1024]{2,1,0:T(8,128)S(1)} %get-tuple-element.21.base_ref, f32[2,32,1024]{2,1,0:T(8,128)S(1)} %get-tuple-element.22.face_ref, f32[2,32,1024]{2,1,0:T(8,128)S(1)} %get-tuple-element.23.square_ref, ...), custom_call_target="tpu_custom_call" | custom-call | tf_op jit(solution)/shard_map/pallas_call | solution.py:364
  8.6 1.2 %collective-permute-start.4 = (bf16[4,16,1024]{2,1,0:T(8,128)(2,1)S(1)}, bf16[4,16,1024]{2,1,0:T(8,128)(2,1)S(1)}, u32[]{:S(2)}, u32[]{:S(2)}) collective-permute-start(bf16[4,16,1024]{2,1,0:T(8,128)(2,1)S(1)} %get-tuple-element.32), channel_id=1, source_target_pairs={{0,4},{4,0},{8,12},{12,8},{16,20},{20,16},{24,28},{28,24},{1,5},{5... | collective-permute-start | bytes 393224 | tf_op jit(solution)/shard_map/ppermute | solution.py:479
  9.8 1.0 %collective-permute-done.4.other_ref = bf16[4,16,1024]{2,1,0:T(8,128)(2,1)S(1)} collective-permute-done((bf16[4,16,1024]{2,1,0:T(8,128)(2,1)S(1)}, bf16[4,16,1024]{2,1,0:T(8,128)(2,1)S(1)}, u32[]{:S(2)}, u32[]{:S(2)}) %collective-permute-start.4) | collective-permute-done | bytes 131104 | tf_op jit(solution)/shard_map/ppermute | solution.py:479
  10.8 0.1 shard_map.40
  10.9 2.0 %collective-permute-start.5 = (bf16[16,1024]{1,0:T(8,128)(2,1)S(1)}, bf16[16,1024]{1,0:T(8,128)(2,1)S(1)}, u32[]{:S(2)}, u32[]{:S(2)}) collective-permute-start(bf16[16,1024]{1,0:T(8,128)(2,1)S(1)} %get-tuple-element.33), channel_id=1, source_target_pairs={{0,28},{4,24},{8,20},{12,16},{16,12},{20,8},{24,4},{28,0},{1,29},{... | collective-permute-start | bytes 98312 | tf_op jit(solution)/shard_map/ppermute | solution.py:479
  12.9 0.3 %collective-permute-start.6 = (bf16[16,1024]{1,0:T(8,128)(2,1)S(1)}, bf16[16,1024]{1,0:T(8,128)(2,1)S(1)}, u32[]{:S(2)}, u32[]{:S(2)}) collective-permute-start(bf16[16,1024]{1,0:T(8,128)(2,1)S(1)} %get-tuple-element.34), channel_id=1, source_target_pairs={{0,20},{4,16},{8,28},{12,24},{16,4},{20,0},{24,12},{28,8},{1,21},{... | collective-permute-start | bytes 98312 | tf_op jit(solution)/shard_map/ppermute | solution.py:479
  13.1 1.0 %collective-permute-start.7 = (bf16[16,1024]{1,0:T(8,128)(2,1)S(1)}, bf16[16,1024]{1,0:T(8,128)(2,1)S(1)}, u32[]{:S(2)}, u32[]{:S(2)}) collective-permute-start(bf16[16,1024]{1,0:T(8,128)(2,1)S(1)} %get-tuple-element.35), channel_id=1, source_target_pairs={{0,12},{4,8},{8,4},{12,0},{16,28},{20,24},{24,20},{28,16},{1,13},{... | collective-permute-start | bytes 98312 | tf_op jit(solution)/shard_map/ppermute | solution.py:479
  14.1 0.2 collective-permute-start.8
  14.3 0.9 %collective-permute-done.5.refs_0_ = bf16[16,1024]{1,0:T(8,128)(2,1)S(1)} collective-permute-done((bf16[16,1024]{1,0:T(8,128)(2,1)S(1)}, bf16[16,1024]{1,0:T(8,128)(2,1)S(1)}, u32[]{:S(2)}, u32[]{:S(2)}) %collective-permute-start.5) | collective-permute-done | bytes 32800 | tf_op jit(solution)/shard_map/ppermute | solution.py:479
  15.2 1.3 %collective-permute-done.6.refs_1_ = bf16[16,1024]{1,0:T(8,128)(2,1)S(1)} collective-permute-done((bf16[16,1024]{1,0:T(8,128)(2,1)S(1)}, bf16[16,1024]{1,0:T(8,128)(2,1)S(1)}, u32[]{:S(2)}, u32[]{:S(2)}) %collective-permute-start.6) | collective-permute-done | bytes 32800 | tf_op jit(solution)/shard_map/ppermute | solution.py:479
  16.4 0.1 collective-permute-done.7.refs_2_
  16.5 0.0 collective-permute-done.8.refs_3_
  16.5 0.7 %shard_map.41 = f32[4,4,1024]{2,1,0:T(4,128)} custom-call(bf16[16,1024]{1,0:T(8,128)(2,1)S(1)} %collective-permute-done.5.refs_0_, bf16[16,1024]{1,0:T(8,128)(2,1)S(1)} %collective-permute-done.6.refs_1_, bf16[16,1024]{1,0:T(8,128)(2,1)S(1)} %collective-permute-done.7.refs_2_, bf16[16,1024]{1,0:T(8,128)(2,1)S(1)} %collective-permute-done.8.refs_3_), custom_call_target="tpu_custom_call" | custom-call | tf_op jit(solution)/shard_map/pallas_call | solution.py:423
Async XLA Ops:
  0.0 5.1 %copy-start = (s32[2,8,32,1024]{3,2,1,0:T(8,128)S(1)}, s32[2,8,32,1024]{3,2,1,0:T(8,128)}, u32[]{:S(2)}) copy-start(s32[2,8,32,1024]{3,2,1,0:T(8,128)} %volume_ref.5) | copy-start | bytes 6291460
  0.0 5.1 %copy-start.2 = (s32[256]{0:T(256)S(1)}, s32[256]{0:T(256)}, u32[]{:S(2)}) copy-start(s32[256]{0:T(256)} %param.5) | copy-start | bytes 3076
  0.0 5.1 %copy-start.1 = (s32[3,256]{1,0:T(4,128)S(1)}, s32[3,256]{1,0:T(4,128)}, u32[]{:S(2)}) copy-start(s32[3,256]{1,0:T(4,128)} %color_ref.1) | copy-start | bytes 9220
  1.2 6.9 %collective-permute-start = (bf16[32,1024]{1,0:T(8,128)(2,1)S(1)}, bf16[32,1024]{1,0:T(8,128)(2,1)S(1)}, u32[]{:S(2)}, u32[]{:S(2)}) collective-permute-start(bf16[32,1024]{1,0:T(8,128)(2,1)S(1)} %get-tuple-element.27), channel_id=1, source_target_pairs={{0,28},{1,5},{2,30},{3,7},{4,8},{5,1},{6,10},{7,3},{8,4},{9,13},{1... | collective-permute-start | bytes 196616 | tf_op jit(solution)/shard_map/ppermute | solution.py:475
  2.0 6.2 %collective-permute-start.1 = (bf16[32,1024]{1,0:T(8,128)(2,1)S(1)}, bf16[32,1024]{1,0:T(8,128)(2,1)S(1)}, u32[]{:S(2)}, u32[]{:S(2)}) collective-permute-start(bf16[32,1024]{1,0:T(8,128)(2,1)S(1)} %get-tuple-element.28), channel_id=1, source_target_pairs={{0,1},{1,0},{2,3},{3,2},{4,5},{5,4},{6,7},{7,6},{8,9},{9,8},{10,11... | collective-permute-start | bytes 196616 | tf_op jit(solution)/shard_map/ppermute | solution.py:475
  3.2 4.9 %collective-permute-start.2 = (bf16[32,1024]{1,0:T(8,128)(2,1)S(1)}, bf16[32,1024]{1,0:T(8,128)(2,1)S(1)}, u32[]{:S(2)}, u32[]{:S(2)}) collective-permute-start(bf16[32,1024]{1,0:T(8,128)(2,1)S(1)} %get-tuple-element.29), channel_id=1, source_target_pairs={{0,4},{1,29},{2,6},{3,31},{4,0},{5,9},{6,2},{7,11},{8,12},{9,5},{1... | collective-permute-start | bytes 196616 | tf_op jit(solution)/shard_map/ppermute | solution.py:475
  3.6 4.6 %collective-permute-start.3 = (bf16[32,1024]{1,0:T(8,128)(2,1)S(1)}, bf16[32,1024]{1,0:T(8,128)(2,1)S(1)}, u32[]{:S(2)}, u32[]{:S(2)}) collective-permute-start(bf16[32,1024]{1,0:T(8,128)(2,1)S(1)} %get-tuple-element.30), channel_id=1, source_target_pairs={{0,4},{1,2},{2,1},{3,7},{4,0},{5,6},{6,5},{7,3},{8,12},{9,10},{10,... | collective-permute-start | bytes 196616 | tf_op jit(solution)/shard_map/ppermute | solution.py:475
  8.6 2.1 %collective-permute-start.4 = (bf16[4,16,1024]{2,1,0:T(8,128)(2,1)S(1)}, bf16[4,16,1024]{2,1,0:T(8,128)(2,1)S(1)}, u32[]{:S(2)}, u32[]{:S(2)}) collective-permute-start(bf16[4,16,1024]{2,1,0:T(8,128)(2,1)S(1)} %get-tuple-element.32), channel_id=1, source_target_pairs={{0,4},{4,0},{8,12},{12,8},{16,20},{20,16},{24,28},{28,24},{1,5},{5... | collective-permute-start | bytes 393224 | tf_op jit(solution)/shard_map/ppermute | solution.py:479
  10.9 4.3 %collective-permute-start.5 = (bf16[16,1024]{1,0:T(8,128)(2,1)S(1)}, bf16[16,1024]{1,0:T(8,128)(2,1)S(1)}, u32[]{:S(2)}, u32[]{:S(2)}) collective-permute-start(bf16[16,1024]{1,0:T(8,128)(2,1)S(1)} %get-tuple-element.33), channel_id=1, source_target_pairs={{0,28},{4,24},{8,20},{12,16},{16,12},{20,8},{24,4},{28,0},{1,29},{... | collective-permute-start | bytes 98312 | tf_op jit(solution)/shard_map/ppermute | solution.py:479
  12.9 3.6 %collective-permute-start.6 = (bf16[16,1024]{1,0:T(8,128)(2,1)S(1)}, bf16[16,1024]{1,0:T(8,128)(2,1)S(1)}, u32[]{:S(2)}, u32[]{:S(2)}) collective-permute-start(bf16[16,1024]{1,0:T(8,128)(2,1)S(1)} %get-tuple-element.34), channel_id=1, source_target_pairs={{0,20},{4,16},{8,28},{12,24},{16,4},{20,0},{24,12},{28,8},{1,21},{... | collective-permute-start | bytes 98312 | tf_op jit(solution)/shard_map/ppermute | solution.py:479
  13.1 3.3 %collective-permute-start.7 = (bf16[16,1024]{1,0:T(8,128)(2,1)S(1)}, bf16[16,1024]{1,0:T(8,128)(2,1)S(1)}, u32[]{:S(2)}, u32[]{:S(2)}) collective-permute-start(bf16[16,1024]{1,0:T(8,128)(2,1)S(1)} %get-tuple-element.35), channel_id=1, source_target_pairs={{0,12},{4,8},{8,4},{12,0},{16,28},{20,24},{24,20},{28,16},{1,13},{... | collective-permute-start | bytes 98312 | tf_op jit(solution)/shard_map/ppermute | solution.py:479
  14.1 2.4 %collective-permute-start.8 = (bf16[16,1024]{1,0:T(8,128)(2,1)S(1)}, bf16[16,1024]{1,0:T(8,128)(2,1)S(1)}, u32[]{:S(2)}, u32[]{:S(2)}) collective-permute-start(bf16[16,1024]{1,0:T(8,128)(2,1)S(1)} %get-tuple-element.36), channel_id=1, source_target_pairs={{0,4},{4,0},{8,12},{12,8},{16,20},{20,16},{24,28},{28,24},{1,5},{5... | collective-permute-start | bytes 98312 | tf_op jit(solution)/shard_map/ppermute | solution.py:479

commit v6 on v5

--- a/solution.py
+++ b/solution.py
@@ -292,6 +292,7 @@
     level = lax.broadcasted_iota(jnp.int32, (slices, LANES), 0)
     front, back = level == 0, level == slices - 1
     odd, odd_row = parity("depth") == 1, parity("rows") == 1
+    chip = lax.axis_index("depth") // 2
     front_came_first = odd == odd_row
     front_end, back_end = ends("depth")
     top_end, bottom_end = ends("rows")
@@ -346,8 +347,9 @@
                 halves = [(planes[c], pltpu.roll(planes[c + 1], SUBLANES // 2, 0)) for c in (0, 2)]
                 even = jnp.concatenate([jnp.where(upper, own, turned) for own, turned in halves], axis=0)
                 uneven = jnp.concatenate([jnp.where(upper, turned, own) for own, turned in halves], axis=0)
-                keep_ref[r, :, here] = jnp.where(odd, even, uneven)
-                give_ref[r, :, here] = jnp.where(odd, uneven, even).astype(jnp.bfloat16)
+                keep_even = odd != (chip == r)
+                keep_ref[r, :, here] = jnp.where(keep_even, even, uneven)
+                give_ref[r, :, here] = jnp.where(keep_even, uneven, even).astype(jnp.bfloat16)
         return carry
 
     lax.fori_loop(0, columns // LANES, chunk, 0)
@@ -376,23 +378,25 @@
     return nearer + jnp.concatenate([clear] * 4, axis=0) * farther
 
 
-def merge_kernel(keep_ref, other_ref, *send_refs):
+def merge_kernel(keep_ref, other_ref, *out_refs):
     position = lax.axis_index("depth")
     odd, chip = position % 2 == 1, position // 2
-    for k, out_ref in enumerate(send_refs):
+    for k, out_ref in enumerate(out_refs):
         keep = keep_ref[chip ^ k]
         other = other_ref[chip ^ k].astype(jnp.float32)
-        block = over(jnp.where(odd, other, keep), jnp.where(odd, keep, other), jnp.logical_not(odd))
+        uneven = jnp.logical_not(odd) if k else odd
+        block = over(jnp.where(odd, other, keep), jnp.where(odd, keep, other), uneven)
         out_ref[...] = block.astype(out_ref.dtype)
 
 
 def merge(keep, other):
     chips, rows, columns = keep.shape
+    shapes = [jax.ShapeDtypeStruct((rows, columns), jnp.bfloat16 if k else jnp.float32) for k in range(chips)]
     return pl.pallas_call(
         merge_kernel,
         in_specs=[WHOLE] * 2,
         out_specs=[WHOLE] * chips,
-        out_shape=[jax.ShapeDtypeStruct((rows, columns), jnp.bfloat16)] * chips,
+        out_shape=shapes,
         compiler_params=pltpu.CompilerParams(vmem_limit_bytes=8 * 1024 * 1024),
     )(keep, other)
 
@@ -494,8 +498,9 @@
     if not paired:
         return finish(lax.all_to_all(outs[0], "depth", 0, 0, tiled=True), share)
     keep, give = outs
-    sends = merge(keep, exchanged(give, 1))
-    return gather([exchanged(send, 2 * k + 1) for k, send in reversed(list(enumerate(sends)))], share)
+    own, *sends = merge(keep, exchanged(give, 1))
+    received = [exchanged(send, 2 * k + 1) for k, send in reversed(list(enumerate(sends, 1)))]
+    return gather((*received, own), share)
 
 
 def solution(mesh):

time: 17.3 us -> 17.3 us (level)
    ppermute x5 -> x4, starting transfers between devices: 4.56 us -> 4.39 us  [exchanged(): lax.ppermute(values, 'depth', [(d, d ^ mask) for d in range(lax.axis_size...]
    ppermute x5 -> x4, waiting for transfers between devices: 3.22 us -> 3.38 us  [exchanged(): lax.ppermute(values, 'depth', [(d, d ^ mask) for d in range(lax.axis_size...]
  transfers between devices with their start and end apart: 9 -> 8, of which waited for: 4 -> 4; matrix products, arithmetic and copies ran while one was open for 0% -> 0% of each run, Pallas kernels for 17% -> 17%
where the time goes in v6:
time: 17.3 us; the launch traced here: 17.2 us
  starting transfers between devices  8.32 us (48%)
  Pallas kernels  5.39 us (31%)
  waiting for transfers between devices  3.39 us (20%)
    ppermute x4, starting transfers between devices, exchanged(): lax.ppermute(values, 'depth', [(d, d ^ mask) for d in range(lax.axis_size...  4.39 us
    ppermute x4, starting transfers between devices, swapped(): return lax.ppermute(values, ('depth', 'rows'), perm)  3.93 us
    ppermute x4, waiting for transfers between devices, exchanged(): lax.ppermute(values, 'depth', [(d, d ^ mask) for d in range(lax.axis_size...  3.38 us
    pallas_call x1, Pallas kernels, march_interior(): pl.pallas_call(functools.partial(interior_kernel, opacity_scale), in_spec...  2.95 us
    pallas_call x1, Pallas kernels, cut_edges(): pl.pallas_call(edges_kernel, in_specs=[pl.BlockSpec(memory_space=pl.ANY)]...  1.2 us
    pallas_call x1, Pallas kernels, gather(): pl.pallas_call(gather_kernel, in_specs=[WHOLE] * len(parts), out_specs=WH...  0.7 us
    pallas_call x1, Pallas kernels, add_edges(): pl.pallas_call(functools.partial(edge_kernel, share), in_specs=[WHOLE] *...  0.47 us
  transfers between devices with their start and end apart: 8, of which 4 were waited for; matrix products, arithmetic and copies ran while one was open for 0% of the time, Pallas kernels for 17%

profile of v6, /device:TPU:9, one launch (start us, length us, event | category | flops | bytes accessed | tf_op | source)
XLA Modules:
  0.0 17.2 jit_solution(1314553707415481036)
XLA Ops:
  0.0 0.0 copy-start
  0.0 0.0 copy-start.2
  0.0 0.0 copy-start.1
  0.0 1.2 %shard_map.38 = (bf16[32,1024]{1,0:T(8,128)(2,1)S(1)}, bf16[32,1024]{1,0:T(8,128)(2,1)S(1)}, bf16[32,1024]{1,0:T(8,128)(2,1)S(1)}, bf16[32,1024]{1,0:T(8,128)(2,1)S(1)}) custom-call(s32[2,8,32,1024]{3,2,1,0:T(8,128)} %volume_ref.5), custom_call_target="tpu_custom_call" | custom-call | tf_op jit(solution)/shard_map/pallas_call | solution.py:63
  1.2 0.7 %collective-permute-start = (bf16[32,1024]{1,0:T(8,128)(2,1)S(1)}, bf16[32,1024]{1,0:T(8,128)(2,1)S(1)}, u32[]{:S(2)}, u32[]{:S(2)}) collective-permute-start(bf16[32,1024]{1,0:T(8,128)(2,1)S(1)} %get-tuple-element.27), channel_id=1, source_target_pairs={{0,28},{1,5},{2,30},{3,7},{4,8},{5,1},{6,10},{7,3},{8,4},{9,13},{1... | collective-permute-start | bytes 196616 | tf_op jit(solution)/shard_map/ppermute | solution.py:479
  2.0 1.3 %collective-permute-start.1 = (bf16[32,1024]{1,0:T(8,128)(2,1)S(1)}, bf16[32,1024]{1,0:T(8,128)(2,1)S(1)}, u32[]{:S(2)}, u32[]{:S(2)}) collective-permute-start(bf16[32,1024]{1,0:T(8,128)(2,1)S(1)} %get-tuple-element.28), channel_id=1, source_target_pairs={{0,1},{1,0},{2,3},{3,2},{4,5},{5,4},{6,7},{7,6},{8,9},{9,8},{10,11... | collective-permute-start | bytes 196616 | tf_op jit(solution)/shard_map/ppermute | solution.py:479
  3.2 0.4 %collective-permute-start.2 = (bf16[32,1024]{1,0:T(8,128)(2,1)S(1)}, bf16[32,1024]{1,0:T(8,128)(2,1)S(1)}, u32[]{:S(2)}, u32[]{:S(2)}) collective-permute-start(bf16[32,1024]{1,0:T(8,128)(2,1)S(1)} %get-tuple-element.29), channel_id=1, source_target_pairs={{0,4},{1,29},{2,6},{3,31},{4,0},{5,9},{6,2},{7,11},{8,12},{9,5},{1... | collective-permute-start | bytes 196616 | tf_op jit(solution)/shard_map/ppermute | solution.py:479
  3.6 1.6 %collective-permute-start.3 = (bf16[32,1024]{1,0:T(8,128)(2,1)S(1)}, bf16[32,1024]{1,0:T(8,128)(2,1)S(1)}, u32[]{:S(2)}, u32[]{:S(2)}) collective-permute-start(bf16[32,1024]{1,0:T(8,128)(2,1)S(1)} %get-tuple-element.30), channel_id=1, source_target_pairs={{0,4},{1,2},{2,1},{3,7},{4,0},{5,6},{6,5},{7,3},{8,12},{9,10},{10,... | collective-permute-start | bytes 196616 | tf_op jit(solution)/shard_map/ppermute | solution.py:479
  5.1 0.0 copy-done
  5.1 0.0 copy-done.2
  5.1 0.0 copy-done.1
  5.2 3.0 %shard_map.37 = (f32[4,32,1024]{2,1,0:T(8,128)S(1)}, f32[2,32,1024]{2,1,0:T(8,128)S(1)}, f32[2,32,1024]{2,1,0:T(8,128)S(1)}, f32[2,3,32,1024]{3,2,1,0:T(8,128)S(...) custom-call(s32[2,8,32,1024]{3,2,1,0:T(8,128)S(1)} %copy-done, s32[3,256]{1,0:T(4,128)S(1)} %copy-done.1, ...), custom_call_target="tpu_custom_call" | custom-call | flops 20971520 | bytes 5242880 | tf_op jit(solution)/shard_map/pallas_call | solution.py:259
  8.1 0.0 collective-permute-done.first_ref
  8.1 0.0 collective-permute-done.1.rows_near_ref
  8.1 0.0 collective-permute-done.2.second_ref
  8.1 0.0 collective-permute-done.3.rows_far_ref
  8.2 0.5 %shard_map.39 = (f32[4,16,1024]{2,1,0:T(8,128)S(1)}, bf16[4,16,1024]{2,1,0:T(8,128)(2,1)S(1)}) custom-call(s32[2,8,32,1024]{3,2,1,0:T(8,128)S(1)} %copy-done, f32[4,32,1024]{2,1,0:T(8,128)S(1)} %get-tuple-element.21.base_ref, f32[2,32,1024]{2,1,0:T(8,128)S(1)} %get-tuple-element.22.face_ref, f32[2,32,1024]{2,1,0:T(8,128)S(1)} %get-tuple-element.23.square_ref, ...), custom_call_target="tpu_custom_call" | custom-call | tf_op jit(solution)/shard_map/pallas_call | solution.py:366
  8.6 1.2 %collective-permute-start.4 = (bf16[4,16,1024]{2,1,0:T(8,128)(2,1)S(1)}, bf16[4,16,1024]{2,1,0:T(8,128)(2,1)S(1)}, u32[]{:S(2)}, u32[]{:S(2)}) collective-permute-start(bf16[4,16,1024]{2,1,0:T(8,128)(2,1)S(1)} %get-tuple-element.32), channel_id=1, source_target_pairs={{0,4},{4,0},{8,12},{12,8},{16,20},{20,16},{24,28},{28,24},{1,5},{5... | collective-permute-start | bytes 393224 | tf_op jit(solution)/shard_map/ppermute | solution.py:483
  9.8 1.0 %collective-permute-done.4.other_ref = bf16[4,16,1024]{2,1,0:T(8,128)(2,1)S(1)} collective-permute-done((bf16[4,16,1024]{2,1,0:T(8,128)(2,1)S(1)}, bf16[4,16,1024]{2,1,0:T(8,128)(2,1)S(1)}, u32[]{:S(2)}, u32[]{:S(2)}) %collective-permute-start.4) | collective-permute-done | bytes 131104 | tf_op jit(solution)/shard_map/ppermute | solution.py:483
  10.8 0.1 shard_map.40
  10.8 2.0 %collective-permute-start.5 = (bf16[16,1024]{1,0:T(8,128)(2,1)S(1)}, bf16[16,1024]{1,0:T(8,128)(2,1)S(1)}, u32[]{:S(2)}, u32[]{:S(2)}) collective-permute-start(bf16[16,1024]{1,0:T(8,128)(2,1)S(1)} %get-tuple-element.33), channel_id=1, source_target_pairs={{0,28},{4,24},{8,20},{12,16},{16,12},{20,8},{24,4},{28,0},{1,29},{... | collective-permute-start | bytes 98312 | tf_op jit(solution)/shard_map/ppermute | solution.py:483
  12.9 0.3 %collective-permute-start.6 = (bf16[16,1024]{1,0:T(8,128)(2,1)S(1)}, bf16[16,1024]{1,0:T(8,128)(2,1)S(1)}, u32[]{:S(2)}, u32[]{:S(2)}) collective-permute-start(bf16[16,1024]{1,0:T(8,128)(2,1)S(1)} %get-tuple-element.34), channel_id=1, source_target_pairs={{0,20},{4,16},{8,28},{12,24},{16,4},{20,0},{24,12},{28,8},{1,21},{... | collective-permute-start | bytes 98312 | tf_op jit(solution)/shard_map/ppermute | solution.py:483
  13.1 1.0 %collective-permute-start.7 = (bf16[16,1024]{1,0:T(8,128)(2,1)S(1)}, bf16[16,1024]{1,0:T(8,128)(2,1)S(1)}, u32[]{:S(2)}, u32[]{:S(2)}) collective-permute-start(bf16[16,1024]{1,0:T(8,128)(2,1)S(1)} %get-tuple-element.35), channel_id=1, source_target_pairs={{0,12},{4,8},{8,4},{12,0},{16,28},{20,24},{24,20},{28,16},{1,13},{... | collective-permute-start | bytes 98312 | tf_op jit(solution)/shard_map/ppermute | solution.py:483
  14.1 1.1 %collective-permute-done.5.refs_0_ = bf16[16,1024]{1,0:T(8,128)(2,1)S(1)} collective-permute-done((bf16[16,1024]{1,0:T(8,128)(2,1)S(1)}, bf16[16,1024]{1,0:T(8,128)(2,1)S(1)}, u32[]{:S(2)}, u32[]{:S(2)}) %collective-permute-start.5) | collective-permute-done | bytes 32800 | tf_op jit(solution)/shard_map/ppermute | solution.py:483
  15.2 1.3 %collective-permute-done.6.refs_1_ = bf16[16,1024]{1,0:T(8,128)(2,1)S(1)} collective-permute-done((bf16[16,1024]{1,0:T(8,128)(2,1)S(1)}, bf16[16,1024]{1,0:T(8,128)(2,1)S(1)}, u32[]{:S(2)}, u32[]{:S(2)}) %collective-permute-start.6) | collective-permute-done | bytes 32800 | tf_op jit(solution)/shard_map/ppermute | solution.py:483
  16.4 0.1 collective-permute-done.7.refs_2_
  16.5 0.7 %shard_map.41 = f32[4,4,1024]{2,1,0:T(4,128)} custom-call(bf16[16,1024]{1,0:T(8,128)(2,1)S(1)} %collective-permute-done.5.refs_0_, bf16[16,1024]{1,0:T(8,128)(2,1)S(1)} %collective-permute-done.6.refs_1_, bf16[16,1024]{1,0:T(8,128)(2,1)S(1)} %collective-permute-done.7.refs_2_, f32[16,1024]{1,0:T(8,128)S(1)} %get-tuple-element.36.refs_3_), custom_call_target="tpu_custom_call" | custom-call | tf_op jit(solution)/shard_map/pallas_call | solution.py:427
Async XLA Ops:
  0.0 5.1 %copy-start = (s32[2,8,32,1024]{3,2,1,0:T(8,128)S(1)}, s32[2,8,32,1024]{3,2,1,0:T(8,128)}, u32[]{:S(2)}) copy-start(s32[2,8,32,1024]{3,2,1,0:T(8,128)} %volume_ref.5) | copy-start | bytes 6291460
  0.0 5.1 %copy-start.2 = (s32[256]{0:T(256)S(1)}, s32[256]{0:T(256)}, u32[]{:S(2)}) copy-start(s32[256]{0:T(256)} %param.5) | copy-start | bytes 3076
  0.0 5.1 %copy-start.1 = (s32[3,256]{1,0:T(4,128)S(1)}, s32[3,256]{1,0:T(4,128)}, u32[]{:S(2)}) copy-start(s32[3,256]{1,0:T(4,128)} %color_ref.1) | copy-start | bytes 9220
  1.2 6.9 %collective-permute-start = (bf16[32,1024]{1,0:T(8,128)(2,1)S(1)}, bf16[32,1024]{1,0:T(8,128)(2,1)S(1)}, u32[]{:S(2)}, u32[]{:S(2)}) collective-permute-start(bf16[32,1024]{1,0:T(8,128)(2,1)S(1)} %get-tuple-element.27), channel_id=1, source_target_pairs={{0,28},{1,5},{2,30},{3,7},{4,8},{5,1},{6,10},{7,3},{8,4},{9,13},{1... | collective-permute-start | bytes 196616 | tf_op jit(solution)/shard_map/ppermute | solution.py:479
  2.0 6.2 %collective-permute-start.1 = (bf16[32,1024]{1,0:T(8,128)(2,1)S(1)}, bf16[32,1024]{1,0:T(8,128)(2,1)S(1)}, u32[]{:S(2)}, u32[]{:S(2)}) collective-permute-start(bf16[32,1024]{1,0:T(8,128)(2,1)S(1)} %get-tuple-element.28), channel_id=1, source_target_pairs={{0,1},{1,0},{2,3},{3,2},{4,5},{5,4},{6,7},{7,6},{8,9},{9,8},{10,11... | collective-permute-start | bytes 196616 | tf_op jit(solution)/shard_map/ppermute | solution.py:479
  3.2 4.9 %collective-permute-start.2 = (bf16[32,1024]{1,0:T(8,128)(2,1)S(1)}, bf16[32,1024]{1,0:T(8,128)(2,1)S(1)}, u32[]{:S(2)}, u32[]{:S(2)}) collective-permute-start(bf16[32,1024]{1,0:T(8,128)(2,1)S(1)} %get-tuple-element.29), channel_id=1, source_target_pairs={{0,4},{1,29},{2,6},{3,31},{4,0},{5,9},{6,2},{7,11},{8,12},{9,5},{1... | collective-permute-start | bytes 196616 | tf_op jit(solution)/shard_map/ppermute | solution.py:479
  3.6 4.6 %collective-permute-start.3 = (bf16[32,1024]{1,0:T(8,128)(2,1)S(1)}, bf16[32,1024]{1,0:T(8,128)(2,1)S(1)}, u32[]{:S(2)}, u32[]{:S(2)}) collective-permute-start(bf16[32,1024]{1,0:T(8,128)(2,1)S(1)} %get-tuple-element.30), channel_id=1, source_target_pairs={{0,4},{1,2},{2,1},{3,7},{4,0},{5,6},{6,5},{7,3},{8,12},{9,10},{10,... | collective-permute-start | bytes 196616 | tf_op jit(solution)/shard_map/ppermute | solution.py:479
  8.6 2.1 %collective-permute-start.4 = (bf16[4,16,1024]{2,1,0:T(8,128)(2,1)S(1)}, bf16[4,16,1024]{2,1,0:T(8,128)(2,1)S(1)}, u32[]{:S(2)}, u32[]{:S(2)}) collective-permute-start(bf16[4,16,1024]{2,1,0:T(8,128)(2,1)S(1)} %get-tuple-element.32), channel_id=1, source_target_pairs={{0,4},{4,0},{8,12},{12,8},{16,20},{20,16},{24,28},{28,24},{1,5},{5... | collective-permute-start | bytes 393224 | tf_op jit(solution)/shard_map/ppermute | solution.py:483
  10.8 4.3 %collective-permute-start.5 = (bf16[16,1024]{1,0:T(8,128)(2,1)S(1)}, bf16[16,1024]{1,0:T(8,128)(2,1)S(1)}, u32[]{:S(2)}, u32[]{:S(2)}) collective-permute-start(bf16[16,1024]{1,0:T(8,128)(2,1)S(1)} %get-tuple-element.33), channel_id=1, source_target_pairs={{0,28},{4,24},{8,20},{12,16},{16,12},{20,8},{24,4},{28,0},{1,29},{... | collective-permute-start | bytes 98312 | tf_op jit(solution)/shard_map/ppermute | solution.py:483
  12.9 3.6 %collective-permute-start.6 = (bf16[16,1024]{1,0:T(8,128)(2,1)S(1)}, bf16[16,1024]{1,0:T(8,128)(2,1)S(1)}, u32[]{:S(2)}, u32[]{:S(2)}) collective-permute-start(bf16[16,1024]{1,0:T(8,128)(2,1)S(1)} %get-tuple-element.34), channel_id=1, source_target_pairs={{0,20},{4,16},{8,28},{12,24},{16,4},{20,0},{24,12},{28,8},{1,21},{... | collective-permute-start | bytes 98312 | tf_op jit(solution)/shard_map/ppermute | solution.py:483
  13.1 3.3 %collective-permute-start.7 = (bf16[16,1024]{1,0:T(8,128)(2,1)S(1)}, bf16[16,1024]{1,0:T(8,128)(2,1)S(1)}, u32[]{:S(2)}, u32[]{:S(2)}) collective-permute-start(bf16[16,1024]{1,0:T(8,128)(2,1)S(1)} %get-tuple-element.35), channel_id=1, source_target_pairs={{0,12},{4,8},{8,4},{12,0},{16,28},{20,24},{24,20},{28,16},{1,13},{... | collective-permute-start | bytes 98312 | tf_op jit(solution)/shard_map/ppermute | solution.py:483

commit v7 on v5

--- a/solution.py
+++ b/solution.py
@@ -342,23 +342,32 @@
                     block = jnp.concatenate([plane[first : first + share] for plane in planes], axis=0)
                     out_refs[0][r * (SUBLANES // share) + i, :, here] = block.astype(jnp.bfloat16)
             else:
-                keep_ref, give_ref = out_refs
                 halves = [(planes[c], pltpu.roll(planes[c + 1], SUBLANES // 2, 0)) for c in (0, 2)]
                 even = jnp.concatenate([jnp.where(upper, own, turned) for own, turned in halves], axis=0)
                 uneven = jnp.concatenate([jnp.where(upper, turned, own) for own, turned in halves], axis=0)
-                keep_ref[r, :, here] = jnp.where(odd, even, uneven)
-                give_ref[r, :, here] = jnp.where(odd, uneven, even).astype(jnp.bfloat16)
+                blocks_ref, _ = out_refs
+                blocks_ref[r, 0, :, here] = even
+                blocks_ref[r, 1, :, here] = uneven
         return carry
 
     lax.fori_loop(0, columns // LANES, chunk, 0)
+    if len(out_refs) > 1:
+        blocks_ref, give_ref = out_refs
+        chip, core, mask = route()
+        given = (blocks_ref[chip, 1 - core], blocks_ref[chip ^ 3, core], blocks_ref[chip ^ mask ^ 3, 0], blocks_ref[chip ^ mask ^ 3, 1])
+        for i, block in enumerate(given):
+            give_ref[i] = block.astype(jnp.bfloat16)
 
 
 def add_edges(volume, interior, halos, depth_count, paired):
     _, slices, height, columns = volume.shape
     share = height // depth_count
     if paired:
-        half = (depth_count // 2, 4 * share, columns)
-        shapes = [jax.ShapeDtypeStruct(half, jnp.float32), jax.ShapeDtypeStruct(half, jnp.bfloat16)]
+        block = (4 * share, columns)
+        shapes = [
+            jax.ShapeDtypeStruct((depth_count // 2, 2, *block), jnp.float32),
+            jax.ShapeDtypeStruct((4, *block), jnp.bfloat16),
+        ]
     else:
         shapes = [jax.ShapeDtypeStruct((depth_count, 4 * share, columns), jnp.bfloat16)]
     return pl.pallas_call(
@@ -370,43 +379,78 @@
     )(volume, *interior, *halos)
 
 
+def served(depth):
+    chip, core = depth // 2, depth % 2
+    return 1 + (core ^ (chip & 1) ^ (chip >> 1))
+
+
+def route():
+    position = lax.axis_index("depth")
+    return position // 2, position % 2, served(position)
+
+
 def over(nearer, farther, uneven):
     share = nearer.shape[0] // 4
     clear = 1.0 - jnp.where(uneven, nearer[2 * share : 3 * share], nearer[3 * share :])
     return nearer + jnp.concatenate([clear] * 4, axis=0) * farther
 
 
-def merge_kernel(keep_ref, other_ref, *send_refs):
-    position = lax.axis_index("depth")
-    odd, chip = position % 2 == 1, position // 2
-    for k, out_ref in enumerate(send_refs):
-        keep = keep_ref[chip ^ k]
-        other = other_ref[chip ^ k].astype(jnp.float32)
-        block = over(jnp.where(odd, other, keep), jnp.where(odd, keep, other), jnp.logical_not(odd))
-        out_ref[...] = block.astype(out_ref.dtype)
-
-
-def merge(keep, other):
-    chips, rows, columns = keep.shape
+def merge_kernel(blocks_ref, other_ref, own_ref, cross_ref, side_ref):
+    chip, core, mask = route()
+    odd = core == 1
+
+    def merged(keep, i, uneven):
+        other = other_ref[i].astype(jnp.float32)
+        return over(jnp.where(odd, other, keep), jnp.where(odd, keep, other), uneven)
+
+    own_ref[...] = merged(blocks_ref[chip, core], 0, odd)
+    for i, p in enumerate((1 - core, core)):
+        side_ref[i] = merged(blocks_ref[chip ^ mask, p], 2 + p, p == 1).astype(jnp.bfloat16)
+    cross_ref[...] = merged(blocks_ref[chip ^ 3, 1 - core], 1, jnp.logical_not(odd)).astype(jnp.bfloat16)
+
+
+def merge(blocks, other):
+    rows, columns = other.shape[1:]
     return pl.pallas_call(
         merge_kernel,
         in_specs=[WHOLE] * 2,
-        out_specs=[WHOLE] * chips,
-        out_shape=[jax.ShapeDtypeStruct((rows, columns), jnp.bfloat16)] * chips,
+        out_specs=[WHOLE] * 3,
+        out_shape=[
+            jax.ShapeDtypeStruct((rows, columns), jnp.float32),
+            jax.ShapeDtypeStruct((rows, columns), jnp.bfloat16),
+            jax.ShapeDtypeStruct((2, rows, columns), jnp.bfloat16),
+        ],
         compiler_params=pltpu.CompilerParams(vmem_limit_bytes=8 * 1024 * 1024),
-    )(keep, other)
-
-
-def gather_kernel(*refs):
-    *part_refs, out_ref = refs
-    part_refs.reverse()
-    count = len(part_refs)
+    )(blocks, other)
+
+
+def pass_kernel(side_ref, out_ref):
+    out_ref[...] = side_ref[1]
+
+
+def pass_on(side):
+    return pl.pallas_call(
+        pass_kernel,
+        in_specs=[WHOLE],
+        out_specs=WHOLE,
+        out_shape=jax.ShapeDtypeStruct(side.shape[1:], side.dtype),
+        compiler_params=pltpu.CompilerParams(vmem_limit_bytes=4 * 1024 * 1024),
+    )(side)
+
+
+def gather_kernel(side_ref, cross_ref, passed_ref, own_ref, out_ref):
     share = out_ref.shape[1]
-    position = lax.axis_index("depth")
-    odd, chip = position % 2 == 1, position // 2
-    parts = [part_ref[...].astype(jnp.float32) for part_ref in part_refs]
+    chip, core, mask = route()
+    odd, serves_x = core == 1, mask == 1
+    side, passed = side_ref[0].astype(jnp.float32), passed_ref[...].astype(jnp.float32)
+    parts = [
+        own_ref[...],
+        jnp.where(serves_x, side, passed),
+        jnp.where(serves_x, passed, side),
+        cross_ref[...].astype(jnp.float32),
+    ]
     step = 1
-    while step < count:
+    while len(parts) > 1:
         swap = (chip & step) != 0
         parts = [
             over(jnp.where(swap, parts[i + 1], parts[i]), jnp.where(swap, parts[i], parts[i + 1]), odd)
@@ -419,7 +463,7 @@
 
 
 def gather(parts, share):
-    columns = parts[0].shape[1]
+    columns = parts[-1].shape[1]
     return pl.pallas_call(
         gather_kernel,
         in_specs=[WHOLE] * len(parts),
@@ -476,7 +520,8 @@
 
 
 def exchanged(values, mask):
-    return lax.ppermute(values, "depth", [(d, d ^ mask) for d in range(lax.axis_size("depth"))])
+    masks = [mask(d) if callable(mask) else mask for d in range(lax.axis_size("depth"))]
+    return lax.ppermute(values, "depth", [(d, d ^ m) for d, m in enumerate(masks)])
 
 
 def body(volume, color_map, alpha_map):
@@ -493,9 +538,11 @@
     outs = add_edges(volume, interior, halos, depth_count, paired)
     if not paired:
         return finish(lax.all_to_all(outs[0], "depth", 0, 0, tiled=True), share)
-    keep, give = outs
-    sends = merge(keep, exchanged(give, 1))
-    return gather([exchanged(send, 2 * k + 1) for k, send in reversed(list(enumerate(sends)))], share)
+    blocks, give = outs
+    own, cross, side = merge(blocks, exchanged(give, 1))
+    side = exchanged(side, lambda d: 2 * served(d) + 1)
+    cross = exchanged(cross, 7)
+    return gather((side, cross, exchanged(pass_on(side), 1), own), share)
 
 
 def solution(mesh):

time: 17.3 us -> 17.3 us (level)
  starting transfers between devices: 8.49 us -> 7.98 us
  waiting for transfers between devices: 3.23 us -> 3.66 us
    ppermute x5 -> x4, starting transfers between devices: 4.56 us -> 4.06 us  [exchanged(): lax.ppermute(values, 'depth', [(d, d ^ m) for d, m in enumerate(masks)])]
    ppermute x5 -> x4, waiting for transfers between devices: 3.22 us -> 3.65 us  [exchanged(): lax.ppermute(values, 'depth', [(d, d ^ m) for d, m in enumerate(masks)])]
  transfers between devices with their start and end apart: 9 -> 8, of which waited for: 4 -> 3; matrix products, arithmetic and copies ran while one was open for 0% -> 0% of each run, Pallas kernels for 17% -> 17%
where the time goes in v7:
time: 17.3 us; the launch traced here: 17.1 us
  starting transfers between devices  7.98 us (46%)
  Pallas kernels  5.42 us (31%)
  waiting for transfers between devices  3.66 us (21%)
    ppermute x4, starting transfers between devices, exchanged(): lax.ppermute(values, 'depth', [(d, d ^ m) for d, m in enumerate(masks)])  4.06 us
    ppermute x4, starting transfers between devices, swapped(): return lax.ppermute(values, ('depth', 'rows'), perm)  3.93 us
    ppermute x4, waiting for transfers between devices, exchanged(): lax.ppermute(values, 'depth', [(d, d ^ m) for d, m in enumerate(masks)])  3.65 us
    pallas_call x1, Pallas kernels, march_interior(): pl.pallas_call(functools.partial(interior_kernel, opacity_scale), in_spec...  2.95 us
    pallas_call x1, Pallas kernels, cut_edges(): pl.pallas_call(edges_kernel, in_specs=[pl.BlockSpec(memory_space=pl.ANY)]...  1.2 us
    pallas_call x1, Pallas kernels, gather(): pl.pallas_call(gather_kernel, in_specs=[WHOLE] * len(parts), out_specs=WH...  0.7 us
    pallas_call x1, Pallas kernels, add_edges(): pl.pallas_call(functools.partial(edge_kernel, share), in_specs=[WHOLE] *...  0.49 us
  transfers between devices with their start and end apart: 8, of which 3 were waited for; matrix products, arithmetic and copies ran while one was open for 0% of the time, Pallas kernels for 17%

profile of v7, /device:TPU:9, one launch (start us, length us, event | category | flops | bytes accessed | tf_op | source)
XLA Modules:
  0.0 17.1 jit_solution(14928239927237163677)
XLA Ops:
  0.0 0.0 copy-start
  0.0 0.0 copy-start.2
  0.0 0.0 copy-start.1
  0.0 1.2 %shard_map.38 = (bf16[32,1024]{1,0:T(8,128)(2,1)S(1)}, bf16[32,1024]{1,0:T(8,128)(2,1)S(1)}, bf16[32,1024]{1,0:T(8,128)(2,1)S(1)}, bf16[32,1024]{1,0:T(8,128)(2,1)S(1)}) custom-call(s32[2,8,32,1024]{3,2,1,0:T(8,128)} %volume_ref.5), custom_call_target="tpu_custom_call" | custom-call | tf_op jit(solution)/shard_map/pallas_call | solution.py:63
  1.2 0.7 %collective-permute-start = (bf16[32,1024]{1,0:T(8,128)(2,1)S(1)}, bf16[32,1024]{1,0:T(8,128)(2,1)S(1)}, u32[]{:S(2)}, u32[]{:S(2)}) collective-permute-start(bf16[32,1024]{1,0:T(8,128)(2,1)S(1)} %get-tuple-element.26), channel_id=1, source_target_pairs={{0,28},{1,5},{2,30},{3,7},{4,8},{5,1},{6,10},{7,3},{8,4},{9,13},{1... | collective-permute-start | bytes 196616 | tf_op jit(solution)/shard_map/ppermute | solution.py:519
  2.0 1.3 %collective-permute-start.1 = (bf16[32,1024]{1,0:T(8,128)(2,1)S(1)}, bf16[32,1024]{1,0:T(8,128)(2,1)S(1)}, u32[]{:S(2)}, u32[]{:S(2)}) collective-permute-start(bf16[32,1024]{1,0:T(8,128)(2,1)S(1)} %get-tuple-element.27), channel_id=1, source_target_pairs={{0,1},{1,0},{2,3},{3,2},{4,5},{5,4},{6,7},{7,6},{8,9},{9,8},{10,11... | collective-permute-start | bytes 196616 | tf_op jit(solution)/shard_map/ppermute | solution.py:519
  3.2 0.4 %collective-permute-start.2 = (bf16[32,1024]{1,0:T(8,128)(2,1)S(1)}, bf16[32,1024]{1,0:T(8,128)(2,1)S(1)}, u32[]{:S(2)}, u32[]{:S(2)}) collective-permute-start(bf16[32,1024]{1,0:T(8,128)(2,1)S(1)} %get-tuple-element.28), channel_id=1, source_target_pairs={{0,4},{1,29},{2,6},{3,31},{4,0},{5,9},{6,2},{7,11},{8,12},{9,5},{1... | collective-permute-start | bytes 196616 | tf_op jit(solution)/shard_map/ppermute | solution.py:519
  3.6 1.6 %collective-permute-start.3 = (bf16[32,1024]{1,0:T(8,128)(2,1)S(1)}, bf16[32,1024]{1,0:T(8,128)(2,1)S(1)}, u32[]{:S(2)}, u32[]{:S(2)}) collective-permute-start(bf16[32,1024]{1,0:T(8,128)(2,1)S(1)} %get-tuple-element.29), channel_id=1, source_target_pairs={{0,4},{1,2},{2,1},{3,7},{4,0},{5,6},{6,5},{7,3},{8,12},{9,10},{10,... | collective-permute-start | bytes 196616 | tf_op jit(solution)/shard_map/ppermute | solution.py:519
  5.1 0.0 copy-done
  5.1 0.0 copy-done.2
  5.1 0.0 copy-done.1
  5.2 3.0 %shard_map.37 = (f32[4,32,1024]{2,1,0:T(8,128)S(1)}, f32[2,32,1024]{2,1,0:T(8,128)S(1)}, f32[2,32,1024]{2,1,0:T(8,128)S(1)}, f32[2,3,32,1024]{3,2,1,0:T(8,128)S(...) custom-call(s32[2,8,32,1024]{3,2,1,0:T(8,128)S(1)} %copy-done, s32[3,256]{1,0:T(4,128)S(1)} %copy-done.1, ...), custom_call_target="tpu_custom_call" | custom-call | flops 20971520 | bytes 5242880 | tf_op jit(solution)/shard_map/pallas_call | solution.py:259
  8.1 0.0 collective-permute-done.first_ref
  8.1 0.0 collective-permute-done.1.rows_near_ref
  8.1 0.0 collective-permute-done.2.second_ref
  8.1 0.0 collective-permute-done.3.rows_far_ref
  8.2 0.5 %shard_map.39 = (f32[4,2,16,1024]{3,2,1,0:T(8,128)S(1)}, bf16[4,16,1024]{2,1,0:T(8,128)(2,1)S(1)}) custom-call(s32[2,8,32,1024]{3,2,1,0:T(8,128)S(1)} %copy-done, f32[4,32,1024]{2,1,0:T(8,128)S(1)} %get-tuple-element.20.base_ref, f32[2,32,1024]{2,1,0:T(8,128)S(1)} %get-tuple-element.21.face_ref, f32[2,32,1024]{2,1,0:T(8,128)S(1)} %get-tuple-element.22.square_ref, ...), custom_call_target="tpu_custom_call" | custom-call | tf_op jit(solution)/shard_map/pallas_call | solution.py:373
  8.6 1.2 %collective-permute-start.4 = (bf16[4,16,1024]{2,1,0:T(8,128)(2,1)S(1)}, bf16[4,16,1024]{2,1,0:T(8,128)(2,1)S(1)}, u32[]{:S(2)}, u32[]{:S(2)}) collective-permute-start(bf16[4,16,1024]{2,1,0:T(8,128)(2,1)S(1)} %get-tuple-element.31), channel_id=1, source_target_pairs={{0,4},{4,0},{8,12},{12,8},{16,20},{20,16},{24,28},{28,24},{1,5},{5... | collective-permute-start | bytes 393224 | tf_op jit(solution)/shard_map/ppermute | solution.py:524
  9.8 1.0 %collective-permute-done.4.other_ref = bf16[4,16,1024]{2,1,0:T(8,128)(2,1)S(1)} collective-permute-done((bf16[4,16,1024]{2,1,0:T(8,128)(2,1)S(1)}, bf16[4,16,1024]{2,1,0:T(8,128)(2,1)S(1)}, u32[]{:S(2)}, u32[]{:S(2)}) %collective-permute-start.4) | collective-permute-done | bytes 131104 | tf_op jit(solution)/shard_map/ppermute | solution.py:524
  10.8 0.1 shard_map.40
  10.9 1.3 %collective-permute-start.5 = (bf16[2,16,1024]{2,1,0:T(8,128)(2,1)S(1)}, bf16[2,16,1024]{2,1,0:T(8,128)(2,1)S(1)}, u32[]{:S(2)}, u32[]{:S(2)}) collective-permute-start(bf16[2,16,1024]{2,1,0:T(8,128)(2,1)S(1)} %get-tuple-element.32), channel_id=1, source_target_pairs={{0,12},{4,16},{8,28},{12,0},{16,4},{20,24},{24,20},{28,8},{1,13},{... | collective-permute-start | bytes 196616 | tf_op jit(solution)/shard_map/ppermute | solution.py:524
  12.2 1.2 %collective-permute-start.6 = (bf16[16,1024]{1,0:T(8,128)(2,1)S(1)}, bf16[16,1024]{1,0:T(8,128)(2,1)S(1)}, u32[]{:S(2)}, u32[]{:S(2)}) collective-permute-start(bf16[16,1024]{1,0:T(8,128)(2,1)S(1)} %get-tuple-element.33), channel_id=1, source_target_pairs={{0,28},{4,24},{8,20},{12,16},{16,12},{20,8},{24,4},{28,0},{1,29},{... | collective-permute-start | bytes 98312 | tf_op jit(solution)/shard_map/ppermute | solution.py:524
  13.4 1.2 %collective-permute-done.5.side_ref = bf16[2,16,1024]{2,1,0:T(8,128)(2,1)S(1)} collective-permute-done((bf16[2,16,1024]{2,1,0:T(8,128)(2,1)S(1)}, bf16[2,16,1024]{2,1,0:T(8,128)(2,1)S(1)}, u32[]{:S(2)}, u32[]{:S(2)}) %collective-permute-start.5) | collective-permute-done | bytes 65568 | tf_op jit(solution)/shard_map/ppermute | solution.py:524
  14.6 0.4 %collective-permute-start.7 = (bf16[16,1024]{1,0:T(8,128)(2,1)S(1)}, bf16[16,1024]{1,0:T(8,128)(2,1)S(1)}, u32[]{:S(2)}, u32[]{:S(2)}) collective-permute-start(bf16[16,1024]{1,0:T(8,128)(2,1)S(1)} %shard_map.41), channel_id=1, source_target_pairs={{0,4},{4,0},{8,12},{12,8},{16,20},{20,16},{24,28},{28,24},{1,5},{5... | collective-permute-start | bytes 98312 | tf_op jit(solution)/shard_map/ppermute | solution.py:524
  15.0 1.4 %collective-permute-done.6.cross_ref = bf16[16,1024]{1,0:T(8,128)(2,1)S(1)} collective-permute-done((bf16[16,1024]{1,0:T(8,128)(2,1)S(1)}, bf16[16,1024]{1,0:T(8,128)(2,1)S(1)}, u32[]{:S(2)}, u32[]{:S(2)}) %collective-permute-start.6) | collective-permute-done | bytes 32800 | tf_op jit(solution)/shard_map/ppermute | solution.py:524
  16.4 0.0 collective-permute-done.7.passed_ref
  16.4 0.7 %shard_map.42 = f32[4,4,1024]{2,1,0:T(4,128)} custom-call(bf16[2,16,1024]{2,1,0:T(8,128)(2,1)S(1)} %collective-permute-done.5.side_ref, bf16[16,1024]{1,0:T(8,128)(2,1)S(1)} %collective-permute-done.6.cross_ref, bf16[16,1024]{1,0:T(8,128)(2,1)S(1)} %collective-permute-done.7.passed_ref, f32[16,1024]{1,0:T(8,128)S(1)} %get-tuple-element.34.own_ref), custom_call_target="tpu_custom_call" | custom-call | tf_op jit(solution)/shard_map/pallas_call | solution.py:467
  (1 shorter events, 0.0 us)
Async XLA Ops:
  0.0 5.1 %copy-start = (s32[2,8,32,1024]{3,2,1,0:T(8,128)S(1)}, s32[2,8,32,1024]{3,2,1,0:T(8,128)}, u32[]{:S(2)}) copy-start(s32[2,8,32,1024]{3,2,1,0:T(8,128)} %volume_ref.5) | copy-start | bytes 6291460
  0.0 5.1 %copy-start.2 = (s32[256]{0:T(256)S(1)}, s32[256]{0:T(256)}, u32[]{:S(2)}) copy-start(s32[256]{0:T(256)} %param.5) | copy-start | bytes 3076
  0.0 5.1 %copy-start.1 = (s32[3,256]{1,0:T(4,128)S(1)}, s32[3,256]{1,0:T(4,128)}, u32[]{:S(2)}) copy-start(s32[3,256]{1,0:T(4,128)} %color_ref.1) | copy-start | bytes 9220
  1.2 6.9 %collective-permute-start = (bf16[32,1024]{1,0:T(8,128)(2,1)S(1)}, bf16[32,1024]{1,0:T(8,128)(2,1)S(1)}, u32[]{:S(2)}, u32[]{:S(2)}) collective-permute-start(bf16[32,1024]{1,0:T(8,128)(2,1)S(1)} %get-tuple-element.26), channel_id=1, source_target_pairs={{0,28},{1,5},{2,30},{3,7},{4,8},{5,1},{6,10},{7,3},{8,4},{9,13},{1... | collective-permute-start | bytes 196616 | tf_op jit(solution)/shard_map/ppermute | solution.py:519
  2.0 6.2 %collective-permute-start.1 = (bf16[32,1024]{1,0:T(8,128)(2,1)S(1)}, bf16[32,1024]{1,0:T(8,128)(2,1)S(1)}, u32[]{:S(2)}, u32[]{:S(2)}) collective-permute-start(bf16[32,1024]{1,0:T(8,128)(2,1)S(1)} %get-tuple-element.27), channel_id=1, source_target_pairs={{0,1},{1,0},{2,3},{3,2},{4,5},{5,4},{6,7},{7,6},{8,9},{9,8},{10,11... | collective-permute-start | bytes 196616 | tf_op jit(solution)/shard_map/ppermute | solution.py:519
  3.2 4.9 %collective-permute-start.2 = (bf16[32,1024]{1,0:T(8,128)(2,1)S(1)}, bf16[32,1024]{1,0:T(8,128)(2,1)S(1)}, u32[]{:S(2)}, u32[]{:S(2)}) collective-permute-start(bf16[32,1024]{1,0:T(8,128)(2,1)S(1)} %get-tuple-element.28), channel_id=1, source_target_pairs={{0,4},{1,29},{2,6},{3,31},{4,0},{5,9},{6,2},{7,11},{8,12},{9,5},{1... | collective-permute-start | bytes 196616 | tf_op jit(solution)/shard_map/ppermute | solution.py:519
  3.6 4.6 %collective-permute-start.3 = (bf16[32,1024]{1,0:T(8,128)(2,1)S(1)}, bf16[32,1024]{1,0:T(8,128)(2,1)S(1)}, u32[]{:S(2)}, u32[]{:S(2)}) collective-permute-start(bf16[32,1024]{1,0:T(8,128)(2,1)S(1)} %get-tuple-element.29), channel_id=1, source_target_pairs={{0,4},{1,2},{2,1},{3,7},{4,0},{5,6},{6,5},{7,3},{8,12},{9,10},{10,... | collective-permute-start | bytes 196616 | tf_op jit(solution)/shard_map/ppermute | solution.py:519
  8.6 2.1 %collective-permute-start.4 = (bf16[4,16,1024]{2,1,0:T(8,128)(2,1)S(1)}, bf16[4,16,1024]{2,1,0:T(8,128)(2,1)S(1)}, u32[]{:S(2)}, u32[]{:S(2)}) collective-permute-start(bf16[4,16,1024]{2,1,0:T(8,128)(2,1)S(1)} %get-tuple-element.31), channel_id=1, source_target_pairs={{0,4},{4,0},{8,12},{12,8},{16,20},{20,16},{24,28},{28,24},{1,5},{5... | collective-permute-start | bytes 393224 | tf_op jit(solution)/shard_map/ppermute | solution.py:524
  10.9 3.8 %collective-permute-start.5 = (bf16[2,16,1024]{2,1,0:T(8,128)(2,1)S(1)}, bf16[2,16,1024]{2,1,0:T(8,128)(2,1)S(1)}, u32[]{:S(2)}, u32[]{:S(2)}) collective-permute-start(bf16[2,16,1024]{2,1,0:T(8,128)(2,1)S(1)} %get-tuple-element.32), channel_id=1, source_target_pairs={{0,12},{4,16},{8,28},{12,0},{16,4},{20,24},{24,20},{28,8},{1,13},{... | collective-permute-start | bytes 196616 | tf_op jit(solution)/shard_map/ppermute | solution.py:524
  12.2 4.2 %collective-permute-start.6 = (bf16[16,1024]{1,0:T(8,128)(2,1)S(1)}, bf16[16,1024]{1,0:T(8,128)(2,1)S(1)}, u32[]{:S(2)}, u32[]{:S(2)}) collective-permute-start(bf16[16,1024]{1,0:T(8,128)(2,1)S(1)} %get-tuple-element.33), channel_id=1, source_target_pairs={{0,28},{4,24},{8,20},{12,16},{16,12},{20,8},{24,4},{28,0},{1,29},{... | collective-permute-start | bytes 98312 | tf_op jit(solution)/shard_map/ppermute | solution.py:524
  14.6 1.8 %collective-permute-start.7 = (bf16[16,1024]{1,0:T(8,128)(2,1)S(1)}, bf16[16,1024]{1,0:T(8,128)(2,1)S(1)}, u32[]{:S(2)}, u32[]{:S(2)}) collective-permute-start(bf16[16,1024]{1,0:T(8,128)(2,1)S(1)} %shard_map.41), channel_id=1, source_target_pairs={{0,4},{4,0},{8,12},{12,8},{16,20},{20,16},{24,28},{28,24},{1,5},{5... | collective-permute-start | bytes 98312 | tf_op jit(solution)/shard_map/ppermute | solution.py:524

commit v8 on v7

--- a/solution.py
+++ b/solution.py
@@ -54,17 +54,18 @@
     copies[2].wait()
     second_out[...] = narrow(plane_ref[1])
     copies[3].wait()
-    rows_far_out[...] = padded(strip_ref[1])
+    rows_far_out[...] = narrow(strip_ref[1])
 
 
 def cut_edges(volume):
     _, slices, height, columns = volume.shape
     plane = jax.ShapeDtypeStruct((height, columns), jnp.bfloat16)
+    strip = jax.ShapeDtypeStruct((slices, columns), jnp.bfloat16)
     return pl.pallas_call(
         edges_kernel,
         in_specs=[pl.BlockSpec(memory_space=pl.ANY)],
         out_specs=[WHOLE] * 4,
-        out_shape=[plane] * 4,
+        out_shape=[plane, plane, plane, strip],
         scratch_shapes=[
             pltpu.VMEM((2, slices, columns), jnp.int32),
             pltpu.VMEM((2, height, columns), jnp.int32),
@@ -299,7 +300,7 @@
     def chunk(j, carry):
         here = pl.ds(pl.multiple_of(j * LANES, LANES), LANES)
         rows_near = rows_near_ref[:, here].astype(jnp.float32)[:slices]
-        rows_far = rows_far_ref[:, here].astype(jnp.float32)[:slices]
+        rows_far = rows_far_ref[:, here].astype(jnp.float32)
         above = jnp.where(top_end, 0.0, jnp.where(odd_row, rows_near, rows_far))
         below = jnp.where(bottom_end, 0.0, jnp.where(odd_row, rows_far, rows_near))
         first = first_ref[:, here].astype(jnp.float32)

time: 17.3 us -> 17 us (0.983)
  the two profiles are of different devices: /device:TPU:9 before, /device:TPU:25 now
where the time goes in v8:
time: 17 us; the launch traced here: 16.8 us
  starting transfers between devices  6.9 us (41%)
  Pallas kernels  5.41 us (32%)
  waiting for transfers between devices  4.43 us (26%)
    ppermute x4, waiting for transfers between devices, exchanged(): lax.ppermute(values, 'depth', [(d, d ^ m) for d, m in enumerate(masks)])  4.42 us
    ppermute x4, starting transfers between devices, swapped(): return lax.ppermute(values, ('depth', 'rows'), perm)  3.55 us
    ppermute x4, starting transfers between devices, exchanged(): lax.ppermute(values, 'depth', [(d, d ^ m) for d, m in enumerate(masks)])  3.34 us
    pallas_call x1, Pallas kernels, march_interior(): pl.pallas_call(functools.partial(interior_kernel, opacity_scale), in_spec...  2.95 us
    pallas_call x1, Pallas kernels, cut_edges(): pl.pallas_call(edges_kernel, in_specs=[pl.BlockSpec(memory_space=pl.ANY)]...  1.2 us
    pallas_call x1, Pallas kernels, gather(): pl.pallas_call(gather_kernel, in_specs=[WHOLE] * len(parts), out_specs=WH...  0.7 us
    pallas_call x1, Pallas kernels, add_edges(): pl.pallas_call(functools.partial(edge_kernel, share), in_specs=[WHOLE] *...  0.48 us
  transfers between devices with their start and end apart: 8, of which 4 were waited for; matrix products, arithmetic and copies ran while one was open for 0% of the time, Pallas kernels for 18%

profile of v8, /device:TPU:25, one launch (start us, length us, event | category | flops | bytes accessed | tf_op | source)
XLA Modules:
  0.0 16.8 jit_solution(10232834114474751588)
XLA Ops:
  0.0 0.0 copy-start
  0.0 0.0 copy-start.2
  0.0 0.0 copy-start.1
  0.0 1.2 %shard_map.38 = (bf16[32,1024]{1,0:T(8,128)(2,1)S(1)}, bf16[32,1024]{1,0:T(8,128)(2,1)S(1)}, bf16[32,1024]{1,0:T(8,128)(2,1)S(1)}, bf16[8,1024]{1,0:T(8,128)(2,1)S(1)}) custom-call(s32[2,8,32,1024]{3,2,1,0:T(8,128)} %volume_ref.5), custom_call_target="tpu_custom_call" | custom-call | tf_op jit(solution)/shard_map/pallas_call | solution.py:64
  1.2 0.7 %collective-permute-start = (bf16[32,1024]{1,0:T(8,128)(2,1)S(1)}, bf16[32,1024]{1,0:T(8,128)(2,1)S(1)}, u32[]{:S(2)}, u32[]{:S(2)}) collective-permute-start(bf16[32,1024]{1,0:T(8,128)(2,1)S(1)} %get-tuple-element.26), channel_id=1, source_target_pairs={{0,28},{1,5},{2,30},{3,7},{4,8},{5,1},{6,10},{7,3},{8,4},{9,13},{1... | collective-permute-start | bytes 196616 | tf_op jit(solution)/shard_map/ppermute | solution.py:520
  2.0 1.3 %collective-permute-start.1 = (bf16[32,1024]{1,0:T(8,128)(2,1)S(1)}, bf16[32,1024]{1,0:T(8,128)(2,1)S(1)}, u32[]{:S(2)}, u32[]{:S(2)}) collective-permute-start(bf16[32,1024]{1,0:T(8,128)(2,1)S(1)} %get-tuple-element.27), channel_id=1, source_target_pairs={{0,1},{1,0},{2,3},{3,2},{4,5},{5,4},{6,7},{7,6},{8,9},{9,8},{10,11... | collective-permute-start | bytes 196616 | tf_op jit(solution)/shard_map/ppermute | solution.py:520
  3.2 0.4 %collective-permute-start.2 = (bf16[32,1024]{1,0:T(8,128)(2,1)S(1)}, bf16[32,1024]{1,0:T(8,128)(2,1)S(1)}, u32[]{:S(2)}, u32[]{:S(2)}) collective-permute-start(bf16[32,1024]{1,0:T(8,128)(2,1)S(1)} %get-tuple-element.28), channel_id=1, source_target_pairs={{0,4},{1,29},{2,6},{3,31},{4,0},{5,9},{6,2},{7,11},{8,12},{9,5},{1... | collective-permute-start | bytes 196616 | tf_op jit(solution)/shard_map/ppermute | solution.py:520
  3.6 1.2 %collective-permute-start.3 = (bf16[8,1024]{1,0:T(8,128)(2,1)S(1)}, bf16[8,1024]{1,0:T(8,128)(2,1)S(1)}, u32[]{:S(2)}, u32[]{:S(2)}) collective-permute-start(bf16[8,1024]{1,0:T(8,128)(2,1)S(1)} %get-tuple-element.29), channel_id=1, source_target_pairs={{0,4},{1,2},{2,1},{3,7},{4,0},{5,6},{6,5},{7,3},{8,12},{9,10},{10,... | collective-permute-start | bytes 49160 | tf_op jit(solution)/shard_map/ppermute | solution.py:520
  4.8 0.0 copy-done
  4.8 0.0 copy-done.2
  4.8 0.0 copy-done.1
  4.8 3.0 %shard_map.37 = (f32[4,32,1024]{2,1,0:T(8,128)S(1)}, f32[2,32,1024]{2,1,0:T(8,128)S(1)}, f32[2,32,1024]{2,1,0:T(8,128)S(1)}, f32[2,3,32,1024]{3,2,1,0:T(8,128)S(...) custom-call(s32[2,8,32,1024]{3,2,1,0:T(8,128)S(1)} %copy-done, s32[3,256]{1,0:T(4,128)S(1)} %copy-done.1, ...), custom_call_target="tpu_custom_call" | custom-call | flops 20971520 | bytes 5242880 | tf_op jit(solution)/shard_map/pallas_call | solution.py:260
  7.7 0.0 collective-permute-done.3.rows_far_ref
  7.8 0.0 collective-permute-done.first_ref
  7.8 0.0 collective-permute-done.1.rows_near_ref
  7.8 0.0 collective-permute-done.2.second_ref
  7.8 0.5 %shard_map.39 = (f32[4,2,16,1024]{3,2,1,0:T(8,128)S(1)}, bf16[4,16,1024]{2,1,0:T(8,128)(2,1)S(1)}) custom-call(s32[2,8,32,1024]{3,2,1,0:T(8,128)S(1)} %copy-done, f32[4,32,1024]{2,1,0:T(8,128)S(1)} %get-tuple-element.20.base_ref, f32[2,32,1024]{2,1,0:T(8,128)S(1)} %get-tuple-element.21.face_ref, f32[2,32,1024]{2,1,0:T(8,128)S(1)} %get-tuple-element.22.square_ref, ...), custom_call_target="tpu_custom_call" | custom-call | tf_op jit(solution)/shard_map/pallas_call | solution.py:374
  8.3 1.5 %collective-permute-start.4 = (bf16[4,16,1024]{2,1,0:T(8,128)(2,1)S(1)}, bf16[4,16,1024]{2,1,0:T(8,128)(2,1)S(1)}, u32[]{:S(2)}, u32[]{:S(2)}) collective-permute-start(bf16[4,16,1024]{2,1,0:T(8,128)(2,1)S(1)} %get-tuple-element.31), channel_id=1, source_target_pairs={{0,4},{4,0},{8,12},{12,8},{16,20},{20,16},{24,28},{28,24},{1,5},{5... | collective-permute-start | bytes 393224 | tf_op jit(solution)/shard_map/ppermute | solution.py:525
  9.8 1.0 %collective-permute-done.4.other_ref = bf16[4,16,1024]{2,1,0:T(8,128)(2,1)S(1)} collective-permute-done((bf16[4,16,1024]{2,1,0:T(8,128)(2,1)S(1)}, bf16[4,16,1024]{2,1,0:T(8,128)(2,1)S(1)}, u32[]{:S(2)}, u32[]{:S(2)}) %collective-permute-start.4) | collective-permute-done | bytes 131104 | tf_op jit(solution)/shard_map/ppermute | solution.py:525
  10.8 0.1 shard_map.40
  10.9 0.5 %collective-permute-start.5 = (bf16[2,16,1024]{2,1,0:T(8,128)(2,1)S(1)}, bf16[2,16,1024]{2,1,0:T(8,128)(2,1)S(1)}, u32[]{:S(2)}, u32[]{:S(2)}) collective-permute-start(bf16[2,16,1024]{2,1,0:T(8,128)(2,1)S(1)} %get-tuple-element.32), channel_id=1, source_target_pairs={{0,12},{4,16},{8,28},{12,0},{16,4},{20,24},{24,20},{28,8},{1,13},{... | collective-permute-start | bytes 196616 | tf_op jit(solution)/shard_map/ppermute | solution.py:525
  11.4 1.2 %collective-permute-start.6 = (bf16[16,1024]{1,0:T(8,128)(2,1)S(1)}, bf16[16,1024]{1,0:T(8,128)(2,1)S(1)}, u32[]{:S(2)}, u32[]{:S(2)}) collective-permute-start(bf16[16,1024]{1,0:T(8,128)(2,1)S(1)} %get-tuple-element.33), channel_id=1, source_target_pairs={{0,28},{4,24},{8,20},{12,16},{16,12},{20,8},{24,4},{28,0},{1,29},{... | collective-permute-start | bytes 98312 | tf_op jit(solution)/shard_map/ppermute | solution.py:525
  12.6 2.3 %collective-permute-done.5.side_ref = bf16[2,16,1024]{2,1,0:T(8,128)(2,1)S(1)} collective-permute-done((bf16[2,16,1024]{2,1,0:T(8,128)(2,1)S(1)}, bf16[2,16,1024]{2,1,0:T(8,128)(2,1)S(1)}, u32[]{:S(2)}, u32[]{:S(2)}) %collective-permute-start.5) | collective-permute-done | bytes 65568 | tf_op jit(solution)/shard_map/ppermute | solution.py:525
  14.9 0.1 collective-permute-start.7
  15.0 0.7 %collective-permute-done.6.cross_ref = bf16[16,1024]{1,0:T(8,128)(2,1)S(1)} collective-permute-done((bf16[16,1024]{1,0:T(8,128)(2,1)S(1)}, bf16[16,1024]{1,0:T(8,128)(2,1)S(1)}, u32[]{:S(2)}, u32[]{:S(2)}) %collective-permute-start.6) | collective-permute-done | bytes 32800 | tf_op jit(solution)/shard_map/ppermute | solution.py:525
  15.6 0.5 %collective-permute-done.7.passed_ref = bf16[16,1024]{1,0:T(8,128)(2,1)S(1)} collective-permute-done((bf16[16,1024]{1,0:T(8,128)(2,1)S(1)}, bf16[16,1024]{1,0:T(8,128)(2,1)S(1)}, u32[]{:S(2)}, u32[]{:S(2)}) %collective-permute-start.7) | collective-permute-done | bytes 32800 | tf_op jit(solution)/shard_map/ppermute | solution.py:525
  16.1 0.7 %shard_map.42 = f32[4,4,1024]{2,1,0:T(4,128)} custom-call(bf16[2,16,1024]{2,1,0:T(8,128)(2,1)S(1)} %collective-permute-done.5.side_ref, bf16[16,1024]{1,0:T(8,128)(2,1)S(1)} %collective-permute-done.6.cross_ref, bf16[16,1024]{1,0:T(8,128)(2,1)S(1)} %collective-permute-done.7.passed_ref, f32[16,1024]{1,0:T(8,128)S(1)} %get-tuple-element.34.own_ref), custom_call_target="tpu_custom_call" | custom-call | tf_op jit(solution)/shard_map/pallas_call | solution.py:468
  (1 shorter events, 0.0 us)
Async XLA Ops:
  0.0 4.8 %copy-start = (s32[2,8,32,1024]{3,2,1,0:T(8,128)S(1)}, s32[2,8,32,1024]{3,2,1,0:T(8,128)}, u32[]{:S(2)}) copy-start(s32[2,8,32,1024]{3,2,1,0:T(8,128)} %volume_ref.5) | copy-start | bytes 6291460
  0.0 4.8 %copy-start.2 = (s32[256]{0:T(256)S(1)}, s32[256]{0:T(256)}, u32[]{:S(2)}) copy-start(s32[256]{0:T(256)} %param.5) | copy-start | bytes 3076
  0.0 4.8 %copy-start.1 = (s32[3,256]{1,0:T(4,128)S(1)}, s32[3,256]{1,0:T(4,128)}, u32[]{:S(2)}) copy-start(s32[3,256]{1,0:T(4,128)} %color_ref.1) | copy-start | bytes 9220
  1.2 6.5 %collective-permute-start = (bf16[32,1024]{1,0:T(8,128)(2,1)S(1)}, bf16[32,1024]{1,0:T(8,128)(2,1)S(1)}, u32[]{:S(2)}, u32[]{:S(2)}) collective-permute-start(bf16[32,1024]{1,0:T(8,128)(2,1)S(1)} %get-tuple-element.26), channel_id=1, source_target_pairs={{0,28},{1,5},{2,30},{3,7},{4,8},{5,1},{6,10},{7,3},{8,4},{9,13},{1... | collective-permute-start | bytes 196616 | tf_op jit(solution)/shard_map/ppermute | solution.py:520
  2.0 5.8 %collective-permute-start.1 = (bf16[32,1024]{1,0:T(8,128)(2,1)S(1)}, bf16[32,1024]{1,0:T(8,128)(2,1)S(1)}, u32[]{:S(2)}, u32[]{:S(2)}) collective-permute-start(bf16[32,1024]{1,0:T(8,128)(2,1)S(1)} %get-tuple-element.27), channel_id=1, source_target_pairs={{0,1},{1,0},{2,3},{3,2},{4,5},{5,4},{6,7},{7,6},{8,9},{9,8},{10,11... | collective-permute-start | bytes 196616 | tf_op jit(solution)/shard_map/ppermute | solution.py:520
  3.2 4.6 %collective-permute-start.2 = (bf16[32,1024]{1,0:T(8,128)(2,1)S(1)}, bf16[32,1024]{1,0:T(8,128)(2,1)S(1)}, u32[]{:S(2)}, u32[]{:S(2)}) collective-permute-start(bf16[32,1024]{1,0:T(8,128)(2,1)S(1)} %get-tuple-element.28), channel_id=1, source_target_pairs={{0,4},{1,29},{2,6},{3,31},{4,0},{5,9},{6,2},{7,11},{8,12},{9,5},{1... | collective-permute-start | bytes 196616 | tf_op jit(solution)/shard_map/ppermute | solution.py:520
  3.6 4.2 %collective-permute-start.3 = (bf16[8,1024]{1,0:T(8,128)(2,1)S(1)}, bf16[8,1024]{1,0:T(8,128)(2,1)S(1)}, u32[]{:S(2)}, u32[]{:S(2)}) collective-permute-start(bf16[8,1024]{1,0:T(8,128)(2,1)S(1)} %get-tuple-element.29), channel_id=1, source_target_pairs={{0,4},{1,2},{2,1},{3,7},{4,0},{5,6},{6,5},{7,3},{8,12},{9,10},{10,... | collective-permute-start | bytes 49160 | tf_op jit(solution)/shard_map/ppermute | solution.py:520
  8.3 2.5 %collective-permute-start.4 = (bf16[4,16,1024]{2,1,0:T(8,128)(2,1)S(1)}, bf16[4,16,1024]{2,1,0:T(8,128)(2,1)S(1)}, u32[]{:S(2)}, u32[]{:S(2)}) collective-permute-start(bf16[4,16,1024]{2,1,0:T(8,128)(2,1)S(1)} %get-tuple-element.31), channel_id=1, source_target_pairs={{0,4},{4,0},{8,12},{12,8},{16,20},{20,16},{24,28},{28,24},{1,5},{5... | collective-permute-start | bytes 393224 | tf_op jit(solution)/shard_map/ppermute | solution.py:525
  10.9 4.1 %collective-permute-start.5 = (bf16[2,16,1024]{2,1,0:T(8,128)(2,1)S(1)}, bf16[2,16,1024]{2,1,0:T(8,128)(2,1)S(1)}, u32[]{:S(2)}, u32[]{:S(2)}) collective-permute-start(bf16[2,16,1024]{2,1,0:T(8,128)(2,1)S(1)} %get-tuple-element.32), channel_id=1, source_target_pairs={{0,12},{4,16},{8,28},{12,0},{16,4},{20,24},{24,20},{28,8},{1,13},{... | collective-permute-start | bytes 196616 | tf_op jit(solution)/shard_map/ppermute | solution.py:525
  11.4 4.2 %collective-permute-start.6 = (bf16[16,1024]{1,0:T(8,128)(2,1)S(1)}, bf16[16,1024]{1,0:T(8,128)(2,1)S(1)}, u32[]{:S(2)}, u32[]{:S(2)}) collective-permute-start(bf16[16,1024]{1,0:T(8,128)(2,1)S(1)} %get-tuple-element.33), channel_id=1, source_target_pairs={{0,28},{4,24},{8,20},{12,16},{16,12},{20,8},{24,4},{28,0},{1,29},{... | collective-permute-start | bytes 98312 | tf_op jit(solution)/shard_map/ppermute | solution.py:525
  14.9 1.2 %collective-permute-start.7 = (bf16[16,1024]{1,0:T(8,128)(2,1)S(1)}, bf16[16,1024]{1,0:T(8,128)(2,1)S(1)}, u32[]{:S(2)}, u32[]{:S(2)}) collective-permute-start(bf16[16,1024]{1,0:T(8,128)(2,1)S(1)} %shard_map.41), channel_id=1, source_target_pairs={{0,4},{4,0},{8,12},{12,8},{16,20},{20,16},{24,28},{28,24},{1,5},{5... | collective-permute-start | bytes 98312 | tf_op jit(solution)/shard_map/ppermute | solution.py:525

commit v9 on v8

--- a/solution.py
+++ b/solution.py
@@ -242,7 +242,7 @@
                 strip_ref[q, c, :, here] = emitted[c] * weight
         return carry
 
-    lax.fori_loop(0, chunks, chunk, 0)
+    lax.fori_loop(0, chunks, chunk, 0, unroll=2)
 
 
 def march_interior(volume, color_map, alpha_map, depth_count):
@@ -351,7 +351,7 @@
                 blocks_ref[r, 1, :, here] = uneven
         return carry
 
-    lax.fori_loop(0, columns // LANES, chunk, 0)
+    lax.fori_loop(0, columns // LANES, chunk, 0, unroll=4)
     if len(out_refs) > 1:
         blocks_ref, give_ref = out_refs
         chip, core, mask = route()

time: 17 us -> 16.9 us (level)
  the two profiles are of different devices: /device:TPU:25 before, /device:TPU:0 now
where the time goes in v9:
time: 16.9 us; the launch traced here: 16.6 us
  starting transfers between devices  5.93 us (35%)
  waiting for transfers between devices  5.62 us (33%)
  Pallas kernels  5.01 us (30%)
    ppermute x4, waiting for transfers between devices, exchanged(): lax.ppermute(values, 'depth', [(d, d ^ m) for d, m in enumerate(masks)])  4.51 us
    ppermute x4, starting transfers between devices, swapped(): return lax.ppermute(values, ('depth', 'rows'), perm)  3.93 us
    pallas_call x1, Pallas kernels, march_interior(): pl.pallas_call(functools.partial(interior_kernel, opacity_scale), in_spec...  2.62 us
    ppermute x4, starting transfers between devices, exchanged(): lax.ppermute(values, 'depth', [(d, d ^ m) for d, m in enumerate(masks)])  2 us
    pallas_call x1, Pallas kernels, cut_edges(): pl.pallas_call(edges_kernel, in_specs=[pl.BlockSpec(memory_space=pl.ANY)]...  1.18 us
    ppermute x4, waiting for transfers between devices, swapped(): return lax.ppermute(values, ('depth', 'rows'), perm)  1.11 us
    pallas_call x1, Pallas kernels, gather(): pl.pallas_call(gather_kernel, in_specs=[WHOLE] * len(parts), out_specs=WH...  0.7 us
    pallas_call x1, Pallas kernels, add_edges(): pl.pallas_call(functools.partial(edge_kernel, share), in_specs=[WHOLE] *...  0.43 us
  transfers between devices with their start and end apart: 8, of which 5 were waited for; matrix products, arithmetic and copies ran while one was open for 0% of the time, Pallas kernels for 16%

profile of v9, /device:TPU:0, one launch (start us, length us, event | category | flops | bytes accessed | tf_op | source)
XLA Modules:
  0.0 16.6 jit_solution(11020107135150942875)
XLA Ops:
  0.0 0.0 copy-start
  0.0 0.0 copy-start.2
  0.0 0.0 copy-start.1
  0.0 1.2 %shard_map.38 = (bf16[32,1024]{1,0:T(8,128)(2,1)S(1)}, bf16[32,1024]{1,0:T(8,128)(2,1)S(1)}, bf16[32,1024]{1,0:T(8,128)(2,1)S(1)}, bf16[8,1024]{1,0:T(8,128)(2,1)S(1)}) custom-call(s32[2,8,32,1024]{3,2,1,0:T(8,128)} %volume_ref.5), custom_call_target="tpu_custom_call" | custom-call | tf_op jit(solution)/shard_map/pallas_call | solution.py:64
  1.2 3.4 %collective-permute-start = (bf16[32,1024]{1,0:T(8,128)(2,1)S(1)}, bf16[32,1024]{1,0:T(8,128)(2,1)S(1)}, u32[]{:S(2)}, u32[]{:S(2)}) collective-permute-start(bf16[32,1024]{1,0:T(8,128)(2,1)S(1)} %get-tuple-element.26), channel_id=1, source_target_pairs={{0,28},{1,5},{2,30},{3,7},{4,8},{5,1},{6,10},{7,3},{8,4},{9,13},{1... | collective-permute-start | bytes 196616 | tf_op jit(solution)/shard_map/ppermute | solution.py:520
  4.6 0.0 collective-permute-start.1
  4.6 0.0 collective-permute-start.2
  4.6 0.5 %collective-permute-start.3 = (bf16[8,1024]{1,0:T(8,128)(2,1)S(1)}, bf16[8,1024]{1,0:T(8,128)(2,1)S(1)}, u32[]{:S(2)}, u32[]{:S(2)}) collective-permute-start(bf16[8,1024]{1,0:T(8,128)(2,1)S(1)} %get-tuple-element.29), channel_id=1, source_target_pairs={{0,4},{1,2},{2,1},{3,7},{4,0},{5,6},{6,5},{7,3},{8,12},{9,10},{10,... | collective-permute-start | bytes 49160 | tf_op jit(solution)/shard_map/ppermute | solution.py:520
  5.1 0.0 copy-done
  5.1 0.0 copy-done.2
  5.1 0.0 copy-done.1
  5.1 2.6 %shard_map.37 = (f32[4,32,1024]{2,1,0:T(8,128)S(1)}, f32[2,32,1024]{2,1,0:T(8,128)S(1)}, f32[2,32,1024]{2,1,0:T(8,128)S(1)}, f32[2,3,32,1024]{3,2,1,0:T(8,128)S(...) custom-call(s32[2,8,32,1024]{3,2,1,0:T(8,128)S(1)} %copy-done, s32[3,256]{1,0:T(4,128)S(1)} %copy-done.1, ...), custom_call_target="tpu_custom_call" | custom-call | flops 20971520 | bytes 5242880 | tf_op jit(solution)/shard_map/pallas_call | solution.py:260
  7.8 0.0 collective-permute-done.3.rows_far_ref
  7.8 0.0 collective-permute-done.first_ref
  7.8 1.1 %collective-permute-done.1.rows_near_ref = bf16[32,1024]{1,0:T(8,128)(2,1)S(1)} collective-permute-done((bf16[32,1024]{1,0:T(8,128)(2,1)S(1)}, bf16[32,1024]{1,0:T(8,128)(2,1)S(1)}, u32[]{:S(2)}, u32[]{:S(2)}) %collective-permute-start.1) | collective-permute-done | bytes 65568 | tf_op jit(solution)/shard_map/ppermute | solution.py:520
  8.9 0.0 collective-permute-done.2.second_ref
  8.9 0.4 %shard_map.39 = (f32[4,2,16,1024]{3,2,1,0:T(8,128)S(1)}, bf16[4,16,1024]{2,1,0:T(8,128)(2,1)S(1)}) custom-call(s32[2,8,32,1024]{3,2,1,0:T(8,128)S(1)} %copy-done, f32[4,32,1024]{2,1,0:T(8,128)S(1)} %get-tuple-element.20.base_ref, f32[2,32,1024]{2,1,0:T(8,128)S(1)} %get-tuple-element.21.face_ref, f32[2,32,1024]{2,1,0:T(8,128)S(1)} %get-tuple-element.22.square_ref, ...), custom_call_target="tpu_custom_call" | custom-call | tf_op jit(solution)/shard_map/pallas_call | solution.py:374
  9.3 0.1 collective-permute-start.4
  9.4 1.3 %collective-permute-done.4.other_ref = bf16[4,16,1024]{2,1,0:T(8,128)(2,1)S(1)} collective-permute-done((bf16[4,16,1024]{2,1,0:T(8,128)(2,1)S(1)}, bf16[4,16,1024]{2,1,0:T(8,128)(2,1)S(1)}, u32[]{:S(2)}, u32[]{:S(2)}) %collective-permute-start.4) | collective-permute-done | bytes 131104 | tf_op jit(solution)/shard_map/ppermute | solution.py:525
  10.7 0.1 shard_map.40
  10.8 0.1 collective-permute-start.5
  10.9 1.3 %collective-permute-start.6 = (bf16[16,1024]{1,0:T(8,128)(2,1)S(1)}, bf16[16,1024]{1,0:T(8,128)(2,1)S(1)}, u32[]{:S(2)}, u32[]{:S(2)}) collective-permute-start(bf16[16,1024]{1,0:T(8,128)(2,1)S(1)} %get-tuple-element.33), channel_id=1, source_target_pairs={{0,28},{4,24},{8,20},{12,16},{16,12},{20,8},{24,4},{28,0},{1,29},{... | collective-permute-start | bytes 98312 | tf_op jit(solution)/shard_map/ppermute | solution.py:525
  12.3 2.3 %collective-permute-done.5.side_ref = bf16[2,16,1024]{2,1,0:T(8,128)(2,1)S(1)} collective-permute-done((bf16[2,16,1024]{2,1,0:T(8,128)(2,1)S(1)}, bf16[2,16,1024]{2,1,0:T(8,128)(2,1)S(1)}, u32[]{:S(2)}, u32[]{:S(2)}) %collective-permute-start.5) | collective-permute-done | bytes 65568 | tf_op jit(solution)/shard_map/ppermute | solution.py:525
  14.6 0.5 %collective-permute-start.7 = (bf16[16,1024]{1,0:T(8,128)(2,1)S(1)}, bf16[16,1024]{1,0:T(8,128)(2,1)S(1)}, u32[]{:S(2)}, u32[]{:S(2)}) collective-permute-start(bf16[16,1024]{1,0:T(8,128)(2,1)S(1)} %shard_map.41), channel_id=1, source_target_pairs={{0,4},{4,0},{8,12},{12,8},{16,20},{20,16},{24,28},{28,24},{1,5},{5... | collective-permute-start | bytes 98312 | tf_op jit(solution)/shard_map/ppermute | solution.py:525
  15.1 0.5 %collective-permute-done.6.cross_ref = bf16[16,1024]{1,0:T(8,128)(2,1)S(1)} collective-permute-done((bf16[16,1024]{1,0:T(8,128)(2,1)S(1)}, bf16[16,1024]{1,0:T(8,128)(2,1)S(1)}, u32[]{:S(2)}, u32[]{:S(2)}) %collective-permute-start.6) | collective-permute-done | bytes 32800 | tf_op jit(solution)/shard_map/ppermute | solution.py:525
  15.6 0.4 %collective-permute-done.7.passed_ref = bf16[16,1024]{1,0:T(8,128)(2,1)S(1)} collective-permute-done((bf16[16,1024]{1,0:T(8,128)(2,1)S(1)}, bf16[16,1024]{1,0:T(8,128)(2,1)S(1)}, u32[]{:S(2)}, u32[]{:S(2)}) %collective-permute-start.7) | collective-permute-done | bytes 32800 | tf_op jit(solution)/shard_map/ppermute | solution.py:525
  15.9 0.7 %shard_map.42 = f32[4,4,1024]{2,1,0:T(4,128)} custom-call(bf16[2,16,1024]{2,1,0:T(8,128)(2,1)S(1)} %collective-permute-done.5.side_ref, bf16[16,1024]{1,0:T(8,128)(2,1)S(1)} %collective-permute-done.6.cross_ref, bf16[16,1024]{1,0:T(8,128)(2,1)S(1)} %collective-permute-done.7.passed_ref, f32[16,1024]{1,0:T(8,128)S(1)} %get-tuple-element.34.own_ref), custom_call_target="tpu_custom_call" | custom-call | tf_op jit(solution)/shard_map/pallas_call | solution.py:468
  (1 shorter events, 0.0 us)
Async XLA Ops:
  0.0 5.1 %copy-start = (s32[2,8,32,1024]{3,2,1,0:T(8,128)S(1)}, s32[2,8,32,1024]{3,2,1,0:T(8,128)}, u32[]{:S(2)}) copy-start(s32[2,8,32,1024]{3,2,1,0:T(8,128)} %volume_ref.5) | copy-start | bytes 6291460
  0.0 5.1 %copy-start.2 = (s32[256]{0:T(256)S(1)}, s32[256]{0:T(256)}, u32[]{:S(2)}) copy-start(s32[256]{0:T(256)} %param.5) | copy-start | bytes 3076
  0.0 5.1 %copy-start.1 = (s32[3,256]{1,0:T(4,128)S(1)}, s32[3,256]{1,0:T(4,128)}, u32[]{:S(2)}) copy-start(s32[3,256]{1,0:T(4,128)} %color_ref.1) | copy-start | bytes 9220
  1.2 6.6 %collective-permute-start = (bf16[32,1024]{1,0:T(8,128)(2,1)S(1)}, bf16[32,1024]{1,0:T(8,128)(2,1)S(1)}, u32[]{:S(2)}, u32[]{:S(2)}) collective-permute-start(bf16[32,1024]{1,0:T(8,128)(2,1)S(1)} %get-tuple-element.26), channel_id=1, source_target_pairs={{0,28},{1,5},{2,30},{3,7},{4,8},{5,1},{6,10},{7,3},{8,4},{9,13},{1... | collective-permute-start | bytes 196616 | tf_op jit(solution)/shard_map/ppermute | solution.py:520
  4.6 4.3 %collective-permute-start.1 = (bf16[32,1024]{1,0:T(8,128)(2,1)S(1)}, bf16[32,1024]{1,0:T(8,128)(2,1)S(1)}, u32[]{:S(2)}, u32[]{:S(2)}) collective-permute-start(bf16[32,1024]{1,0:T(8,128)(2,1)S(1)} %get-tuple-element.27), channel_id=1, source_target_pairs={{0,1},{1,0},{2,3},{3,2},{4,5},{5,4},{6,7},{7,6},{8,9},{9,8},{10,11... | collective-permute-start | bytes 196616 | tf_op jit(solution)/shard_map/ppermute | solution.py:520
  4.6 4.3 %collective-permute-start.2 = (bf16[32,1024]{1,0:T(8,128)(2,1)S(1)}, bf16[32,1024]{1,0:T(8,128)(2,1)S(1)}, u32[]{:S(2)}, u32[]{:S(2)}) collective-permute-start(bf16[32,1024]{1,0:T(8,128)(2,1)S(1)} %get-tuple-element.28), channel_id=1, source_target_pairs={{0,4},{1,29},{2,6},{3,31},{4,0},{5,9},{6,2},{7,11},{8,12},{9,5},{1... | collective-permute-start | bytes 196616 | tf_op jit(solution)/shard_map/ppermute | solution.py:520
  4.6 3.1 %collective-permute-start.3 = (bf16[8,1024]{1,0:T(8,128)(2,1)S(1)}, bf16[8,1024]{1,0:T(8,128)(2,1)S(1)}, u32[]{:S(2)}, u32[]{:S(2)}) collective-permute-start(bf16[8,1024]{1,0:T(8,128)(2,1)S(1)} %get-tuple-element.29), channel_id=1, source_target_pairs={{0,4},{1,2},{2,1},{3,7},{4,0},{5,6},{6,5},{7,3},{8,12},{9,10},{10,... | collective-permute-start | bytes 49160 | tf_op jit(solution)/shard_map/ppermute | solution.py:520
  9.3 1.4 %collective-permute-start.4 = (bf16[4,16,1024]{2,1,0:T(8,128)(2,1)S(1)}, bf16[4,16,1024]{2,1,0:T(8,128)(2,1)S(1)}, u32[]{:S(2)}, u32[]{:S(2)}) collective-permute-start(bf16[4,16,1024]{2,1,0:T(8,128)(2,1)S(1)} %get-tuple-element.31), channel_id=1, source_target_pairs={{0,4},{4,0},{8,12},{12,8},{16,20},{20,16},{24,28},{28,24},{1,5},{5... | collective-permute-start | bytes 393224 | tf_op jit(solution)/shard_map/ppermute | solution.py:525
  10.8 3.8 %collective-permute-start.5 = (bf16[2,16,1024]{2,1,0:T(8,128)(2,1)S(1)}, bf16[2,16,1024]{2,1,0:T(8,128)(2,1)S(1)}, u32[]{:S(2)}, u32[]{:S(2)}) collective-permute-start(bf16[2,16,1024]{2,1,0:T(8,128)(2,1)S(1)} %get-tuple-element.32), channel_id=1, source_target_pairs={{0,12},{4,16},{8,28},{12,0},{16,4},{20,24},{24,20},{28,8},{1,13},{... | collective-permute-start | bytes 196616 | tf_op jit(solution)/shard_map/ppermute | solution.py:525
  10.9 4.6 %collective-permute-start.6 = (bf16[16,1024]{1,0:T(8,128)(2,1)S(1)}, bf16[16,1024]{1,0:T(8,128)(2,1)S(1)}, u32[]{:S(2)}, u32[]{:S(2)}) collective-permute-start(bf16[16,1024]{1,0:T(8,128)(2,1)S(1)} %get-tuple-element.33), channel_id=1, source_target_pairs={{0,28},{4,24},{8,20},{12,16},{16,12},{20,8},{24,4},{28,0},{1,29},{... | collective-permute-start | bytes 98312 | tf_op jit(solution)/shard_map/ppermute | solution.py:525
  14.6 1.3 %collective-permute-start.7 = (bf16[16,1024]{1,0:T(8,128)(2,1)S(1)}, bf16[16,1024]{1,0:T(8,128)(2,1)S(1)}, u32[]{:S(2)}, u32[]{:S(2)}) collective-permute-start(bf16[16,1024]{1,0:T(8,128)(2,1)S(1)} %shard_map.41), channel_id=1, source_target_pairs={{0,4},{4,0},{8,12},{12,8},{16,20},{20,16},{24,28},{28,24},{1,5},{5... | collective-permute-start | bytes 98312 | tf_op jit(solution)/shard_map/ppermute | solution.py:525

commit v10 on v9

--- a/solution.py
+++ b/solution.py
@@ -32,14 +32,29 @@
     odd, odd_row = parity("depth"), parity("rows")
     far_first = 1 - odd_row
     last_first = odd ^ far_first ^ 1
+    tiles = height // SUBLANES
+
+    def plane_copies(i, s):
+        for t in range(tiles):
+            rows = pl.ds(t * SUBLANES, SUBLANES)
+            yield pltpu.make_async_copy(volume_ref.at[0, s, rows], plane_ref.at[i, rows], sems.at[i, t])
+
+    def strip_copy(i, row):
+        return pltpu.make_async_copy(volume_ref.at[0, :, row], strip_ref.at[i], sems.at[2, i])
+
     copies = [
-        pltpu.make_async_copy(volume_ref.at[0, last_first * (slices - 1)], plane_ref.at[0], sems.at[0]),
-        pltpu.make_async_copy(volume_ref.at[0, :, (1 - odd_row) * (height - 1)], strip_ref.at[0], sems.at[1]),
-        pltpu.make_async_copy(volume_ref.at[0, (1 - last_first) * (slices - 1)], plane_ref.at[1], sems.at[2]),
-        pltpu.make_async_copy(volume_ref.at[0, :, odd_row * (height - 1)], strip_ref.at[1], sems.at[3]),
+        list(plane_copies(0, last_first * (slices - 1))),
+        [strip_copy(0, (1 - odd_row) * (height - 1))],
+        list(plane_copies(1, (1 - last_first) * (slices - 1))),
+        [strip_copy(1, odd_row * (height - 1))],
     ]
-    for copy in copies:
-        copy.start()
+    for group in copies:
+        for copy in group:
+            copy.start()
+
+    def arrive(group):
+        for copy in group:
+            copy.wait()
 
     def narrow(values):
         return values.astype(jnp.float32).astype(jnp.bfloat16)
@@ -47,13 +62,13 @@
     def padded(strip):
         return narrow(jnp.concatenate([strip, jnp.zeros((height - slices, columns), jnp.int32)], axis=0))
 
-    copies[0].wait()
+    arrive(copies[0])
     first_out[...] = narrow(plane_ref[0])
-    copies[1].wait()
+    arrive(copies[1])
     rows_near_out[...] = padded(strip_ref[0])
-    copies[2].wait()
+    arrive(copies[2])
     second_out[...] = narrow(plane_ref[1])
-    copies[3].wait()
+    arrive(copies[3])
     rows_far_out[...] = narrow(strip_ref[1])
 
 
@@ -69,7 +84,7 @@
         scratch_shapes=[
             pltpu.VMEM((2, slices, columns), jnp.int32),
             pltpu.VMEM((2, height, columns), jnp.int32),
-            pltpu.SemaphoreType.DMA((4,)),
+            pltpu.SemaphoreType.DMA((3, max(2, height // SUBLANES))),
         ],
         compiler_params=pltpu.CompilerParams(vmem_limit_bytes=52 * 1024 * 1024),
     )(volume)
@@ -439,7 +454,7 @@
     )(side)
 
 
-def gather_kernel(side_ref, cross_ref, passed_ref, own_ref, out_ref):
+def gather_kernel(side_ref, cross_ref, passed_ref, own_ref, out_ref, plane_ref, sems):
     share = out_ref.shape[1]
     chip, core, mask = route()
     odd, serves_x = core == 1, mask == 1
@@ -459,8 +474,12 @@
         ]
         step *= 2
     planes = [parts[0][c * share : (c + 1) * share] for c in range(4)]
-    for c in range(4):
-        out_ref[c] = jnp.where(odd, planes[c ^ 1], planes[c])
+    copies = [pltpu.make_async_copy(plane_ref.at[c], out_ref.at[c], sems.at[c]) for c in range(4)]
+    for c, copy in enumerate(copies):
+        plane_ref[c] = jnp.where(odd, planes[c ^ 1], planes[c])
+        copy.start()
+    for copy in copies:
+        copy.wait()
 
 
 def gather(parts, share):
@@ -468,8 +487,9 @@
     return pl.pallas_call(
         gather_kernel,
         in_specs=[WHOLE] * len(parts),
-        out_specs=WHOLE,
+        out_specs=pl.BlockSpec(memory_space=pl.ANY),
         out_shape=jax.ShapeDtypeStruct((4, share, columns), jnp.float32),
+        scratch_shapes=[pltpu.VMEM((4, share, columns), jnp.float32), pltpu.SemaphoreType.DMA((4,))],
         compiler_params=pltpu.CompilerParams(vmem_limit_bytes=4 * 1024 * 1024),
     )(*parts)
 

time: 16.9 us -> 16.9 us (level)
  no operation moved by 1% of the time
where the time goes in v10:
time: 16.9 us; the launch traced here: 16.6 us
  starting transfers between devices  5.93 us (35%)
  waiting for transfers between devices  5.62 us (33%)
  Pallas kernels  5.02 us (30%)
    ppermute x4, waiting for transfers between devices, exchanged(): lax.ppermute(values, 'depth', [(d, d ^ m) for d, m in enumerate(masks)])  4.51 us
    ppermute x4, starting transfers between devices, swapped(): return lax.ppermute(values, ('depth', 'rows'), perm)  3.93 us
    pallas_call x1, Pallas kernels, march_interior(): pl.pallas_call(functools.partial(interior_kernel, opacity_scale), in_spec...  2.62 us
    ppermute x4, starting transfers between devices, exchanged(): lax.ppermute(values, 'depth', [(d, d ^ m) for d, m in enumerate(masks)])  2 us
    pallas_call x1, Pallas kernels, cut_edges(): pl.pallas_call(edges_kernel, in_specs=[pl.BlockSpec(memory_space=pl.ANY)]...  1.17 us
    ppermute x4, waiting for transfers between devices, swapped(): return lax.ppermute(values, ('depth', 'rows'), perm)  1.11 us
    pallas_call x1, Pallas kernels, gather(): pl.pallas_call(gather_kernel, in_specs=[WHOLE] * len(parts), out_specs=pl...  0.73 us
    pallas_call x1, Pallas kernels, add_edges(): pl.pallas_call(functools.partial(edge_kernel, share), in_specs=[WHOLE] *...  0.43 us
  transfers between devices with their start and end apart: 8, of which 5 were waited for; matrix products, arithmetic and copies ran while one was open for 0% of the time, Pallas kernels for 16%

profile of v10, /device:TPU:0, one launch (start us, length us, event | category | flops | bytes accessed | tf_op | source)
XLA Modules:
  0.0 16.6 jit_solution(8219200984537930842)
XLA Ops:
  0.0 0.0 copy-start
  0.0 0.0 copy-start.2
  0.0 0.0 copy-start.1
  0.0 1.2 %shard_map.38 = (bf16[32,1024]{1,0:T(8,128)(2,1)S(1)}, bf16[32,1024]{1,0:T(8,128)(2,1)S(1)}, bf16[32,1024]{1,0:T(8,128)(2,1)S(1)}, bf16[8,1024]{1,0:T(8,128)(2,1)S(1)}) custom-call(s32[2,8,32,1024]{3,2,1,0:T(8,128)} %volume_ref.5), custom_call_target="tpu_custom_call" | custom-call | tf_op jit(solution)/shard_map/pallas_call | solution.py:79
  1.2 3.4 %collective-permute-start = (bf16[32,1024]{1,0:T(8,128)(2,1)S(1)}, bf16[32,1024]{1,0:T(8,128)(2,1)S(1)}, u32[]{:S(2)}, u32[]{:S(2)}) collective-permute-start(bf16[32,1024]{1,0:T(8,128)(2,1)S(1)} %get-tuple-element.26), channel_id=1, source_target_pairs={{0,28},{1,5},{2,30},{3,7},{4,8},{5,1},{6,10},{7,3},{8,4},{9,13},{1... | collective-permute-start | bytes 196616 | tf_op jit(solution)/shard_map/ppermute | solution.py:540
  4.6 0.0 collective-permute-start.1
  4.6 0.0 collective-permute-start.2
  4.6 0.5 %collective-permute-start.3 = (bf16[8,1024]{1,0:T(8,128)(2,1)S(1)}, bf16[8,1024]{1,0:T(8,128)(2,1)S(1)}, u32[]{:S(2)}, u32[]{:S(2)}) collective-permute-start(bf16[8,1024]{1,0:T(8,128)(2,1)S(1)} %get-tuple-element.29), channel_id=1, source_target_pairs={{0,4},{1,2},{2,1},{3,7},{4,0},{5,6},{6,5},{7,3},{8,12},{9,10},{10,... | collective-permute-start | bytes 49160 | tf_op jit(solution)/shard_map/ppermute | solution.py:540
  5.1 0.0 copy-done
  5.1 0.0 copy-done.2
  5.1 0.0 copy-done.1
  5.1 2.6 %shard_map.37 = (f32[4,32,1024]{2,1,0:T(8,128)S(1)}, f32[2,32,1024]{2,1,0:T(8,128)S(1)}, f32[2,32,1024]{2,1,0:T(8,128)S(1)}, f32[2,3,32,1024]{3,2,1,0:T(8,128)S(...) custom-call(s32[2,8,32,1024]{3,2,1,0:T(8,128)S(1)} %copy-done, s32[3,256]{1,0:T(4,128)S(1)} %copy-done.1, ...), custom_call_target="tpu_custom_call" | custom-call | flops 20971520 | bytes 5242880 | tf_op jit(solution)/shard_map/pallas_call | solution.py:275
  7.7 0.0 collective-permute-done.3.rows_far_ref
  7.8 0.0 collective-permute-done.first_ref
  7.8 1.1 %collective-permute-done.1.rows_near_ref = bf16[32,1024]{1,0:T(8,128)(2,1)S(1)} collective-permute-done((bf16[32,1024]{1,0:T(8,128)(2,1)S(1)}, bf16[32,1024]{1,0:T(8,128)(2,1)S(1)}, u32[]{:S(2)}, u32[]{:S(2)}) %collective-permute-start.1) | collective-permute-done | bytes 65568 | tf_op jit(solution)/shard_map/ppermute | solution.py:540
  8.9 0.0 collective-permute-done.2.second_ref
  8.9 0.4 %shard_map.39 = (f32[4,2,16,1024]{3,2,1,0:T(8,128)S(1)}, bf16[4,16,1024]{2,1,0:T(8,128)(2,1)S(1)}) custom-call(s32[2,8,32,1024]{3,2,1,0:T(8,128)S(1)} %copy-done, f32[4,32,1024]{2,1,0:T(8,128)S(1)} %get-tuple-element.20.base_ref, f32[2,32,1024]{2,1,0:T(8,128)S(1)} %get-tuple-element.21.face_ref, f32[2,32,1024]{2,1,0:T(8,128)S(1)} %get-tuple-element.22.square_ref, ...), custom_call_target="tpu_custom_call" | custom-call | tf_op jit(solution)/shard_map/pallas_call | solution.py:389
  9.3 0.1 collective-permute-start.4
  9.4 1.3 %collective-permute-done.4.other_ref = bf16[4,16,1024]{2,1,0:T(8,128)(2,1)S(1)} collective-permute-done((bf16[4,16,1024]{2,1,0:T(8,128)(2,1)S(1)}, bf16[4,16,1024]{2,1,0:T(8,128)(2,1)S(1)}, u32[]{:S(2)}, u32[]{:S(2)}) %collective-permute-start.4) | collective-permute-done | bytes 131104 | tf_op jit(solution)/shard_map/ppermute | solution.py:545
  10.7 0.1 shard_map.40
  10.8 0.1 collective-permute-start.5
  10.9 1.3 %collective-permute-start.6 = (bf16[16,1024]{1,0:T(8,128)(2,1)S(1)}, bf16[16,1024]{1,0:T(8,128)(2,1)S(1)}, u32[]{:S(2)}, u32[]{:S(2)}) collective-permute-start(bf16[16,1024]{1,0:T(8,128)(2,1)S(1)} %get-tuple-element.33), channel_id=1, source_target_pairs={{0,28},{4,24},{8,20},{12,16},{16,12},{20,8},{24,4},{28,0},{1,29},{... | collective-permute-start | bytes 98312 | tf_op jit(solution)/shard_map/ppermute | solution.py:545
  12.2 2.3 %collective-permute-done.5.side_ref = bf16[2,16,1024]{2,1,0:T(8,128)(2,1)S(1)} collective-permute-done((bf16[2,16,1024]{2,1,0:T(8,128)(2,1)S(1)}, bf16[2,16,1024]{2,1,0:T(8,128)(2,1)S(1)}, u32[]{:S(2)}, u32[]{:S(2)}) %collective-permute-start.5) | collective-permute-done | bytes 65568 | tf_op jit(solution)/shard_map/ppermute | solution.py:545
  14.6 0.5 %collective-permute-start.7 = (bf16[16,1024]{1,0:T(8,128)(2,1)S(1)}, bf16[16,1024]{1,0:T(8,128)(2,1)S(1)}, u32[]{:S(2)}, u32[]{:S(2)}) collective-permute-start(bf16[16,1024]{1,0:T(8,128)(2,1)S(1)} %shard_map.41), channel_id=1, source_target_pairs={{0,4},{4,0},{8,12},{12,8},{16,20},{20,16},{24,28},{28,24},{1,5},{5... | collective-permute-start | bytes 98312 | tf_op jit(solution)/shard_map/ppermute | solution.py:545
  15.0 0.5 %collective-permute-done.6.cross_ref = bf16[16,1024]{1,0:T(8,128)(2,1)S(1)} collective-permute-done((bf16[16,1024]{1,0:T(8,128)(2,1)S(1)}, bf16[16,1024]{1,0:T(8,128)(2,1)S(1)}, u32[]{:S(2)}, u32[]{:S(2)}) %collective-permute-start.6) | collective-permute-done | bytes 32800 | tf_op jit(solution)/shard_map/ppermute | solution.py:545
  15.5 0.4 %collective-permute-done.7.passed_ref = bf16[16,1024]{1,0:T(8,128)(2,1)S(1)} collective-permute-done((bf16[16,1024]{1,0:T(8,128)(2,1)S(1)}, bf16[16,1024]{1,0:T(8,128)(2,1)S(1)}, u32[]{:S(2)}, u32[]{:S(2)}) %collective-permute-start.7) | collective-permute-done | bytes 32800 | tf_op jit(solution)/shard_map/ppermute | solution.py:545
  15.9 0.7 %shard_map.42 = f32[4,4,1024]{2,1,0:T(4,128)} custom-call(bf16[2,16,1024]{2,1,0:T(8,128)(2,1)S(1)} %collective-permute-done.5.side_ref, bf16[16,1024]{1,0:T(8,128)(2,1)S(1)} %collective-permute-done.6.cross_ref, bf16[16,1024]{1,0:T(8,128)(2,1)S(1)} %collective-permute-done.7.passed_ref, f32[16,1024]{1,0:T(8,128)S(1)} %get-tuple-element.34.own_ref), custom_call_target="tpu_custom_call" | custom-call | tf_op jit(solution)/shard_map/pallas_call | solution.py:487
  (1 shorter events, 0.0 us)
Async XLA Ops:
  0.0 5.1 %copy-start = (s32[2,8,32,1024]{3,2,1,0:T(8,128)S(1)}, s32[2,8,32,1024]{3,2,1,0:T(8,128)}, u32[]{:S(2)}) copy-start(s32[2,8,32,1024]{3,2,1,0:T(8,128)} %volume_ref.5) | copy-start | bytes 6291460
  0.0 5.1 %copy-start.2 = (s32[256]{0:T(256)S(1)}, s32[256]{0:T(256)}, u32[]{:S(2)}) copy-start(s32[256]{0:T(256)} %param.5) | copy-start | bytes 3076
  0.0 5.1 %copy-start.1 = (s32[3,256]{1,0:T(4,128)S(1)}, s32[3,256]{1,0:T(4,128)}, u32[]{:S(2)}) copy-start(s32[3,256]{1,0:T(4,128)} %color_ref.1) | copy-start | bytes 9220
  1.2 6.6 %collective-permute-start = (bf16[32,1024]{1,0:T(8,128)(2,1)S(1)}, bf16[32,1024]{1,0:T(8,128)(2,1)S(1)}, u32[]{:S(2)}, u32[]{:S(2)}) collective-permute-start(bf16[32,1024]{1,0:T(8,128)(2,1)S(1)} %get-tuple-element.26), channel_id=1, source_target_pairs={{0,28},{1,5},{2,30},{3,7},{4,8},{5,1},{6,10},{7,3},{8,4},{9,13},{1... | collective-permute-start | bytes 196616 | tf_op jit(solution)/shard_map/ppermute | solution.py:540
  4.6 4.3 %collective-permute-start.1 = (bf16[32,1024]{1,0:T(8,128)(2,1)S(1)}, bf16[32,1024]{1,0:T(8,128)(2,1)S(1)}, u32[]{:S(2)}, u32[]{:S(2)}) collective-permute-start(bf16[32,1024]{1,0:T(8,128)(2,1)S(1)} %get-tuple-element.27), channel_id=1, source_target_pairs={{0,1},{1,0},{2,3},{3,2},{4,5},{5,4},{6,7},{7,6},{8,9},{9,8},{10,11... | collective-permute-start | bytes 196616 | tf_op jit(solution)/shard_map/ppermute | solution.py:540
  4.6 4.3 %collective-permute-start.2 = (bf16[32,1024]{1,0:T(8,128)(2,1)S(1)}, bf16[32,1024]{1,0:T(8,128)(2,1)S(1)}, u32[]{:S(2)}, u32[]{:S(2)}) collective-permute-start(bf16[32,1024]{1,0:T(8,128)(2,1)S(1)} %get-tuple-element.28), channel_id=1, source_target_pairs={{0,4},{1,29},{2,6},{3,31},{4,0},{5,9},{6,2},{7,11},{8,12},{9,5},{1... | collective-permute-start | bytes 196616 | tf_op jit(solution)/shard_map/ppermute | solution.py:540
  4.6 3.1 %collective-permute-start.3 = (bf16[8,1024]{1,0:T(8,128)(2,1)S(1)}, bf16[8,1024]{1,0:T(8,128)(2,1)S(1)}, u32[]{:S(2)}, u32[]{:S(2)}) collective-permute-start(bf16[8,1024]{1,0:T(8,128)(2,1)S(1)} %get-tuple-element.29), channel_id=1, source_target_pairs={{0,4},{1,2},{2,1},{3,7},{4,0},{5,6},{6,5},{7,3},{8,12},{9,10},{10,... | collective-permute-start | bytes 49160 | tf_op jit(solution)/shard_map/ppermute | solution.py:540
  9.3 1.4 %collective-permute-start.4 = (bf16[4,16,1024]{2,1,0:T(8,128)(2,1)S(1)}, bf16[4,16,1024]{2,1,0:T(8,128)(2,1)S(1)}, u32[]{:S(2)}, u32[]{:S(2)}) collective-permute-start(bf16[4,16,1024]{2,1,0:T(8,128)(2,1)S(1)} %get-tuple-element.31), channel_id=1, source_target_pairs={{0,4},{4,0},{8,12},{12,8},{16,20},{20,16},{24,28},{28,24},{1,5},{5... | collective-permute-start | bytes 393224 | tf_op jit(solution)/shard_map/ppermute | solution.py:545
  10.8 3.8 %collective-permute-start.5 = (bf16[2,16,1024]{2,1,0:T(8,128)(2,1)S(1)}, bf16[2,16,1024]{2,1,0:T(8,128)(2,1)S(1)}, u32[]{:S(2)}, u32[]{:S(2)}) collective-permute-start(bf16[2,16,1024]{2,1,0:T(8,128)(2,1)S(1)} %get-tuple-element.32), channel_id=1, source_target_pairs={{0,12},{4,16},{8,28},{12,0},{16,4},{20,24},{24,20},{28,8},{1,13},{... | collective-permute-start | bytes 196616 | tf_op jit(solution)/shard_map/ppermute | solution.py:545
  10.9 4.6 %collective-permute-start.6 = (bf16[16,1024]{1,0:T(8,128)(2,1)S(1)}, bf16[16,1024]{1,0:T(8,128)(2,1)S(1)}, u32[]{:S(2)}, u32[]{:S(2)}) collective-permute-start(bf16[16,1024]{1,0:T(8,128)(2,1)S(1)} %get-tuple-element.33), channel_id=1, source_target_pairs={{0,28},{4,24},{8,20},{12,16},{16,12},{20,8},{24,4},{28,0},{1,29},{... | collective-permute-start | bytes 98312 | tf_op jit(solution)/shard_map/ppermute | solution.py:545
  14.6 1.3 %collective-permute-start.7 = (bf16[16,1024]{1,0:T(8,128)(2,1)S(1)}, bf16[16,1024]{1,0:T(8,128)(2,1)S(1)}, u32[]{:S(2)}, u32[]{:S(2)}) collective-permute-start(bf16[16,1024]{1,0:T(8,128)(2,1)S(1)} %shard_map.41), channel_id=1, source_target_pairs={{0,4},{4,0},{8,12},{12,8},{16,20},{20,16},{24,28},{28,24},{1,5},{5... | collective-permute-start | bytes 98312 | tf_op jit(solution)/shard_map/ppermute | solution.py:545

commit v11 on v10

--- a/solution.py
+++ b/solution.py
@@ -297,8 +297,50 @@
     return both, pltpu.roll(both, 3, 0)
 
 
+def plane_terms(volume_ref, face_ref, square_ref, lit_ref, halo, end, rows, here):
+    slices = volume_ref.shape[1]
+    inner = volume_ref[0, jnp.where(end == 1, slices - 2, 1), rows, here].astype(jnp.float32)
+    grad_depth = jnp.where(end == 1, halo - inner, inner - halo)
+    shading = shade(grad_depth, face_ref[end, rows, here], square_ref[end, rows, here])
+    return [lit_ref[end, c, rows, here] * shading for c in range(3)]
+
+
+def first_end():
+    front_end, back_end = ends("depth")
+    end = jnp.where(parity("depth") == parity("rows"), 0, 1)
+    return end, jnp.where(end == 1, back_end, front_end), jnp.where(end == 1, front_end, back_end)
+
+
+def first_plane_kernel(volume_ref, base_ref, face_ref, square_ref, lit_ref, first_ref, sums_ref):
+    _, height, columns = base_ref.shape
+    end, outside, _ = first_end()
+
+    def chunk(j, carry):
+        here = pl.ds(pl.multiple_of(j * LANES, LANES), LANES)
+        first = jnp.where(outside, 0.0, first_ref[:, here].astype(jnp.float32))
+        for r in range(height // SUBLANES):
+            rows = slice(r * SUBLANES, (r + 1) * SUBLANES)
+            terms = plane_terms(volume_ref, face_ref, square_ref, lit_ref, first[rows], end, rows, here)
+            for c in range(3):
+                sums_ref[c, rows, here] = base_ref[c, rows, here] + terms[c]
+        return carry
+
+    lax.fori_loop(0, columns // LANES, chunk, 0, unroll=4)
+
+
+def add_first_plane(volume, base, face, square, lit, first):
+    return pl.pallas_call(
+        first_plane_kernel,
+        in_specs=[WHOLE] * 6,
+        out_specs=WHOLE,
+        out_shape=jax.ShapeDtypeStruct((3, *base.shape[1:]), jnp.float32),
+        compiler_params=pltpu.CompilerParams(vmem_limit_bytes=8 * 1024 * 1024),
+        cost_estimate=pl.CostEstimate(flops=base.size * 20, bytes_accessed=base.size * 12, transcendentals=base.size // 4),
+    )(volume, base, face, square, lit, first)
+
+
 def edge_kernel(
-    share, volume_ref, base_ref, face_ref, square_ref, lit_ref, grad_ref, strip_ref, first_ref, rows_near_ref, second_ref, rows_far_ref, *out_refs
+    share, volume_ref, sums_ref, base_ref, face_ref, square_ref, lit_ref, grad_ref, strip_ref, first_ref, rows_near_ref, second_ref, rows_far_ref, *out_refs
 ):
     _, slices, height, columns = volume_ref.shape
     tiles = height // SUBLANES
@@ -311,6 +353,7 @@
     front_came_first = odd == odd_row
     front_end, back_end = ends("depth")
     top_end, bottom_end = ends("rows")
+    end, _, outside = first_end()
 
     def chunk(j, carry):
         here = pl.ds(pl.multiple_of(j * LANES, LANES), LANES)
@@ -322,6 +365,7 @@
         second = second_ref[:, here].astype(jnp.float32)
         before = jnp.where(front_end, 0.0, jnp.where(front_came_first, first, second))
         after = jnp.where(back_end, 0.0, jnp.where(front_came_first, second, first))
+        last = jnp.where(outside, 0.0, second)
         extra = []
         for q, edge in enumerate((0, height - 1)):
             inner = grad_ref[q, 1, :, here]
@@ -339,15 +383,8 @@
         extra = [row_sums(extra[0][c], extra[1][c]) for c in range(3)]
         for r in range(tiles):
             rows = slice(r * SUBLANES, (r + 1) * SUBLANES)
-            planes = [base_ref[c, rows, here] for c in range(4)]
-            for end in range(2):
-                if end:
-                    grad_depth = after[rows] - volume_ref[0, slices - 2, rows, here].astype(jnp.float32)
-                else:
-                    grad_depth = volume_ref[0, 1, rows, here].astype(jnp.float32) - before[rows]
-                shading = shade(grad_depth, face_ref[end, rows, here], square_ref[end, rows, here])
-                for c in range(3):
-                    planes[c] = planes[c] + lit_ref[end, c, rows, here] * shading
+            terms = plane_terms(volume_ref, face_ref, square_ref, lit_ref, last[rows], 1 - end, rows, here)
+            planes = [sums_ref[c, rows, here] + terms[c] for c in range(3)] + [base_ref[3, rows, here]]
             for c in range(3):
                 if r == 0:
                     planes[c] = planes[c] + jnp.where(first_row, extra[c][0], 0.0)
@@ -375,7 +412,7 @@
             give_ref[i] = block.astype(jnp.bfloat16)
 
 
-def add_edges(volume, interior, halos, depth_count, paired):
+def add_edges(volume, sums, interior, halos, depth_count, paired):
     _, slices, height, columns = volume.shape
     share = height // depth_count
     if paired:
@@ -388,11 +425,11 @@
         shapes = [jax.ShapeDtypeStruct((depth_count, 4 * share, columns), jnp.bfloat16)]
     return pl.pallas_call(
         functools.partial(edge_kernel, share),
-        in_specs=[WHOLE] * 11,
+        in_specs=[WHOLE] * 12,
         out_specs=[WHOLE] * len(shapes),
         out_shape=shapes,
         compiler_params=pltpu.CompilerParams(vmem_limit_bytes=24 * 1024 * 1024),
-    )(volume, *interior, *halos)
+    )(volume, sums, *interior, *halos)
 
 
 def served(depth):
@@ -556,7 +593,8 @@
     interior = march_interior(volume, color_map, alpha_map, depth_count)
     halos = (first, rows_near, second, rows_far)
     paired = depth_count == 8 and 2 * share == SUBLANES
-    outs = add_edges(volume, interior, halos, depth_count, paired)
+    sums = add_first_plane(volume, *interior[:4], first)
+    outs = add_edges(volume, sums, interior, halos, depth_count, paired)
     if not paired:
         return finish(lax.all_to_all(outs[0], "depth", 0, 0, tiled=True), share)
     blocks, give = outs

time: 16.9 us -> 16.8 us (level)
  the two profiles are of different devices: /device:TPU:0 before, /device:TPU:25 now
where the time goes in v11:
time: 16.8 us; the launch traced here: 16.7 us
  starting transfers between devices  7.01 us (42%)
  Pallas kernels  5.18 us (31%)
  waiting for transfers between devices  4.43 us (26%)
    ppermute x4, waiting for transfers between devices, exchanged(): lax.ppermute(values, 'depth', [(d, d ^ m) for d, m in enumerate(masks)])  4.42 us
    ppermute x4, starting transfers between devices, swapped(): return lax.ppermute(values, ('depth', 'rows'), perm)  3.55 us
    ppermute x4, starting transfers between devices, exchanged(): lax.ppermute(values, 'depth', [(d, d ^ m) for d, m in enumerate(masks)])  3.45 us
    pallas_call x1, Pallas kernels, march_interior(): pl.pallas_call(functools.partial(interior_kernel, opacity_scale), in_spec...  2.62 us
    pallas_call x1, Pallas kernels, cut_edges(): pl.pallas_call(edges_kernel, in_specs=[pl.BlockSpec(memory_space=pl.ANY)]...  1.18 us
    pallas_call x1, Pallas kernels, gather(): pl.pallas_call(gather_kernel, in_specs=[WHOLE] * len(parts), out_specs=pl...  0.73 us
    pallas_call x1, Pallas kernels, add_edges(): pl.pallas_call(functools.partial(edge_kernel, share), in_specs=[WHOLE] *...  0.35 us
  transfers between devices with their start and end apart: 8, of which 4 were waited for; matrix products, arithmetic and copies ran while one was open for 0% of the time, Pallas kernels for 17%

profile of v11, /device:TPU:25, one launch (start us, length us, event | category | flops | bytes accessed | tf_op | source)
XLA Modules:
  0.0 16.7 jit_solution(17101371520463051596)
XLA Ops:
  0.0 0.0 copy-start
  0.0 0.0 copy-start.2
  0.0 0.0 copy-start.1
  0.0 1.2 %shard_map.38 = (bf16[32,1024]{1,0:T(8,128)(2,1)S(1)}, bf16[32,1024]{1,0:T(8,128)(2,1)S(1)}, bf16[32,1024]{1,0:T(8,128)(2,1)S(1)}, bf16[8,1024]{1,0:T(8,128)(2,1)S(1)}) custom-call(s32[2,8,32,1024]{3,2,1,0:T(8,128)} %volume_ref.7), custom_call_target="tpu_custom_call" | custom-call | tf_op jit(solution)/shard_map/pallas_call | solution.py:79
  1.2 0.7 %collective-permute-start = (bf16[32,1024]{1,0:T(8,128)(2,1)S(1)}, bf16[32,1024]{1,0:T(8,128)(2,1)S(1)}, u32[]{:S(2)}, u32[]{:S(2)}) collective-permute-start(bf16[32,1024]{1,0:T(8,128)(2,1)S(1)} %get-tuple-element.24), channel_id=1, source_target_pairs={{0,28},{1,5},{2,30},{3,7},{4,8},{5,1},{6,10},{7,3},{8,4},{9,13},{1... | collective-permute-start | bytes 196616 | tf_op jit(solution)/shard_map/ppermute | solution.py:577
  1.9 1.3 %collective-permute-start.1 = (bf16[32,1024]{1,0:T(8,128)(2,1)S(1)}, bf16[32,1024]{1,0:T(8,128)(2,1)S(1)}, u32[]{:S(2)}, u32[]{:S(2)}) collective-permute-start(bf16[32,1024]{1,0:T(8,128)(2,1)S(1)} %get-tuple-element.27), channel_id=1, source_target_pairs={{0,1},{1,0},{2,3},{3,2},{4,5},{5,4},{6,7},{7,6},{8,9},{9,8},{10,11... | collective-permute-start | bytes 196616 | tf_op jit(solution)/shard_map/ppermute | solution.py:577
  3.2 0.4 %collective-permute-start.2 = (bf16[32,1024]{1,0:T(8,128)(2,1)S(1)}, bf16[32,1024]{1,0:T(8,128)(2,1)S(1)}, u32[]{:S(2)}, u32[]{:S(2)}) collective-permute-start(bf16[32,1024]{1,0:T(8,128)(2,1)S(1)} %get-tuple-element.28), channel_id=1, source_target_pairs={{0,4},{1,29},{2,6},{3,31},{4,0},{5,9},{6,2},{7,11},{8,12},{9,5},{1... | collective-permute-start | bytes 196616 | tf_op jit(solution)/shard_map/ppermute | solution.py:577
  3.6 1.2 %collective-permute-start.3 = (bf16[8,1024]{1,0:T(8,128)(2,1)S(1)}, bf16[8,1024]{1,0:T(8,128)(2,1)S(1)}, u32[]{:S(2)}, u32[]{:S(2)}) collective-permute-start(bf16[8,1024]{1,0:T(8,128)(2,1)S(1)} %get-tuple-element.29), channel_id=1, source_target_pairs={{0,4},{1,2},{2,1},{3,7},{4,0},{5,6},{6,5},{7,3},{8,12},{9,10},{10,... | collective-permute-start | bytes 49160 | tf_op jit(solution)/shard_map/ppermute | solution.py:577
  4.8 0.0 copy-done
  4.8 0.0 copy-done.2
  4.8 0.0 copy-done.1
  4.8 2.6 %shard_map.37 = (f32[4,32,1024]{2,1,0:T(8,128)S(1)}, f32[2,32,1024]{2,1,0:T(8,128)S(1)}, f32[2,32,1024]{2,1,0:T(8,128)S(1)}, f32[2,3,32,1024]{3,2,1,0:T(8,128)S(...) custom-call(s32[2,8,32,1024]{3,2,1,0:T(8,128)S(1)} %copy-done, s32[3,256]{1,0:T(4,128)S(1)} %copy-done.1, ...), custom_call_target="tpu_custom_call" | custom-call | flops 20971520 | bytes 5242880 | tf_op jit(solution)/shard_map/pallas_call | solution.py:275
  7.4 0.0 collective-permute-done.first_ref
  7.4 0.2 %shard_map.39.sums_ref = f32[3,32,1024]{2,1,0:T(8,128)S(1)} custom-call(s32[2,8,32,1024]{3,2,1,0:T(8,128)S(1)} %copy-done, f32[4,32,1024]{2,1,0:T(8,128)S(1)} %get-tuple-element.20.base_ref, f32[2,32,1024]{2,1,0:T(8,128)S(1)} %get-tuple-element.21.face_ref, f32[2,32,1024]{2,1,0:T(8,128)S(1)} %get-tuple-element.22.square_ref, ...), custom_call_target="tpu_custom_call" | custom-call | flops 2621440 | bytes 1572864 | tf_op jit(solution)/shard_map/pallas_call | solution.py:332
  7.6 0.0 collective-permute-done.3.rows_far_ref
  7.6 0.0 collective-permute-done.1.rows_near_ref
  7.6 0.0 collective-permute-done.2.second_ref
  7.7 0.4 %shard_map.40 = (f32[4,2,16,1024]{3,2,1,0:T(8,128)S(1)}, bf16[4,16,1024]{2,1,0:T(8,128)(2,1)S(1)}) custom-call(s32[2,8,32,1024]{3,2,1,0:T(8,128)S(1)} %copy-done, f32[3,32,1024]{2,1,0:T(8,128)S(1)} %shard_map.39.sums_ref, f32[4,32,1024]{2,1,0:T(8,128)S(1)} %get-tuple-element.20.base_ref, f32[2,32,1024]{2,1,0:T(8,128)S(1)} %get-tuple-element.21.face_ref, ...), custom_call_target="tpu_custom_call" | custom-call | tf_op jit(solution)/shard_map/pallas_call | solution.py:426
  8.0 1.6 %collective-permute-start.4 = (bf16[4,16,1024]{2,1,0:T(8,128)(2,1)S(1)}, bf16[4,16,1024]{2,1,0:T(8,128)(2,1)S(1)}, u32[]{:S(2)}, u32[]{:S(2)}) collective-permute-start(bf16[4,16,1024]{2,1,0:T(8,128)(2,1)S(1)} %get-tuple-element.31), channel_id=1, source_target_pairs={{0,4},{4,0},{8,12},{12,8},{16,20},{20,16},{24,28},{28,24},{1,5},{5... | collective-permute-start | bytes 393224 | tf_op jit(solution)/shard_map/ppermute | solution.py:582
  9.6 1.0 %collective-permute-done.4.other_ref = bf16[4,16,1024]{2,1,0:T(8,128)(2,1)S(1)} collective-permute-done((bf16[4,16,1024]{2,1,0:T(8,128)(2,1)S(1)}, bf16[4,16,1024]{2,1,0:T(8,128)(2,1)S(1)}, u32[]{:S(2)}, u32[]{:S(2)}) %collective-permute-start.4) | collective-permute-done | bytes 131104 | tf_op jit(solution)/shard_map/ppermute | solution.py:582
  10.6 0.1 shard_map.41
  10.7 0.5 %collective-permute-start.5 = (bf16[2,16,1024]{2,1,0:T(8,128)(2,1)S(1)}, bf16[2,16,1024]{2,1,0:T(8,128)(2,1)S(1)}, u32[]{:S(2)}, u32[]{:S(2)}) collective-permute-start(bf16[2,16,1024]{2,1,0:T(8,128)(2,1)S(1)} %get-tuple-element.32), channel_id=1, source_target_pairs={{0,12},{4,16},{8,28},{12,0},{16,4},{20,24},{24,20},{28,8},{1,13},{... | collective-permute-start | bytes 196616 | tf_op jit(solution)/shard_map/ppermute | solution.py:582
  11.3 1.2 %collective-permute-start.6 = (bf16[16,1024]{1,0:T(8,128)(2,1)S(1)}, bf16[16,1024]{1,0:T(8,128)(2,1)S(1)}, u32[]{:S(2)}, u32[]{:S(2)}) collective-permute-start(bf16[16,1024]{1,0:T(8,128)(2,1)S(1)} %get-tuple-element.33), channel_id=1, source_target_pairs={{0,28},{4,24},{8,20},{12,16},{16,12},{20,8},{24,4},{28,0},{1,29},{... | collective-permute-start | bytes 98312 | tf_op jit(solution)/shard_map/ppermute | solution.py:582
  12.5 2.3 %collective-permute-done.5.side_ref = bf16[2,16,1024]{2,1,0:T(8,128)(2,1)S(1)} collective-permute-done((bf16[2,16,1024]{2,1,0:T(8,128)(2,1)S(1)}, bf16[2,16,1024]{2,1,0:T(8,128)(2,1)S(1)}, u32[]{:S(2)}, u32[]{:S(2)}) %collective-permute-start.5) | collective-permute-done | bytes 65568 | tf_op jit(solution)/shard_map/ppermute | solution.py:582
  14.8 0.1 collective-permute-start.7
  14.8 0.7 %collective-permute-done.6.cross_ref = bf16[16,1024]{1,0:T(8,128)(2,1)S(1)} collective-permute-done((bf16[16,1024]{1,0:T(8,128)(2,1)S(1)}, bf16[16,1024]{1,0:T(8,128)(2,1)S(1)}, u32[]{:S(2)}, u32[]{:S(2)}) %collective-permute-start.6) | collective-permute-done | bytes 32800 | tf_op jit(solution)/shard_map/ppermute | solution.py:582
  15.5 0.5 %collective-permute-done.7.passed_ref = bf16[16,1024]{1,0:T(8,128)(2,1)S(1)} collective-permute-done((bf16[16,1024]{1,0:T(8,128)(2,1)S(1)}, bf16[16,1024]{1,0:T(8,128)(2,1)S(1)}, u32[]{:S(2)}, u32[]{:S(2)}) %collective-permute-start.7) | collective-permute-done | bytes 32800 | tf_op jit(solution)/shard_map/ppermute | solution.py:582
  16.0 0.7 %shard_map.43 = f32[4,4,1024]{2,1,0:T(4,128)} custom-call(bf16[2,16,1024]{2,1,0:T(8,128)(2,1)S(1)} %collective-permute-done.5.side_ref, bf16[16,1024]{1,0:T(8,128)(2,1)S(1)} %collective-permute-done.6.cross_ref, bf16[16,1024]{1,0:T(8,128)(2,1)S(1)} %collective-permute-done.7.passed_ref, f32[16,1024]{1,0:T(8,128)S(1)} %get-tuple-element.34.own_ref), custom_call_target="tpu_custom_call" | custom-call | tf_op jit(solution)/shard_map/pallas_call | solution.py:524
  (1 shorter events, 0.0 us)
Async XLA Ops:
  0.0 4.8 %copy-start = (s32[2,8,32,1024]{3,2,1,0:T(8,128)S(1)}, s32[2,8,32,1024]{3,2,1,0:T(8,128)}, u32[]{:S(2)}) copy-start(s32[2,8,32,1024]{3,2,1,0:T(8,128)} %volume_ref.7) | copy-start | bytes 6291460
  0.0 4.8 %copy-start.2 = (s32[256]{0:T(256)S(1)}, s32[256]{0:T(256)}, u32[]{:S(2)}) copy-start(s32[256]{0:T(256)} %param.5) | copy-start | bytes 3076
  0.0 4.8 %copy-start.1 = (s32[3,256]{1,0:T(4,128)S(1)}, s32[3,256]{1,0:T(4,128)}, u32[]{:S(2)}) copy-start(s32[3,256]{1,0:T(4,128)} %color_ref.1) | copy-start | bytes 9220
  1.2 6.2 %collective-permute-start = (bf16[32,1024]{1,0:T(8,128)(2,1)S(1)}, bf16[32,1024]{1,0:T(8,128)(2,1)S(1)}, u32[]{:S(2)}, u32[]{:S(2)}) collective-permute-start(bf16[32,1024]{1,0:T(8,128)(2,1)S(1)} %get-tuple-element.24), channel_id=1, source_target_pairs={{0,28},{1,5},{2,30},{3,7},{4,8},{5,1},{6,10},{7,3},{8,4},{9,13},{1... | collective-permute-start | bytes 196616 | tf_op jit(solution)/shard_map/ppermute | solution.py:577
  1.9 5.7 %collective-permute-start.1 = (bf16[32,1024]{1,0:T(8,128)(2,1)S(1)}, bf16[32,1024]{1,0:T(8,128)(2,1)S(1)}, u32[]{:S(2)}, u32[]{:S(2)}) collective-permute-start(bf16[32,1024]{1,0:T(8,128)(2,1)S(1)} %get-tuple-element.27), channel_id=1, source_target_pairs={{0,1},{1,0},{2,3},{3,2},{4,5},{5,4},{6,7},{7,6},{8,9},{9,8},{10,11... | collective-permute-start | bytes 196616 | tf_op jit(solution)/shard_map/ppermute | solution.py:577
  3.2 4.4 %collective-permute-start.2 = (bf16[32,1024]{1,0:T(8,128)(2,1)S(1)}, bf16[32,1024]{1,0:T(8,128)(2,1)S(1)}, u32[]{:S(2)}, u32[]{:S(2)}) collective-permute-start(bf16[32,1024]{1,0:T(8,128)(2,1)S(1)} %get-tuple-element.28), channel_id=1, source_target_pairs={{0,4},{1,29},{2,6},{3,31},{4,0},{5,9},{6,2},{7,11},{8,12},{9,5},{1... | collective-permute-start | bytes 196616 | tf_op jit(solution)/shard_map/ppermute | solution.py:577
  3.6 4.1 %collective-permute-start.3 = (bf16[8,1024]{1,0:T(8,128)(2,1)S(1)}, bf16[8,1024]{1,0:T(8,128)(2,1)S(1)}, u32[]{:S(2)}, u32[]{:S(2)}) collective-permute-start(bf16[8,1024]{1,0:T(8,128)(2,1)S(1)} %get-tuple-element.29), channel_id=1, source_target_pairs={{0,4},{1,2},{2,1},{3,7},{4,0},{5,6},{6,5},{7,3},{8,12},{9,10},{10,... | collective-permute-start | bytes 49160 | tf_op jit(solution)/shard_map/ppermute | solution.py:577
  8.0 2.6 %collective-permute-start.4 = (bf16[4,16,1024]{2,1,0:T(8,128)(2,1)S(1)}, bf16[4,16,1024]{2,1,0:T(8,128)(2,1)S(1)}, u32[]{:S(2)}, u32[]{:S(2)}) collective-permute-start(bf16[4,16,1024]{2,1,0:T(8,128)(2,1)S(1)} %get-tuple-element.31), channel_id=1, source_target_pairs={{0,4},{4,0},{8,12},{12,8},{16,20},{20,16},{24,28},{28,24},{1,5},{5... | collective-permute-start | bytes 393224 | tf_op jit(solution)/shard_map/ppermute | solution.py:582
  10.7 4.1 %collective-permute-start.5 = (bf16[2,16,1024]{2,1,0:T(8,128)(2,1)S(1)}, bf16[2,16,1024]{2,1,0:T(8,128)(2,1)S(1)}, u32[]{:S(2)}, u32[]{:S(2)}) collective-permute-start(bf16[2,16,1024]{2,1,0:T(8,128)(2,1)S(1)} %get-tuple-element.32), channel_id=1, source_target_pairs={{0,12},{4,16},{8,28},{12,0},{16,4},{20,24},{24,20},{28,8},{1,13},{... | collective-permute-start | bytes 196616 | tf_op jit(solution)/shard_map/ppermute | solution.py:582
  11.3 4.2 %collective-permute-start.6 = (bf16[16,1024]{1,0:T(8,128)(2,1)S(1)}, bf16[16,1024]{1,0:T(8,128)(2,1)S(1)}, u32[]{:S(2)}, u32[]{:S(2)}) collective-permute-start(bf16[16,1024]{1,0:T(8,128)(2,1)S(1)} %get-tuple-element.33), channel_id=1, source_target_pairs={{0,28},{4,24},{8,20},{12,16},{16,12},{20,8},{24,4},{28,0},{1,29},{... | collective-permute-start | bytes 98312 | tf_op jit(solution)/shard_map/ppermute | solution.py:582
  14.8 1.2 %collective-permute-start.7 = (bf16[16,1024]{1,0:T(8,128)(2,1)S(1)}, bf16[16,1024]{1,0:T(8,128)(2,1)S(1)}, u32[]{:S(2)}, u32[]{:S(2)}) collective-permute-start(bf16[16,1024]{1,0:T(8,128)(2,1)S(1)} %shard_map.42), channel_id=1, source_target_pairs={{0,4},{4,0},{8,12},{12,8},{16,20},{20,16},{24,28},{28,24},{1,5},{5... | collective-permute-start | bytes 98312 | tf_op jit(solution)/shard_map/ppermute | solution.py:582

commit v12 on v11

--- a/solution.py
+++ b/solution.py
@@ -257,7 +257,7 @@
                 strip_ref[q, c, :, here] = emitted[c] * weight
         return carry
 
-    lax.fori_loop(0, chunks, chunk, 0, unroll=2)
+    lax.fori_loop(0, chunks, chunk, 0, unroll=4)
 
 
 def march_interior(volume, color_map, alpha_map, depth_count):
@@ -403,7 +403,7 @@
                 blocks_ref[r, 1, :, here] = uneven
         return carry
 
-    lax.fori_loop(0, columns // LANES, chunk, 0, unroll=4)
+    lax.fori_loop(0, columns // LANES, chunk, 0, unroll=8)
     if len(out_refs) > 1:
         blocks_ref, give_ref = out_refs
         chip, core, mask = route()
@@ -491,7 +491,7 @@
     )(side)
 
 
-def gather_kernel(side_ref, cross_ref, passed_ref, own_ref, out_ref, plane_ref, sems):
+def gather_kernel(side_ref, cross_ref, passed_ref, own_ref, out_ref):
     share = out_ref.shape[1]
     chip, core, mask = route()
     odd, serves_x = core == 1, mask == 1
@@ -511,12 +511,8 @@
         ]
         step *= 2
     planes = [parts[0][c * share : (c + 1) * share] for c in range(4)]
-    copies = [pltpu.make_async_copy(plane_ref.at[c], out_ref.at[c], sems.at[c]) for c in range(4)]
-    for c, copy in enumerate(copies):
-        plane_ref[c] = jnp.where(odd, planes[c ^ 1], planes[c])
-        copy.start()
-    for copy in copies:
-        copy.wait()
+    for c in range(4):
+        out_ref[c] = jnp.where(odd, planes[c ^ 1], planes[c])
 
 
 def gather(parts, share):
@@ -524,9 +520,8 @@
     return pl.pallas_call(
         gather_kernel,
         in_specs=[WHOLE] * len(parts),
-        out_specs=pl.BlockSpec(memory_space=pl.ANY),
+        out_specs=WHOLE,
         out_shape=jax.ShapeDtypeStruct((4, share, columns), jnp.float32),
-        scratch_shapes=[pltpu.VMEM((4, share, columns), jnp.float32), pltpu.SemaphoreType.DMA((4,))],
         compiler_params=pltpu.CompilerParams(vmem_limit_bytes=4 * 1024 * 1024),
     )(*parts)
 

time: 16.8 us -> 16.8 us (level)
  Pallas kernels: 5.18 us -> 4.92 us
  starting transfers between devices: 7.01 us -> 7.18 us
    ppermute x4, starting transfers between devices: 3.45 us -> 3.63 us  [exchanged(): lax.ppermute(values, 'depth', [(d, d ^ m) for d, m in enumerate(masks)])]
  transfers between devices with their start and end apart: 8 -> 8, of which waited for: 4 -> 4; matrix products, arithmetic and copies ran while one was open for 0% -> 0% of each run, Pallas kernels for 17% -> 16%
where the time goes in v12:
time: 16.8 us; the launch traced here: 16.6 us
  starting transfers between devices  7.18 us (43%)
  Pallas kernels  4.92 us (29%)
  waiting for transfers between devices  4.43 us (26%)
    ppermute x4, waiting for transfers between devices, exchanged(): lax.ppermute(values, 'depth', [(d, d ^ m) for d, m in enumerate(masks)])  4.42 us
    ppermute x4, starting transfers between devices, exchanged(): lax.ppermute(values, 'depth', [(d, d ^ m) for d, m in enumerate(masks)])  3.63 us
    ppermute x4, starting transfers between devices, swapped(): return lax.ppermute(values, ('depth', 'rows'), perm)  3.55 us
    pallas_call x1, Pallas kernels, march_interior(): pl.pallas_call(functools.partial(interior_kernel, opacity_scale), in_spec...  2.46 us
    pallas_call x1, Pallas kernels, cut_edges(): pl.pallas_call(edges_kernel, in_specs=[pl.BlockSpec(memory_space=pl.ANY)]...  1.18 us
    pallas_call x1, Pallas kernels, gather(): pl.pallas_call(gather_kernel, in_specs=[WHOLE] * len(parts), out_specs=WH...  0.7 us
  transfers between devices with their start and end apart: 8, of which 4 were waited for; matrix products, arithmetic and copies ran while one was open for 0% of the time, Pallas kernels for 16%

profile of v12, /device:TPU:25, one launch (start us, length us, event | category | flops | bytes accessed | tf_op | source)
XLA Modules:
  0.0 16.6 jit_solution(10669385707785989670)
XLA Ops:
  0.0 0.0 copy-start
  0.0 0.0 copy-start.2
  0.0 0.0 copy-start.1
  0.0 1.2 %shard_map.38 = (bf16[32,1024]{1,0:T(8,128)(2,1)S(1)}, bf16[32,1024]{1,0:T(8,128)(2,1)S(1)}, bf16[32,1024]{1,0:T(8,128)(2,1)S(1)}, bf16[8,1024]{1,0:T(8,128)(2,1)S(1)}) custom-call(s32[2,8,32,1024]{3,2,1,0:T(8,128)} %volume_ref.7), custom_call_target="tpu_custom_call" | custom-call | tf_op jit(solution)/shard_map/pallas_call | solution.py:79
  1.2 0.7 %collective-permute-start = (bf16[32,1024]{1,0:T(8,128)(2,1)S(1)}, bf16[32,1024]{1,0:T(8,128)(2,1)S(1)}, u32[]{:S(2)}, u32[]{:S(2)}) collective-permute-start(bf16[32,1024]{1,0:T(8,128)(2,1)S(1)} %get-tuple-element.24), channel_id=1, source_target_pairs={{0,28},{1,5},{2,30},{3,7},{4,8},{5,1},{6,10},{7,3},{8,4},{9,13},{1... | collective-permute-start | bytes 196616 | tf_op jit(solution)/shard_map/ppermute | solution.py:572
  1.9 1.3 %collective-permute-start.1 = (bf16[32,1024]{1,0:T(8,128)(2,1)S(1)}, bf16[32,1024]{1,0:T(8,128)(2,1)S(1)}, u32[]{:S(2)}, u32[]{:S(2)}) collective-permute-start(bf16[32,1024]{1,0:T(8,128)(2,1)S(1)} %get-tuple-element.27), channel_id=1, source_target_pairs={{0,1},{1,0},{2,3},{3,2},{4,5},{5,4},{6,7},{7,6},{8,9},{9,8},{10,11... | collective-permute-start | bytes 196616 | tf_op jit(solution)/shard_map/ppermute | solution.py:572
  3.2 0.4 %collective-permute-start.2 = (bf16[32,1024]{1,0:T(8,128)(2,1)S(1)}, bf16[32,1024]{1,0:T(8,128)(2,1)S(1)}, u32[]{:S(2)}, u32[]{:S(2)}) collective-permute-start(bf16[32,1024]{1,0:T(8,128)(2,1)S(1)} %get-tuple-element.28), channel_id=1, source_target_pairs={{0,4},{1,29},{2,6},{3,31},{4,0},{5,9},{6,2},{7,11},{8,12},{9,5},{1... | collective-permute-start | bytes 196616 | tf_op jit(solution)/shard_map/ppermute | solution.py:572
  3.6 1.2 %collective-permute-start.3 = (bf16[8,1024]{1,0:T(8,128)(2,1)S(1)}, bf16[8,1024]{1,0:T(8,128)(2,1)S(1)}, u32[]{:S(2)}, u32[]{:S(2)}) collective-permute-start(bf16[8,1024]{1,0:T(8,128)(2,1)S(1)} %get-tuple-element.29), channel_id=1, source_target_pairs={{0,4},{1,2},{2,1},{3,7},{4,0},{5,6},{6,5},{7,3},{8,12},{9,10},{10,... | collective-permute-start | bytes 49160 | tf_op jit(solution)/shard_map/ppermute | solution.py:572
  4.8 0.0 copy-done
  4.8 0.0 copy-done.2
  4.8 0.0 copy-done.1
  4.8 2.5 %shard_map.37 = (f32[4,32,1024]{2,1,0:T(8,128)S(1)}, f32[2,32,1024]{2,1,0:T(8,128)S(1)}, f32[2,32,1024]{2,1,0:T(8,128)S(1)}, f32[2,3,32,1024]{3,2,1,0:T(8,128)S(...) custom-call(s32[2,8,32,1024]{3,2,1,0:T(8,128)S(1)} %copy-done, s32[3,256]{1,0:T(4,128)S(1)} %copy-done.1, ...), custom_call_target="tpu_custom_call" | custom-call | flops 20971520 | bytes 5242880 | tf_op jit(solution)/shard_map/pallas_call | solution.py:275
  7.2 0.0 collective-permute-done.first_ref
  7.2 0.2 %shard_map.39.sums_ref = f32[3,32,1024]{2,1,0:T(8,128)S(1)} custom-call(s32[2,8,32,1024]{3,2,1,0:T(8,128)S(1)} %copy-done, f32[4,32,1024]{2,1,0:T(8,128)S(1)} %get-tuple-element.20.base_ref, f32[2,32,1024]{2,1,0:T(8,128)S(1)} %get-tuple-element.21.face_ref, f32[2,32,1024]{2,1,0:T(8,128)S(1)} %get-tuple-element.22.square_ref, ...), custom_call_target="tpu_custom_call" | custom-call | flops 2621440 | bytes 1572864 | tf_op jit(solution)/shard_map/pallas_call | solution.py:332
  7.5 0.0 collective-permute-done.3.rows_far_ref
  7.5 0.0 collective-permute-done.1.rows_near_ref
  7.5 0.0 collective-permute-done.2.second_ref
  7.5 0.3 %shard_map.40 = (f32[4,2,16,1024]{3,2,1,0:T(8,128)S(1)}, bf16[4,16,1024]{2,1,0:T(8,128)(2,1)S(1)}) custom-call(s32[2,8,32,1024]{3,2,1,0:T(8,128)S(1)} %copy-done, f32[3,32,1024]{2,1,0:T(8,128)S(1)} %shard_map.39.sums_ref, f32[4,32,1024]{2,1,0:T(8,128)S(1)} %get-tuple-element.20.base_ref, f32[2,32,1024]{2,1,0:T(8,128)S(1)} %get-tuple-element.21.face_ref, ...), custom_call_target="tpu_custom_call" | custom-call | tf_op jit(solution)/shard_map/pallas_call | solution.py:426
  7.8 1.8 %collective-permute-start.4 = (bf16[4,16,1024]{2,1,0:T(8,128)(2,1)S(1)}, bf16[4,16,1024]{2,1,0:T(8,128)(2,1)S(1)}, u32[]{:S(2)}, u32[]{:S(2)}) collective-permute-start(bf16[4,16,1024]{2,1,0:T(8,128)(2,1)S(1)} %get-tuple-element.31), channel_id=1, source_target_pairs={{0,4},{4,0},{8,12},{12,8},{16,20},{20,16},{24,28},{28,24},{1,5},{5... | collective-permute-start | bytes 393224 | tf_op jit(solution)/shard_map/ppermute | solution.py:577
  9.6 1.0 %collective-permute-done.4.other_ref = bf16[4,16,1024]{2,1,0:T(8,128)(2,1)S(1)} collective-permute-done((bf16[4,16,1024]{2,1,0:T(8,128)(2,1)S(1)}, bf16[4,16,1024]{2,1,0:T(8,128)(2,1)S(1)}, u32[]{:S(2)}, u32[]{:S(2)}) %collective-permute-start.4) | collective-permute-done | bytes 131104 | tf_op jit(solution)/shard_map/ppermute | solution.py:577
  10.6 0.1 shard_map.41
  10.7 0.5 %collective-permute-start.5 = (bf16[2,16,1024]{2,1,0:T(8,128)(2,1)S(1)}, bf16[2,16,1024]{2,1,0:T(8,128)(2,1)S(1)}, u32[]{:S(2)}, u32[]{:S(2)}) collective-permute-start(bf16[2,16,1024]{2,1,0:T(8,128)(2,1)S(1)} %get-tuple-element.32), channel_id=1, source_target_pairs={{0,12},{4,16},{8,28},{12,0},{16,4},{20,24},{24,20},{28,8},{1,13},{... | collective-permute-start | bytes 196616 | tf_op jit(solution)/shard_map/ppermute | solution.py:577
  11.2 1.2 %collective-permute-start.6 = (bf16[16,1024]{1,0:T(8,128)(2,1)S(1)}, bf16[16,1024]{1,0:T(8,128)(2,1)S(1)}, u32[]{:S(2)}, u32[]{:S(2)}) collective-permute-start(bf16[16,1024]{1,0:T(8,128)(2,1)S(1)} %get-tuple-element.33), channel_id=1, source_target_pairs={{0,28},{4,24},{8,20},{12,16},{16,12},{20,8},{24,4},{28,0},{1,29},{... | collective-permute-start | bytes 98312 | tf_op jit(solution)/shard_map/ppermute | solution.py:577
  12.4 2.3 %collective-permute-done.5.side_ref = bf16[2,16,1024]{2,1,0:T(8,128)(2,1)S(1)} collective-permute-done((bf16[2,16,1024]{2,1,0:T(8,128)(2,1)S(1)}, bf16[2,16,1024]{2,1,0:T(8,128)(2,1)S(1)}, u32[]{:S(2)}, u32[]{:S(2)}) %collective-permute-start.5) | collective-permute-done | bytes 65568 | tf_op jit(solution)/shard_map/ppermute | solution.py:577
  14.7 0.1 collective-permute-start.7
  14.8 0.7 %collective-permute-done.6.cross_ref = bf16[16,1024]{1,0:T(8,128)(2,1)S(1)} collective-permute-done((bf16[16,1024]{1,0:T(8,128)(2,1)S(1)}, bf16[16,1024]{1,0:T(8,128)(2,1)S(1)}, u32[]{:S(2)}, u32[]{:S(2)}) %collective-permute-start.6) | collective-permute-done | bytes 32800 | tf_op jit(solution)/shard_map/ppermute | solution.py:577
  15.4 0.5 %collective-permute-done.7.passed_ref = bf16[16,1024]{1,0:T(8,128)(2,1)S(1)} collective-permute-done((bf16[16,1024]{1,0:T(8,128)(2,1)S(1)}, bf16[16,1024]{1,0:T(8,128)(2,1)S(1)}, u32[]{:S(2)}, u32[]{:S(2)}) %collective-permute-start.7) | collective-permute-done | bytes 32800 | tf_op jit(solution)/shard_map/ppermute | solution.py:577
  15.9 0.7 %shard_map.43 = f32[4,4,1024]{2,1,0:T(4,128)} custom-call(bf16[2,16,1024]{2,1,0:T(8,128)(2,1)S(1)} %collective-permute-done.5.side_ref, bf16[16,1024]{1,0:T(8,128)(2,1)S(1)} %collective-permute-done.6.cross_ref, bf16[16,1024]{1,0:T(8,128)(2,1)S(1)} %collective-permute-done.7.passed_ref, f32[16,1024]{1,0:T(8,128)S(1)} %get-tuple-element.34.own_ref), custom_call_target="tpu_custom_call" | custom-call | tf_op jit(solution)/shard_map/pallas_call | solution.py:520
  (1 shorter events, 0.0 us)
Async XLA Ops:
  0.0 4.8 %copy-start = (s32[2,8,32,1024]{3,2,1,0:T(8,128)S(1)}, s32[2,8,32,1024]{3,2,1,0:T(8,128)}, u32[]{:S(2)}) copy-start(s32[2,8,32,1024]{3,2,1,0:T(8,128)} %volume_ref.7) | copy-start | bytes 6291460
  0.0 4.8 %copy-start.2 = (s32[256]{0:T(256)S(1)}, s32[256]{0:T(256)}, u32[]{:S(2)}) copy-start(s32[256]{0:T(256)} %param.5) | copy-start | bytes 3076
  0.0 4.8 %copy-start.1 = (s32[3,256]{1,0:T(4,128)S(1)}, s32[3,256]{1,0:T(4,128)}, u32[]{:S(2)}) copy-start(s32[3,256]{1,0:T(4,128)} %color_ref.1) | copy-start | bytes 9220
  1.2 6.0 %collective-permute-start = (bf16[32,1024]{1,0:T(8,128)(2,1)S(1)}, bf16[32,1024]{1,0:T(8,128)(2,1)S(1)}, u32[]{:S(2)}, u32[]{:S(2)}) collective-permute-start(bf16[32,1024]{1,0:T(8,128)(2,1)S(1)} %get-tuple-element.24), channel_id=1, source_target_pairs={{0,28},{1,5},{2,30},{3,7},{4,8},{5,1},{6,10},{7,3},{8,4},{9,13},{1... | collective-permute-start | bytes 196616 | tf_op jit(solution)/shard_map/ppermute | solution.py:572
  1.9 5.5 %collective-permute-start.1 = (bf16[32,1024]{1,0:T(8,128)(2,1)S(1)}, bf16[32,1024]{1,0:T(8,128)(2,1)S(1)}, u32[]{:S(2)}, u32[]{:S(2)}) collective-permute-start(bf16[32,1024]{1,0:T(8,128)(2,1)S(1)} %get-tuple-element.27), channel_id=1, source_target_pairs={{0,1},{1,0},{2,3},{3,2},{4,5},{5,4},{6,7},{7,6},{8,9},{9,8},{10,11... | collective-permute-start | bytes 196616 | tf_op jit(solution)/shard_map/ppermute | solution.py:572
  3.2 4.3 %collective-permute-start.2 = (bf16[32,1024]{1,0:T(8,128)(2,1)S(1)}, bf16[32,1024]{1,0:T(8,128)(2,1)S(1)}, u32[]{:S(2)}, u32[]{:S(2)}) collective-permute-start(bf16[32,1024]{1,0:T(8,128)(2,1)S(1)} %get-tuple-element.28), channel_id=1, source_target_pairs={{0,4},{1,29},{2,6},{3,31},{4,0},{5,9},{6,2},{7,11},{8,12},{9,5},{1... | collective-permute-start | bytes 196616 | tf_op jit(solution)/shard_map/ppermute | solution.py:572
  3.6 3.9 %collective-permute-start.3 = (bf16[8,1024]{1,0:T(8,128)(2,1)S(1)}, bf16[8,1024]{1,0:T(8,128)(2,1)S(1)}, u32[]{:S(2)}, u32[]{:S(2)}) collective-permute-start(bf16[8,1024]{1,0:T(8,128)(2,1)S(1)} %get-tuple-element.29), channel_id=1, source_target_pairs={{0,4},{1,2},{2,1},{3,7},{4,0},{5,6},{6,5},{7,3},{8,12},{9,10},{10,... | collective-permute-start | bytes 49160 | tf_op jit(solution)/shard_map/ppermute | solution.py:572
  7.8 2.8 %collective-permute-start.4 = (bf16[4,16,1024]{2,1,0:T(8,128)(2,1)S(1)}, bf16[4,16,1024]{2,1,0:T(8,128)(2,1)S(1)}, u32[]{:S(2)}, u32[]{:S(2)}) collective-permute-start(bf16[4,16,1024]{2,1,0:T(8,128)(2,1)S(1)} %get-tuple-element.31), channel_id=1, source_target_pairs={{0,4},{4,0},{8,12},{12,8},{16,20},{20,16},{24,28},{28,24},{1,5},{5... | collective-permute-start | bytes 393224 | tf_op jit(solution)/shard_map/ppermute | solution.py:577
  10.7 4.1 %collective-permute-start.5 = (bf16[2,16,1024]{2,1,0:T(8,128)(2,1)S(1)}, bf16[2,16,1024]{2,1,0:T(8,128)(2,1)S(1)}, u32[]{:S(2)}, u32[]{:S(2)}) collective-permute-start(bf16[2,16,1024]{2,1,0:T(8,128)(2,1)S(1)} %get-tuple-element.32), channel_id=1, source_target_pairs={{0,12},{4,16},{8,28},{12,0},{16,4},{20,24},{24,20},{28,8},{1,13},{... | collective-permute-start | bytes 196616 | tf_op jit(solution)/shard_map/ppermute | solution.py:577
  11.2 4.2 %collective-permute-start.6 = (bf16[16,1024]{1,0:T(8,128)(2,1)S(1)}, bf16[16,1024]{1,0:T(8,128)(2,1)S(1)}, u32[]{:S(2)}, u32[]{:S(2)}) collective-permute-start(bf16[16,1024]{1,0:T(8,128)(2,1)S(1)} %get-tuple-element.33), channel_id=1, source_target_pairs={{0,28},{4,24},{8,20},{12,16},{16,12},{20,8},{24,4},{28,0},{1,29},{... | collective-permute-start | bytes 98312 | tf_op jit(solution)/shard_map/ppermute | solution.py:577
  14.7 1.2 %collective-permute-start.7 = (bf16[16,1024]{1,0:T(8,128)(2,1)S(1)}, bf16[16,1024]{1,0:T(8,128)(2,1)S(1)}, u32[]{:S(2)}, u32[]{:S(2)}) collective-permute-start(bf16[16,1024]{1,0:T(8,128)(2,1)S(1)} %shard_map.42), channel_id=1, source_target_pairs={{0,4},{4,0},{8,12},{12,8},{16,20},{20,16},{24,28},{28,24},{1,5},{5... | collective-permute-start | bytes 98312 | tf_op jit(solution)/shard_map/ppermute | solution.py:577

commit v13 on v6

--- a/solution.py
+++ b/solution.py
@@ -32,14 +32,29 @@
     odd, odd_row = parity("depth"), parity("rows")
     far_first = 1 - odd_row
     last_first = odd ^ far_first ^ 1
+    tiles = height // SUBLANES
+
+    def plane_copies(i, s):
+        for t in range(tiles):
+            rows = pl.ds(t * SUBLANES, SUBLANES)
+            yield pltpu.make_async_copy(volume_ref.at[0, s, rows], plane_ref.at[i, rows], sems.at[i, t])
+
+    def strip_copy(i, row):
+        return pltpu.make_async_copy(volume_ref.at[0, :, row], strip_ref.at[i], sems.at[2, i])
+
     copies = [
-        pltpu.make_async_copy(volume_ref.at[0, last_first * (slices - 1)], plane_ref.at[0], sems.at[0]),
-        pltpu.make_async_copy(volume_ref.at[0, :, (1 - odd_row) * (height - 1)], strip_ref.at[0], sems.at[1]),
-        pltpu.make_async_copy(volume_ref.at[0, (1 - last_first) * (slices - 1)], plane_ref.at[1], sems.at[2]),
-        pltpu.make_async_copy(volume_ref.at[0, :, odd_row * (height - 1)], strip_ref.at[1], sems.at[3]),
+        list(plane_copies(0, last_first * (slices - 1))),
+        [strip_copy(0, (1 - odd_row) * (height - 1))],
+        list(plane_copies(1, (1 - last_first) * (slices - 1))),
+        [strip_copy(1, odd_row * (height - 1))],
     ]
-    for copy in copies:
-        copy.start()
+    for group in copies:
+        for copy in group:
+            copy.start()
+
+    def arrive(group):
+        for copy in group:
+            copy.wait()
 
     def narrow(values):
         return values.astype(jnp.float32).astype(jnp.bfloat16)
@@ -47,28 +62,29 @@
     def padded(strip):
         return narrow(jnp.concatenate([strip, jnp.zeros((height - slices, columns), jnp.int32)], axis=0))
 
-    copies[0].wait()
+    arrive(copies[0])
     first_out[...] = narrow(plane_ref[0])
-    copies[1].wait()
+    arrive(copies[1])
     rows_near_out[...] = padded(strip_ref[0])
-    copies[2].wait()
+    arrive(copies[2])
     second_out[...] = narrow(plane_ref[1])
-    copies[3].wait()
-    rows_far_out[...] = padded(strip_ref[1])
+    arrive(copies[3])
+    rows_far_out[...] = narrow(strip_ref[1])
 
 
 def cut_edges(volume):
     _, slices, height, columns = volume.shape
     plane = jax.ShapeDtypeStruct((height, columns), jnp.bfloat16)
+    strip = jax.ShapeDtypeStruct((slices, columns), jnp.bfloat16)
     return pl.pallas_call(
         edges_kernel,
         in_specs=[pl.BlockSpec(memory_space=pl.ANY)],
         out_specs=[WHOLE] * 4,
-        out_shape=[plane] * 4,
+        out_shape=[plane, plane, plane, strip],
         scratch_shapes=[
             pltpu.VMEM((2, slices, columns), jnp.int32),
             pltpu.VMEM((2, height, columns), jnp.int32),
-            pltpu.SemaphoreType.DMA((4,)),
+            pltpu.SemaphoreType.DMA((3, max(2, height // SUBLANES))),
         ],
         compiler_params=pltpu.CompilerParams(vmem_limit_bytes=52 * 1024 * 1024),
     )(volume)
@@ -241,7 +257,7 @@
                 strip_ref[q, c, :, here] = emitted[c] * weight
         return carry
 
-    lax.fori_loop(0, chunks, chunk, 0)
+    lax.fori_loop(0, chunks, chunk, 0, unroll=4)
 
 
 def march_interior(volume, color_map, alpha_map, depth_count):
@@ -281,8 +297,50 @@
     return both, pltpu.roll(both, 3, 0)
 
 
+def plane_terms(volume_ref, face_ref, square_ref, lit_ref, halo, end, rows, here):
+    slices = volume_ref.shape[1]
+    inner = volume_ref[0, jnp.where(end == 1, slices - 2, 1), rows, here].astype(jnp.float32)
+    grad_depth = jnp.where(end == 1, halo - inner, inner - halo)
+    shading = shade(grad_depth, face_ref[end, rows, here], square_ref[end, rows, here])
+    return [lit_ref[end, c, rows, here] * shading for c in range(3)]
+
+
+def first_end():
+    front_end, back_end = ends("depth")
+    end = jnp.where(parity("depth") == parity("rows"), 0, 1)
+    return end, jnp.where(end == 1, back_end, front_end), jnp.where(end == 1, front_end, back_end)
+
+
+def first_plane_kernel(volume_ref, base_ref, face_ref, square_ref, lit_ref, first_ref, sums_ref):
+    _, height, columns = base_ref.shape
+    end, outside, _ = first_end()
+
+    def chunk(j, carry):
+        here = pl.ds(pl.multiple_of(j * LANES, LANES), LANES)
+        first = jnp.where(outside, 0.0, first_ref[:, here].astype(jnp.float32))
+        for r in range(height // SUBLANES):
+            rows = slice(r * SUBLANES, (r + 1) * SUBLANES)
+            terms = plane_terms(volume_ref, face_ref, square_ref, lit_ref, first[rows], end, rows, here)
+            for c in range(3):
+                sums_ref[c, rows, here] = base_ref[c, rows, here] + terms[c]
+        return carry
+
+    lax.fori_loop(0, columns // LANES, chunk, 0, unroll=4)
+
+
+def add_first_plane(volume, base, face, square, lit, first):
+    return pl.pallas_call(
+        first_plane_kernel,
+        in_specs=[WHOLE] * 6,
+        out_specs=WHOLE,
+        out_shape=jax.ShapeDtypeStruct((3, *base.shape[1:]), jnp.float32),
+        compiler_params=pltpu.CompilerParams(vmem_limit_bytes=8 * 1024 * 1024),
+        cost_estimate=pl.CostEstimate(flops=base.size * 20, bytes_accessed=base.size * 12, transcendentals=base.size // 4),
+    )(volume, base, face, square, lit, first)
+
+
 def edge_kernel(
-    share, volume_ref, base_ref, face_ref, square_ref, lit_ref, grad_ref, strip_ref, first_ref, rows_near_ref, second_ref, rows_far_ref, *out_refs
+    share, volume_ref, sums_ref, base_ref, face_ref, square_ref, lit_ref, grad_ref, strip_ref, first_ref, rows_near_ref, second_ref, rows_far_ref, *out_refs
 ):
     _, slices, height, columns = volume_ref.shape
     tiles = height // SUBLANES
@@ -296,17 +354,19 @@
     front_came_first = odd == odd_row
     front_end, back_end = ends("depth")
     top_end, bottom_end = ends("rows")
+    end, _, outside = first_end()
 
     def chunk(j, carry):
         here = pl.ds(pl.multiple_of(j * LANES, LANES), LANES)
         rows_near = rows_near_ref[:, here].astype(jnp.float32)[:slices]
-        rows_far = rows_far_ref[:, here].astype(jnp.float32)[:slices]
+        rows_far = rows_far_ref[:, here].astype(jnp.float32)
         above = jnp.where(top_end, 0.0, jnp.where(odd_row, rows_near, rows_far))
         below = jnp.where(bottom_end, 0.0, jnp.where(odd_row, rows_far, rows_near))
         first = first_ref[:, here].astype(jnp.float32)
         second = second_ref[:, here].astype(jnp.float32)
         before = jnp.where(front_end, 0.0, jnp.where(front_came_first, first, second))
         after = jnp.where(back_end, 0.0, jnp.where(front_came_first, second, first))
+        last = jnp.where(outside, 0.0, second)
         extra = []
         for q, edge in enumerate((0, height - 1)):
             inner = grad_ref[q, 1, :, here]
@@ -324,15 +384,8 @@
         extra = [row_sums(extra[0][c], extra[1][c]) for c in range(3)]
         for r in range(tiles):
             rows = slice(r * SUBLANES, (r + 1) * SUBLANES)
-            planes = [base_ref[c, rows, here] for c in range(4)]
-            for end in range(2):
-                if end:
-                    grad_depth = after[rows] - volume_ref[0, slices - 2, rows, here].astype(jnp.float32)
-                else:
-                    grad_depth = volume_ref[0, 1, rows, here].astype(jnp.float32) - before[rows]
-                shading = shade(grad_depth, face_ref[end, rows, here], square_ref[end, rows, here])
-                for c in range(3):
-                    planes[c] = planes[c] + lit_ref[end, c, rows, here] * shading
+            terms = plane_terms(volume_ref, face_ref, square_ref, lit_ref, last[rows], 1 - end, rows, here)
+            planes = [sums_ref[c, rows, here] + terms[c] for c in range(3)] + [base_ref[3, rows, here]]
             for c in range(3):
                 if r == 0:
                     planes[c] = planes[c] + jnp.where(first_row, extra[c][0], 0.0)
@@ -343,19 +396,19 @@
                     block = jnp.concatenate([plane[first : first + share] for plane in planes], axis=0)
                     out_refs[0][r * (SUBLANES // share) + i, :, here] = block.astype(jnp.bfloat16)
             else:
-                keep_ref, give_ref = out_refs
                 halves = [(planes[c], pltpu.roll(planes[c + 1], SUBLANES // 2, 0)) for c in (0, 2)]
                 even = jnp.concatenate([jnp.where(upper, own, turned) for own, turned in halves], axis=0)
                 uneven = jnp.concatenate([jnp.where(upper, turned, own) for own, turned in halves], axis=0)
+                keep_ref, give_ref = out_refs
                 keep_even = odd != (chip == r)
                 keep_ref[r, :, here] = jnp.where(keep_even, even, uneven)
                 give_ref[r, :, here] = jnp.where(keep_even, uneven, even).astype(jnp.bfloat16)
         return carry
 
-    lax.fori_loop(0, columns // LANES, chunk, 0)
-
-
-def add_edges(volume, interior, halos, depth_count, paired):
+    lax.fori_loop(0, columns // LANES, chunk, 0, unroll=8)
+
+
+def add_edges(volume, sums, interior, halos, depth_count, paired):
     _, slices, height, columns = volume.shape
     share = height // depth_count
     if paired:
@@ -365,11 +418,11 @@
         shapes = [jax.ShapeDtypeStruct((depth_count, 4 * share, columns), jnp.bfloat16)]
     return pl.pallas_call(
         functools.partial(edge_kernel, share),
-        in_specs=[WHOLE] * 11,
+        in_specs=[WHOLE] * 12,
         out_specs=[WHOLE] * len(shapes),
         out_shape=shapes,
         compiler_params=pltpu.CompilerParams(vmem_limit_bytes=24 * 1024 * 1024),
-    )(volume, *interior, *halos)
+    )(volume, sums, *interior, *halos)
 
 
 def over(nearer, farther, uneven):
@@ -494,7 +547,8 @@
     interior = march_interior(volume, color_map, alpha_map, depth_count)
     halos = (first, rows_near, second, rows_far)
     paired = depth_count == 8 and 2 * share == SUBLANES
-    outs = add_edges(volume, interior, halos, depth_count, paired)
+    sums = add_first_plane(volume, *interior[:4], first)
+    outs = add_edges(volume, sums, interior, halos, depth_count, paired)
     if not paired:
         return finish(lax.all_to_all(outs[0], "depth", 0, 0, tiled=True), share)
     keep, give = outs

time: 17.3 us -> 16.8 us (0.971)
  the two profiles are of different devices: /device:TPU:9 before, /device:TPU:0 now
where the time goes in v13:
time: 16.8 us; the launch traced here: 16.7 us
  starting transfers between devices  7.04 us (42%)
  Pallas kernels  4.9 us (29%)
  waiting for transfers between devices  4.64 us (28%)
    ppermute x4, starting transfers between devices, swapped(): return lax.ppermute(values, ('depth', 'rows'), perm)  3.93 us
    ppermute x4, waiting for transfers between devices, exchanged(): lax.ppermute(values, 'depth', [(d, d ^ mask) for d in range(lax.axis_size...  3.6 us
    ppermute x4, starting transfers between devices, exchanged(): lax.ppermute(values, 'depth', [(d, d ^ mask) for d in range(lax.axis_size...  3.11 us
    pallas_call x1, Pallas kernels, march_interior(): pl.pallas_call(functools.partial(interior_kernel, opacity_scale), in_spec...  2.46 us
    pallas_call x1, Pallas kernels, cut_edges(): pl.pallas_call(edges_kernel, in_specs=[pl.BlockSpec(memory_space=pl.ANY)]...  1.17 us
    ppermute x4, waiting for transfers between devices, swapped(): return lax.ppermute(values, ('depth', 'rows'), perm)  1.04 us
    pallas_call x1, Pallas kernels, gather(): pl.pallas_call(gather_kernel, in_specs=[WHOLE] * len(parts), out_specs=WH...  0.7 us
  transfers between devices with their start and end apart: 8, of which 4 were waited for; matrix products, arithmetic and copies ran while one was open for 0% of the time, Pallas kernels for 16%

profile of v13, /device:TPU:0, one launch (start us, length us, event | category | flops | bytes accessed | tf_op | source)
XLA Modules:
  0.0 16.7 jit_solution(6277587730337752943)
XLA Ops:
  0.0 0.0 copy-start
  0.0 0.0 copy-start.2
  0.0 0.0 copy-start.1
  0.0 1.2 %shard_map.38 = (bf16[32,1024]{1,0:T(8,128)(2,1)S(1)}, bf16[32,1024]{1,0:T(8,128)(2,1)S(1)}, bf16[32,1024]{1,0:T(8,128)(2,1)S(1)}, bf16[8,1024]{1,0:T(8,128)(2,1)S(1)}) custom-call(s32[2,8,32,1024]{3,2,1,0:T(8,128)} %volume_ref.7), custom_call_target="tpu_custom_call" | custom-call | tf_op jit(solution)/shard_map/pallas_call | solution.py:79
  1.2 3.4 %collective-permute-start = (bf16[32,1024]{1,0:T(8,128)(2,1)S(1)}, bf16[32,1024]{1,0:T(8,128)(2,1)S(1)}, u32[]{:S(2)}, u32[]{:S(2)}) collective-permute-start(bf16[32,1024]{1,0:T(8,128)(2,1)S(1)} %get-tuple-element.25), channel_id=1, source_target_pairs={{0,28},{1,5},{2,30},{3,7},{4,8},{5,1},{6,10},{7,3},{8,4},{9,13},{1... | collective-permute-start | bytes 196616 | tf_op jit(solution)/shard_map/ppermute | solution.py:532
  4.6 0.0 collective-permute-start.1
  4.6 0.0 collective-permute-start.2
  4.6 0.5 %collective-permute-start.3 = (bf16[8,1024]{1,0:T(8,128)(2,1)S(1)}, bf16[8,1024]{1,0:T(8,128)(2,1)S(1)}, u32[]{:S(2)}, u32[]{:S(2)}) collective-permute-start(bf16[8,1024]{1,0:T(8,128)(2,1)S(1)} %get-tuple-element.30), channel_id=1, source_target_pairs={{0,4},{1,2},{2,1},{3,7},{4,0},{5,6},{6,5},{7,3},{8,12},{9,10},{10,... | collective-permute-start | bytes 49160 | tf_op jit(solution)/shard_map/ppermute | solution.py:532
  5.1 0.0 copy-done
  5.1 0.0 copy-done.2
  5.1 0.0 copy-done.1
  5.1 2.5 %shard_map.37 = (f32[4,32,1024]{2,1,0:T(8,128)S(1)}, f32[2,32,1024]{2,1,0:T(8,128)S(1)}, f32[2,32,1024]{2,1,0:T(8,128)S(1)}, f32[2,3,32,1024]{3,2,1,0:T(8,128)S(...) custom-call(s32[2,8,32,1024]{3,2,1,0:T(8,128)S(1)} %copy-done, s32[3,256]{1,0:T(4,128)S(1)} %copy-done.1, ...), custom_call_target="tpu_custom_call" | custom-call | flops 20971520 | bytes 5242880 | tf_op jit(solution)/shard_map/pallas_call | solution.py:275
  7.6 0.0 collective-permute-done.first_ref
  7.6 0.2 %shard_map.39.sums_ref = f32[3,32,1024]{2,1,0:T(8,128)S(1)} custom-call(s32[2,8,32,1024]{3,2,1,0:T(8,128)S(1)} %copy-done, f32[4,32,1024]{2,1,0:T(8,128)S(1)} %get-tuple-element.21.base_ref, f32[2,32,1024]{2,1,0:T(8,128)S(1)} %get-tuple-element.22.face_ref, f32[2,32,1024]{2,1,0:T(8,128)S(1)} %get-tuple-element.23.square_ref, ...), custom_call_target="tpu_custom_call" | custom-call | flops 2621440 | bytes 1572864 | tf_op jit(solution)/shard_map/pallas_call | solution.py:332
  7.8 0.0 collective-permute-done.3.rows_far_ref
  7.8 1.0 %collective-permute-done.1.rows_near_ref = bf16[32,1024]{1,0:T(8,128)(2,1)S(1)} collective-permute-done((bf16[32,1024]{1,0:T(8,128)(2,1)S(1)}, bf16[32,1024]{1,0:T(8,128)(2,1)S(1)}, u32[]{:S(2)}, u32[]{:S(2)}) %collective-permute-start.1) | collective-permute-done | bytes 65568 | tf_op jit(solution)/shard_map/ppermute | solution.py:532
  8.9 0.0 collective-permute-done.2.second_ref
  8.9 0.3 %shard_map.40 = (f32[4,16,1024]{2,1,0:T(8,128)S(1)}, bf16[4,16,1024]{2,1,0:T(8,128)(2,1)S(1)}) custom-call(s32[2,8,32,1024]{3,2,1,0:T(8,128)S(1)} %copy-done, f32[3,32,1024]{2,1,0:T(8,128)S(1)} %shard_map.39.sums_ref, f32[4,32,1024]{2,1,0:T(8,128)S(1)} %get-tuple-element.21.base_ref, f32[2,32,1024]{2,1,0:T(8,128)S(1)} %get-tuple-element.22.face_ref, ...), custom_call_target="tpu_custom_call" | custom-call | tf_op jit(solution)/shard_map/pallas_call | solution.py:419
  9.2 0.1 collective-permute-start.4
  9.2 1.3 %collective-permute-done.4.other_ref = bf16[4,16,1024]{2,1,0:T(8,128)(2,1)S(1)} collective-permute-done((bf16[4,16,1024]{2,1,0:T(8,128)(2,1)S(1)}, bf16[4,16,1024]{2,1,0:T(8,128)(2,1)S(1)}, u32[]{:S(2)}, u32[]{:S(2)}) %collective-permute-start.4) | collective-permute-done | bytes 131104 | tf_op jit(solution)/shard_map/ppermute | solution.py:536
  10.6 0.1 shard_map.41
  10.6 1.0 %collective-permute-start.5 = (bf16[16,1024]{1,0:T(8,128)(2,1)S(1)}, bf16[16,1024]{1,0:T(8,128)(2,1)S(1)}, u32[]{:S(2)}, u32[]{:S(2)}) collective-permute-start(bf16[16,1024]{1,0:T(8,128)(2,1)S(1)} %get-tuple-element.33), channel_id=1, source_target_pairs={{0,28},{4,24},{8,20},{12,16},{16,12},{20,8},{24,4},{28,0},{1,29},{... | collective-permute-start | bytes 98312 | tf_op jit(solution)/shard_map/ppermute | solution.py:536
  11.7 0.5 %collective-permute-start.6 = (bf16[16,1024]{1,0:T(8,128)(2,1)S(1)}, bf16[16,1024]{1,0:T(8,128)(2,1)S(1)}, u32[]{:S(2)}, u32[]{:S(2)}) collective-permute-start(bf16[16,1024]{1,0:T(8,128)(2,1)S(1)} %get-tuple-element.34), channel_id=1, source_target_pairs={{0,20},{4,16},{8,28},{12,24},{16,4},{20,0},{24,12},{28,8},{1,21},{... | collective-permute-start | bytes 98312 | tf_op jit(solution)/shard_map/ppermute | solution.py:536
  12.2 1.5 %collective-permute-start.7 = (bf16[16,1024]{1,0:T(8,128)(2,1)S(1)}, bf16[16,1024]{1,0:T(8,128)(2,1)S(1)}, u32[]{:S(2)}, u32[]{:S(2)}) collective-permute-start(bf16[16,1024]{1,0:T(8,128)(2,1)S(1)} %get-tuple-element.35), channel_id=1, source_target_pairs={{0,12},{4,8},{8,4},{12,0},{16,28},{20,24},{24,20},{28,16},{1,13},{... | collective-permute-start | bytes 98312 | tf_op jit(solution)/shard_map/ppermute | solution.py:536
  13.7 1.3 %collective-permute-done.5.refs_0_ = bf16[16,1024]{1,0:T(8,128)(2,1)S(1)} collective-permute-done((bf16[16,1024]{1,0:T(8,128)(2,1)S(1)}, bf16[16,1024]{1,0:T(8,128)(2,1)S(1)}, u32[]{:S(2)}, u32[]{:S(2)}) %collective-permute-start.5) | collective-permute-done | bytes 32800 | tf_op jit(solution)/shard_map/ppermute | solution.py:536
  15.0 1.0 %collective-permute-done.6.refs_1_ = bf16[16,1024]{1,0:T(8,128)(2,1)S(1)} collective-permute-done((bf16[16,1024]{1,0:T(8,128)(2,1)S(1)}, bf16[16,1024]{1,0:T(8,128)(2,1)S(1)}, u32[]{:S(2)}, u32[]{:S(2)}) %collective-permute-start.6) | collective-permute-done | bytes 32800 | tf_op jit(solution)/shard_map/ppermute | solution.py:536
  16.0 0.0 collective-permute-done.7.refs_2_
  16.0 0.7 %shard_map.42 = f32[4,4,1024]{2,1,0:T(4,128)} custom-call(bf16[16,1024]{1,0:T(8,128)(2,1)S(1)} %collective-permute-done.5.refs_0_, bf16[16,1024]{1,0:T(8,128)(2,1)S(1)} %collective-permute-done.6.refs_1_, bf16[16,1024]{1,0:T(8,128)(2,1)S(1)} %collective-permute-done.7.refs_2_, f32[16,1024]{1,0:T(8,128)S(1)} %get-tuple-element.36.refs_3_), custom_call_target="tpu_custom_call" | custom-call | tf_op jit(solution)/shard_map/pallas_call | solution.py:480
Async XLA Ops:
  0.0 5.1 %copy-start = (s32[2,8,32,1024]{3,2,1,0:T(8,128)S(1)}, s32[2,8,32,1024]{3,2,1,0:T(8,128)}, u32[]{:S(2)}) copy-start(s32[2,8,32,1024]{3,2,1,0:T(8,128)} %volume_ref.7) | copy-start | bytes 6291460
  0.0 5.1 %copy-start.2 = (s32[256]{0:T(256)S(1)}, s32[256]{0:T(256)}, u32[]{:S(2)}) copy-start(s32[256]{0:T(256)} %param.5) | copy-start | bytes 3076
  0.0 5.1 %copy-start.1 = (s32[3,256]{1,0:T(4,128)S(1)}, s32[3,256]{1,0:T(4,128)}, u32[]{:S(2)}) copy-start(s32[3,256]{1,0:T(4,128)} %color_ref.1) | copy-start | bytes 9220
  1.2 6.4 %collective-permute-start = (bf16[32,1024]{1,0:T(8,128)(2,1)S(1)}, bf16[32,1024]{1,0:T(8,128)(2,1)S(1)}, u32[]{:S(2)}, u32[]{:S(2)}) collective-permute-start(bf16[32,1024]{1,0:T(8,128)(2,1)S(1)} %get-tuple-element.25), channel_id=1, source_target_pairs={{0,28},{1,5},{2,30},{3,7},{4,8},{5,1},{6,10},{7,3},{8,4},{9,13},{1... | collective-permute-start | bytes 196616 | tf_op jit(solution)/shard_map/ppermute | solution.py:532
  4.6 4.3 %collective-permute-start.1 = (bf16[32,1024]{1,0:T(8,128)(2,1)S(1)}, bf16[32,1024]{1,0:T(8,128)(2,1)S(1)}, u32[]{:S(2)}, u32[]{:S(2)}) collective-permute-start(bf16[32,1024]{1,0:T(8,128)(2,1)S(1)} %get-tuple-element.28), channel_id=1, source_target_pairs={{0,1},{1,0},{2,3},{3,2},{4,5},{5,4},{6,7},{7,6},{8,9},{9,8},{10,11... | collective-permute-start | bytes 196616 | tf_op jit(solution)/shard_map/ppermute | solution.py:532
  4.6 4.3 %collective-permute-start.2 = (bf16[32,1024]{1,0:T(8,128)(2,1)S(1)}, bf16[32,1024]{1,0:T(8,128)(2,1)S(1)}, u32[]{:S(2)}, u32[]{:S(2)}) collective-permute-start(bf16[32,1024]{1,0:T(8,128)(2,1)S(1)} %get-tuple-element.29), channel_id=1, source_target_pairs={{0,4},{1,29},{2,6},{3,31},{4,0},{5,9},{6,2},{7,11},{8,12},{9,5},{1... | collective-permute-start | bytes 196616 | tf_op jit(solution)/shard_map/ppermute | solution.py:532
  4.6 3.2 %collective-permute-start.3 = (bf16[8,1024]{1,0:T(8,128)(2,1)S(1)}, bf16[8,1024]{1,0:T(8,128)(2,1)S(1)}, u32[]{:S(2)}, u32[]{:S(2)}) collective-permute-start(bf16[8,1024]{1,0:T(8,128)(2,1)S(1)} %get-tuple-element.30), channel_id=1, source_target_pairs={{0,4},{1,2},{2,1},{3,7},{4,0},{5,6},{6,5},{7,3},{8,12},{9,10},{10,... | collective-permute-start | bytes 49160 | tf_op jit(solution)/shard_map/ppermute | solution.py:532
  9.2 1.4 %collective-permute-start.4 = (bf16[4,16,1024]{2,1,0:T(8,128)(2,1)S(1)}, bf16[4,16,1024]{2,1,0:T(8,128)(2,1)S(1)}, u32[]{:S(2)}, u32[]{:S(2)}) collective-permute-start(bf16[4,16,1024]{2,1,0:T(8,128)(2,1)S(1)} %get-tuple-element.32), channel_id=1, source_target_pairs={{0,4},{4,0},{8,12},{12,8},{16,20},{20,16},{24,28},{28,24},{1,5},{5... | collective-permute-start | bytes 393224 | tf_op jit(solution)/shard_map/ppermute | solution.py:536
  10.6 4.4 %collective-permute-start.5 = (bf16[16,1024]{1,0:T(8,128)(2,1)S(1)}, bf16[16,1024]{1,0:T(8,128)(2,1)S(1)}, u32[]{:S(2)}, u32[]{:S(2)}) collective-permute-start(bf16[16,1024]{1,0:T(8,128)(2,1)S(1)} %get-tuple-element.33), channel_id=1, source_target_pairs={{0,28},{4,24},{8,20},{12,16},{16,12},{20,8},{24,4},{28,0},{1,29},{... | collective-permute-start | bytes 98312 | tf_op jit(solution)/shard_map/ppermute | solution.py:536
  11.7 4.3 %collective-permute-start.6 = (bf16[16,1024]{1,0:T(8,128)(2,1)S(1)}, bf16[16,1024]{1,0:T(8,128)(2,1)S(1)}, u32[]{:S(2)}, u32[]{:S(2)}) collective-permute-start(bf16[16,1024]{1,0:T(8,128)(2,1)S(1)} %get-tuple-element.34), channel_id=1, source_target_pairs={{0,20},{4,16},{8,28},{12,24},{16,4},{20,0},{24,12},{28,8},{1,21},{... | collective-permute-start | bytes 98312 | tf_op jit(solution)/shard_map/ppermute | solution.py:536
  12.2 3.8 %collective-permute-start.7 = (bf16[16,1024]{1,0:T(8,128)(2,1)S(1)}, bf16[16,1024]{1,0:T(8,128)(2,1)S(1)}, u32[]{:S(2)}, u32[]{:S(2)}) collective-permute-start(bf16[16,1024]{1,0:T(8,128)(2,1)S(1)} %get-tuple-element.35), channel_id=1, source_target_pairs={{0,12},{4,8},{8,4},{12,0},{16,28},{20,24},{24,20},{28,16},{1,13},{... | collective-permute-start | bytes 98312 | tf_op jit(solution)/shard_map/ppermute | solution.py:536

commit v14 on v12

--- a/solution.py
+++ b/solution.py
@@ -48,7 +48,7 @@
         list(plane_copies(1, (1 - last_first) * (slices - 1))),
         [strip_copy(1, odd_row * (height - 1))],
     ]
-    for group in copies:
+    for group in (copies[1], copies[3], copies[0], copies[2]):
         for copy in group:
             copy.start()
 
@@ -64,10 +64,10 @@
 
     arrive(copies[0])
     first_out[...] = narrow(plane_ref[0])
+    arrive(copies[2])
+    second_out[...] = narrow(plane_ref[1])
     arrive(copies[1])
     rows_near_out[...] = padded(strip_ref[0])
-    arrive(copies[2])
-    second_out[...] = narrow(plane_ref[1])
     arrive(copies[3])
     rows_far_out[...] = narrow(strip_ref[1])
 
@@ -491,28 +491,36 @@
     )(side)
 
 
-def gather_kernel(side_ref, cross_ref, passed_ref, own_ref, out_ref):
-    share = out_ref.shape[1]
+def gather_kernel(side_ref, cross_ref, passed_ref, own_ref, out_ref, plane_ref, sems):
+    _, share, columns = out_ref.shape
     chip, core, mask = route()
     odd, serves_x = core == 1, mask == 1
-    side, passed = side_ref[0].astype(jnp.float32), passed_ref[...].astype(jnp.float32)
-    parts = [
-        own_ref[...],
-        jnp.where(serves_x, side, passed),
-        jnp.where(serves_x, passed, side),
-        cross_ref[...].astype(jnp.float32),
-    ]
-    step = 1
-    while len(parts) > 1:
-        swap = (chip & step) != 0
+    half = columns // 2
+    copies = []
+    for h in range(2):
+        here = pl.ds(h * half, half)
+        side, passed = side_ref[0, :, here].astype(jnp.float32), passed_ref[:, here].astype(jnp.float32)
         parts = [
-            over(jnp.where(swap, parts[i + 1], parts[i]), jnp.where(swap, parts[i], parts[i + 1]), odd)
-            for i in range(0, len(parts), 2)
+            own_ref[:, here],
+            jnp.where(serves_x, side, passed),
+            jnp.where(serves_x, passed, side),
+            cross_ref[:, here].astype(jnp.float32),
         ]
-        step *= 2
-    planes = [parts[0][c * share : (c + 1) * share] for c in range(4)]
-    for c in range(4):
-        out_ref[c] = jnp.where(odd, planes[c ^ 1], planes[c])
+        step = 1
+        while len(parts) > 1:
+            swap = (chip & step) != 0
+            parts = [
+                over(jnp.where(swap, parts[i + 1], parts[i]), jnp.where(swap, parts[i], parts[i + 1]), odd)
+                for i in range(0, len(parts), 2)
+            ]
+            step *= 2
+        planes = [parts[0][c * share : (c + 1) * share] for c in range(4)]
+        for c in range(4):
+            plane_ref[c, :, here] = jnp.where(odd, planes[c ^ 1], planes[c])
+        copies.append(pltpu.make_async_copy(plane_ref.at[:, :, here], out_ref.at[:, :, here], sems.at[h]))
+        copies[h].start()
+    for copy in copies:
+        copy.wait()
 
 
 def gather(parts, share):
@@ -520,8 +528,9 @@
     return pl.pallas_call(
         gather_kernel,
         in_specs=[WHOLE] * len(parts),
-        out_specs=WHOLE,
+        out_specs=pl.BlockSpec(memory_space=pl.ANY),
         out_shape=jax.ShapeDtypeStruct((4, share, columns), jnp.float32),
+        scratch_shapes=[pltpu.VMEM((4, share, columns), jnp.float32), pltpu.SemaphoreType.DMA((2,))],
         compiler_params=pltpu.CompilerParams(vmem_limit_bytes=4 * 1024 * 1024),
     )(*parts)
 

time: 16.8 us -> 16.8 us (level)
  no operation moved by 1% of the time
where the time goes in v14:
time: 16.8 us; the launch traced here: 16.6 us
  starting transfers between devices  7.18 us (43%)
  Pallas kernels  4.95 us (29%)
  waiting for transfers between devices  4.43 us (26%)
    ppermute x4, waiting for transfers between devices, exchanged(): lax.ppermute(values, 'depth', [(d, d ^ m) for d, m in enumerate(masks)])  4.42 us
    ppermute x4, starting transfers between devices, exchanged(): lax.ppermute(values, 'depth', [(d, d ^ m) for d, m in enumerate(masks)])  3.63 us
    ppermute x4, starting transfers between devices, swapped(): return lax.ppermute(values, ('depth', 'rows'), perm)  3.55 us
    pallas_call x1, Pallas kernels, march_interior(): pl.pallas_call(functools.partial(interior_kernel, opacity_scale), in_spec...  2.46 us
    pallas_call x1, Pallas kernels, cut_edges(): pl.pallas_call(edges_kernel, in_specs=[pl.BlockSpec(memory_space=pl.ANY)]...  1.19 us
    pallas_call x1, Pallas kernels, gather(): pl.pallas_call(gather_kernel, in_specs=[WHOLE] * len(parts), out_specs=pl...  0.71 us
  transfers between devices with their start and end apart: 8, of which 4 were waited for; matrix products, arithmetic and copies ran while one was open for 0% of the time, Pallas kernels for 16%

profile of v14, /device:TPU:25, one launch (start us, length us, event | category | flops | bytes accessed | tf_op | source)
XLA Modules:
  0.0 16.6 jit_solution(7288579289934235876)
XLA Ops:
  0.0 0.0 copy-start
  0.0 0.0 copy-start.2
  0.0 0.0 copy-start.1
  0.0 1.2 %shard_map.38 = (bf16[32,1024]{1,0:T(8,128)(2,1)S(1)}, bf16[32,1024]{1,0:T(8,128)(2,1)S(1)}, bf16[32,1024]{1,0:T(8,128)(2,1)S(1)}, bf16[8,1024]{1,0:T(8,128)(2,1)S(1)}) custom-call(s32[2,8,32,1024]{3,2,1,0:T(8,128)} %volume_ref.7), custom_call_target="tpu_custom_call" | custom-call | tf_op jit(solution)/shard_map/pallas_call | solution.py:79
  1.2 0.7 %collective-permute-start = (bf16[32,1024]{1,0:T(8,128)(2,1)S(1)}, bf16[32,1024]{1,0:T(8,128)(2,1)S(1)}, u32[]{:S(2)}, u32[]{:S(2)}) collective-permute-start(bf16[32,1024]{1,0:T(8,128)(2,1)S(1)} %get-tuple-element.24), channel_id=1, source_target_pairs={{0,28},{1,5},{2,30},{3,7},{4,8},{5,1},{6,10},{7,3},{8,4},{9,13},{1... | collective-permute-start | bytes 196616 | tf_op jit(solution)/shard_map/ppermute | solution.py:581
  2.0 1.3 %collective-permute-start.1 = (bf16[32,1024]{1,0:T(8,128)(2,1)S(1)}, bf16[32,1024]{1,0:T(8,128)(2,1)S(1)}, u32[]{:S(2)}, u32[]{:S(2)}) collective-permute-start(bf16[32,1024]{1,0:T(8,128)(2,1)S(1)} %get-tuple-element.27), channel_id=1, source_target_pairs={{0,1},{1,0},{2,3},{3,2},{4,5},{5,4},{6,7},{7,6},{8,9},{9,8},{10,11... | collective-permute-start | bytes 196616 | tf_op jit(solution)/shard_map/ppermute | solution.py:581
  3.2 0.4 %collective-permute-start.2 = (bf16[32,1024]{1,0:T(8,128)(2,1)S(1)}, bf16[32,1024]{1,0:T(8,128)(2,1)S(1)}, u32[]{:S(2)}, u32[]{:S(2)}) collective-permute-start(bf16[32,1024]{1,0:T(8,128)(2,1)S(1)} %get-tuple-element.28), channel_id=1, source_target_pairs={{0,4},{1,29},{2,6},{3,31},{4,0},{5,9},{6,2},{7,11},{8,12},{9,5},{1... | collective-permute-start | bytes 196616 | tf_op jit(solution)/shard_map/ppermute | solution.py:581
  3.6 1.2 %collective-permute-start.3 = (bf16[8,1024]{1,0:T(8,128)(2,1)S(1)}, bf16[8,1024]{1,0:T(8,128)(2,1)S(1)}, u32[]{:S(2)}, u32[]{:S(2)}) collective-permute-start(bf16[8,1024]{1,0:T(8,128)(2,1)S(1)} %get-tuple-element.29), channel_id=1, source_target_pairs={{0,4},{1,2},{2,1},{3,7},{4,0},{5,6},{6,5},{7,3},{8,12},{9,10},{10,... | collective-permute-start | bytes 49160 | tf_op jit(solution)/shard_map/ppermute | solution.py:581
  4.8 0.0 copy-done
  4.8 0.0 copy-done.2
  4.8 0.0 copy-done.1
  4.8 2.5 %shard_map.37 = (f32[4,32,1024]{2,1,0:T(8,128)S(1)}, f32[2,32,1024]{2,1,0:T(8,128)S(1)}, f32[2,32,1024]{2,1,0:T(8,128)S(1)}, f32[2,3,32,1024]{3,2,1,0:T(8,128)S(...) custom-call(s32[2,8,32,1024]{3,2,1,0:T(8,128)S(1)} %copy-done, s32[3,256]{1,0:T(4,128)S(1)} %copy-done.1, ...), custom_call_target="tpu_custom_call" | custom-call | flops 20971520 | bytes 5242880 | tf_op jit(solution)/shard_map/pallas_call | solution.py:275
  7.2 0.0 collective-permute-done.first_ref
  7.2 0.2 %shard_map.39.sums_ref = f32[3,32,1024]{2,1,0:T(8,128)S(1)} custom-call(s32[2,8,32,1024]{3,2,1,0:T(8,128)S(1)} %copy-done, f32[4,32,1024]{2,1,0:T(8,128)S(1)} %get-tuple-element.20.base_ref, f32[2,32,1024]{2,1,0:T(8,128)S(1)} %get-tuple-element.21.face_ref, f32[2,32,1024]{2,1,0:T(8,128)S(1)} %get-tuple-element.22.square_ref, ...), custom_call_target="tpu_custom_call" | custom-call | flops 2621440 | bytes 1572864 | tf_op jit(solution)/shard_map/pallas_call | solution.py:332
  7.5 0.0 collective-permute-done.3.rows_far_ref
  7.5 0.0 collective-permute-done.1.rows_near_ref
  7.5 0.0 collective-permute-done.2.second_ref
  7.5 0.3 %shard_map.40 = (f32[4,2,16,1024]{3,2,1,0:T(8,128)S(1)}, bf16[4,16,1024]{2,1,0:T(8,128)(2,1)S(1)}) custom-call(s32[2,8,32,1024]{3,2,1,0:T(8,128)S(1)} %copy-done, f32[3,32,1024]{2,1,0:T(8,128)S(1)} %shard_map.39.sums_ref, f32[4,32,1024]{2,1,0:T(8,128)S(1)} %get-tuple-element.20.base_ref, f32[2,32,1024]{2,1,0:T(8,128)S(1)} %get-tuple-element.21.face_ref, ...), custom_call_target="tpu_custom_call" | custom-call | tf_op jit(solution)/shard_map/pallas_call | solution.py:426
  7.8 1.8 %collective-permute-start.4 = (bf16[4,16,1024]{2,1,0:T(8,128)(2,1)S(1)}, bf16[4,16,1024]{2,1,0:T(8,128)(2,1)S(1)}, u32[]{:S(2)}, u32[]{:S(2)}) collective-permute-start(bf16[4,16,1024]{2,1,0:T(8,128)(2,1)S(1)} %get-tuple-element.31), channel_id=1, source_target_pairs={{0,4},{4,0},{8,12},{12,8},{16,20},{20,16},{24,28},{28,24},{1,5},{5... | collective-permute-start | bytes 393224 | tf_op jit(solution)/shard_map/ppermute | solution.py:586
  9.6 1.0 %collective-permute-done.4.other_ref = bf16[4,16,1024]{2,1,0:T(8,128)(2,1)S(1)} collective-permute-done((bf16[4,16,1024]{2,1,0:T(8,128)(2,1)S(1)}, bf16[4,16,1024]{2,1,0:T(8,128)(2,1)S(1)}, u32[]{:S(2)}, u32[]{:S(2)}) %collective-permute-start.4) | collective-permute-done | bytes 131104 | tf_op jit(solution)/shard_map/ppermute | solution.py:586
  10.6 0.1 shard_map.41
  10.7 0.5 %collective-permute-start.5 = (bf16[2,16,1024]{2,1,0:T(8,128)(2,1)S(1)}, bf16[2,16,1024]{2,1,0:T(8,128)(2,1)S(1)}, u32[]{:S(2)}, u32[]{:S(2)}) collective-permute-start(bf16[2,16,1024]{2,1,0:T(8,128)(2,1)S(1)} %get-tuple-element.32), channel_id=1, source_target_pairs={{0,12},{4,16},{8,28},{12,0},{16,4},{20,24},{24,20},{28,8},{1,13},{... | collective-permute-start | bytes 196616 | tf_op jit(solution)/shard_map/ppermute | solution.py:586
  11.2 1.2 %collective-permute-start.6 = (bf16[16,1024]{1,0:T(8,128)(2,1)S(1)}, bf16[16,1024]{1,0:T(8,128)(2,1)S(1)}, u32[]{:S(2)}, u32[]{:S(2)}) collective-permute-start(bf16[16,1024]{1,0:T(8,128)(2,1)S(1)} %get-tuple-element.33), channel_id=1, source_target_pairs={{0,28},{4,24},{8,20},{12,16},{16,12},{20,8},{24,4},{28,0},{1,29},{... | collective-permute-start | bytes 98312 | tf_op jit(solution)/shard_map/ppermute | solution.py:586
  12.4 2.3 %collective-permute-done.5.side_ref = bf16[2,16,1024]{2,1,0:T(8,128)(2,1)S(1)} collective-permute-done((bf16[2,16,1024]{2,1,0:T(8,128)(2,1)S(1)}, bf16[2,16,1024]{2,1,0:T(8,128)(2,1)S(1)}, u32[]{:S(2)}, u32[]{:S(2)}) %collective-permute-start.5) | collective-permute-done | bytes 65568 | tf_op jit(solution)/shard_map/ppermute | solution.py:586
  14.7 0.1 collective-permute-start.7
  14.8 0.7 %collective-permute-done.6.cross_ref = bf16[16,1024]{1,0:T(8,128)(2,1)S(1)} collective-permute-done((bf16[16,1024]{1,0:T(8,128)(2,1)S(1)}, bf16[16,1024]{1,0:T(8,128)(2,1)S(1)}, u32[]{:S(2)}, u32[]{:S(2)}) %collective-permute-start.6) | collective-permute-done | bytes 32800 | tf_op jit(solution)/shard_map/ppermute | solution.py:586
  15.4 0.5 %collective-permute-done.7.passed_ref = bf16[16,1024]{1,0:T(8,128)(2,1)S(1)} collective-permute-done((bf16[16,1024]{1,0:T(8,128)(2,1)S(1)}, bf16[16,1024]{1,0:T(8,128)(2,1)S(1)}, u32[]{:S(2)}, u32[]{:S(2)}) %collective-permute-start.7) | collective-permute-done | bytes 32800 | tf_op jit(solution)/shard_map/ppermute | solution.py:586
  15.9 0.7 %shard_map.43 = f32[4,4,1024]{2,1,0:T(4,128)} custom-call(bf16[2,16,1024]{2,1,0:T(8,128)(2,1)S(1)} %collective-permute-done.5.side_ref, bf16[16,1024]{1,0:T(8,128)(2,1)S(1)} %collective-permute-done.6.cross_ref, bf16[16,1024]{1,0:T(8,128)(2,1)S(1)} %collective-permute-done.7.passed_ref, f32[16,1024]{1,0:T(8,128)S(1)} %get-tuple-element.34.own_ref), custom_call_target="tpu_custom_call" | custom-call | tf_op jit(solution)/shard_map/pallas_call | solution.py:528
  (1 shorter events, 0.0 us)
Async XLA Ops:
  0.0 4.8 %copy-start = (s32[2,8,32,1024]{3,2,1,0:T(8,128)S(1)}, s32[2,8,32,1024]{3,2,1,0:T(8,128)}, u32[]{:S(2)}) copy-start(s32[2,8,32,1024]{3,2,1,0:T(8,128)} %volume_ref.7) | copy-start | bytes 6291460
  0.0 4.8 %copy-start.2 = (s32[256]{0:T(256)S(1)}, s32[256]{0:T(256)}, u32[]{:S(2)}) copy-start(s32[256]{0:T(256)} %param.5) | copy-start | bytes 3076
  0.0 4.8 %copy-start.1 = (s32[3,256]{1,0:T(4,128)S(1)}, s32[3,256]{1,0:T(4,128)}, u32[]{:S(2)}) copy-start(s32[3,256]{1,0:T(4,128)} %color_ref.1) | copy-start | bytes 9220
  1.2 6.0 %collective-permute-start = (bf16[32,1024]{1,0:T(8,128)(2,1)S(1)}, bf16[32,1024]{1,0:T(8,128)(2,1)S(1)}, u32[]{:S(2)}, u32[]{:S(2)}) collective-permute-start(bf16[32,1024]{1,0:T(8,128)(2,1)S(1)} %get-tuple-element.24), channel_id=1, source_target_pairs={{0,28},{1,5},{2,30},{3,7},{4,8},{5,1},{6,10},{7,3},{8,4},{9,13},{1... | collective-permute-start | bytes 196616 | tf_op jit(solution)/shard_map/ppermute | solution.py:581
  2.0 5.5 %collective-permute-start.1 = (bf16[32,1024]{1,0:T(8,128)(2,1)S(1)}, bf16[32,1024]{1,0:T(8,128)(2,1)S(1)}, u32[]{:S(2)}, u32[]{:S(2)}) collective-permute-start(bf16[32,1024]{1,0:T(8,128)(2,1)S(1)} %get-tuple-element.27), channel_id=1, source_target_pairs={{0,1},{1,0},{2,3},{3,2},{4,5},{5,4},{6,7},{7,6},{8,9},{9,8},{10,11... | collective-permute-start | bytes 196616 | tf_op jit(solution)/shard_map/ppermute | solution.py:581
  3.2 4.3 %collective-permute-start.2 = (bf16[32,1024]{1,0:T(8,128)(2,1)S(1)}, bf16[32,1024]{1,0:T(8,128)(2,1)S(1)}, u32[]{:S(2)}, u32[]{:S(2)}) collective-permute-start(bf16[32,1024]{1,0:T(8,128)(2,1)S(1)} %get-tuple-element.28), channel_id=1, source_target_pairs={{0,4},{1,29},{2,6},{3,31},{4,0},{5,9},{6,2},{7,11},{8,12},{9,5},{1... | collective-permute-start | bytes 196616 | tf_op jit(solution)/shard_map/ppermute | solution.py:581
  3.6 3.9 %collective-permute-start.3 = (bf16[8,1024]{1,0:T(8,128)(2,1)S(1)}, bf16[8,1024]{1,0:T(8,128)(2,1)S(1)}, u32[]{:S(2)}, u32[]{:S(2)}) collective-permute-start(bf16[8,1024]{1,0:T(8,128)(2,1)S(1)} %get-tuple-element.29), channel_id=1, source_target_pairs={{0,4},{1,2},{2,1},{3,7},{4,0},{5,6},{6,5},{7,3},{8,12},{9,10},{10,... | collective-permute-start | bytes 49160 | tf_op jit(solution)/shard_map/ppermute | solution.py:581
  7.8 2.8 %collective-permute-start.4 = (bf16[4,16,1024]{2,1,0:T(8,128)(2,1)S(1)}, bf16[4,16,1024]{2,1,0:T(8,128)(2,1)S(1)}, u32[]{:S(2)}, u32[]{:S(2)}) collective-permute-start(bf16[4,16,1024]{2,1,0:T(8,128)(2,1)S(1)} %get-tuple-element.31), channel_id=1, source_target_pairs={{0,4},{4,0},{8,12},{12,8},{16,20},{20,16},{24,28},{28,24},{1,5},{5... | collective-permute-start | bytes 393224 | tf_op jit(solution)/shard_map/ppermute | solution.py:586
  10.7 4.1 %collective-permute-start.5 = (bf16[2,16,1024]{2,1,0:T(8,128)(2,1)S(1)}, bf16[2,16,1024]{2,1,0:T(8,128)(2,1)S(1)}, u32[]{:S(2)}, u32[]{:S(2)}) collective-permute-start(bf16[2,16,1024]{2,1,0:T(8,128)(2,1)S(1)} %get-tuple-element.32), channel_id=1, source_target_pairs={{0,12},{4,16},{8,28},{12,0},{16,4},{20,24},{24,20},{28,8},{1,13},{... | collective-permute-start | bytes 196616 | tf_op jit(solution)/shard_map/ppermute | solution.py:586
  11.2 4.2 %collective-permute-start.6 = (bf16[16,1024]{1,0:T(8,128)(2,1)S(1)}, bf16[16,1024]{1,0:T(8,128)(2,1)S(1)}, u32[]{:S(2)}, u32[]{:S(2)}) collective-permute-start(bf16[16,1024]{1,0:T(8,128)(2,1)S(1)} %get-tuple-element.33), channel_id=1, source_target_pairs={{0,28},{4,24},{8,20},{12,16},{16,12},{20,8},{24,4},{28,0},{1,29},{... | collective-permute-start | bytes 98312 | tf_op jit(solution)/shard_map/ppermute | solution.py:586
  14.7 1.2 %collective-permute-start.7 = (bf16[16,1024]{1,0:T(8,128)(2,1)S(1)}, bf16[16,1024]{1,0:T(8,128)(2,1)S(1)}, u32[]{:S(2)}, u32[]{:S(2)}) collective-permute-start(bf16[16,1024]{1,0:T(8,128)(2,1)S(1)} %shard_map.42), channel_id=1, source_target_pairs={{0,4},{4,0},{8,12},{12,8},{16,20},{20,16},{24,28},{28,24},{1,5},{5... | collective-permute-start | bytes 98312 | tf_op jit(solution)/shard_map/ppermute | solution.py:586

commit v15 on v12

--- a/solution.py
+++ b/solution.py
@@ -434,7 +434,7 @@
 
 def served(depth):
     chip, core = depth // 2, depth % 2
-    return 1 + (core ^ (chip & 1) ^ (chip >> 1))
+    return 2 - (core ^ (chip & 1) ^ (chip >> 1))
 
 
 def route():

time: 16.8 us -> 17.1 us (1.018)
  waiting for transfers between devices: 4.43 us -> 4.95 us
    ppermute x4, waiting for transfers between devices: 4.42 us -> 4.94 us  [exchanged(): lax.ppermute(values, 'depth', [(d, d ^ m) for d, m in enumerate(masks)])]
where the time goes in v15:
time: 17.1 us; the launch traced here: 17 us
  starting transfers between devices  7.01 us (41%)
  waiting for transfers between devices  4.95 us (29%)
  Pallas kernels  4.92 us (29%)
    ppermute x4, waiting for transfers between devices, exchanged(): lax.ppermute(values, 'depth', [(d, d ^ m) for d, m in enumerate(masks)])  4.94 us
    ppermute x4, starting transfers between devices, swapped(): return lax.ppermute(values, ('depth', 'rows'), perm)  3.55 us
    ppermute x4, starting transfers between devices, exchanged(): lax.ppermute(values, 'depth', [(d, d ^ m) for d, m in enumerate(masks)])  3.46 us
    pallas_call x1, Pallas kernels, march_interior(): pl.pallas_call(functools.partial(interior_kernel, opacity_scale), in_spec...  2.46 us
    pallas_call x1, Pallas kernels, cut_edges(): pl.pallas_call(edges_kernel, in_specs=[pl.BlockSpec(memory_space=pl.ANY)]...  1.18 us
    pallas_call x1, Pallas kernels, gather(): pl.pallas_call(gather_kernel, in_specs=[WHOLE] * len(parts), out_specs=WH...  0.7 us
  transfers between devices with their start and end apart: 8, of which 4 were waited for; matrix products, arithmetic and copies ran while one was open for 0% of the time, Pallas kernels for 16%

profile of v15, /device:TPU:25, one launch (start us, length us, event | category | flops | bytes accessed | tf_op | source)
XLA Modules:
  0.0 17.0 jit_solution(4333329318619236293)
XLA Ops:
  0.0 0.0 copy-start
  0.0 0.0 copy-start.2
  0.0 0.0 copy-start.1
  0.0 1.2 %shard_map.38 = (bf16[32,1024]{1,0:T(8,128)(2,1)S(1)}, bf16[32,1024]{1,0:T(8,128)(2,1)S(1)}, bf16[32,1024]{1,0:T(8,128)(2,1)S(1)}, bf16[8,1024]{1,0:T(8,128)(2,1)S(1)}) custom-call(s32[2,8,32,1024]{3,2,1,0:T(8,128)} %volume_ref.7), custom_call_target="tpu_custom_call" | custom-call | tf_op jit(solution)/shard_map/pallas_call | solution.py:79
  1.2 0.7 %collective-permute-start = (bf16[32,1024]{1,0:T(8,128)(2,1)S(1)}, bf16[32,1024]{1,0:T(8,128)(2,1)S(1)}, u32[]{:S(2)}, u32[]{:S(2)}) collective-permute-start(bf16[32,1024]{1,0:T(8,128)(2,1)S(1)} %get-tuple-element.24), channel_id=1, source_target_pairs={{0,28},{1,5},{2,30},{3,7},{4,8},{5,1},{6,10},{7,3},{8,4},{9,13},{1... | collective-permute-start | bytes 196616 | tf_op jit(solution)/shard_map/ppermute | solution.py:572
  1.9 1.3 %collective-permute-start.1 = (bf16[32,1024]{1,0:T(8,128)(2,1)S(1)}, bf16[32,1024]{1,0:T(8,128)(2,1)S(1)}, u32[]{:S(2)}, u32[]{:S(2)}) collective-permute-start(bf16[32,1024]{1,0:T(8,128)(2,1)S(1)} %get-tuple-element.27), channel_id=1, source_target_pairs={{0,1},{1,0},{2,3},{3,2},{4,5},{5,4},{6,7},{7,6},{8,9},{9,8},{10,11... | collective-permute-start | bytes 196616 | tf_op jit(solution)/shard_map/ppermute | solution.py:572
  3.2 0.4 %collective-permute-start.2 = (bf16[32,1024]{1,0:T(8,128)(2,1)S(1)}, bf16[32,1024]{1,0:T(8,128)(2,1)S(1)}, u32[]{:S(2)}, u32[]{:S(2)}) collective-permute-start(bf16[32,1024]{1,0:T(8,128)(2,1)S(1)} %get-tuple-element.28), channel_id=1, source_target_pairs={{0,4},{1,29},{2,6},{3,31},{4,0},{5,9},{6,2},{7,11},{8,12},{9,5},{1... | collective-permute-start | bytes 196616 | tf_op jit(solution)/shard_map/ppermute | solution.py:572
  3.6 1.2 %collective-permute-start.3 = (bf16[8,1024]{1,0:T(8,128)(2,1)S(1)}, bf16[8,1024]{1,0:T(8,128)(2,1)S(1)}, u32[]{:S(2)}, u32[]{:S(2)}) collective-permute-start(bf16[8,1024]{1,0:T(8,128)(2,1)S(1)} %get-tuple-element.29), channel_id=1, source_target_pairs={{0,4},{1,2},{2,1},{3,7},{4,0},{5,6},{6,5},{7,3},{8,12},{9,10},{10,... | collective-permute-start | bytes 49160 | tf_op jit(solution)/shard_map/ppermute | solution.py:572
  4.8 0.0 copy-done
  4.8 0.0 copy-done.2
  4.8 0.0 copy-done.1
  4.8 2.5 %shard_map.37 = (f32[4,32,1024]{2,1,0:T(8,128)S(1)}, f32[2,32,1024]{2,1,0:T(8,128)S(1)}, f32[2,32,1024]{2,1,0:T(8,128)S(1)}, f32[2,3,32,1024]{3,2,1,0:T(8,128)S(...) custom-call(s32[2,8,32,1024]{3,2,1,0:T(8,128)S(1)} %copy-done, s32[3,256]{1,0:T(4,128)S(1)} %copy-done.1, ...), custom_call_target="tpu_custom_call" | custom-call | flops 20971520 | bytes 5242880 | tf_op jit(solution)/shard_map/pallas_call | solution.py:275
  7.2 0.0 collective-permute-done.first_ref
  7.2 0.2 %shard_map.39.sums_ref = f32[3,32,1024]{2,1,0:T(8,128)S(1)} custom-call(s32[2,8,32,1024]{3,2,1,0:T(8,128)S(1)} %copy-done, f32[4,32,1024]{2,1,0:T(8,128)S(1)} %get-tuple-element.20.base_ref, f32[2,32,1024]{2,1,0:T(8,128)S(1)} %get-tuple-element.21.face_ref, f32[2,32,1024]{2,1,0:T(8,128)S(1)} %get-tuple-element.22.square_ref, ...), custom_call_target="tpu_custom_call" | custom-call | flops 2621440 | bytes 1572864 | tf_op jit(solution)/shard_map/pallas_call | solution.py:332
  7.5 0.0 collective-permute-done.3.rows_far_ref
  7.5 0.0 collective-permute-done.1.rows_near_ref
  7.5 0.0 collective-permute-done.2.second_ref
  7.5 0.3 %shard_map.40 = (f32[4,2,16,1024]{3,2,1,0:T(8,128)S(1)}, bf16[4,16,1024]{2,1,0:T(8,128)(2,1)S(1)}) custom-call(s32[2,8,32,1024]{3,2,1,0:T(8,128)S(1)} %copy-done, f32[3,32,1024]{2,1,0:T(8,128)S(1)} %shard_map.39.sums_ref, f32[4,32,1024]{2,1,0:T(8,128)S(1)} %get-tuple-element.20.base_ref, f32[2,32,1024]{2,1,0:T(8,128)S(1)} %get-tuple-element.21.face_ref, ...), custom_call_target="tpu_custom_call" | custom-call | tf_op jit(solution)/shard_map/pallas_call | solution.py:426
  7.8 1.8 %collective-permute-start.4 = (bf16[4,16,1024]{2,1,0:T(8,128)(2,1)S(1)}, bf16[4,16,1024]{2,1,0:T(8,128)(2,1)S(1)}, u32[]{:S(2)}, u32[]{:S(2)}) collective-permute-start(bf16[4,16,1024]{2,1,0:T(8,128)(2,1)S(1)} %get-tuple-element.31), channel_id=1, source_target_pairs={{0,4},{4,0},{8,12},{12,8},{16,20},{20,16},{24,28},{28,24},{1,5},{5... | collective-permute-start | bytes 393224 | tf_op jit(solution)/shard_map/ppermute | solution.py:577
  9.6 1.0 %collective-permute-done.4.other_ref = bf16[4,16,1024]{2,1,0:T(8,128)(2,1)S(1)} collective-permute-done((bf16[4,16,1024]{2,1,0:T(8,128)(2,1)S(1)}, bf16[4,16,1024]{2,1,0:T(8,128)(2,1)S(1)}, u32[]{:S(2)}, u32[]{:S(2)}) %collective-permute-start.4) | collective-permute-done | bytes 131104 | tf_op jit(solution)/shard_map/ppermute | solution.py:577
  10.6 0.1 shard_map.41
  10.7 0.2 %collective-permute-start.5 = (bf16[2,16,1024]{2,1,0:T(8,128)(2,1)S(1)}, bf16[2,16,1024]{2,1,0:T(8,128)(2,1)S(1)}, u32[]{:S(2)}, u32[]{:S(2)}) collective-permute-start(bf16[2,16,1024]{2,1,0:T(8,128)(2,1)S(1)} %get-tuple-element.32), channel_id=1, source_target_pairs={{0,20},{4,8},{8,4},{12,24},{16,28},{20,0},{24,12},{28,16},{1,21},{... | collective-permute-start | bytes 196616 | tf_op jit(solution)/shard_map/ppermute | solution.py:577
  10.9 1.4 %collective-permute-start.6 = (bf16[16,1024]{1,0:T(8,128)(2,1)S(1)}, bf16[16,1024]{1,0:T(8,128)(2,1)S(1)}, u32[]{:S(2)}, u32[]{:S(2)}) collective-permute-start(bf16[16,1024]{1,0:T(8,128)(2,1)S(1)} %get-tuple-element.33), channel_id=1, source_target_pairs={{0,28},{4,24},{8,20},{12,16},{16,12},{20,8},{24,4},{28,0},{1,29},{... | collective-permute-start | bytes 98312 | tf_op jit(solution)/shard_map/ppermute | solution.py:577
  12.3 2.8 %collective-permute-done.5.side_ref = bf16[2,16,1024]{2,1,0:T(8,128)(2,1)S(1)} collective-permute-done((bf16[2,16,1024]{2,1,0:T(8,128)(2,1)S(1)}, bf16[2,16,1024]{2,1,0:T(8,128)(2,1)S(1)}, u32[]{:S(2)}, u32[]{:S(2)}) %collective-permute-start.5) | collective-permute-done | bytes 65568 | tf_op jit(solution)/shard_map/ppermute | solution.py:577
  15.1 0.0 collective-permute-start.7
  15.1 0.2 %collective-permute-done.6.cross_ref = bf16[16,1024]{1,0:T(8,128)(2,1)S(1)} collective-permute-done((bf16[16,1024]{1,0:T(8,128)(2,1)S(1)}, bf16[16,1024]{1,0:T(8,128)(2,1)S(1)}, u32[]{:S(2)}, u32[]{:S(2)}) %collective-permute-start.6) | collective-permute-done | bytes 32800 | tf_op jit(solution)/shard_map/ppermute | solution.py:577
  15.3 1.0 %collective-permute-done.7.passed_ref = bf16[16,1024]{1,0:T(8,128)(2,1)S(1)} collective-permute-done((bf16[16,1024]{1,0:T(8,128)(2,1)S(1)}, bf16[16,1024]{1,0:T(8,128)(2,1)S(1)}, u32[]{:S(2)}, u32[]{:S(2)}) %collective-permute-start.7) | collective-permute-done | bytes 32800 | tf_op jit(solution)/shard_map/ppermute | solution.py:577
  16.3 0.7 %shard_map.43 = f32[4,4,1024]{2,1,0:T(4,128)} custom-call(bf16[2,16,1024]{2,1,0:T(8,128)(2,1)S(1)} %collective-permute-done.5.side_ref, bf16[16,1024]{1,0:T(8,128)(2,1)S(1)} %collective-permute-done.6.cross_ref, bf16[16,1024]{1,0:T(8,128)(2,1)S(1)} %collective-permute-done.7.passed_ref, f32[16,1024]{1,0:T(8,128)S(1)} %get-tuple-element.34.own_ref), custom_call_target="tpu_custom_call" | custom-call | tf_op jit(solution)/shard_map/pallas_call | solution.py:520
  (1 shorter events, 0.0 us)
Async XLA Ops:
  0.0 4.8 %copy-start = (s32[2,8,32,1024]{3,2,1,0:T(8,128)S(1)}, s32[2,8,32,1024]{3,2,1,0:T(8,128)}, u32[]{:S(2)}) copy-start(s32[2,8,32,1024]{3,2,1,0:T(8,128)} %volume_ref.7) | copy-start | bytes 6291460
  0.0 4.8 %copy-start.2 = (s32[256]{0:T(256)S(1)}, s32[256]{0:T(256)}, u32[]{:S(2)}) copy-start(s32[256]{0:T(256)} %param.5) | copy-start | bytes 3076
  0.0 4.8 %copy-start.1 = (s32[3,256]{1,0:T(4,128)S(1)}, s32[3,256]{1,0:T(4,128)}, u32[]{:S(2)}) copy-start(s32[3,256]{1,0:T(4,128)} %color_ref.1) | copy-start | bytes 9220
  1.2 6.0 %collective-permute-start = (bf16[32,1024]{1,0:T(8,128)(2,1)S(1)}, bf16[32,1024]{1,0:T(8,128)(2,1)S(1)}, u32[]{:S(2)}, u32[]{:S(2)}) collective-permute-start(bf16[32,1024]{1,0:T(8,128)(2,1)S(1)} %get-tuple-element.24), channel_id=1, source_target_pairs={{0,28},{1,5},{2,30},{3,7},{4,8},{5,1},{6,10},{7,3},{8,4},{9,13},{1... | collective-permute-start | bytes 196616 | tf_op jit(solution)/shard_map/ppermute | solution.py:572
  1.9 5.5 %collective-permute-start.1 = (bf16[32,1024]{1,0:T(8,128)(2,1)S(1)}, bf16[32,1024]{1,0:T(8,128)(2,1)S(1)}, u32[]{:S(2)}, u32[]{:S(2)}) collective-permute-start(bf16[32,1024]{1,0:T(8,128)(2,1)S(1)} %get-tuple-element.27), channel_id=1, source_target_pairs={{0,1},{1,0},{2,3},{3,2},{4,5},{5,4},{6,7},{7,6},{8,9},{9,8},{10,11... | collective-permute-start | bytes 196616 | tf_op jit(solution)/shard_map/ppermute | solution.py:572
  3.2 4.3 %collective-permute-start.2 = (bf16[32,1024]{1,0:T(8,128)(2,1)S(1)}, bf16[32,1024]{1,0:T(8,128)(2,1)S(1)}, u32[]{:S(2)}, u32[]{:S(2)}) collective-permute-start(bf16[32,1024]{1,0:T(8,128)(2,1)S(1)} %get-tuple-element.28), channel_id=1, source_target_pairs={{0,4},{1,29},{2,6},{3,31},{4,0},{5,9},{6,2},{7,11},{8,12},{9,5},{1... | collective-permute-start | bytes 196616 | tf_op jit(solution)/shard_map/ppermute | solution.py:572
  3.6 3.9 %collective-permute-start.3 = (bf16[8,1024]{1,0:T(8,128)(2,1)S(1)}, bf16[8,1024]{1,0:T(8,128)(2,1)S(1)}, u32[]{:S(2)}, u32[]{:S(2)}) collective-permute-start(bf16[8,1024]{1,0:T(8,128)(2,1)S(1)} %get-tuple-element.29), channel_id=1, source_target_pairs={{0,4},{1,2},{2,1},{3,7},{4,0},{5,6},{6,5},{7,3},{8,12},{9,10},{10,... | collective-permute-start | bytes 49160 | tf_op jit(solution)/shard_map/ppermute | solution.py:572
  7.8 2.8 %collective-permute-start.4 = (bf16[4,16,1024]{2,1,0:T(8,128)(2,1)S(1)}, bf16[4,16,1024]{2,1,0:T(8,128)(2,1)S(1)}, u32[]{:S(2)}, u32[]{:S(2)}) collective-permute-start(bf16[4,16,1024]{2,1,0:T(8,128)(2,1)S(1)} %get-tuple-element.31), channel_id=1, source_target_pairs={{0,4},{4,0},{8,12},{12,8},{16,20},{20,16},{24,28},{28,24},{1,5},{5... | collective-permute-start | bytes 393224 | tf_op jit(solution)/shard_map/ppermute | solution.py:577
  10.7 4.4 %collective-permute-start.5 = (bf16[2,16,1024]{2,1,0:T(8,128)(2,1)S(1)}, bf16[2,16,1024]{2,1,0:T(8,128)(2,1)S(1)}, u32[]{:S(2)}, u32[]{:S(2)}) collective-permute-start(bf16[2,16,1024]{2,1,0:T(8,128)(2,1)S(1)} %get-tuple-element.32), channel_id=1, source_target_pairs={{0,20},{4,8},{8,4},{12,24},{16,28},{20,0},{24,12},{28,16},{1,21},{... | collective-permute-start | bytes 196616 | tf_op jit(solution)/shard_map/ppermute | solution.py:577
  10.9 4.4 %collective-permute-start.6 = (bf16[16,1024]{1,0:T(8,128)(2,1)S(1)}, bf16[16,1024]{1,0:T(8,128)(2,1)S(1)}, u32[]{:S(2)}, u32[]{:S(2)}) collective-permute-start(bf16[16,1024]{1,0:T(8,128)(2,1)S(1)} %get-tuple-element.33), channel_id=1, source_target_pairs={{0,28},{4,24},{8,20},{12,16},{16,12},{20,8},{24,4},{28,0},{1,29},{... | collective-permute-start | bytes 98312 | tf_op jit(solution)/shard_map/ppermute | solution.py:577
  15.1 1.2 %collective-permute-start.7 = (bf16[16,1024]{1,0:T(8,128)(2,1)S(1)}, bf16[16,1024]{1,0:T(8,128)(2,1)S(1)}, u32[]{:S(2)}, u32[]{:S(2)}) collective-permute-start(bf16[16,1024]{1,0:T(8,128)(2,1)S(1)} %shard_map.42), channel_id=1, source_target_pairs={{0,4},{4,0},{8,12},{12,8},{16,20},{20,16},{24,28},{28,24},{1,5},{5... | collective-permute-start | bytes 98312 | tf_op jit(solution)/shard_map/ppermute | solution.py:577

commit v16 on v12

--- a/solution.py
+++ b/solution.py
@@ -257,7 +257,7 @@
                 strip_ref[q, c, :, here] = emitted[c] * weight
         return carry
 
-    lax.fori_loop(0, chunks, chunk, 0, unroll=4)
+    lax.fori_loop(0, chunks, chunk, 0, unroll=8)
 
 
 def march_interior(volume, color_map, alpha_map, depth_count):
@@ -325,7 +325,7 @@
                 sums_ref[c, rows, here] = base_ref[c, rows, here] + terms[c]
         return carry
 
-    lax.fori_loop(0, columns // LANES, chunk, 0, unroll=4)
+    lax.fori_loop(0, columns // LANES, chunk, 0, unroll=8)
 
 
 def add_first_plane(volume, base, face, square, lit, first):

time: 16.8 us -> 16.8 us (level)
  starting transfers between devices: 7.18 us -> 7.41 us
  Pallas kernels: 4.92 us -> 4.7 us
    ppermute x4, starting transfers between devices: 3.63 us -> 3.85 us  [exchanged(): lax.ppermute(values, 'depth', [(d, d ^ m) for d, m in enumerate(masks)])]
  transfers between devices with their start and end apart: 8 -> 8, of which waited for: 4 -> 4; matrix products, arithmetic and copies ran while one was open for 0% -> 0% of each run, Pallas kernels for 16% -> 15%
where the time goes in v16:
time: 16.8 us; the launch traced here: 16.6 us
  starting transfers between devices  7.41 us (44%)
  Pallas kernels  4.7 us (28%)
  waiting for transfers between devices  4.44 us (26%)
    ppermute x4, waiting for transfers between devices, exchanged(): lax.ppermute(values, 'depth', [(d, d ^ m) for d, m in enumerate(masks)])  4.42 us
    ppermute x4, starting transfers between devices, exchanged(): lax.ppermute(values, 'depth', [(d, d ^ m) for d, m in enumerate(masks)])  3.85 us
    ppermute x4, starting transfers between devices, swapped(): return lax.ppermute(values, ('depth', 'rows'), perm)  3.55 us
    pallas_call x1, Pallas kernels, march_interior(): pl.pallas_call(functools.partial(interior_kernel, opacity_scale), in_spec...  2.33 us
    pallas_call x1, Pallas kernels, cut_edges(): pl.pallas_call(edges_kernel, in_specs=[pl.BlockSpec(memory_space=pl.ANY)]...  1.18 us
    pallas_call x1, Pallas kernels, gather(): pl.pallas_call(gather_kernel, in_specs=[WHOLE] * len(parts), out_specs=WH...  0.7 us
  transfers between devices with their start and end apart: 8, of which 4 were waited for; matrix products, arithmetic and copies ran while one was open for 0% of the time, Pallas kernels for 15%

profile of v16, /device:TPU:25, one launch (start us, length us, event | category | flops | bytes accessed | tf_op | source)
XLA Modules:
  0.0 16.6 jit_solution(11821277244240347506)
XLA Ops:
  0.0 0.0 copy-start
  0.0 0.0 copy-start.2
  0.0 0.0 copy-start.1
  0.0 1.2 %shard_map.38 = (bf16[32,1024]{1,0:T(8,128)(2,1)S(1)}, bf16[32,1024]{1,0:T(8,128)(2,1)S(1)}, bf16[32,1024]{1,0:T(8,128)(2,1)S(1)}, bf16[8,1024]{1,0:T(8,128)(2,1)S(1)}) custom-call(s32[2,8,32,1024]{3,2,1,0:T(8,128)} %volume_ref.7), custom_call_target="tpu_custom_call" | custom-call | tf_op jit(solution)/shard_map/pallas_call | solution.py:79
  1.2 0.7 %collective-permute-start = (bf16[32,1024]{1,0:T(8,128)(2,1)S(1)}, bf16[32,1024]{1,0:T(8,128)(2,1)S(1)}, u32[]{:S(2)}, u32[]{:S(2)}) collective-permute-start(bf16[32,1024]{1,0:T(8,128)(2,1)S(1)} %get-tuple-element.24), channel_id=1, source_target_pairs={{0,28},{1,5},{2,30},{3,7},{4,8},{5,1},{6,10},{7,3},{8,4},{9,13},{1... | collective-permute-start | bytes 196616 | tf_op jit(solution)/shard_map/ppermute | solution.py:572
  1.9 1.3 %collective-permute-start.1 = (bf16[32,1024]{1,0:T(8,128)(2,1)S(1)}, bf16[32,1024]{1,0:T(8,128)(2,1)S(1)}, u32[]{:S(2)}, u32[]{:S(2)}) collective-permute-start(bf16[32,1024]{1,0:T(8,128)(2,1)S(1)} %get-tuple-element.27), channel_id=1, source_target_pairs={{0,1},{1,0},{2,3},{3,2},{4,5},{5,4},{6,7},{7,6},{8,9},{9,8},{10,11... | collective-permute-start | bytes 196616 | tf_op jit(solution)/shard_map/ppermute | solution.py:572
  3.2 0.4 %collective-permute-start.2 = (bf16[32,1024]{1,0:T(8,128)(2,1)S(1)}, bf16[32,1024]{1,0:T(8,128)(2,1)S(1)}, u32[]{:S(2)}, u32[]{:S(2)}) collective-permute-start(bf16[32,1024]{1,0:T(8,128)(2,1)S(1)} %get-tuple-element.28), channel_id=1, source_target_pairs={{0,4},{1,29},{2,6},{3,31},{4,0},{5,9},{6,2},{7,11},{8,12},{9,5},{1... | collective-permute-start | bytes 196616 | tf_op jit(solution)/shard_map/ppermute | solution.py:572
  3.6 1.2 %collective-permute-start.3 = (bf16[8,1024]{1,0:T(8,128)(2,1)S(1)}, bf16[8,1024]{1,0:T(8,128)(2,1)S(1)}, u32[]{:S(2)}, u32[]{:S(2)}) collective-permute-start(bf16[8,1024]{1,0:T(8,128)(2,1)S(1)} %get-tuple-element.29), channel_id=1, source_target_pairs={{0,4},{1,2},{2,1},{3,7},{4,0},{5,6},{6,5},{7,3},{8,12},{9,10},{10,... | collective-permute-start | bytes 49160 | tf_op jit(solution)/shard_map/ppermute | solution.py:572
  4.8 0.0 copy-done
  4.8 0.0 copy-done.2
  4.8 0.0 copy-done.1
  4.8 2.3 %shard_map.37 = (f32[4,32,1024]{2,1,0:T(8,128)S(1)}, f32[2,32,1024]{2,1,0:T(8,128)S(1)}, f32[2,32,1024]{2,1,0:T(8,128)S(1)}, f32[2,3,32,1024]{3,2,1,0:T(8,128)S(...) custom-call(s32[2,8,32,1024]{3,2,1,0:T(8,128)S(1)} %copy-done, s32[3,256]{1,0:T(4,128)S(1)} %copy-done.1, ...), custom_call_target="tpu_custom_call" | custom-call | flops 20971520 | bytes 5242880 | tf_op jit(solution)/shard_map/pallas_call | solution.py:275
  7.1 0.0 collective-permute-done.first_ref
  7.1 0.1 shard_map.39.sums_ref
  7.2 0.0 collective-permute-done.3.rows_far_ref
  7.3 0.0 collective-permute-done.1.rows_near_ref
  7.3 0.0 collective-permute-done.2.second_ref
  7.3 0.3 %shard_map.40 = (f32[4,2,16,1024]{3,2,1,0:T(8,128)S(1)}, bf16[4,16,1024]{2,1,0:T(8,128)(2,1)S(1)}) custom-call(s32[2,8,32,1024]{3,2,1,0:T(8,128)S(1)} %copy-done, f32[3,32,1024]{2,1,0:T(8,128)S(1)} %shard_map.39.sums_ref, f32[4,32,1024]{2,1,0:T(8,128)S(1)} %get-tuple-element.20.base_ref, f32[2,32,1024]{2,1,0:T(8,128)S(1)} %get-tuple-element.21.face_ref, ...), custom_call_target="tpu_custom_call" | custom-call | tf_op jit(solution)/shard_map/pallas_call | solution.py:426
  7.6 2.0 %collective-permute-start.4 = (bf16[4,16,1024]{2,1,0:T(8,128)(2,1)S(1)}, bf16[4,16,1024]{2,1,0:T(8,128)(2,1)S(1)}, u32[]{:S(2)}, u32[]{:S(2)}) collective-permute-start(bf16[4,16,1024]{2,1,0:T(8,128)(2,1)S(1)} %get-tuple-element.31), channel_id=1, source_target_pairs={{0,4},{4,0},{8,12},{12,8},{16,20},{20,16},{24,28},{28,24},{1,5},{5... | collective-permute-start | bytes 393224 | tf_op jit(solution)/shard_map/ppermute | solution.py:577
  9.6 1.0 %collective-permute-done.4.other_ref = bf16[4,16,1024]{2,1,0:T(8,128)(2,1)S(1)} collective-permute-done((bf16[4,16,1024]{2,1,0:T(8,128)(2,1)S(1)}, bf16[4,16,1024]{2,1,0:T(8,128)(2,1)S(1)}, u32[]{:S(2)}, u32[]{:S(2)}) %collective-permute-start.4) | collective-permute-done | bytes 131104 | tf_op jit(solution)/shard_map/ppermute | solution.py:577
  10.6 0.1 shard_map.41
  10.7 0.5 %collective-permute-start.5 = (bf16[2,16,1024]{2,1,0:T(8,128)(2,1)S(1)}, bf16[2,16,1024]{2,1,0:T(8,128)(2,1)S(1)}, u32[]{:S(2)}, u32[]{:S(2)}) collective-permute-start(bf16[2,16,1024]{2,1,0:T(8,128)(2,1)S(1)} %get-tuple-element.32), channel_id=1, source_target_pairs={{0,12},{4,16},{8,28},{12,0},{16,4},{20,24},{24,20},{28,8},{1,13},{... | collective-permute-start | bytes 196616 | tf_op jit(solution)/shard_map/ppermute | solution.py:577
  11.2 1.2 %collective-permute-start.6 = (bf16[16,1024]{1,0:T(8,128)(2,1)S(1)}, bf16[16,1024]{1,0:T(8,128)(2,1)S(1)}, u32[]{:S(2)}, u32[]{:S(2)}) collective-permute-start(bf16[16,1024]{1,0:T(8,128)(2,1)S(1)} %get-tuple-element.33), channel_id=1, source_target_pairs={{0,28},{4,24},{8,20},{12,16},{16,12},{20,8},{24,4},{28,0},{1,29},{... | collective-permute-start | bytes 98312 | tf_op jit(solution)/shard_map/ppermute | solution.py:577
  12.4 2.3 %collective-permute-done.5.side_ref = bf16[2,16,1024]{2,1,0:T(8,128)(2,1)S(1)} collective-permute-done((bf16[2,16,1024]{2,1,0:T(8,128)(2,1)S(1)}, bf16[2,16,1024]{2,1,0:T(8,128)(2,1)S(1)}, u32[]{:S(2)}, u32[]{:S(2)}) %collective-permute-start.5) | collective-permute-done | bytes 65568 | tf_op jit(solution)/shard_map/ppermute | solution.py:577
  14.7 0.1 collective-permute-start.7
  14.8 0.7 %collective-permute-done.6.cross_ref = bf16[16,1024]{1,0:T(8,128)(2,1)S(1)} collective-permute-done((bf16[16,1024]{1,0:T(8,128)(2,1)S(1)}, bf16[16,1024]{1,0:T(8,128)(2,1)S(1)}, u32[]{:S(2)}, u32[]{:S(2)}) %collective-permute-start.6) | collective-permute-done | bytes 32800 | tf_op jit(solution)/shard_map/ppermute | solution.py:577
  15.4 0.5 %collective-permute-done.7.passed_ref = bf16[16,1024]{1,0:T(8,128)(2,1)S(1)} collective-permute-done((bf16[16,1024]{1,0:T(8,128)(2,1)S(1)}, bf16[16,1024]{1,0:T(8,128)(2,1)S(1)}, u32[]{:S(2)}, u32[]{:S(2)}) %collective-permute-start.7) | collective-permute-done | bytes 32800 | tf_op jit(solution)/shard_map/ppermute | solution.py:577
  15.9 0.7 %shard_map.43 = f32[4,4,1024]{2,1,0:T(4,128)} custom-call(bf16[2,16,1024]{2,1,0:T(8,128)(2,1)S(1)} %collective-permute-done.5.side_ref, bf16[16,1024]{1,0:T(8,128)(2,1)S(1)} %collective-permute-done.6.cross_ref, bf16[16,1024]{1,0:T(8,128)(2,1)S(1)} %collective-permute-done.7.passed_ref, f32[16,1024]{1,0:T(8,128)S(1)} %get-tuple-element.34.own_ref), custom_call_target="tpu_custom_call" | custom-call | tf_op jit(solution)/shard_map/pallas_call | solution.py:520
  (1 shorter events, 0.0 us)
Async XLA Ops:
  0.0 4.8 %copy-start = (s32[2,8,32,1024]{3,2,1,0:T(8,128)S(1)}, s32[2,8,32,1024]{3,2,1,0:T(8,128)}, u32[]{:S(2)}) copy-start(s32[2,8,32,1024]{3,2,1,0:T(8,128)} %volume_ref.7) | copy-start | bytes 6291460
  0.0 4.8 %copy-start.2 = (s32[256]{0:T(256)S(1)}, s32[256]{0:T(256)}, u32[]{:S(2)}) copy-start(s32[256]{0:T(256)} %param.5) | copy-start | bytes 3076
  0.0 4.8 %copy-start.1 = (s32[3,256]{1,0:T(4,128)S(1)}, s32[3,256]{1,0:T(4,128)}, u32[]{:S(2)}) copy-start(s32[3,256]{1,0:T(4,128)} %color_ref.1) | copy-start | bytes 9220
  1.2 5.9 %collective-permute-start = (bf16[32,1024]{1,0:T(8,128)(2,1)S(1)}, bf16[32,1024]{1,0:T(8,128)(2,1)S(1)}, u32[]{:S(2)}, u32[]{:S(2)}) collective-permute-start(bf16[32,1024]{1,0:T(8,128)(2,1)S(1)} %get-tuple-element.24), channel_id=1, source_target_pairs={{0,28},{1,5},{2,30},{3,7},{4,8},{5,1},{6,10},{7,3},{8,4},{9,13},{1... | collective-permute-start | bytes 196616 | tf_op jit(solution)/shard_map/ppermute | solution.py:572
  1.9 5.3 %collective-permute-start.1 = (bf16[32,1024]{1,0:T(8,128)(2,1)S(1)}, bf16[32,1024]{1,0:T(8,128)(2,1)S(1)}, u32[]{:S(2)}, u32[]{:S(2)}) collective-permute-start(bf16[32,1024]{1,0:T(8,128)(2,1)S(1)} %get-tuple-element.27), channel_id=1, source_target_pairs={{0,1},{1,0},{2,3},{3,2},{4,5},{5,4},{6,7},{7,6},{8,9},{9,8},{10,11... | collective-permute-start | bytes 196616 | tf_op jit(solution)/shard_map/ppermute | solution.py:572
  3.2 4.1 %collective-permute-start.2 = (bf16[32,1024]{1,0:T(8,128)(2,1)S(1)}, bf16[32,1024]{1,0:T(8,128)(2,1)S(1)}, u32[]{:S(2)}, u32[]{:S(2)}) collective-permute-start(bf16[32,1024]{1,0:T(8,128)(2,1)S(1)} %get-tuple-element.28), channel_id=1, source_target_pairs={{0,4},{1,29},{2,6},{3,31},{4,0},{5,9},{6,2},{7,11},{8,12},{9,5},{1... | collective-permute-start | bytes 196616 | tf_op jit(solution)/shard_map/ppermute | solution.py:572
  3.6 3.7 %collective-permute-start.3 = (bf16[8,1024]{1,0:T(8,128)(2,1)S(1)}, bf16[8,1024]{1,0:T(8,128)(2,1)S(1)}, u32[]{:S(2)}, u32[]{:S(2)}) collective-permute-start(bf16[8,1024]{1,0:T(8,128)(2,1)S(1)} %get-tuple-element.29), channel_id=1, source_target_pairs={{0,4},{1,2},{2,1},{3,7},{4,0},{5,6},{6,5},{7,3},{8,12},{9,10},{10,... | collective-permute-start | bytes 49160 | tf_op jit(solution)/shard_map/ppermute | solution.py:572
  7.6 3.0 %collective-permute-start.4 = (bf16[4,16,1024]{2,1,0:T(8,128)(2,1)S(1)}, bf16[4,16,1024]{2,1,0:T(8,128)(2,1)S(1)}, u32[]{:S(2)}, u32[]{:S(2)}) collective-permute-start(bf16[4,16,1024]{2,1,0:T(8,128)(2,1)S(1)} %get-tuple-element.31), channel_id=1, source_target_pairs={{0,4},{4,0},{8,12},{12,8},{16,20},{20,16},{24,28},{28,24},{1,5},{5... | collective-permute-start | bytes 393224 | tf_op jit(solution)/shard_map/ppermute | solution.py:577
  10.7 4.1 %collective-permute-start.5 = (bf16[2,16,1024]{2,1,0:T(8,128)(2,1)S(1)}, bf16[2,16,1024]{2,1,0:T(8,128)(2,1)S(1)}, u32[]{:S(2)}, u32[]{:S(2)}) collective-permute-start(bf16[2,16,1024]{2,1,0:T(8,128)(2,1)S(1)} %get-tuple-element.32), channel_id=1, source_target_pairs={{0,12},{4,16},{8,28},{12,0},{16,4},{20,24},{24,20},{28,8},{1,13},{... | collective-permute-start | bytes 196616 | tf_op jit(solution)/shard_map/ppermute | solution.py:577
  11.2 4.2 %collective-permute-start.6 = (bf16[16,1024]{1,0:T(8,128)(2,1)S(1)}, bf16[16,1024]{1,0:T(8,128)(2,1)S(1)}, u32[]{:S(2)}, u32[]{:S(2)}) collective-permute-start(bf16[16,1024]{1,0:T(8,128)(2,1)S(1)} %get-tuple-element.33), channel_id=1, source_target_pairs={{0,28},{4,24},{8,20},{12,16},{16,12},{20,8},{24,4},{28,0},{1,29},{... | collective-permute-start | bytes 98312 | tf_op jit(solution)/shard_map/ppermute | solution.py:577
  14.7 1.2 %collective-permute-start.7 = (bf16[16,1024]{1,0:T(8,128)(2,1)S(1)}, bf16[16,1024]{1,0:T(8,128)(2,1)S(1)}, u32[]{:S(2)}, u32[]{:S(2)}) collective-permute-start(bf16[16,1024]{1,0:T(8,128)(2,1)S(1)} %shard_map.42), channel_id=1, source_target_pairs={{0,4},{4,0},{8,12},{12,8},{16,20},{20,16},{24,28},{28,24},{1,5},{5... | collective-permute-start | bytes 98312 | tf_op jit(solution)/shard_map/ppermute | solution.py:577

commit v17 on v13

--- a/solution.py
+++ b/solution.py
@@ -257,7 +257,7 @@
                 strip_ref[q, c, :, here] = emitted[c] * weight
         return carry
 
-    lax.fori_loop(0, chunks, chunk, 0, unroll=4)
+    lax.fori_loop(0, chunks, chunk, 0, unroll=8)
 
 
 def march_interior(volume, color_map, alpha_map, depth_count):
@@ -325,7 +325,7 @@
                 sums_ref[c, rows, here] = base_ref[c, rows, here] + terms[c]
         return carry
 
-    lax.fori_loop(0, columns // LANES, chunk, 0, unroll=4)
+    lax.fori_loop(0, columns // LANES, chunk, 0, unroll=8)
 
 
 def add_first_plane(volume, base, face, square, lit, first):

time: 16.8 us -> 16.6 us (0.988)
  the two profiles are of different devices: /device:TPU:0 before, /device:TPU:11 now
where the time goes in v17:
time: 16.6 us; the launch traced here: 16.5 us
  starting transfers between devices  6.86 us (41%)
  waiting for transfers between devices  4.88 us (29%)
  Pallas kernels  4.69 us (28%)
    ppermute x4, waiting for transfers between devices, exchanged(): lax.ppermute(values, 'depth', [(d, d ^ mask) for d in range(lax.axis_size...  4.47 us
    ppermute x4, starting transfers between devices, swapped(): return lax.ppermute(values, ('depth', 'rows'), perm)  3.69 us
    ppermute x4, starting transfers between devices, exchanged(): lax.ppermute(values, 'depth', [(d, d ^ mask) for d in range(lax.axis_size...  3.17 us
    pallas_call x1, Pallas kernels, march_interior(): pl.pallas_call(functools.partial(interior_kernel, opacity_scale), in_spec...  2.33 us
    pallas_call x1, Pallas kernels, cut_edges(): pl.pallas_call(edges_kernel, in_specs=[pl.BlockSpec(memory_space=pl.ANY)]...  1.18 us
    pallas_call x1, Pallas kernels, gather(): pl.pallas_call(gather_kernel, in_specs=[WHOLE] * len(parts), out_specs=WH...  0.7 us
    ppermute x4, waiting for transfers between devices, swapped(): return lax.ppermute(values, ('depth', 'rows'), perm)  0.41 us
  transfers between devices with their start and end apart: 8, of which 5 were waited for; matrix products, arithmetic and copies ran while one was open for 0% of the time, Pallas kernels for 15%

profile of v17, /device:TPU:11, one launch (start us, length us, event | category | flops | bytes accessed | tf_op | source)
XLA Modules:
  0.0 16.5 jit_solution(5420524380811211277)
XLA Ops:
  0.0 0.0 copy-start
  0.0 0.0 copy-start.2
  0.0 0.0 copy-start.1
  0.0 1.2 %shard_map.38 = (bf16[32,1024]{1,0:T(8,128)(2,1)S(1)}, bf16[32,1024]{1,0:T(8,128)(2,1)S(1)}, bf16[32,1024]{1,0:T(8,128)(2,1)S(1)}, bf16[8,1024]{1,0:T(8,128)(2,1)S(1)}) custom-call(s32[2,8,32,1024]{3,2,1,0:T(8,128)} %volume_ref.7), custom_call_target="tpu_custom_call" | custom-call | tf_op jit(solution)/shard_map/pallas_call | solution.py:79
  1.2 0.7 %collective-permute-start = (bf16[32,1024]{1,0:T(8,128)(2,1)S(1)}, bf16[32,1024]{1,0:T(8,128)(2,1)S(1)}, u32[]{:S(2)}, u32[]{:S(2)}) collective-permute-start(bf16[32,1024]{1,0:T(8,128)(2,1)S(1)} %get-tuple-element.25), channel_id=1, source_target_pairs={{0,28},{1,5},{2,30},{3,7},{4,8},{5,1},{6,10},{7,3},{8,4},{9,13},{1... | collective-permute-start | bytes 196616 | tf_op jit(solution)/shard_map/ppermute | solution.py:532
  1.9 1.3 %collective-permute-start.1 = (bf16[32,1024]{1,0:T(8,128)(2,1)S(1)}, bf16[32,1024]{1,0:T(8,128)(2,1)S(1)}, u32[]{:S(2)}, u32[]{:S(2)}) collective-permute-start(bf16[32,1024]{1,0:T(8,128)(2,1)S(1)} %get-tuple-element.28), channel_id=1, source_target_pairs={{0,1},{1,0},{2,3},{3,2},{4,5},{5,4},{6,7},{7,6},{8,9},{9,8},{10,11... | collective-permute-start | bytes 196616 | tf_op jit(solution)/shard_map/ppermute | solution.py:532
  3.2 1.2 %collective-permute-start.2 = (bf16[32,1024]{1,0:T(8,128)(2,1)S(1)}, bf16[32,1024]{1,0:T(8,128)(2,1)S(1)}, u32[]{:S(2)}, u32[]{:S(2)}) collective-permute-start(bf16[32,1024]{1,0:T(8,128)(2,1)S(1)} %get-tuple-element.29), channel_id=1, source_target_pairs={{0,4},{1,29},{2,6},{3,31},{4,0},{5,9},{6,2},{7,11},{8,12},{9,5},{1... | collective-permute-start | bytes 196616 | tf_op jit(solution)/shard_map/ppermute | solution.py:532
  4.4 0.5 %collective-permute-start.3 = (bf16[8,1024]{1,0:T(8,128)(2,1)S(1)}, bf16[8,1024]{1,0:T(8,128)(2,1)S(1)}, u32[]{:S(2)}, u32[]{:S(2)}) collective-permute-start(bf16[8,1024]{1,0:T(8,128)(2,1)S(1)} %get-tuple-element.30), channel_id=1, source_target_pairs={{0,4},{1,2},{2,1},{3,7},{4,0},{5,6},{6,5},{7,3},{8,12},{9,10},{10,... | collective-permute-start | bytes 49160 | tf_op jit(solution)/shard_map/ppermute | solution.py:532
  4.9 0.0 copy-done
  4.9 0.0 copy-done.2
  4.9 0.0 copy-done.1
  4.9 2.3 %shard_map.37 = (f32[4,32,1024]{2,1,0:T(8,128)S(1)}, f32[2,32,1024]{2,1,0:T(8,128)S(1)}, f32[2,32,1024]{2,1,0:T(8,128)S(1)}, f32[2,3,32,1024]{3,2,1,0:T(8,128)S(...) custom-call(s32[2,8,32,1024]{3,2,1,0:T(8,128)S(1)} %copy-done, s32[3,256]{1,0:T(4,128)S(1)} %copy-done.1, ...), custom_call_target="tpu_custom_call" | custom-call | flops 20971520 | bytes 5242880 | tf_op jit(solution)/shard_map/pallas_call | solution.py:275
  7.2 0.0 collective-permute-done.first_ref
  7.2 0.1 shard_map.39.sums_ref
  7.4 0.0 collective-permute-done.3.rows_far_ref
  7.4 0.0 collective-permute-done.1.rows_near_ref
  7.4 0.4 %collective-permute-done.2.second_ref = bf16[32,1024]{1,0:T(8,128)(2,1)S(1)} collective-permute-done((bf16[32,1024]{1,0:T(8,128)(2,1)S(1)}, bf16[32,1024]{1,0:T(8,128)(2,1)S(1)}, u32[]{:S(2)}, u32[]{:S(2)}) %collective-permute-start.2) | collective-permute-done | bytes 65568 | tf_op jit(solution)/shard_map/ppermute | solution.py:532
  7.8 0.3 %shard_map.40 = (f32[4,16,1024]{2,1,0:T(8,128)S(1)}, bf16[4,16,1024]{2,1,0:T(8,128)(2,1)S(1)}) custom-call(s32[2,8,32,1024]{3,2,1,0:T(8,128)S(1)} %copy-done, f32[3,32,1024]{2,1,0:T(8,128)S(1)} %shard_map.39.sums_ref, f32[4,32,1024]{2,1,0:T(8,128)S(1)} %get-tuple-element.21.base_ref, f32[2,32,1024]{2,1,0:T(8,128)S(1)} %get-tuple-element.22.face_ref, ...), custom_call_target="tpu_custom_call" | custom-call | tf_op jit(solution)/shard_map/pallas_call | solution.py:419
  8.1 0.1 collective-permute-start.4
  8.2 1.3 %collective-permute-done.4.other_ref = bf16[4,16,1024]{2,1,0:T(8,128)(2,1)S(1)} collective-permute-done((bf16[4,16,1024]{2,1,0:T(8,128)(2,1)S(1)}, bf16[4,16,1024]{2,1,0:T(8,128)(2,1)S(1)}, u32[]{:S(2)}, u32[]{:S(2)}) %collective-permute-start.4) | collective-permute-done | bytes 131104 | tf_op jit(solution)/shard_map/ppermute | solution.py:536
  9.5 0.1 shard_map.41
  9.6 1.9 %collective-permute-start.5 = (bf16[16,1024]{1,0:T(8,128)(2,1)S(1)}, bf16[16,1024]{1,0:T(8,128)(2,1)S(1)}, u32[]{:S(2)}, u32[]{:S(2)}) collective-permute-start(bf16[16,1024]{1,0:T(8,128)(2,1)S(1)} %get-tuple-element.33), channel_id=1, source_target_pairs={{0,28},{4,24},{8,20},{12,16},{16,12},{20,8},{24,4},{28,0},{1,29},{... | collective-permute-start | bytes 98312 | tf_op jit(solution)/shard_map/ppermute | solution.py:536
  11.4 1.0 %collective-permute-start.6 = (bf16[16,1024]{1,0:T(8,128)(2,1)S(1)}, bf16[16,1024]{1,0:T(8,128)(2,1)S(1)}, u32[]{:S(2)}, u32[]{:S(2)}) collective-permute-start(bf16[16,1024]{1,0:T(8,128)(2,1)S(1)} %get-tuple-element.34), channel_id=1, source_target_pairs={{0,20},{4,16},{8,28},{12,24},{16,4},{20,0},{24,12},{28,8},{1,21},{... | collective-permute-start | bytes 98312 | tf_op jit(solution)/shard_map/ppermute | solution.py:536
  12.5 0.2 collective-permute-start.7
  12.6 1.3 %collective-permute-done.5.refs_0_ = bf16[16,1024]{1,0:T(8,128)(2,1)S(1)} collective-permute-done((bf16[16,1024]{1,0:T(8,128)(2,1)S(1)}, bf16[16,1024]{1,0:T(8,128)(2,1)S(1)}, u32[]{:S(2)}, u32[]{:S(2)}) %collective-permute-start.5) | collective-permute-done | bytes 32800 | tf_op jit(solution)/shard_map/ppermute | solution.py:536
  13.9 0.9 %collective-permute-done.6.refs_1_ = bf16[16,1024]{1,0:T(8,128)(2,1)S(1)} collective-permute-done((bf16[16,1024]{1,0:T(8,128)(2,1)S(1)}, bf16[16,1024]{1,0:T(8,128)(2,1)S(1)}, u32[]{:S(2)}, u32[]{:S(2)}) %collective-permute-start.6) | collective-permute-done | bytes 32800 | tf_op jit(solution)/shard_map/ppermute | solution.py:536
  14.8 1.0 %collective-permute-done.7.refs_2_ = bf16[16,1024]{1,0:T(8,128)(2,1)S(1)} collective-permute-done((bf16[16,1024]{1,0:T(8,128)(2,1)S(1)}, bf16[16,1024]{1,0:T(8,128)(2,1)S(1)}, u32[]{:S(2)}, u32[]{:S(2)}) %collective-permute-start.7) | collective-permute-done | bytes 32800 | tf_op jit(solution)/shard_map/ppermute | solution.py:536
  15.8 0.7 %shard_map.42 = f32[4,4,1024]{2,1,0:T(4,128)} custom-call(bf16[16,1024]{1,0:T(8,128)(2,1)S(1)} %collective-permute-done.5.refs_0_, bf16[16,1024]{1,0:T(8,128)(2,1)S(1)} %collective-permute-done.6.refs_1_, bf16[16,1024]{1,0:T(8,128)(2,1)S(1)} %collective-permute-done.7.refs_2_, f32[16,1024]{1,0:T(8,128)S(1)} %get-tuple-element.36.refs_3_), custom_call_target="tpu_custom_call" | custom-call | tf_op jit(solution)/shard_map/pallas_call | solution.py:480
Async XLA Ops:
  0.0 4.9 %copy-start = (s32[2,8,32,1024]{3,2,1,0:T(8,128)S(1)}, s32[2,8,32,1024]{3,2,1,0:T(8,128)}, u32[]{:S(2)}) copy-start(s32[2,8,32,1024]{3,2,1,0:T(8,128)} %volume_ref.7) | copy-start | bytes 6291460
  0.0 4.9 %copy-start.2 = (s32[256]{0:T(256)S(1)}, s32[256]{0:T(256)}, u32[]{:S(2)}) copy-start(s32[256]{0:T(256)} %param.5) | copy-start | bytes 3076
  0.0 4.9 %copy-start.1 = (s32[3,256]{1,0:T(4,128)S(1)}, s32[3,256]{1,0:T(4,128)}, u32[]{:S(2)}) copy-start(s32[3,256]{1,0:T(4,128)} %color_ref.1) | copy-start | bytes 9220
  1.2 6.0 %collective-permute-start = (bf16[32,1024]{1,0:T(8,128)(2,1)S(1)}, bf16[32,1024]{1,0:T(8,128)(2,1)S(1)}, u32[]{:S(2)}, u32[]{:S(2)}) collective-permute-start(bf16[32,1024]{1,0:T(8,128)(2,1)S(1)} %get-tuple-element.25), channel_id=1, source_target_pairs={{0,28},{1,5},{2,30},{3,7},{4,8},{5,1},{6,10},{7,3},{8,4},{9,13},{1... | collective-permute-start | bytes 196616 | tf_op jit(solution)/shard_map/ppermute | solution.py:532
  1.9 5.4 %collective-permute-start.1 = (bf16[32,1024]{1,0:T(8,128)(2,1)S(1)}, bf16[32,1024]{1,0:T(8,128)(2,1)S(1)}, u32[]{:S(2)}, u32[]{:S(2)}) collective-permute-start(bf16[32,1024]{1,0:T(8,128)(2,1)S(1)} %get-tuple-element.28), channel_id=1, source_target_pairs={{0,1},{1,0},{2,3},{3,2},{4,5},{5,4},{6,7},{7,6},{8,9},{9,8},{10,11... | collective-permute-start | bytes 196616 | tf_op jit(solution)/shard_map/ppermute | solution.py:532
  3.2 4.6 %collective-permute-start.2 = (bf16[32,1024]{1,0:T(8,128)(2,1)S(1)}, bf16[32,1024]{1,0:T(8,128)(2,1)S(1)}, u32[]{:S(2)}, u32[]{:S(2)}) collective-permute-start(bf16[32,1024]{1,0:T(8,128)(2,1)S(1)} %get-tuple-element.29), channel_id=1, source_target_pairs={{0,4},{1,29},{2,6},{3,31},{4,0},{5,9},{6,2},{7,11},{8,12},{9,5},{1... | collective-permute-start | bytes 196616 | tf_op jit(solution)/shard_map/ppermute | solution.py:532
  4.4 3.0 %collective-permute-start.3 = (bf16[8,1024]{1,0:T(8,128)(2,1)S(1)}, bf16[8,1024]{1,0:T(8,128)(2,1)S(1)}, u32[]{:S(2)}, u32[]{:S(2)}) collective-permute-start(bf16[8,1024]{1,0:T(8,128)(2,1)S(1)} %get-tuple-element.30), channel_id=1, source_target_pairs={{0,4},{1,2},{2,1},{3,7},{4,0},{5,6},{6,5},{7,3},{8,12},{9,10},{10,... | collective-permute-start | bytes 49160 | tf_op jit(solution)/shard_map/ppermute | solution.py:532
  8.1 1.4 %collective-permute-start.4 = (bf16[4,16,1024]{2,1,0:T(8,128)(2,1)S(1)}, bf16[4,16,1024]{2,1,0:T(8,128)(2,1)S(1)}, u32[]{:S(2)}, u32[]{:S(2)}) collective-permute-start(bf16[4,16,1024]{2,1,0:T(8,128)(2,1)S(1)} %get-tuple-element.32), channel_id=1, source_target_pairs={{0,4},{4,0},{8,12},{12,8},{16,20},{20,16},{24,28},{28,24},{1,5},{5... | collective-permute-start | bytes 393224 | tf_op jit(solution)/shard_map/ppermute | solution.py:536
  9.6 4.3 %collective-permute-start.5 = (bf16[16,1024]{1,0:T(8,128)(2,1)S(1)}, bf16[16,1024]{1,0:T(8,128)(2,1)S(1)}, u32[]{:S(2)}, u32[]{:S(2)}) collective-permute-start(bf16[16,1024]{1,0:T(8,128)(2,1)S(1)} %get-tuple-element.33), channel_id=1, source_target_pairs={{0,28},{4,24},{8,20},{12,16},{16,12},{20,8},{24,4},{28,0},{1,29},{... | collective-permute-start | bytes 98312 | tf_op jit(solution)/shard_map/ppermute | solution.py:536
  11.4 3.3 %collective-permute-start.6 = (bf16[16,1024]{1,0:T(8,128)(2,1)S(1)}, bf16[16,1024]{1,0:T(8,128)(2,1)S(1)}, u32[]{:S(2)}, u32[]{:S(2)}) collective-permute-start(bf16[16,1024]{1,0:T(8,128)(2,1)S(1)} %get-tuple-element.34), channel_id=1, source_target_pairs={{0,20},{4,16},{8,28},{12,24},{16,4},{20,0},{24,12},{28,8},{1,21},{... | collective-permute-start | bytes 98312 | tf_op jit(solution)/shard_map/ppermute | solution.py:536
  12.5 3.3 %collective-permute-start.7 = (bf16[16,1024]{1,0:T(8,128)(2,1)S(1)}, bf16[16,1024]{1,0:T(8,128)(2,1)S(1)}, u32[]{:S(2)}, u32[]{:S(2)}) collective-permute-start(bf16[16,1024]{1,0:T(8,128)(2,1)S(1)} %get-tuple-element.35), channel_id=1, source_target_pairs={{0,12},{4,8},{8,4},{12,0},{16,28},{20,24},{24,20},{28,16},{1,13},{... | collective-permute-start | bytes 98312 | tf_op jit(solution)/shard_map/ppermute | solution.py:536
